TPU v7x, 32 devices: a whole 2x2x4 slice. The times are simulated.
32 devices in a mesh: blk: 16 (over z, y, x), fld: 2 (over core).
Axes of the slice: x: 2, y: 2, z: 4, core: 2. Of those that a mesh axis runs over, the one named last changes fastest.
Arguments:
- seed_fine: float32 [8, 128, 4096], P('fld', 'blk'), may hold values from -6 to 6
- seed_coarse: float32 [8, 32, 4096], P('fld', 'blk'), may hold values from -6 to 6
- saved_fine: float32 [4, 8, 128, 4096], P(None, 'fld', 'blk'), may hold values from 0.5 to 2
- saved_coarse: float32 [2, 8, 32, 4096], P(None, 'fld', 'blk'), may hold values from 0.5 to 2
- diffusion: float32 [8], P('fld'), may hold values from 0.02 to 0.15
- species_shares: float32 [8], P('fld'), may hold values from 0.1 to 1
- fine_nbr: int32 [128, 6], P('blk'), may hold values from -1 to 127, as said below
- coarse_nbr: int32 [32, 6], P('blk'), may hold values from -1 to 31, as said below
- children: int32 [32, 8], P('blk'), may hold values from -1 to 127, as said below
- fine_counts: int32 [128], P('blk'), may hold values from 1 to 4
- coarse_counts: int32 [32], P('blk'), may hold values from 1 to 4
Outputs:
- adj_fine: float32 [8, 128, 4096], P('fld', 'blk')
- adj_coarse: float32 [8, 32, 4096], P('fld', 'blk')
Inputs may be any that keep to these rules, and one draw needn't show every extreme that they name: `fine_nbr`: slot of the block beside each face (first and last along cell dimensions 0, 1, 2), -1 at a wall. The relation is symmetric with faces 2a and 2a+1 paired. Across faces 0 to 3 the neighbour is held by the same index of blk, across face 4 by the same or the one below, across face 5 by the same or the one above. `coarse_nbr`: as for the fine level: symmetric, faces 2a and 2a+1 paired; across faces 0 to 3 the same index of blk, across face 4 the same or the one below, across face 5 the same or the one above. `children`: the fine block that refines each coarse octant, or -1. Every fine block refines exactly one octant. The octants held by index i of blk that are refined are refined by blocks of the indices i + d modulo 16 for d = 0 .. 7, exactly 1 of them by the blocks of each such index.
All inputs are finite; a program needn't handle non-finite values.
Results may differ from a plain program's by a relative error of at most 0.0003.
Values sent between devices are 32-bit elements; how exact they have to be, the bound alone decides.
No kernel may reach another device: no remote copies, remote signals or barrier semaphores. Data moves between devices by JAX's collectives and lax.ppermute only.
A program may use at most 128 MiB of HBM per device.

v0:
```python
import jax
import jax.numpy as jnp
from jax import lax
from jax.sharding import PartitionSpec as P

B = 16
NSUB = 4
CYCLES = 2


heat_gain = 0.5
energy = 2.0
precise = lax.Precision.HIGHEST


def shifted(value, axis, steps):
    count = lax.axis_size(axis)
    leading, last = (max(0, -steps), min(count, count - steps))
    return lax.ppermute(value, axis, [(source, source + steps) for source in range(leading, last)])


def broadcast(value, axis, source):
    kept = jnp.where(lax.axis_index(axis) == source, value, 0).astype(value.dtype)
    return lax.psum(kept, axis)


def shifted_2(block, axis, distance):
    devices = range(lax.axis_size(axis))
    route = [((i - distance) % len(devices), i) for i in devices]
    return lax.ppermute(block, axis, route)


def cell_coords():
    cells = jnp.arange(B**3, dtype=jnp.int32)
    return (cells // (B * B), cells // B % B, cells % B)


def middle_table(layer):
    plane = jnp.arange(B * B, dtype=jnp.int32)
    return (
        (plane[:, None] // B == layer)
        & (plane[:, None] % B == jnp.arange(B, dtype=jnp.int32)[None, :])
    ).astype(jnp.float32)


def inner_table(layer):
    plane = jnp.arange(B * B, dtype=jnp.int32)
    return (
        (plane[:, None] % B == layer)
        & (plane[:, None] // B == jnp.arange(B, dtype=jnp.int32)[None, :])
    ).astype(jnp.float32)


def face_list(flat):
    fields, blocks = (flat.shape[0], flat.shape[1])
    planes = flat.reshape(fields, blocks, B, B * B)
    first = flat[:, :, : B * B].reshape(fields, blocks, B, B)
    last = flat[:, :, -B * B :].reshape(fields, blocks, B, B)
    result = [first, last]
    for table in (middle_table(0), middle_table(B - 1), inner_table(0), inner_table(B - 1)):
        result.append(jnp.dot(planes, table, precision=precise))
    return result


def place_ghost(ghost, table):
    fields, blocks = (ghost.shape[0], ghost.shape[1])
    return jnp.dot(ghost, table.T, precision=precise).reshape(fields, blocks, B**3)


def with_ghosts(flat, ghosts):
    fields, blocks = (flat.shape[0], flat.shape[1])
    plane = B * B
    zeros_plane = jnp.zeros((fields, blocks, plane), jnp.float32)
    zeros_rest = jnp.zeros((fields, blocks, B**3 - plane), jnp.float32)
    zeros_row = jnp.zeros((fields, blocks, B), jnp.float32)
    zeros_one = jnp.zeros((fields, blocks, 1), jnp.float32)
    cell_i, cell_j, cell_k = cell_coords()
    j_low = (cell_j != 0).astype(jnp.float32)
    j_high = (cell_j != B - 1).astype(jnp.float32)
    k_low = (cell_k != 0).astype(jnp.float32)
    k_high = (cell_k != B - 1).astype(jnp.float32)
    ghost_first = jnp.concatenate([ghosts[0].reshape(fields, blocks, plane), zeros_rest], axis=2)
    ghost_last = jnp.concatenate([zeros_rest, ghosts[1].reshape(fields, blocks, plane)], axis=2)
    running = -6.0 * flat
    running = running + (jnp.concatenate([zeros_plane, flat[:, :, :-plane]], axis=2) + ghost_first)
    running = running + (jnp.concatenate([flat[:, :, plane:], zeros_plane], axis=2) + ghost_last)
    running = running + (
        jnp.concatenate([zeros_row, flat[:, :, :-B]], axis=2) * j_low
        + place_ghost(ghosts[2], middle_table(0))
    )
    running = running + (
        jnp.concatenate([flat[:, :, B:], zeros_row], axis=2) * j_high
        + place_ghost(ghosts[3], middle_table(B - 1))
    )
    running = running + (
        jnp.concatenate([zeros_one, flat[:, :, :-1]], axis=2) * k_low
        + place_ghost(ghosts[4], inner_table(0))
    )
    running = running + (
        jnp.concatenate([flat[:, :, 1:], zeros_one], axis=2) * k_high
        + place_ghost(ghosts[5], inner_table(B - 1))
    )
    return running


def pick_rows(candidates, position, present):
    fields = candidates.shape[0]
    row_count = candidates.shape[1]
    onehot = (
        (position[:, None] == jnp.arange(row_count, dtype=jnp.int32)[None, :]) & present[:, None]
    ).astype(jnp.float32)
    flat_rows = candidates.reshape(fields, row_count, B * B)
    chosen = jnp.einsum("br,wrf->wbf", onehot, flat_rows, precision=precise)
    return chosen.reshape(fields, position.shape[0], B, B)


def ghost_faces(faces, neighbours, refinement_rank):
    blocks = neighbours.shape[0]
    own_base = lax.axis_index("blk") * blocks
    present = neighbours >= 0
    if refinement_rank == "fine":
        from_below = shifted(faces[5], "blk", 1)
        from_above = shifted(faces[4], "blk", -1)
    else:
        from_below = shifted(faces[5], "blk", 1)
        from_above = shifted(faces[4], "blk", -1)
    position = neighbours - own_base
    result = [
        pick_rows(faces[face_no ^ 1], position[:, face_no], present[:, face_no])
        for face_no in range(4)
    ]
    result.append(
        pick_rows(
            jnp.concatenate([from_below, faces[5]], axis=1), position[:, 4] + blocks, present[:, 4]
        )
    )
    result.append(
        pick_rows(jnp.concatenate([faces[4], from_above], axis=1), position[:, 5], present[:, 5])
    )
    return result


def laplace(flat, neighbours, refinement_rank):
    ghosts = ghost_faces(face_list(flat), neighbours, refinement_rank)
    return with_ghosts(flat, ghosts)


def diffuse_adjoint(costate_values, neighbours, rates, refinement_rank):
    first = rates * laplace(costate_values, neighbours, refinement_rank)
    second = rates * laplace(first, neighbours, refinement_rank)
    return costate_values + first + 0.5 * second


def exothermic_sources(thermal_costate, thermal_profile, tally_grid, blend_aggregate):
    substep = 1.0 / tally_grid.astype(jnp.float32)[:, None]
    history = []
    present_refinement = thermal_profile
    for counter in range(NSUB):
        history.append(present_refinement)
        active = (counter < tally_grid)[:, None]
        present_refinement = present_refinement + jnp.where(
            active,
            substep * heat_gain * blend_aggregate * jnp.exp(-energy / present_refinement),
            0.0,
        )
    remainder_passed = thermal_costate
    scaling_coefficient = jnp.zeros_like(thermal_costate)
    for counter in reversed(range(NSUB)):
        earlier = history[counter]
        active = (counter < tally_grid)[:, None]
        decay = jnp.exp(-energy / earlier)
        scaling_coefficient = scaling_coefficient + jnp.where(
            active, substep * heat_gain * decay * remainder_passed, 0.0
        )
        remainder_passed = jnp.where(
            active,
            remainder_passed
            * (1.0 + substep * heat_gain * blend_aggregate * energy * decay / (earlier * earlier)),
            remainder_passed,
        )
    return (remainder_passed, scaling_coefficient)


def reaction_adjoint(
    costate_values, thermal_profile, tally_grid, blend_aggregate, species_shares, refinement_rank
):
    remainder_passed, scaling_coefficient = exothermic_sources(
        costate_values[0], thermal_profile, tally_grid, blend_aggregate
    )
    if refinement_rank == "fine":
        scaling_coefficient = broadcast(scaling_coefficient, "fld", 0)
    else:
        scaling_coefficient = broadcast(scaling_coefficient, "fld", 0)
    leading = jnp.where(lax.axis_index("fld") == 0, remainder_passed, costate_values[0])
    costate_values = jnp.concatenate([leading[None], costate_values[1:]], axis=0)
    return costate_values + species_shares[:, None, None] * scaling_coefficient[None]


def restrict_adjoint(fine_adj, coarse_adj, children):
    fields = coarse_adj.shape[0]
    count_c = coarse_adj.shape[1]
    count_f = fine_adj.shape[1]
    half_edge = B // 2
    shaped = coarse_adj.reshape(fields, count_c, 2, half_edge, 2, half_edge, 2, half_edge)
    octants = shaped.transpose(1, 2, 4, 6, 0, 3, 5, 7).reshape(count_c * 8, fields * half_edge**3)
    width = octants.shape[1]
    flat_child = children.reshape(-1)
    present = flat_child >= 0
    own_index = lax.axis_index("blk")
    own_ids = (own_index * count_f + jnp.arange(count_f, dtype=jnp.int32)).astype(jnp.float32)
    devices = lax.axis_size("blk")
    links = min(count_f, devices)
    per_link = count_f // links
    target = jnp.where(present, flat_child // count_f, own_index)
    offset = (target - own_index) % devices
    serial = jnp.arange(count_c * 8, dtype=jnp.int32)
    earlier = (
        (offset[None, :] == offset[:, None])
        & (serial[None, :] < serial[:, None])
        & present[None, :]
    )
    place_in = jnp.sum(earlier.astype(jnp.int32), axis=1)
    row_index = offset * per_link + place_in
    placing = (
        (row_index[None, :] == jnp.arange(count_f, dtype=jnp.int32)[:, None]) & present[None, :]
    ).astype(jnp.float32)
    outgoing = jnp.dot(placing, octants, precision=precise).reshape(links, per_link, width)
    out_labels = jnp.dot(placing, flat_child.astype(jnp.float32), precision=precise).reshape(
        links, per_link
    )
    values_list = [outgoing[0]]
    labels_list = [out_labels[0]]
    for distance in range(1, links):
        moved, moved_labels = shifted_2((outgoing[distance], out_labels[distance]), "blk", distance)
        values_list.append(moved)
        labels_list.append(moved_labels)
    incoming = jnp.stack(values_list, axis=0)
    in_labels = jnp.stack(labels_list, axis=0)
    incoming = incoming.reshape(count_f, width)
    in_labels = in_labels.reshape(count_f)
    match = (own_ids[:, None] == in_labels[None, :]).astype(jnp.float32)
    arrived = jnp.dot(match, incoming, precision=precise)
    arrived = arrived.reshape(count_f, fields, half_edge**3).transpose(1, 0, 2)
    cell_i, cell_j, cell_k = cell_coords()
    parent_cell = cell_i // 2 * half_edge * half_edge + cell_j // 2 * half_edge + cell_k // 2
    spread = (parent_cell[None, :] == jnp.arange(half_edge**3, dtype=jnp.int32)[:, None]).astype(
        jnp.float32
    ) * 0.125
    fine_adj = fine_adj + jnp.dot(arrived, spread, precision=precise)
    octant_of_cell = 4 * (cell_i // half_edge) + 2 * (cell_j // half_edge) + cell_k // half_edge
    octant_onehot = (octant_of_cell[None, :] == jnp.arange(8, dtype=jnp.int32)[:, None]).astype(
        jnp.float32
    )
    keeping = jnp.dot(
        (flat_child < 0).astype(jnp.float32).reshape(count_c, 8), octant_onehot, precision=precise
    )
    coarse_adj = coarse_adj * keeping[None]
    return (fine_adj, coarse_adj)


def shards(
    seed_fine,
    seed_coarse,
    saved_fine,
    saved_coarse,
    diffusion,
    species_shares,
    fine_nbr,
    coarse_nbr,
    children,
    fine_counts,
    coarse_counts,
):
    fields = seed_fine.shape[0]
    partial_f = jnp.sum(species_shares[None, :, None, None] * saved_fine, axis=1)
    partial_c = jnp.sum(species_shares[None, :, None, None] * saved_coarse, axis=1)
    mix_fine, mix_coarse = lax.psum((partial_f, partial_c), "fld")
    fine_adj = seed_fine
    coarse_adj = seed_coarse
    fine_rates = diffusion.reshape(fields, 1, 1)
    coarse_rates = 0.5 * fine_rates
    for sweep_no in reversed(range(CYCLES)):
        fine_adj, coarse_adj = restrict_adjoint(fine_adj, coarse_adj, children)
        for stepno in (2 * sweep_no + 1, 2 * sweep_no):
            flat_fine = reaction_adjoint(
                fine_adj,
                saved_fine[stepno, 0],
                fine_counts,
                mix_fine[stepno],
                species_shares,
                "fine",
            )
            fine_adj = diffuse_adjoint(flat_fine, fine_nbr, fine_rates, "fine")
        flat_coarse = reaction_adjoint(
            coarse_adj,
            saved_coarse[sweep_no, 0],
            coarse_counts,
            mix_coarse[sweep_no],
            species_shares,
            "coarse",
        )
        coarse_adj = diffuse_adjoint(flat_coarse, coarse_nbr, coarse_rates, "coarse")
    return (fine_adj, coarse_adj)


def solution(mesh):
    return jax.shard_map(
        shards,
        mesh=mesh,
        in_specs=(
            P("fld", "blk", None),
            P("fld", "blk", None),
            P(None, "fld", "blk", None),
            P(None, "fld", "blk", None),
            P("fld"),
            P("fld"),
            P("blk", None),
            P("blk", None),
            P("blk", None),
            P("blk"),
            P("blk"),
        ),
        out_specs=(P("fld", "blk", None), P("fld", "blk", None)),
        check_vma=False,
    )
```

profile of v0, /device:TPU:0, one launch (start us, length us, event | category | flops | bytes accessed | tf_op | source)
XLA Modules:
  0.0 534.3 jit_solution(10789503541042070026)
XLA Ops:
  37.8 4.9 collective-permute-done.1
  43.3 5.8 %collective-permute-done.2 = f32[1]{0:T(128)} collective-permute-done((f32[1]{0:T(128)}, f32[1]{0:T(128)}, u32[]{:S(2)}, u32[]{:S(2)}) %collective-permute-start.2) | collective-permute-done | bytes 36 | tf_op jit(solution)/shard_map/ppermute | solution.py:30
  49.1 5.7 %collective-permute-done.3 = f32[1]{0:T(128)} collective-permute-done((f32[1]{0:T(128)}, f32[1]{0:T(128)}, u32[]{:S(2)}, u32[]{:S(2)}) %collective-permute-start.3) | collective-permute-done | bytes 36 | tf_op jit(solution)/shard_map/ppermute | solution.py:30
  55.6 5.5 %collective-permute-done.4 = f32[1]{0:T(128)} collective-permute-done((f32[1]{0:T(128)}, f32[1]{0:T(128)}, u32[]{:S(2)}, u32[]{:S(2)}) %collective-permute-start.4) | collective-permute-done | bytes 36 | tf_op jit(solution)/shard_map/ppermute | solution.py:30
  72.2 5.0 stack.87
  86.2 5.6 %fusion.6 = f32[4,8,4096]{2,1,0:T(8,128)S(1)} fusion(f32[4,8,4096]{2,1,0:T(8,128)S(1)} %copy-done.165, f32[4,8,512]{2,1,0:T(8,128)S(1)} %convolution_bitcast_fusion.1, s32[4096]{0:T(1024)S(1)} %fusion.145), kind=kOutput, calls=%fused_computation.7 | convolution fusion | flops 809631744 | bytes 1130496 | tf_op jit(solution)/shard_map/dot_general | solution.py:249
  95.5 18.2 %all-reduce.105.cloned.1.call-done = f32[8,4096]{1,0:T(8,128)} async-done(((f32[8,4096]{1,0:T(8,128)}), f32[8,4096]{1,0:T(8,128)}) %all-reduce.105.cloned.1.call-update) | async-done | bytes 131088 | tf_op jit(solution)/shard_map/psum | solution.py:24
  121.7 5.4 %collective-permute-start.14 = (f32[4,8,16,16]{3,2,1,0:T(8,128)}, f32[4,8,16,16]{3,2,1,0:T(8,128)}, u32[]{:S(2)}, u32[]{:S(2)}) collective-permute-start(f32[4,8,16,16]{3,2,1,0:T(8,128)} %fusion.398), channel_id=1, source_target_pairs={{0,2},{2,4},{4,6},{6,8},{8,10},{10,12},{12,14},{14,16},{16,18},{18... | collective-permute-start | bytes 98312 | tf_op jit(solution)/shard_map/ppermute | solution.py:19
  150.4 5.7 %collective-permute-start.16 = (f32[4,8,16,16]{3,2,1,0:T(8,128)}, f32[4,8,16,16]{3,2,1,0:T(8,128)}, u32[]{:S(2)}, u32[]{:S(2)}) collective-permute-start(f32[4,8,16,16]{3,2,1,0:T(8,128)} %fusion.44), channel_id=1, source_target_pairs={{0,2},{2,4},{4,6},{6,8},{8,10},{10,12},{12,14},{14,16},{16,18},{18... | collective-permute-start | bytes 98312 | tf_op jit(solution)/shard_map/ppermute | solution.py:19
  177.3 17.8 %all-reduce.111.cloned.1.call-done = (f32[2,2,4096]{2,1,0:T(2,128)}, f32[8,4096]{1,0:T(8,128)}) async-done(((f32[2,2,4096]{2,1,0:T(2,128)}, f32[8,4096]{1,0:T(8,128)}), (f32[2,2,4096]{2,1,0:T(2,128)}, f32[8,4096]{1,0:T(8,128)})) %all-reduce.111.cloned.1.call-update) | async-done | bytes 196624 | tf_op jit(solution)/shard_map/psum | solution.py:277
  214.9 5.2 collective-permute-start.22
  223.2 5.4 %collective-permute-start.18 = (f32[4,8,16,16]{3,2,1,0:T(8,128)}, f32[4,8,16,16]{3,2,1,0:T(8,128)}, u32[]{:S(2)}, u32[]{:S(2)}) collective-permute-start(f32[4,8,16,16]{3,2,1,0:T(8,128)} %fusion.391), channel_id=1, source_target_pairs={{0,2},{2,4},{4,6},{6,8},{8,10},{10,12},{12,14},{14,16},{16,18},{18... | collective-permute-start | bytes 98312 | tf_op jit(solution)/shard_map/ppermute | solution.py:19
  242.7 4.9 collective-permute-start.24
  278.3 5.2 collective-permute-done.42
  283.4 4.8 collective-permute-start.41
  311.6 5.8 %collective-permute-start.43 = (f32[4,2,16,16]{3,2,1,0:T(8,128)}, f32[4,2,16,16]{3,2,1,0:T(8,128)}, u32[]{:S(2)}, u32[]{:S(2)}) collective-permute-start(f32[4,2,16,16]{3,2,1,0:T(8,128)} %fusion.360), channel_id=1, source_target_pairs={{0,2},{2,4},{4,6},{6,8},{8,10},{10,12},{12,14},{14,16},{16,18},{18... | collective-permute-start | bytes 24584 | tf_op jit(solution)/shard_map/ppermute | solution.py:19
  335.4 5.6 %collective-permute-start.20 = (f32[4,8,16,16]{3,2,1,0:T(8,128)S(1)}, f32[4,8,16,16]{3,2,1,0:T(8,128)}, u32[]{:S(2)}, u32[]{:S(2)}) collective-permute-start(f32[4,8,16,16]{3,2,1,0:T(8,128)S(1)} %fusion.36), channel_id=1, source_target_pairs={{0,2},{2,4},{4,6},{6,8},{8,10},{10,12},{12,14},{14,16},{16,18},{18... | collective-permute-start | bytes 98312 | tf_op jit(solution)/shard_map/ppermute | solution.py:19
  361.1 7.4 %fusion.9 = f32[4,8,4096]{2,1,0:T(8,128)S(1)} fusion(f32[4,8,512]{2,1,0:T(8,128)S(1)} %copy-done.35, s32[4096]{0:T(1024)S(1)} %copy-done.60, f32[4,8,4096]{2,1,0:T(8,128)S(1)} %copy-done.16, f32[4,8,4095]{2,1,0:T(8,128)} %get-tuple-element.59, f32[4,8,4096]{2,1,0:T(8,128)} %reshape.1312, f32[4,8,4095]{2,1,0:T(8,128)} %get-tuple-element.58, ...), kind=kOutput, calls=%fused_computation.8 | convolution fusion | flops 812384256 | bytes 6958864 | tf_op jit(solution)/shard_map/dot_general | solution.py:249
  372.0 18.7 %all-reduce.107.cloned.1.call-done = f32[8,4096]{1,0:T(8,128)} async-done(((f32[8,4096]{1,0:T(8,128)}), f32[8,4096]{1,0:T(8,128)}) %all-reduce.107.cloned.1.call-update) | async-done | bytes 131088 | tf_op jit(solution)/shard_map/psum | solution.py:24
  398.6 5.4 %collective-permute-start.33 = (f32[4,8,16,16]{3,2,1,0:T(8,128)S(1)}, f32[4,8,16,16]{3,2,1,0:T(8,128)}, u32[]{:S(2)}, u32[]{:S(2)}) collective-permute-start(f32[4,8,16,16]{3,2,1,0:T(8,128)S(1)} %fusion.377), channel_id=1, source_target_pairs={{0,2},{2,4},{4,6},{6,8},{8,10},{10,12},{12,14},{14,16},{16,18},{18... | collective-permute-start | bytes 98312 | tf_op jit(solution)/shard_map/ppermute | solution.py:19
  426.3 5.8 %collective-permute-start.35 = (f32[4,8,16,16]{3,2,1,0:T(8,128)}, f32[4,8,16,16]{3,2,1,0:T(8,128)}, u32[]{:S(2)}, u32[]{:S(2)}) collective-permute-start(f32[4,8,16,16]{3,2,1,0:T(8,128)} %fusion.28), channel_id=1, source_target_pairs={{0,2},{2,4},{4,6},{6,8},{8,10},{10,12},{12,14},{14,16},{16,18},{18... | collective-permute-start | bytes 98312 | tf_op jit(solution)/shard_map/ppermute | solution.py:19
  451.8 18.8 %all-reduce.109.cloned.1.call-done = f32[8,4096]{1,0:T(8,128)} async-done(((f32[8,4096]{1,0:T(8,128)}), f32[8,4096]{1,0:T(8,128)}) %all-reduce.109.cloned.1.call-update) | async-done | bytes 131088 | tf_op jit(solution)/shard_map/psum | solution.py:24
  478.5 5.5 %collective-permute-start.37 = (f32[4,8,16,16]{3,2,1,0:T(8,128)S(1)}, f32[4,8,16,16]{3,2,1,0:T(8,128)}, u32[]{:S(2)}, u32[]{:S(2)}) collective-permute-start(f32[4,8,16,16]{3,2,1,0:T(8,128)S(1)} %fusion.370), channel_id=1, source_target_pairs={{0,2},{2,4},{4,6},{6,8},{8,10},{10,12},{12,14},{14,16},{16,18},{18... | collective-permute-start | bytes 98312 | tf_op jit(solution)/shard_map/ppermute | solution.py:19
  506.2 5.8 %collective-permute-start.39 = (f32[4,8,16,16]{3,2,1,0:T(8,128)}, f32[4,8,16,16]{3,2,1,0:T(8,128)}, u32[]{:S(2)}, u32[]{:S(2)}) collective-permute-start(f32[4,8,16,16]{3,2,1,0:T(8,128)} %fusion.20), channel_id=1, source_target_pairs={{0,2},{2,4},{4,6},{6,8},{8,10},{10,12},{12,14},{14,16},{16,18},{18... | collective-permute-start | bytes 98312 | tf_op jit(solution)/shard_map/ppermute | solution.py:19
  (919 shorter events, 332.2 us)
Async XLA Ops:
  7.2 84.9 %all-reduce.103.cloned.1.call-start = ((), (), s32[]{:S(2)}) async-start(), calls=%async_computation | async-start | bytes 1048576 | tf_op jit(solution)/shard_map/psum | solution.py:277
  9.9 103.8 %all-reduce.105.cloned.1.call-start = ((), (), s32[]{:S(2)}) async-start(), calls=%async_computation.1 | async-start | bytes 262144 | tf_op jit(solution)/shard_map/psum | solution.py:24
  18.4 58.8 %collective-permute-start.7 = (f32[1,2048]{1,0:T(1,128)S(1)}, f32[1,2048]{1,0:T(1,128)S(1)}, u32[]{:S(2)}, u32[]{:S(2)}) collective-permute-start(f32[1,2048]{1,0:T(1,128)S(1)} %get-tuple-element.115), channel_id=1, source_target_pairs={{30,0},{0,2},{2,4},{4,6},{6,8},{8,10},{10,12},{12,14},{14,16},{16,... | collective-permute-start | bytes 24584 | tf_op jit(solution)/shard_map/ppermute | solution.py:30
  21.4 59.0 %collective-permute-start.8 = (f32[1,2048]{1,0:T(1,128)S(1)}, f32[1,2048]{1,0:T(1,128)S(1)}, u32[]{:S(2)}, u32[]{:S(2)}) collective-permute-start(f32[1,2048]{1,0:T(1,128)S(1)} %get-tuple-element.114), channel_id=1, source_target_pairs={{28,0},{30,2},{0,4},{2,6},{4,8},{6,10},{8,12},{10,14},{12,16},{14,... | collective-permute-start | bytes 24584 | tf_op jit(solution)/shard_map/ppermute | solution.py:30
  22.9 60.8 %collective-permute-start.9 = (f32[1,2048]{1,0:T(1,128)S(1)}, f32[1,2048]{1,0:T(1,128)S(1)}, u32[]{:S(2)}, u32[]{:S(2)}) collective-permute-start(f32[1,2048]{1,0:T(1,128)S(1)} %get-tuple-element.113), channel_id=1, source_target_pairs={{26,0},{28,2},{30,4},{0,6},{2,8},{4,10},{6,12},{8,14},{10,16},{12,... | collective-permute-start | bytes 24584 | tf_op jit(solution)/shard_map/ppermute | solution.py:30
  25.3 58.3 %collective-permute-start.10 = (f32[1,2048]{1,0:T(1,128)S(1)}, f32[1,2048]{1,0:T(1,128)S(1)}, u32[]{:S(2)}, u32[]{:S(2)}) collective-permute-start(f32[1,2048]{1,0:T(1,128)S(1)} %get-tuple-element.112), channel_id=1, source_target_pairs={{24,0},{26,2},{28,4},{30,6},{0,8},{2,10},{4,12},{6,14},{8,16},{10,... | collective-permute-start | bytes 24584 | tf_op jit(solution)/shard_map/ppermute | solution.py:30
  94.1 101.1 %all-reduce.111.cloned.1.call-start = ((), (), s32[]{:S(2)}) async-start(), calls=%async_computation.4 | async-start | bytes 393216 | tf_op jit(solution)/shard_map/psum | solution.py:277
  121.7 14.9 %collective-permute-start.14 = (f32[4,8,16,16]{3,2,1,0:T(8,128)}, f32[4,8,16,16]{3,2,1,0:T(8,128)}, u32[]{:S(2)}, u32[]{:S(2)}) collective-permute-start(f32[4,8,16,16]{3,2,1,0:T(8,128)} %fusion.398), channel_id=1, source_target_pairs={{0,2},{2,4},{4,6},{6,8},{8,10},{10,12},{12,14},{14,16},{16,18},{18... | collective-permute-start | bytes 98312 | tf_op jit(solution)/shard_map/ppermute | solution.py:19
  175.3 215.4 %all-reduce.107.cloned.1.call-start = ((), (), s32[]{:S(2)}) async-start(), calls=%async_computation.2 | async-start | bytes 262144 | tf_op jit(solution)/shard_map/psum | solution.py:24
  213.6 20.2 %collective-permute-start.23 = (f32[4,2,16,16]{3,2,1,0:T(8,128)}, f32[4,2,16,16]{3,2,1,0:T(8,128)}, u32[]{:S(2)}, u32[]{:S(2)}) collective-permute-start(f32[4,2,16,16]{3,2,1,0:T(8,128)} %fusion.312), channel_id=1, source_target_pairs={{2,0},{4,2},{6,4},{8,6},{10,8},{12,10},{14,12},{16,14},{18,16},{20... | collective-permute-start | bytes 24584 | tf_op jit(solution)/shard_map/ppermute | solution.py:19
  214.9 21.0 %collective-permute-start.22 = (f32[4,2,16,16]{3,2,1,0:T(8,128)}, f32[4,2,16,16]{3,2,1,0:T(8,128)}, u32[]{:S(2)}, u32[]{:S(2)}) collective-permute-start(f32[4,2,16,16]{3,2,1,0:T(8,128)} %fusion.313), channel_id=1, source_target_pairs={{0,2},{2,4},{4,6},{6,8},{8,10},{10,12},{12,14},{14,16},{16,18},{18... | collective-permute-start | bytes 24584 | tf_op jit(solution)/shard_map/ppermute | solution.py:19
  221.9 98.1 %collective-permute-start.19 = (f32[4,8,16,16]{3,2,1,0:T(8,128)}, f32[4,8,16,16]{3,2,1,0:T(8,128)}, u32[]{:S(2)}, u32[]{:S(2)}) collective-permute-start(f32[4,8,16,16]{3,2,1,0:T(8,128)} %fusion.347), channel_id=1, source_target_pairs={{2,0},{4,2},{6,4},{8,6},{10,8},{12,10},{14,12},{16,14},{18,16},{20... | collective-permute-start | bytes 98312 | tf_op jit(solution)/shard_map/ppermute | solution.py:19
  223.2 99.8 %collective-permute-start.18 = (f32[4,8,16,16]{3,2,1,0:T(8,128)}, f32[4,8,16,16]{3,2,1,0:T(8,128)}, u32[]{:S(2)}, u32[]{:S(2)}) collective-permute-start(f32[4,8,16,16]{3,2,1,0:T(8,128)} %fusion.391), channel_id=1, source_target_pairs={{0,2},{2,4},{4,6},{6,8},{8,10},{10,12},{12,14},{14,16},{16,18},{18... | collective-permute-start | bytes 98312 | tf_op jit(solution)/shard_map/ppermute | solution.py:19
  268.4 28.2 %collective-permute-start.26 = (f32[1,2048]{1,0:T(1,128)S(1)}, f32[1,2048]{1,0:T(1,128)S(1)}, u32[]{:S(2)}, u32[]{:S(2)}) collective-permute-start(f32[1,2048]{1,0:T(1,128)S(1)} %get-tuple-element.108), channel_id=1, source_target_pairs={{30,0},{0,2},{2,4},{4,6},{6,8},{8,10},{10,12},{12,14},{14,16},{16,... | collective-permute-start | bytes 24584 | tf_op jit(solution)/shard_map/ppermute | solution.py:30
  271.4 27.6 %collective-permute-start.27 = (f32[1,2048]{1,0:T(1,128)S(1)}, f32[1,2048]{1,0:T(1,128)S(1)}, u32[]{:S(2)}, u32[]{:S(2)}) collective-permute-start(f32[1,2048]{1,0:T(1,128)S(1)} %get-tuple-element.107), channel_id=1, source_target_pairs={{28,0},{30,2},{0,4},{2,6},{4,8},{6,10},{8,12},{10,14},{12,16},{14,... | collective-permute-start | bytes 24584 | tf_op jit(solution)/shard_map/ppermute | solution.py:30
  310.3 32.4 %collective-permute-start.44 = (f32[4,2,16,16]{3,2,1,0:T(8,128)}, f32[4,2,16,16]{3,2,1,0:T(8,128)}, u32[]{:S(2)}, u32[]{:S(2)}) collective-permute-start(f32[4,2,16,16]{3,2,1,0:T(8,128)} %fusion.316), channel_id=1, source_target_pairs={{2,0},{4,2},{6,4},{8,6},{10,8},{12,10},{14,12},{16,14},{18,16},{20... | collective-permute-start | bytes 24584 | tf_op jit(solution)/shard_map/ppermute | solution.py:19
  311.6 34.7 %collective-permute-start.43 = (f32[4,2,16,16]{3,2,1,0:T(8,128)}, f32[4,2,16,16]{3,2,1,0:T(8,128)}, u32[]{:S(2)}, u32[]{:S(2)}) collective-permute-start(f32[4,2,16,16]{3,2,1,0:T(8,128)} %fusion.360), channel_id=1, source_target_pairs={{0,2},{2,4},{4,6},{6,8},{8,10},{10,12},{12,14},{14,16},{16,18},{18... | collective-permute-start | bytes 24584 | tf_op jit(solution)/shard_map/ppermute | solution.py:19
  334.1 21.1 %collective-permute-start.21 = (f32[4,8,16,16]{3,2,1,0:T(8,128)S(1)}, f32[4,8,16,16]{3,2,1,0:T(8,128)}, u32[]{:S(2)}, u32[]{:S(2)}) collective-permute-start(f32[4,8,16,16]{3,2,1,0:T(8,128)S(1)} %fusion.34), channel_id=1, source_target_pairs={{2,0},{4,2},{6,4},{8,6},{10,8},{12,10},{14,12},{16,14},{18,16},{20... | collective-permute-start | bytes 98312 | tf_op jit(solution)/shard_map/ppermute | solution.py:19
  335.4 22.7 %collective-permute-start.20 = (f32[4,8,16,16]{3,2,1,0:T(8,128)S(1)}, f32[4,8,16,16]{3,2,1,0:T(8,128)}, u32[]{:S(2)}, u32[]{:S(2)}) collective-permute-start(f32[4,8,16,16]{3,2,1,0:T(8,128)S(1)} %fusion.36), channel_id=1, source_target_pairs={{0,2},{2,4},{4,6},{6,8},{8,10},{10,12},{12,14},{14,16},{16,18},{18... | collective-permute-start | bytes 98312 | tf_op jit(solution)/shard_map/ppermute | solution.py:19
  370.5 100.2 %all-reduce.109.cloned.1.call-start = ((), (), s32[]{:S(2)}) async-start(), calls=%async_computation.3 | async-start | bytes 262144 | tf_op jit(solution)/shard_map/psum | solution.py:24
  398.6 15.8 %collective-permute-start.33 = (f32[4,8,16,16]{3,2,1,0:T(8,128)S(1)}, f32[4,8,16,16]{3,2,1,0:T(8,128)}, u32[]{:S(2)}, u32[]{:S(2)}) collective-permute-start(f32[4,8,16,16]{3,2,1,0:T(8,128)S(1)} %fusion.377), channel_id=1, source_target_pairs={{0,2},{2,4},{4,6},{6,8},{8,10},{10,12},{12,14},{14,16},{16,18},{18... | collective-permute-start | bytes 98312 | tf_op jit(solution)/shard_map/ppermute | solution.py:19
  426.3 14.1 %collective-permute-start.35 = (f32[4,8,16,16]{3,2,1,0:T(8,128)}, f32[4,8,16,16]{3,2,1,0:T(8,128)}, u32[]{:S(2)}, u32[]{:S(2)}) collective-permute-start(f32[4,8,16,16]{3,2,1,0:T(8,128)} %fusion.28), channel_id=1, source_target_pairs={{0,2},{2,4},{4,6},{6,8},{8,10},{10,12},{12,14},{14,16},{16,18},{18... | collective-permute-start | bytes 98312 | tf_op jit(solution)/shard_map/ppermute | solution.py:19
  478.5 15.8 %collective-permute-start.37 = (f32[4,8,16,16]{3,2,1,0:T(8,128)S(1)}, f32[4,8,16,16]{3,2,1,0:T(8,128)}, u32[]{:S(2)}, u32[]{:S(2)}) collective-permute-start(f32[4,8,16,16]{3,2,1,0:T(8,128)S(1)} %fusion.370), channel_id=1, source_target_pairs={{0,2},{2,4},{4,6},{6,8},{8,10},{10,12},{12,14},{14,16},{16,18},{18... | collective-permute-start | bytes 98312 | tf_op jit(solution)/shard_map/ppermute | solution.py:19
  506.2 14.1 %collective-permute-start.39 = (f32[4,8,16,16]{3,2,1,0:T(8,128)}, f32[4,8,16,16]{3,2,1,0:T(8,128)}, u32[]{:S(2)}, u32[]{:S(2)}) collective-permute-start(f32[4,8,16,16]{3,2,1,0:T(8,128)} %fusion.20), channel_id=1, source_target_pairs={{0,2},{2,4},{4,6},{6,8},{8,10},{10,12},{12,14},{14,16},{16,18},{18... | collective-permute-start | bytes 98312 | tf_op jit(solution)/shard_map/ppermute | solution.py:19
  (194 other events, 3291.0 us)
Sparse Core Ops, SparseCore 0:
  10.9 21.4 all-reduce.102
  94.2 19.4 all-reduce.104
  175.4 19.6 all-reduce.110
  370.6 20.0 all-reduce.106
  450.4 20.1 all-reduce.108
where the time goes:
time: 543 us; the launch traced here: 534 us
  waiting for transfers between devices  142 us (26%)
  starting transfers between devices  122 us (22%)
  local copies, waits for them, and re-layouts  91.2 us (17%)
  matrix products  83.2 us (15%)
  other arithmetic  71.3 us (13%)
  between operations  18.4 us (3%)
  blocking collectives  6.85 us (1%)
    ppermute x24, starting transfers between devices, shifted(): lax.ppermute(value, axis, [(source, source + steps) for source in range(l...  80.7 us
    psum x3, waiting for transfers between devices, broadcast(): return lax.psum(kept, axis)  55.7 us
    ppermute x21, starting transfers between devices, shifted_2(): return lax.ppermute(block, axis, route)  40.6 us
    ppermute x24, waiting for transfers between devices, shifted(): lax.ppermute(value, axis, [(source, source + steps) for source in range(l...  35.5 us
    ppermute x21, waiting for transfers between devices, shifted_2(): return lax.ppermute(block, axis, route)  32.4 us
    dot_general x48, matrix products, face_list(): result.append(jnp.dot(planes, table, precision=precise))  26 us
    dot_general x72, matrix products, pick_rows(): chosen = jnp.einsum('br,wrf->wbf', onehot, flat_rows, precision=precise)  25 us
    psum x2, waiting for transfers between devices, shards(): mix_fine, mix_coarse = lax.psum((partial_f, partial_c), 'fld')  17.9 us
  transfers between devices with their start and end apart: 50, of which 24 were waited for; matrix products, arithmetic and copies ran while one was open for 25% of the time, Pallas kernels for 0%

commit v1 on v0

v1 whole, which is shorter than its diff:
```python
import functools
import jax
import jax.numpy as jnp
from jax import lax
from jax.experimental import pallas as pl
from jax.experimental.pallas import tpu as pltpu
from jax.sharding import PartitionSpec as P

B = 16
H = B // 2
NSUB = 4
CYCLES = 2
LANES = 128
TILES = B**3 // LANES
HEAT = 0.5
ENERGY = 2.0
FAR = -(1 << 20)
VMEM = pl.BlockSpec(memory_space=pltpu.VMEM)
SMEM = pl.BlockSpec(memory_space=pltpu.SMEM)
F32 = jnp.float32


def core_swap(value):
    return lax.ppermute(value, "fld", [(0, 1), (1, 0)])


def pair_swap(value, first):
    n = lax.axis_size("blk")
    pairs = []
    for i in range(first, n + first, 2):
        a, b = i % n, (i + 1) % n
        pairs += [(a, b), (b, a)]
    return lax.ppermute(value, "blk", sorted(pairs))


def octant_sends(count):
    half = count // 2
    return [(1 + s if 1 + s < half else count - 1, half + s) for s in range(half)]


def octant_move(value, distances):
    n = lax.axis_size("blk")
    pairs = []
    for i in range(n):
        for core in range(2):
            pairs.append((2 * i + core, 2 * ((i + distances[core]) % n) + core))
    return lax.ppermute(value, ("blk", "fld"), pairs)


def lane_ids():
    return lax.broadcasted_iota(jnp.int32, (8, LANES), 1)


def row_ids():
    return lax.broadcasted_iota(jnp.int32, (8, LANES), 0)


def roll(x, steps):
    steps = steps % LANES
    return x if steps == 0 else pltpu.roll(x, steps, 1)


def odd_lanes():
    return lane_ids() % 2 == 1


def cols(i, jh, width=1):
    return pl.ds((2 * i + jh) * LANES, width * LANES)


class Links:
    def __init__(self, column, base, count, by_rows, remote_base=None):
        self.count = count
        self.by_rows = by_rows
        self.column = column
        self.base = base
        self.cache = {}

    def place(self, slab, face, base):
        raw = jnp.broadcast_to(self.column(slab, face), (8, LANES))
        return jnp.where(raw >= 0, raw - base, FAR)

    def prepare(self, name, slab, make):
        key = (name, None if self.by_rows else slab)
        if key not in self.cache:
            self.cache[key] = make(slab)
        return self.cache[key]

    def index(self, name, slab):
        base, count = self.base, self.count

        def one(face, shift=0):
            return lambda s: self.place(s, face, base + shift)

        lane = lane_ids()
        if name == "i0":
            return self.prepare(name, slab, one(0))
        if name == "i1":
            return self.prepare(name, slab, one(1))
        if name == "j":
            return self.prepare(
                name, slab, lambda s: jnp.where(lane < LANES // 2, one(2)(s), one(3)(s))
            )
        if name == "k":
            return self.prepare(name, slab, lambda s: jnp.where(odd_lanes(), one(4)(s), one(5)(s)))
        if name == "k_far":
            return self.prepare(
                name,
                slab,
                lambda s: jnp.where(odd_lanes(), one(4, -count)(s), one(5, count)(s)),
            )
        if name == "from_below":
            return self.prepare(name, slab, one(5, count))
        return self.prepare(name, slab, one(4, -count))

    def read(self, name, slab, tile):
        where = self.index(name, slab)
        if self.by_rows:
            there = (where >= 0) & (where < self.count)
            got = jnp.take_along_axis(
                tile(slab), jnp.clip(where, 0, self.count - 1), axis=0, mode="promise_in_bounds"
            )
            return jnp.where(there, got, 0.0)
        result = jnp.zeros((8, LANES), F32)
        for q in range(self.count):
            result = jnp.where(where == q, tile(q), result)
        return result


def in_plane(links, slab, c, tile, h_or_i):
    lane = lane_ids()
    low = [roll(c[0], B), roll(c[1], B)]
    high = [roll(c[0], -B), roll(c[1], -B)]
    edge = links.read(
        "j",
        slab,
        lambda q: jnp.where(
            lane < LANES // 2, roll(tile(q, h_or_i, 1), B), roll(tile(q, h_or_i, 0), -B)
        ),
    )
    first = jnp.where(lane < B, edge, low[0]) + jnp.where(lane >= LANES - B, high[1], high[0])
    second = jnp.where(lane < B, low[0], low[1]) + jnp.where(lane >= LANES - B, edge, high[1])
    return first, second


def laplace_slab(links, slab, tile, ghost, emit):
    lane = lane_ids()
    k = lane % B
    for h in range(2):
        packed = [ghost(h, 0), ghost(h, 1)]
        for q in range(H):
            i = h * H + q
            c = [tile(slab, i, 0), tile(slab, i, 1)]
            plane = in_plane(links, slab, c, tile, i)
            for jh in range(2):
                if i > 0:
                    before = tile(slab, i - 1, jh)
                else:
                    before = links.read("i0", slab, lambda s, jh=jh: tile(s, B - 1, jh))
                if i < B - 1:
                    after = tile(slab, i + 1, jh)
                else:
                    after = links.read("i1", slab, lambda s, jh=jh: tile(s, 0, jh))
                edge = roll(packed[jh], -(2 * q + 1))
                line = jnp.where(k == 0, edge, roll(c[jh], 1)) + jnp.where(
                    k == B - 1, edge, roll(c[jh], -1)
                )
                lap = (before + after) + (plane[jh] + line) - 6.0 * c[jh]
                emit(i, jh, c[jh], lap)


def laplace_far(links, slab, tile, inward, outward, emit):
    k = lane_ids() % B
    for h in range(2):
        c = [tile(slab, h, 0), tile(slab, h, 1)]
        plane = in_plane(links, slab, c, tile, h)
        for jh in range(2):
            if h == 1:
                head = roll(tile(slab, 0, jh), 2 - B)
                tail = links.read("i1", slab, lambda s, jh=jh: roll(tile(s, 0, jh), B - 2))
            else:
                head = links.read("i0", slab, lambda s, jh=jh: roll(tile(s, 1, jh), 2 - B))
                tail = roll(tile(slab, 1, jh), B - 2)
            before = jnp.where(k < 2, head, roll(c[jh], 2))
            after = jnp.where(k >= B - 2, tail, roll(c[jh], -2))
            lap = (before + after) + plane[jh] + inward(c[jh]) + outward(h, jh) - 6.0 * c[jh]
            emit(h, jh, lap)


def pack_into(store, q, value, shift):
    k = lane_ids() % B
    return jnp.where(k // 2 == q, roll(value, shift), store)


def zero_tile():
    return jnp.zeros((8, LANES), F32)


def diffuse(links, far_links, slabs, loop, tile, rate, up, down, far_up, far_down, work, finish):
    first_ref, edge_ref, below_ref, above_ref = work
    odd = odd_lanes()
    k = lane_ids() % B
    from_below, from_above = far_links

    def first_of(s):
        def ghost(h, jh):
            near = links.read(
                "k", s, lambda q: jnp.where(odd, up(q, h, jh), roll(down(q, h, jh), B))
            )
            far = links.read(
                "k_far", s, lambda q: jnp.where(odd, far_up(q, h, jh), roll(far_down(q, h, jh), B))
            )
            return near + far

        edges = [zero_tile(), zero_tile()]

        def emit(i, jh, c, lap):
            value = rate(s) * lap
            first_ref[s, :, cols(i, jh)] = value
            q = i % H
            edges[jh] = pack_into(zero_tile() if q == 0 else edges[jh], q, value, 2 * q + 1)
            if q == H - 1:
                edge_ref[s, i // H, jh] = edges[jh]

        laplace_slab(links, s, tile, ghost, emit)

        def emit_below(h, jh, lap):
            below_ref[s, h, jh] = rate(s) * lap

        def emit_above(h, jh, lap):
            above_ref[s, h, jh] = rate(s) * lap

        laplace_far(
            from_below,
            s,
            far_up,
            lambda c: roll(c, 1),
            lambda h, jh: from_below.read("from_below", s, lambda q: roll(down(q, h, jh), 1)),
            emit_below,
        )
        laplace_far(
            from_above,
            s,
            far_down,
            lambda c: roll(c, -1),
            lambda h, jh: from_above.read("from_above", s, lambda q: roll(up(q, h, jh), -1)),
            emit_above,
        )

    def second_of(s):
        def ghost(h, jh):
            near = links.read(
                "k",
                s,
                lambda q: jnp.where(
                    odd, roll(edge_ref[q, h, jh], 1 - B), roll(edge_ref[q, h, jh], B - 1)
                ),
            )
            far = links.read(
                "k_far",
                s,
                lambda q: jnp.where(odd, below_ref[q, h, jh], roll(above_ref[q, h, jh], B)),
            )
            return near + far

        def emit(i, jh, c, lap):
            finish(s, i, jh, tile(s, i, jh) + c + 0.5 * rate(s) * lap)

        laplace_slab(
            links, s, lambda q, i, jh: first_ref[q, :, cols(i, jh)], ghost, emit
        )

    if loop:
        def body(s, carry):
            first_of(s)
            second_of(s)
            return carry

        lax.fori_loop(0, slabs, body, 0)
    else:
        for s in range(slabs):
            first_of(s)
        for s in range(slabs):
            second_of(s)


def pick(core, a, b):
    return jnp.where(core == 0, a, b)


def spread_vector(core, own, other, row, fields):
    rows = row_ids()
    result = jnp.zeros((8, LANES), F32)
    for f in range(2 * fields):
        value = pick(core, own[row, f], other[row, f]) if f < fields else pick(
            core, other[row, f - fields], own[row, f - fields]
        )
        result = jnp.where(rows == f, value, result)
    return result


def mix_kernel(saved_f, saved_c, seed_f, par, pay, payc):
    steps, fields = saved_f.shape[0], saved_f.shape[1]
    cycles, blocks = saved_c.shape[0], saved_c.shape[2]
    for s in range(steps):
        total = par[1, 0] * saved_f[s, 0]
        for v in range(1, fields):
            total = total + par[1, v] * saved_f[s, v]
        pay[s] = total
        pay[steps + s] = saved_f[s, 0]
    pay[2 * steps] = seed_f[0]
    for c in range(cycles):
        total = par[1, 0] * saved_c[c, 0]
        for v in range(1, fields):
            total = total + par[1, v] * saved_c[c, v]
        payc[0, pl.ds(c * blocks, blocks), :] = total
        payc[1, pl.ds(c * blocks, blocks), :] = saved_c[c, 0]


def reaction_tables(mix, start, counts):
    step = HEAT / counts.astype(F32)
    state = start
    history = []
    for n in range(NSUB):
        inverse = 1.0 / state
        decay = jnp.exp(-ENERGY * inverse)
        active = n < counts
        history.append((active, inverse, decay))
        state = state + jnp.where(active, step * mix * decay, 0.0)
    passed = jnp.ones_like(start)
    weight = jnp.zeros_like(start)
    for active, inverse, decay in reversed(history):
        grown = jnp.where(active, step * decay, 0.0)
        weight = weight + grown * passed
        passed = passed * (1.0 + grown * mix * ENERGY * (inverse * inverse))
    return passed - 1.0, weight


def chem_kernel(pay, pay_o, payc, payc_o, fine_counts, coarse_counts, gain, weight, gain_c, weight_c):
    core = lax.axis_index("fld")
    steps = gain.shape[0]
    rows = row_ids()
    counts = jnp.ones((8, LANES), jnp.int32)
    for b in range(fine_counts.shape[0]):
        counts = jnp.where(rows == b, fine_counts[b], counts)
    blocks = coarse_counts.shape[0]
    entries = gain_c.shape[0]
    counts_c = jnp.ones((entries, LANES), jnp.int32)
    rows_c = lax.broadcasted_iota(jnp.int32, (entries, LANES), 0)
    for r in range(entries):
        counts_c = jnp.where(rows_c == r, coarse_counts[r % blocks], counts_c)

    def body(t, carry):
        at = pl.ds(pl.multiple_of(t * LANES, LANES), LANES)
        for s in range(steps):
            start = pick(core, pay[steps + s, :, at], pay_o[steps + s, :, at])
            a, w = reaction_tables(pay[s, :, at] + pay_o[s, :, at], start, counts)
            gain[s, :, at] = a
            weight[s, :, at] = w
        start = pick(core, payc[1, :, at], payc_o[1, :, at])
        a, w = reaction_tables(payc[0, :, at] + payc_o[0, :, at], start, counts_c)
        gain_c[:, at] = a
        weight_c[:, at] = w
        return carry

    lax.fori_loop(0, TILES, body, 0)


def octants_out(read, children, count_f, outs, cells):
    core = lax.axis_index("fld")
    me = lax.axis_index("blk")
    devices = lax.axis_size("blk")
    count_c = children.shape[0]
    fields = 8
    for p in range(count_c):
        for i in range(B):
            for jh in range(2):
                cells[p, jh, pl.ds(i, fields, stride=B), :] = read(p, i, jh)
    half = lane_ids() % B // H
    found = []
    for p in range(count_c):
        for o in range(8):
            child = children[p, o]
            distance = jnp.where(child >= 0, (child // count_f - me) % devices, -1)
            found.append((distance, child, p, o))
    sends = octant_sends(count_f)
    for s, out in enumerate(outs):
        if s < len(sends):
            want = jnp.where(core == 0, sends[s][0], sends[s][1])
        else:
            want = 0
        slot = jnp.int32(0)
        label = jnp.int32(-1)
        for distance, child, p, o in found:
            hit = distance == want
            slot = jnp.where(hit, p * 8 + o, slot)
            label = jnp.where(hit, child % count_f, label)
        if s < len(sends):
            label = jnp.where((core == 0) & (sends[s][0] == count_f - 1), -1, label)
        else:
            label = jnp.where(core == 0, label, -1)
        p, a, b, c = slot // 8, slot // 4 % 2, slot // 2 % 2, slot % 2
        kept = half == c
        for f in range(fields):
            from_row = pl.multiple_of(f * B + a * H, H)
            out[f] = jnp.where(kept, cells[p, b, pl.ds(from_row, H), :], 0.0)
        out[fields] = jnp.full((H, LANES), label.astype(F32))


def kept_octants(children, p):
    half = lane_ids() % B // H
    result = {}
    for a in range(2):
        for b in range(2):
            low = jnp.where(children[p, 4 * a + 2 * b] < 0, 1.0, 0.0)
            high = jnp.where(children[p, 4 * a + 2 * b + 1] < 0, 1.0, 0.0)
            result[a, b] = jnp.where(half == 0, low, high)
    return result


def seed_kernel(seed_c, seed_o, children, count_f, coarse, *rest):
    outs, cells = rest[:-1], rest[-1]
    core = lax.axis_index("fld")
    fields, count_c = seed_c.shape[0], seed_c.shape[1]
    for p in range(count_c):
        for v in range(fields):
            own = seed_c[v, pl.ds(p, 1), :]
            other = seed_o[v, pl.ds(p, 1), :]
            coarse[p, pl.ds(v, 1), :] = pick(core, own, other)
            coarse[p, pl.ds(fields + v, 1), :] = pick(core, other, own)
    octants_out(lambda p, i, jh: coarse[p, :, cols(i, jh)], children, count_f, outs, cells)
    for p in range(count_c):
        kept = kept_octants(children, p)
        for i in range(B):
            for jh in range(2):
                coarse[p, :, cols(i, jh)] = coarse[p, :, cols(i, jh)] * kept[i // H, jh]


def add_octants(messages, state, stage, fields):
    core = lax.axis_index("fld")
    slots = state.shape[0]
    rows = row_ids()
    lane = lane_ids()
    source = jnp.zeros((8, LANES), jnp.int32)
    order = jnp.full((8, LANES), 0, jnp.int32)
    serial = 0
    for d, message in enumerate(messages):
        label = message[2 * fields].astype(jnp.int32)
        source = jnp.where(label == rows, d, source)
        for s in range(slots):
            if s == fields:
                value = message[0]
            else:
                value = message[pl.ds(core * fields + s, 1)][0]
            stage[d // 8, s, pl.ds(d % 8, H, stride=8), :] = value
    lanes_of = [((H // 2 * jh + lane // B // 2) * B + lane % B // 2) for jh in range(2)]
    groups = (len(messages) + 7) // 8
    for s in range(slots):
        for i in range(H):
            got = None
            for g in range(groups):
                index = source - 8 * g
                part = jnp.take_along_axis(
                    stage[g, s, pl.ds(8 * i, 8), :],
                    jnp.clip(index, 0, 7),
                    axis=0,
                    mode="promise_in_bounds",
                )
                part = jnp.where((index >= 0) & (index < 8), part, 0.0)
                got = part if got is None else got + part
            got = 0.125 * (got + roll(got, -H))
            for jh in range(2):
                wide = jnp.take_along_axis(got, lanes_of[jh], axis=1, mode="promise_in_bounds")
                for ii in range(2):
                    at = cols(2 * i + ii, jh)
                    state[s, :, at] = state[s, :, at] + wide


def react_and_pack(state, fields, par, par_o, gain, weight, up, down):
    core = lax.axis_index("fld")
    share = [par[1, s] for s in range(fields)] + [pick(core, par[1, 0], par_o[1, 0])]
    extra = jnp.where(core == 0, 1.0, 0.0)
    for h in range(2):
        for jh in range(2):
            ups = [zero_tile() for _ in range(fields + 1)]
            downs = [zero_tile() for _ in range(fields + 1)]
            for q in range(H):
                at = cols(h * H + q, jh)
                driver = state[fields, :, at]
                heat = weight[:, at] * driver
                grown = gain[:, at] * driver
                for s in range(fields + 1):
                    value = state[s, :, at] + share[s] * heat
                    if s == 0:
                        value = value + extra * grown
                    if s == fields:
                        value = value + grown
                    state[s, :, at] = value
                    ups[s] = pack_into(ups[s], q, value, 2 * q + 2 - B)
                    downs[s] = pack_into(downs[s], q, value, 2 * q)
            for s in range(fields + 1):
                up(s, h, jh, ups[s])
                down(s, h, jh, downs[s])


def react_coarse_and_pack(state, shares, gain, weight, first_row, up, down):
    rows = row_ids()
    own = jnp.where(rows == 0, 1.0, 0.0)
    for p in range(state.shape[0]):
        for h in range(2):
            for jh in range(2):
                ups, downs = zero_tile(), zero_tile()
                for q in range(H):
                    at = cols(h * H + q, jh)
                    driver = jnp.broadcast_to(state[p, pl.ds(0, 1), at], (8, LANES))
                    heat = weight[pl.ds(first_row + p, 1), at] * driver
                    grown = gain[pl.ds(first_row + p, 1), at] * driver
                    value = state[p, :, at] + shares * heat + own * grown
                    state[p, :, at] = value
                    ups = pack_into(ups, q, value, 2 * q + 2 - B)
                    downs = pack_into(downs, q, value, 2 * q)
                up(p, h, jh, ups)
                down(p, h, jh, downs)


def step_kernel(plan, names, *refs):
    r = dict(zip(names, refs))
    core = lax.axis_index("fld")
    me = lax.axis_index("blk")
    even = me % 2 == 0
    fields = plan["fields"]
    slots = fields + 1
    count_f, count_c = plan["count_f"], plan["count_c"]
    par, par_o = r["par"], r["par_o"]
    coarse_slabs = count_c
    tables_at = 4 * (slots + coarse_slabs)

    def fine_at(s, h, jh):
        return 4 * s + 2 * h + jh

    def coarse_at(p, h, jh):
        return 4 * (slots + p) + 2 * h + jh

    far_b, far_a, own_up, own_down = (r.get(x) for x in ("far_b", "far_a", "own_up", "own_down"))

    if plan["diffuse_fine"]:

        @pl.when(even)
        def _():
            own_up[...] = r["sent_e"][...]
            own_down[...] = r["sent_o"][...]
            far_a[...] = r["got_e"][...]
            far_b[...] = r["got_o"][...]

        @pl.when(jnp.logical_not(even))
        def _():
            own_up[...] = r["sent_o"][...]
            own_down[...] = r["sent_e"][...]
            far_b[...] = r["got_e"][...]
            far_a[...] = r["got_o"][...]

        work = (r["first"], r["edge"], r["below"], r["above"])
        base = me * count_f
        base_c = me * count_c

        def table(ref, offset, rowwise):
            def column(slab, face):
                if rowwise:
                    return ref[tables_at, :, pl.ds(face, 1)].astype(jnp.int32)
                return ref[tables_at, pl.ds(slab, 1), pl.ds(offset + face, 1)].astype(jnp.int32)

            return column

        near = Links(table(own_up, 0, True), base, count_f, True)
        below = Links(table(far_b, 0, True), base - count_f, count_f, True)
        above = Links(table(far_a, 0, True), base + count_f, count_f, True)
        for links, names_used in (
            (near, ("i0", "i1", "j", "k", "k_far")),
            (below, ("i0", "i1", "j", "from_below")),
            (above, ("i0", "i1", "j", "from_above")),
        ):
            for name in names_used:
                links.index(name, 0)

        rate_of = [par[0, s] for s in range(fields)] + [pick(core, par[0, 0], par_o[0, 0])]

        def rate(s):
            value = rate_of[0]
            for n in range(1, slots):
                value = jnp.where(s == n, rate_of[n], value)
            return value

        done = r["fine_out"]

        def finish(s, i, jh, value):
            done[s, :, cols(i, jh)] = value

        diffuse(
            near,
            (below, above),
            done.shape[0],
            True,
            lambda s, i, jh: r["fine"][s, :, cols(i, jh)],
            rate,
            lambda s, h, jh: own_up[fine_at(s, h, jh)],
            lambda s, h, jh: own_down[fine_at(s, h, jh)],
            lambda s, h, jh: far_b[fine_at(s, h, jh)],
            lambda s, h, jh: far_a[fine_at(s, h, jh)],
            work,
            finish,
        )
        if plan["diffuse_coarse"]:
            near = Links(table(own_up, 8, False), base_c, count_c, False)
            below = Links(table(far_b, 8, False), base_c - count_c, count_c, False)
            above = Links(table(far_a, 8, False), base_c + count_c, count_c, False)
            rates = 0.5 * spread_vector(core, par, par_o, 0, fields)
            grown = r["coarse_out"] if plan["diffuse_coarse"] == "keep" else r["coarse_next"]

            def finish_c(p, i, jh, value):
                grown[p, :, cols(i, jh)] = value

            diffuse(
                near,
                (below, above),
                count_c,
                False,
                lambda p, i, jh: r["coarse"][p, :, cols(i, jh)],
                lambda p: rates,
                lambda p, h, jh: own_up[coarse_at(p, h, jh)],
                lambda p, h, jh: own_down[coarse_at(p, h, jh)],
                lambda p, h, jh: far_b[coarse_at(p, h, jh)],
                lambda p, h, jh: far_a[coarse_at(p, h, jh)],
                work,
                finish_c,
            )
            if plan["diffuse_coarse"] == "last":
                out = r["coarse_final"]
                for p in range(count_c):
                    for v in range(fields):
                        out[v, pl.ds(p, 1), :] = pick(
                            core,
                            grown[p, pl.ds(v, 1), :],
                            grown[p, pl.ds(fields + v, 1), :],
                        )
            else:
                octants_out(
                    lambda p, i, jh: grown[p, :, cols(i, jh)],
                    r["children"],
                    count_f,
                    [r[f"octant{s}"] for s in range(plan["messages"])],
                    r["cells"],
                )
                for p in range(count_c):
                    kept = kept_octants(r["children"], p)
                    for i in range(B):
                        for jh in range(2):
                            at = cols(i, jh)
                            grown[p, :, at] = grown[p, :, at] * kept[i // H, jh]
    else:
        done = r["fine_out"]
        for s in range(fields):
            done[s] = r["seed_f"][s]
        done[fields] = pick(core, r["pay"][r["pay"].shape[0] - 1], r["pay_o"][r["pay"].shape[0] - 1])
        grown = r["coarse_out"]
        grown[...] = r["coarse"][...]
        rows = row_ids()
        lane = lane_ids()
        faces = jnp.zeros((8, LANES), F32)
        for f in range(6):
            column = r["fine_nbr"][:, pl.ds(f, 1)].astype(F32)
            faces = jnp.where(lane == f, jnp.broadcast_to(column, (8, LANES)), faces)
            for p in range(count_c):
                column = r["coarse_nbr"][pl.ds(p, 1), pl.ds(f, 1)].astype(F32)
                faces = jnp.where(
                    (lane == 8 + f) & (rows == p), jnp.broadcast_to(column, (8, LANES)), faces
                )

    if plan["add"]:
        add_octants([r[f"arrived{s}"] for s in range(plan["arrivals"])], done, r["stage"], fields)
    if plan["react"]:
        up, down = r["up"], r["down"]

        def put(ref, place):
            def go(s, h, jh, value):
                ref[place(s, h, jh)] = value

            return go

        react_and_pack(
            done, fields, par, par_o, r["gain"].at[plan["step"]], r["weight"].at[plan["step"]],
            put(up, fine_at), put(down, fine_at),
        )
        if plan["react_coarse"] is not None:
            react_coarse_and_pack(
                grown,
                spread_vector(core, par, par_o, 1, fields),
                r["gain_c"],
                r["weight_c"],
                plan["react_coarse"] * count_c,
                put(up, coarse_at),
                put(down, coarse_at),
            )
        else:
            for n in range(4 * slots, tables_at):
                up[n] = zero_tile()
                down[n] = zero_tile()
        if plan["diffuse_fine"]:
            faces = own_up[tables_at]
        up[tables_at] = faces
        down[tables_at] = faces

        @pl.when(even)
        def _():
            r["send_e"][...] = up[...]
            r["send_o"][...] = down[...]

        @pl.when(jnp.logical_not(even))
        def _():
            r["send_e"][...] = down[...]
            r["send_o"][...] = up[...]


SCALARS = ("par", "par_o", "children", "fine_counts", "coarse_counts")


def call(kernel, inputs, outputs, scratch, cost=2_000_000):
    names = list(inputs) + list(outputs) + list(scratch)
    result = pl.pallas_call(
        functools.partial(kernel, names),
        out_shape=[jax.ShapeDtypeStruct(shape, F32) for shape in outputs.values()],
        in_specs=[SMEM if name in SCALARS else VMEM for name in inputs],
        out_specs=[VMEM] * len(outputs),
        scratch_shapes=[pltpu.VMEM(shape, F32) for shape in scratch.values()],
        compiler_params=pltpu.CompilerParams(vmem_limit_bytes=48 * 1024 * 1024),
        cost_estimate=pl.CostEstimate(flops=cost, bytes_accessed=cost, transcendentals=0),
    )(*inputs.values())
    return dict(zip(outputs, result))


def shards(
    seed_fine,
    seed_coarse,
    saved_fine,
    saved_coarse,
    diffusion,
    species_shares,
    fine_nbr,
    coarse_nbr,
    children,
    fine_counts,
    coarse_counts,
):
    fields, count_f, cells = seed_fine.shape
    count_c = seed_coarse.shape[1]
    steps = saved_fine.shape[0]
    cycles = saved_coarse.shape[0]
    slots = fields + 1
    sends = octant_sends(count_f)
    messages = len(sends) + 1
    par = jnp.stack([diffusion, species_shares])
    par_o = core_swap(par)
    seed_o = core_swap(seed_coarse)

    def wrapped(kernel):
        return lambda names, *refs: kernel(*refs)

    octant_shapes = {f"octant{s}": (2 * fields + 1, H, LANES) for s in range(messages)}
    cell_shape = (count_c, 2, 2 * fields * B, LANES)

    def seed_call(names, seed_c, seed_other, kids, *rest):
        seed_kernel(seed_c, seed_other, kids, count_f, *rest)

    opened = call(
        seed_call,
        dict(seed_c=seed_coarse, seed_o=seed_o, children=children),
        dict(coarse=(count_c, 2 * fields, cells), **octant_shapes),
        dict(cells=cell_shape),
    )

    def travel(made):
        landed = [octant_move(made[f"octant{s}"], d) for s, d in enumerate(sends)]
        landed.append(made[f"octant{len(sends)}"])
        return landed + [core_swap(value) for value in landed]

    arrived = travel(opened)

    paid = call(
        wrapped(mix_kernel),
        dict(saved_f=saved_fine, saved_c=saved_coarse, seed_f=seed_fine, par=par),
        dict(pay=(2 * steps + 1, count_f, cells), payc=(2, cycles * count_c, cells)),
        {},
    )
    pay, payc = paid["pay"], paid["payc"]
    pay_o, payc_o = core_swap(pay), core_swap(payc)
    tables = call(
        wrapped(chem_kernel),
        dict(
            pay=pay,
            pay_o=pay_o,
            payc=payc,
            payc_o=payc_o,
            fine_counts=fine_counts,
            coarse_counts=coarse_counts,
        ),
        dict(
            gain=(steps, count_f, cells),
            weight=(steps, count_f, cells),
            gain_c=(cycles * count_c, cells),
            weight_c=(cycles * count_c, cells),
        ),
        {},
    )

    rows = 4 * (slots + count_c) + 1
    strip = (rows, 8, LANES)
    most = max(slots, count_c)
    common = dict(par=par, par_o=par_o)
    edge_scratch = dict(
        far_b=strip,
        far_a=strip,
        own_up=strip,
        own_down=strip,
        first=(most, 8, cells),
        edge=(most, 2, 2, 8, LANES),
        below=(most, 2, 2, 8, LANES),
        above=(most, 2, 2, 8, LANES),
    )
    up_scratch = dict(up=strip, down=strip)
    stage_scratch = dict(stage=((2 * messages + 7) // 8, slots, 8 * H, LANES))
    fine_shape = (slots, count_f, cells)
    coarse_shape = (count_c, 2 * fields, cells)

    def plan_of(**changes):
        plan = dict(
            fields=fields,
            count_f=count_f,
            count_c=count_c,
            messages=messages,
            arrivals=2 * messages,
            diffuse_fine=True,
            diffuse_coarse=None,
            add=False,
            react=True,
            react_coarse=None,
            step=0,
        )
        plan.update(changes)
        return plan

    def run(plan, inputs, outputs, scratch):
        return call(functools.partial(step_kernel, plan), inputs, outputs, scratch)

    def halo(made):
        return dict(
            sent_e=made["send_e"],
            sent_o=made["send_o"],
            got_e=pair_swap(made["send_e"], 0),
            got_o=pair_swap(made["send_o"], 1),
        )

    def arrivals(values):
        return {f"arrived{s}": value for s, value in enumerate(values)}

    chem = {name: tables[name] for name in ("gain", "weight")}
    chem_c = {name: tables[name] for name in ("gain_c", "weight_c")}
    send_shapes = dict(send_e=strip, send_o=strip)

    made = run(
        plan_of(diffuse_fine=False, add=True, react_coarse=cycles - 1, step=steps - 1),
        dict(
            common,
            **chem,
            **chem_c,
            seed_f=seed_fine,
            pay=pay,
            pay_o=pay_o,
            coarse=opened["coarse"],
            fine_nbr=fine_nbr,
            coarse_nbr=coarse_nbr,
            **arrivals(arrived),
        ),
        dict(fine_out=fine_shape, coarse_out=coarse_shape, **send_shapes),
        dict(up_scratch, **stage_scratch),
    )
    coarse = made["coarse_out"]
    coarse_final = None
    for step in reversed(range(1, steps)):
        cycle, late = step // 2, step % 2 == 1
        inputs = dict(common, **chem, fine=made["fine_out"], **halo(made))
        outputs = dict(fine_out=fine_shape, **send_shapes)
        scratch = dict(edge_scratch, **up_scratch)
        if late and cycle > 0:
            inputs.update(chem_c, coarse=coarse, children=children)
            outputs.update(coarse_out=coarse_shape, **octant_shapes)
            scratch.update(cells=cell_shape)
            plan = plan_of(diffuse_coarse="keep", react_coarse=cycle - 1, step=step - 1)
        elif late:
            plan = plan_of(step=step - 1)
        else:
            inputs.update(arrivals(arrived))
            scratch.update(stage_scratch)
            plan = plan_of(add=True, step=step - 1)
            if cycle == 1:
                inputs.update(coarse=coarse)
                outputs.update(coarse_final=seed_coarse.shape)
                scratch.update(coarse_next=coarse_shape)
                plan.update(diffuse_coarse="last")
        made = run(plan, inputs, outputs, scratch)
        if "coarse_out" in made:
            coarse = made["coarse_out"]
            arrived = travel(made)
        if "coarse_final" in made:
            coarse_final = made["coarse_final"]
    made = run(
        plan_of(react=False),
        dict(common, fine=made["fine_out"], **halo(made)),
        dict(fine_out=seed_fine.shape),
        edge_scratch,
    )
    return made["fine_out"], coarse_final


def solution(mesh):
    return jax.shard_map(
        shards,
        mesh=mesh,
        in_specs=(
            P("fld", "blk", None),
            P("fld", "blk", None),
            P(None, "fld", "blk", None),
            P(None, "fld", "blk", None),
            P("fld"),
            P("fld"),
            P("blk", None),
            P("blk", None),
            P("blk", None),
            P("blk"),
            P("blk"),
        ),
        out_specs=(P("fld", "blk", None), P("fld", "blk", None)),
        check_vma=False,
    )
```

time: 543 us -> 123 us (0.23); the launches traced: 534 us -> 123 us
  waiting for transfers between devices: 142 us -> 38.2 us
  starting transfers between devices: 122 us -> 24.3 us
  local copies, waits for them, and re-layouts: 91.2 us -> 3.61 us
  matrix products: 83.2 us -> 0 us
  other arithmetic: 71.3 us -> 0.68 us
  Pallas kernels: 0 us -> 55.5 us
  between operations: 18.4 us -> 0.8 us
  blocking collectives: 6.85 us -> 0 us
    ppermute x45 -> x30, starting transfers between devices: 121 us -> 24.3 us  [the longest x8 11.7 us: octant_move(): return lax.ppermute(value, ('blk', 'fld'), pairs)]
    dot_general x176 -> x0, matrix products: 83.2 us -> none  [the longest x48 26 us: face_list(): result.append(jnp.dot(planes, table, precision=precise))]
    psum x5 -> x0, waiting for transfers between devices: 73.6 us -> none  [the longest x3 55.7 us: broadcast(): return lax.psum(kept, axis)]
    pallas_call x0 -> x8, Pallas kernels: none -> 55.5 us  [call(): pl.pallas_call(functools.partial(kernel, names), out_shape=[jax.ShapeDtyp...]
    reshape x153 -> x0, local copies, waits for them, and re-layouts: 48.7 us -> none  [the longest x48 16.7 us: place_ghost(): jnp.dot(ghost, table.T, precision=precise).reshape(fields, blocks, B ** 3)]
    slice x47 -> x0, local copies, waits for them, and re-layouts: 33.6 us -> none  [the longest x12 11.2 us: with_ghosts(): flat[:, :, :-B]]
    ppermute x45 -> x30, waiting for transfers between devices: 67.9 us -> 38.2 us  [the longest x8 21.2 us: pair_swap(): return lax.ppermute(value, 'blk', sorted(pairs))]
    concatenate x24 -> x0, other arithmetic: 18.3 us -> none  [the longest x12 10.3 us: ghost_faces(): jnp.concatenate([from_below, faces[5]], axis=1)]
  transfers between devices with their start and end apart: 50 -> 30, of which waited for: 24 -> 15; matrix products, arithmetic and copies ran while one was open for 25% -> 0% of each run, Pallas kernels for 0% -> 3%
where the time goes in v1:
time: 123 us
  Pallas kernels  55.5 us (45%)
  waiting for transfers between devices  38.2 us (31%)
  starting transfers between devices  24.3 us (20%)
  local copies, waits for them, and re-layouts  3.61 us (3%)
    pallas_call x8, Pallas kernels, call(): pl.pallas_call(functools.partial(kernel, names), out_shape=[jax.ShapeDtyp...  55.5 us
    ppermute x8, waiting for transfers between devices, pair_swap(): return lax.ppermute(value, 'blk', sorted(pairs))  21.2 us
    ppermute x8, waiting for transfers between devices, octant_move(): return lax.ppermute(value, ('blk', 'fld'), pairs)  13.8 us
    ppermute x8, starting transfers between devices, octant_move(): return lax.ppermute(value, ('blk', 'fld'), pairs)  11.7 us
    ppermute x8, starting transfers between devices, pair_swap(): return lax.ppermute(value, 'blk', sorted(pairs))  9.54 us
    unnamed x20, local copies, waits for them, and re-layouts  3.61 us
    ppermute x14, waiting for transfers between devices, core_swap(): return lax.ppermute(value, 'fld', [(0, 1), (1, 0)])  3.21 us
    ppermute x14, starting transfers between devices, core_swap(): return lax.ppermute(value, 'fld', [(0, 1), (1, 0)])  2.99 us
  transfers between devices with their start and end apart: 30, of which 15 were waited for; matrix products, arithmetic and copies ran while one was open for 0% of the time, Pallas kernels for 3%

profile of v1, /device:TPU:0, one launch (start us, length us, event | category | flops | bytes accessed | tf_op | source)
XLA Modules:
  0.0 123.0 jit_solution(16253042048234849575)
XLA Ops:
  1.3 1.6 %copy-done = f32[4,4,8,4096]{3,2,1,0:T(8,128)S(1)} copy-done((f32[4,4,8,4096]{3,2,1,0:T(8,128)S(1)}, f32[4,4,8,4096]{3,2,1,0:T(8,128)}, u32[]{:S(2)}) %copy-start) | copy-done | bytes 2097176
  6.8 2.0 %collective-permute-done.3.seed_other = f32[4,2,4096]{2,1,0:T(2,128)S(1)} collective-permute-done((f32[4,2,4096]{2,1,0:T(2,128)S(1)}, f32[4,2,4096]{2,1,0:T(2,128)S(1)}, u32[]{:S(2)}, u32[]{:S(2)}) %collective-permute-start.3) | collective-permute-done | bytes 131104 | tf_op jit(solution)/shard_map/ppermute | solution.py:24
  9.8 2.9 %collective-permute-start.4 = (f32[9,8,128]{2,1,0:T(8,128)S(1)}, f32[9,8,128]{2,1,0:T(8,128)S(1)}, u32[]{:S(2)}, u32[]{:S(2)}) collective-permute-start(f32[9,8,128]{2,1,0:T(8,128)S(1)} %get-tuple-element.41), channel_id=1, source_target_pairs={{0,2},{1,9},{2,4},{3,11},{4,6},{5,13},{6,8},{7,15},{8,10},{9,17},{... | collective-permute-start | bytes 110600 | tf_op jit(solution)/shard_map/ppermute | solution.py:47
  12.7 1.5 %collective-permute-start.5 = (f32[9,8,128]{2,1,0:T(8,128)S(1)}, f32[9,8,128]{2,1,0:T(8,128)S(1)}, u32[]{:S(2)}, u32[]{:S(2)}) collective-permute-start(f32[9,8,128]{2,1,0:T(8,128)S(1)} %get-tuple-element.42), channel_id=1, source_target_pairs={{0,4},{1,11},{2,6},{3,13},{4,8},{5,15},{6,10},{7,17},{8,12},{9,19}... | collective-permute-start | bytes 110600 | tf_op jit(solution)/shard_map/ppermute | solution.py:47
  14.3 2.4 %collective-permute-start.6 = (f32[9,8,128]{2,1,0:T(8,128)S(1)}, f32[9,8,128]{2,1,0:T(8,128)S(1)}, u32[]{:S(2)}, u32[]{:S(2)}) collective-permute-start(f32[9,8,128]{2,1,0:T(8,128)S(1)} %get-tuple-element.43), channel_id=1, source_target_pairs={{0,6},{1,13},{2,8},{3,15},{4,10},{5,17},{6,12},{7,19},{8,14},{9,21... | collective-permute-start | bytes 110600 | tf_op jit(solution)/shard_map/ppermute | solution.py:47
  16.7 2.6 %collective-permute-start.7 = (f32[9,8,128]{2,1,0:T(8,128)S(1)}, f32[9,8,128]{2,1,0:T(8,128)S(1)}, u32[]{:S(2)}, u32[]{:S(2)}) collective-permute-start(f32[9,8,128]{2,1,0:T(8,128)S(1)} %get-tuple-element.44), channel_id=1, source_target_pairs={{0,14},{1,15},{2,16},{3,17},{4,18},{5,19},{6,20},{7,21},{8,22},{9,... | collective-permute-start | bytes 110600 | tf_op jit(solution)/shard_map/ppermute | solution.py:47
  20.9 1.8 %collective-permute-done.7.refs_15_ = f32[9,8,128]{2,1,0:T(8,128)S(1)} collective-permute-done((f32[9,8,128]{2,1,0:T(8,128)S(1)}, f32[9,8,128]{2,1,0:T(8,128)S(1)}, u32[]{:S(2)}, u32[]{:S(2)}) %collective-permute-start.7) | collective-permute-done | bytes 36896 | tf_op jit(solution)/shard_map/ppermute | solution.py:47
  23.3 3.2 %shard_map.123 = (f32[4,8,4096]{2,1,0:T(8,128)S(1)}, f32[4,8,4096]{2,1,0:T(8,128)S(1)}, f32[4,4096]{1,0:T(4,128)S(1)}, f32[4,4096]{1,0:T(4,128)S(1)}) custom-call(f32[9,8,4096]{2,1,0:T(8,128)S(1)} %get-tuple-element.34.refs_0_.refs_7_, f32[9,8,4096]{2,1,0:T(8,128)S(1)} %collective-permute-done.1.refs_1_.refs_8_, ...), custom_call_target="tpu_custom_call" | custom-call | flops 2000000 | bytes 2000000 | tf_op jit(solution)/shard_map/pallas_call | solution.py:728
  26.6 2.5 %shard_map.125 = (f32[5,8,4096]{2,1,0:T(8,128)S(1)}, f32[2,8,4096]{2,1,0:T(8,128)S(1)}, f32[29,8,128]{2,1,0:T(8,128)S(1)}, f32[29,8,128]{2,1,0:T(8,128)S(1)}) custom-call(f32[2,4]{1,0:T(2,128)S(1)} %pad_maximum_fusion.refs_3_.refs_0_, f32[2,4]{1,0:T(2,128)S(1)} %collective-permute-done.refs_1_, f32[4,8,4096]{2,1,0:T(8,128)S(1)} %get-tuple-element.36.refs_2_, ...), custom_call_target="tpu_custom_call" | custom-call | flops 2000000 | bytes 2000000 | tf_op jit(solution)/shard_map/pallas_call | solution.py:728
  29.2 1.6 %collective-permute-start.13 = (f32[29,8,128]{2,1,0:T(8,128)S(1)}, f32[29,8,128]{2,1,0:T(8,128)S(1)}, u32[]{:S(2)}, u32[]{:S(2)}) collective-permute-start(f32[29,8,128]{2,1,0:T(8,128)S(1)} %get-tuple-element.47.refs_5_), channel_id=1, source_target_pairs={{0,2},{2,0},{4,6},{6,4},{8,10},{10,8},{12,14},{14,12},{16,18},{18,... | collective-permute-start | bytes 356360 | tf_op jit(solution)/shard_map/ppermute | solution.py:33
  30.8 3.0 %collective-permute-start.14 = (f32[29,8,128]{2,1,0:T(8,128)S(1)}, f32[29,8,128]{2,1,0:T(8,128)S(1)}, u32[]{:S(2)}, u32[]{:S(2)}) collective-permute-start(f32[29,8,128]{2,1,0:T(8,128)S(1)} %get-tuple-element.48.refs_6_), channel_id=1, source_target_pairs={{0,30},{2,4},{4,2},{6,8},{8,6},{10,12},{12,10},{14,16},{16,14},{18... | collective-permute-start | bytes 356360 | tf_op jit(solution)/shard_map/ppermute | solution.py:33
  34.4 4.9 %collective-permute-done.14.refs_8_ = f32[29,8,128]{2,1,0:T(8,128)S(1)} collective-permute-done((f32[29,8,128]{2,1,0:T(8,128)S(1)}, f32[29,8,128]{2,1,0:T(8,128)S(1)}, u32[]{:S(2)}, u32[]{:S(2)}) %collective-permute-start.14) | collective-permute-done | bytes 118816 | tf_op jit(solution)/shard_map/ppermute | solution.py:33
  39.2 14.3 %shard_map.126 = (f32[5,8,4096]{2,1,0:T(8,128)S(1)}, f32[29,8,128]{2,1,0:T(8,128)S(1)}, f32[29,8,128]{2,1,0:T(8,128)S(1)}, f32[2,8,4096]{2,1,0:T(8,128)S(1)}, f3...) custom-call(f32[2,4]{1,0:T(2,128)S(1)} %pad_maximum_fusion.refs_3_.r, ...), custom_call_target="tpu_custom_call" | custom-call | flops 2000000 | bytes 2000000 | tf_op jit(solution)/shard_map/pallas_call | solution.py:728
  54.4 2.4 %collective-permute-start.16 = (f32[29,8,128]{2,1,0:T(8,128)S(1)}, f32[29,8,128]{2,1,0:T(8,128)S(1)}, u32[]{:S(2)}, u32[]{:S(2)}) collective-permute-start(f32[29,8,128]{2,1,0:T(8,128)S(1)} %get-tuple-element.52.refs_6_), channel_id=1, source_target_pairs={{0,30},{2,4},{4,2},{6,8},{8,6},{10,12},{12,10},{14,16},{16,14},{18... | collective-permute-start | bytes 356360 | tf_op jit(solution)/shard_map/ppermute | solution.py:33
  57.1 1.9 %collective-permute-start.19 = (f32[9,8,128]{2,1,0:T(8,128)S(1)}, f32[9,8,128]{2,1,0:T(8,128)S(1)}, u32[]{:S(2)}, u32[]{:S(2)}) collective-permute-start(f32[9,8,128]{2,1,0:T(8,128)S(1)} %get-tuple-element.55), channel_id=1, source_target_pairs={{0,6},{1,13},{2,8},{3,15},{4,10},{5,17},{6,12},{7,19},{8,14},{9,21... | collective-permute-start | bytes 110600 | tf_op jit(solution)/shard_map/ppermute | solution.py:47
  59.0 5.3 %collective-permute-done.17.refs_9_ = f32[9,8,128]{2,1,0:T(8,128)S(1)} collective-permute-done((f32[9,8,128]{2,1,0:T(8,128)S(1)}, f32[9,8,128]{2,1,0:T(8,128)S(1)}, u32[]{:S(2)}, u32[]{:S(2)}) %collective-permute-start.17) | collective-permute-done | bytes 36896 | tf_op jit(solution)/shard_map/ppermute | solution.py:47
  65.0 5.1 %collective-permute-done.20.refs_12_ = f32[9,8,128]{2,1,0:T(8,128)S(1)} collective-permute-done((f32[9,8,128]{2,1,0:T(8,128)S(1)}, f32[9,8,128]{2,1,0:T(8,128)S(1)}, u32[]{:S(2)}, u32[]{:S(2)}) %collective-permute-start.20) | collective-permute-done | bytes 36896 | tf_op jit(solution)/shard_map/ppermute | solution.py:47
  71.9 16.9 %shard_map.127 = (f32[5,8,4096]{2,1,0:T(8,128)S(1)}, f32[29,8,128]{2,1,0:T(8,128)S(1)}, f32[29,8,128]{2,1,0:T(8,128)S(1)}, f32[4,2,4096]{2,1,0:T(2,128)}) custom-call(f32[2,4]{1,0:T(2,128)S(1)} %pad_maximum_fusion.refs_3_.refs_0_, f32[2,4]{1,0:T(2,128)S(1)} %collective-permute-done.refs_1_, f32[4,8,4096]{2,1,0:T(8,128)S(1)} %get-tuple-element.36.refs_2_, ...), custom_call_target="tpu_custom_call" | custom-call | flops 2000000 | bytes 2000000 | tf_op jit(solution)/shard_map/pallas_call | solution.py:728
  89.7 5.2 %collective-permute-done.26.refs_7_ = f32[29,8,128]{2,1,0:T(8,128)S(1)} collective-permute-done((f32[29,8,128]{2,1,0:T(8,128)S(1)}, f32[29,8,128]{2,1,0:T(8,128)S(1)}, u32[]{:S(2)}, u32[]{:S(2)}) %collective-permute-start.26) | collective-permute-done | bytes 118816 | tf_op jit(solution)/shard_map/ppermute | solution.py:33
  94.8 2.8 %collective-permute-done.27.refs_8_ = f32[29,8,128]{2,1,0:T(8,128)S(1)} collective-permute-done((f32[29,8,128]{2,1,0:T(8,128)S(1)}, f32[29,8,128]{2,1,0:T(8,128)S(1)}, u32[]{:S(2)}, u32[]{:S(2)}) %collective-permute-start.27) | collective-permute-done | bytes 118816 | tf_op jit(solution)/shard_map/ppermute | solution.py:33
  97.6 9.0 %shard_map.128 = (f32[5,8,4096]{2,1,0:T(8,128)S(1)}, f32[29,8,128]{2,1,0:T(8,128)S(1)}, f32[29,8,128]{2,1,0:T(8,128)S(1)}) custom-call(f32[2,4]{1,0:T(2,128)S(1)} %pad_maximum_fusion.refs_3_.refs_0_, f32[2,4]{1,0:T(2,128)S(1)} %collective-permute-done.refs_1_, f32[4,8,4096]{2,1,0:T(8,128)S(1)} %get-tuple-element.36.refs_2_, ...), custom_call_target="tpu_custom_call" | custom-call | flops 2000000 | bytes 2000000 | tf_op jit(solution)/shard_map/pallas_call | solution.py:728
  107.4 5.0 %collective-permute-done.28.refs_5_ = f32[29,8,128]{2,1,0:T(8,128)S(1)} collective-permute-done((f32[29,8,128]{2,1,0:T(8,128)S(1)}, f32[29,8,128]{2,1,0:T(8,128)S(1)}, u32[]{:S(2)}, u32[]{:S(2)}) %collective-permute-start.28) | collective-permute-done | bytes 118816 | tf_op jit(solution)/shard_map/ppermute | solution.py:33
  112.4 2.8 %collective-permute-done.29.refs_6_ = f32[29,8,128]{2,1,0:T(8,128)S(1)} collective-permute-done((f32[29,8,128]{2,1,0:T(8,128)S(1)}, f32[29,8,128]{2,1,0:T(8,128)S(1)}, u32[]{:S(2)}, u32[]{:S(2)}) %collective-permute-start.29) | collective-permute-done | bytes 118816 | tf_op jit(solution)/shard_map/ppermute | solution.py:33
  115.2 7.8 %shard_map.129 = f32[4,8,4096]{2,1,0:T(8,128)} custom-call(f32[2,4]{1,0:T(2,128)S(1)} %pad_maximum_fusion.refs_3_.refs_0_, f32[2,4]{1,0:T(2,128)S(1)} %collective-permute-done.refs_1_, f32[5,8,4096]{2,1,0:T(8,128)S(1)} %get-tuple-element.62.refs_2_, f32[29,8,128]{2,1,0:T(8,128)S(1)} %get-tuple-element.63.refs_3_, ...), custom_call_target="tpu_custom_call" | custom-call | flops 2000000 | bytes 2000000 | tf_op jit(solution)/shard_map/pallas_call | solution.py:728
  (65 shorter events, 13.5 us)
Async XLA Ops:
  5.6 17.1 %collective-permute-start.1 = (f32[9,8,4096]{2,1,0:T(8,128)S(1)}, f32[9,8,4096]{2,1,0:T(8,128)S(1)}, u32[]{:S(2)}, u32[]{:S(2)}) collective-permute-start(f32[9,8,4096]{2,1,0:T(8,128)S(1)} %get-tuple-element.34.refs_0_.refs_7_), channel_id=1, source_target_pairs={{0,1},{1,0},{2,3},{3,2},{4,5},{5,4},{6,7},{7,6},{8,9},{9,8},{10,11... | collective-permute-start | bytes 3538952 | tf_op jit(solution)/shard_map/ppermute | solution.py:24
  6.3 10.5 %collective-permute-start.2 = (f32[2,4,4096]{2,1,0:T(4,128)S(1)}, f32[2,4,4096]{2,1,0:T(4,128)S(1)}, u32[]{:S(2)}, u32[]{:S(2)}) collective-permute-start(f32[2,4,4096]{2,1,0:T(4,128)S(1)} %get-tuple-element.35.refs_2_), channel_id=1, source_target_pairs={{0,1},{1,0},{2,3},{3,2},{4,5},{5,4},{6,7},{7,6},{8,9},{9,8},{10,11... | collective-permute-start | bytes 393224 | tf_op jit(solution)/shard_map/ppermute | solution.py:24
  6.7 7.6 %collective-permute-start = (f32[2,4]{1,0:T(2,128)S(1)}, f32[2,4]{1,0:T(2,128)S(1)}, u32[]{:S(2)}, u32[]{:S(2)}) collective-permute-start(f32[2,4]{1,0:T(2,128)S(1)} %pad_maximum_fusion.refs_3_.refs_0_), channel_id=1, source_target_pairs={{0,1},{1,0},{2,3},{3,2},{4,5},{5,4},{6,7},{7,6},{8,9},{9,8},{10,11... | collective-permute-start | bytes 104 | tf_op jit(solution)/shard_map/ppermute | solution.py:24
  9.8 9.5 %collective-permute-start.4 = (f32[9,8,128]{2,1,0:T(8,128)S(1)}, f32[9,8,128]{2,1,0:T(8,128)S(1)}, u32[]{:S(2)}, u32[]{:S(2)}) collective-permute-start(f32[9,8,128]{2,1,0:T(8,128)S(1)} %get-tuple-element.41), channel_id=1, source_target_pairs={{0,2},{1,9},{2,4},{3,11},{4,6},{5,13},{6,8},{7,15},{8,10},{9,17},{... | collective-permute-start | bytes 110600 | tf_op jit(solution)/shard_map/ppermute | solution.py:47
  12.7 7.0 %collective-permute-start.5 = (f32[9,8,128]{2,1,0:T(8,128)S(1)}, f32[9,8,128]{2,1,0:T(8,128)S(1)}, u32[]{:S(2)}, u32[]{:S(2)}) collective-permute-start(f32[9,8,128]{2,1,0:T(8,128)S(1)} %get-tuple-element.42), channel_id=1, source_target_pairs={{0,4},{1,11},{2,6},{3,13},{4,8},{5,15},{6,10},{7,17},{8,12},{9,19}... | collective-permute-start | bytes 110600 | tf_op jit(solution)/shard_map/ppermute | solution.py:47
  14.3 6.7 %collective-permute-start.6 = (f32[9,8,128]{2,1,0:T(8,128)S(1)}, f32[9,8,128]{2,1,0:T(8,128)S(1)}, u32[]{:S(2)}, u32[]{:S(2)}) collective-permute-start(f32[9,8,128]{2,1,0:T(8,128)S(1)} %get-tuple-element.43), channel_id=1, source_target_pairs={{0,6},{1,13},{2,8},{3,15},{4,10},{5,17},{6,12},{7,19},{8,14},{9,21... | collective-permute-start | bytes 110600 | tf_op jit(solution)/shard_map/ppermute | solution.py:47
  16.7 6.0 %collective-permute-start.7 = (f32[9,8,128]{2,1,0:T(8,128)S(1)}, f32[9,8,128]{2,1,0:T(8,128)S(1)}, u32[]{:S(2)}, u32[]{:S(2)}) collective-permute-start(f32[9,8,128]{2,1,0:T(8,128)S(1)} %get-tuple-element.44), channel_id=1, source_target_pairs={{0,14},{1,15},{2,16},{3,17},{4,18},{5,19},{6,20},{7,21},{8,22},{9,... | collective-permute-start | bytes 110600 | tf_op jit(solution)/shard_map/ppermute | solution.py:47
  19.3 7.2 %collective-permute-start.12 = (f32[9,8,128]{2,1,0:T(8,128)S(1)}, f32[9,8,128]{2,1,0:T(8,128)S(1)}, u32[]{:S(2)}, u32[]{:S(2)}) collective-permute-start(f32[9,8,128]{2,1,0:T(8,128)S(1)} %get-tuple-element.45.refs_16_), channel_id=1, source_target_pairs={{0,1},{1,0},{2,3},{3,2},{4,5},{5,4},{6,7},{7,6},{8,9},{9,8},{10,11... | collective-permute-start | bytes 110600 | tf_op jit(solution)/shard_map/ppermute | solution.py:24
  19.8 6.7 %collective-permute-start.8 = (f32[9,8,128]{2,1,0:T(8,128)S(1)}, f32[9,8,128]{2,1,0:T(8,128)S(1)}, u32[]{:S(2)}, u32[]{:S(2)}) collective-permute-start(f32[9,8,128]{2,1,0:T(8,128)S(1)} %collective-permute-done.4.refs_12_), channel_id=1, source_target_pairs={{0,1},{1,0},{2,3},{3,2},{4,5},{5,4},{6,7},{7,6},{8,9},{9,8},{10,11... | collective-permute-start | bytes 110600 | tf_op jit(solution)/shard_map/ppermute | solution.py:24
  20.9 5.6 %collective-permute-start.9 = (f32[9,8,128]{2,1,0:T(8,128)S(1)}, f32[9,8,128]{2,1,0:T(8,128)S(1)}, u32[]{:S(2)}, u32[]{:S(2)}) collective-permute-start(f32[9,8,128]{2,1,0:T(8,128)S(1)} %collective-permute-done.5.refs_13_), channel_id=1, source_target_pairs={{0,1},{1,0},{2,3},{3,2},{4,5},{5,4},{6,7},{7,6},{8,9},{9,8},{10,11... | collective-permute-start | bytes 110600 | tf_op jit(solution)/shard_map/ppermute | solution.py:24
  29.2 5.2 %collective-permute-start.13 = (f32[29,8,128]{2,1,0:T(8,128)S(1)}, f32[29,8,128]{2,1,0:T(8,128)S(1)}, u32[]{:S(2)}, u32[]{:S(2)}) collective-permute-start(f32[29,8,128]{2,1,0:T(8,128)S(1)} %get-tuple-element.47.refs_5_), channel_id=1, source_target_pairs={{0,2},{2,0},{4,6},{6,4},{8,10},{10,8},{12,14},{14,12},{16,18},{18,... | collective-permute-start | bytes 356360 | tf_op jit(solution)/shard_map/ppermute | solution.py:33
  30.8 8.5 %collective-permute-start.14 = (f32[29,8,128]{2,1,0:T(8,128)S(1)}, f32[29,8,128]{2,1,0:T(8,128)S(1)}, u32[]{:S(2)}, u32[]{:S(2)}) collective-permute-start(f32[29,8,128]{2,1,0:T(8,128)S(1)} %get-tuple-element.48.refs_6_), channel_id=1, source_target_pairs={{0,30},{2,4},{4,2},{6,8},{8,6},{10,12},{12,10},{14,16},{16,14},{18... | collective-permute-start | bytes 356360 | tf_op jit(solution)/shard_map/ppermute | solution.py:33
  53.6 18.3 %collective-permute-start.15 = (f32[29,8,128]{2,1,0:T(8,128)S(1)}, f32[29,8,128]{2,1,0:T(8,128)S(1)}, u32[]{:S(2)}, u32[]{:S(2)}) collective-permute-start(f32[29,8,128]{2,1,0:T(8,128)S(1)} %get-tuple-element.51.refs_5_), channel_id=1, source_target_pairs={{0,2},{2,0},{4,6},{6,4},{8,10},{10,8},{12,14},{14,12},{16,18},{18,... | collective-permute-start | bytes 356360 | tf_op jit(solution)/shard_map/ppermute | solution.py:33
  54.4 17.5 %collective-permute-start.16 = (f32[29,8,128]{2,1,0:T(8,128)S(1)}, f32[29,8,128]{2,1,0:T(8,128)S(1)}, u32[]{:S(2)}, u32[]{:S(2)}) collective-permute-start(f32[29,8,128]{2,1,0:T(8,128)S(1)} %get-tuple-element.52.refs_6_), channel_id=1, source_target_pairs={{0,30},{2,4},{4,2},{6,8},{8,6},{10,12},{12,10},{14,16},{16,14},{18... | collective-permute-start | bytes 356360 | tf_op jit(solution)/shard_map/ppermute | solution.py:33
  56.8 7.6 %collective-permute-start.17 = (f32[9,8,128]{2,1,0:T(8,128)S(1)}, f32[9,8,128]{2,1,0:T(8,128)S(1)}, u32[]{:S(2)}, u32[]{:S(2)}) collective-permute-start(f32[9,8,128]{2,1,0:T(8,128)S(1)} %get-tuple-element.53), channel_id=1, source_target_pairs={{0,2},{1,9},{2,4},{3,11},{4,6},{5,13},{6,8},{7,15},{8,10},{9,17},{... | collective-permute-start | bytes 110600 | tf_op jit(solution)/shard_map/ppermute | solution.py:47
  56.8 7.6 %collective-permute-start.18 = (f32[9,8,128]{2,1,0:T(8,128)S(1)}, f32[9,8,128]{2,1,0:T(8,128)S(1)}, u32[]{:S(2)}, u32[]{:S(2)}) collective-permute-start(f32[9,8,128]{2,1,0:T(8,128)S(1)} %get-tuple-element.54), channel_id=1, source_target_pairs={{0,4},{1,11},{2,6},{3,13},{4,8},{5,15},{6,10},{7,17},{8,12},{9,19}... | collective-permute-start | bytes 110600 | tf_op jit(solution)/shard_map/ppermute | solution.py:47
  57.1 7.9 %collective-permute-start.19 = (f32[9,8,128]{2,1,0:T(8,128)S(1)}, f32[9,8,128]{2,1,0:T(8,128)S(1)}, u32[]{:S(2)}, u32[]{:S(2)}) collective-permute-start(f32[9,8,128]{2,1,0:T(8,128)S(1)} %get-tuple-element.55), channel_id=1, source_target_pairs={{0,6},{1,13},{2,8},{3,15},{4,10},{5,17},{6,12},{7,19},{8,14},{9,21... | collective-permute-start | bytes 110600 | tf_op jit(solution)/shard_map/ppermute | solution.py:47
  64.4 5.8 %collective-permute-start.20 = (f32[9,8,128]{2,1,0:T(8,128)S(1)}, f32[9,8,128]{2,1,0:T(8,128)S(1)}, u32[]{:S(2)}, u32[]{:S(2)}) collective-permute-start(f32[9,8,128]{2,1,0:T(8,128)S(1)} %get-tuple-element.56), channel_id=1, source_target_pairs={{0,14},{1,15},{2,16},{3,17},{4,18},{5,19},{6,20},{7,21},{8,22},{9,... | collective-permute-start | bytes 110600 | tf_op jit(solution)/shard_map/ppermute | solution.py:47
  64.4 5.8 %collective-permute-start.25 = (f32[9,8,128]{2,1,0:T(8,128)S(1)}, f32[9,8,128]{2,1,0:T(8,128)S(1)}, u32[]{:S(2)}, u32[]{:S(2)}) collective-permute-start(f32[9,8,128]{2,1,0:T(8,128)S(1)} %get-tuple-element.57.refs_13_), channel_id=1, source_target_pairs={{0,1},{1,0},{2,3},{3,2},{4,5},{5,4},{6,7},{7,6},{8,9},{9,8},{10,11... | collective-permute-start | bytes 110600 | tf_op jit(solution)/shard_map/ppermute | solution.py:24
  65.0 5.7 %collective-permute-start.21 = (f32[9,8,128]{2,1,0:T(8,128)S(1)}, f32[9,8,128]{2,1,0:T(8,128)S(1)}, u32[]{:S(2)}, u32[]{:S(2)}) collective-permute-start(f32[9,8,128]{2,1,0:T(8,128)S(1)} %collective-permute-done.17.refs_9_), channel_id=1, source_target_pairs={{0,1},{1,0},{2,3},{3,2},{4,5},{5,4},{6,7},{7,6},{8,9},{9,8},{10,11... | collective-permute-start | bytes 110600 | tf_op jit(solution)/shard_map/ppermute | solution.py:24
  88.7 6.1 %collective-permute-start.26 = (f32[29,8,128]{2,1,0:T(8,128)S(1)}, f32[29,8,128]{2,1,0:T(8,128)S(1)}, u32[]{:S(2)}, u32[]{:S(2)}) collective-permute-start(f32[29,8,128]{2,1,0:T(8,128)S(1)} %get-tuple-element.60.refs_5_), channel_id=1, source_target_pairs={{0,2},{2,0},{4,6},{6,4},{8,10},{10,8},{12,14},{14,12},{16,18},{18,... | collective-permute-start | bytes 356360 | tf_op jit(solution)/shard_map/ppermute | solution.py:33
  88.7 8.9 %collective-permute-start.27 = (f32[29,8,128]{2,1,0:T(8,128)S(1)}, f32[29,8,128]{2,1,0:T(8,128)S(1)}, u32[]{:S(2)}, u32[]{:S(2)}) collective-permute-start(f32[29,8,128]{2,1,0:T(8,128)S(1)} %get-tuple-element.61.refs_6_), channel_id=1, source_target_pairs={{0,30},{2,4},{4,2},{6,8},{8,6},{10,12},{12,10},{14,16},{16,14},{18... | collective-permute-start | bytes 356360 | tf_op jit(solution)/shard_map/ppermute | solution.py:33
  106.6 5.8 %collective-permute-start.28 = (f32[29,8,128]{2,1,0:T(8,128)S(1)}, f32[29,8,128]{2,1,0:T(8,128)S(1)}, u32[]{:S(2)}, u32[]{:S(2)}) collective-permute-start(f32[29,8,128]{2,1,0:T(8,128)S(1)} %get-tuple-element.63.refs_3_), channel_id=1, source_target_pairs={{0,2},{2,0},{4,6},{6,4},{8,10},{10,8},{12,14},{14,12},{16,18},{18,... | collective-permute-start | bytes 356360 | tf_op jit(solution)/shard_map/ppermute | solution.py:33
  106.7 8.5 %collective-permute-start.29 = (f32[29,8,128]{2,1,0:T(8,128)S(1)}, f32[29,8,128]{2,1,0:T(8,128)S(1)}, u32[]{:S(2)}, u32[]{:S(2)}) collective-permute-start(f32[29,8,128]{2,1,0:T(8,128)S(1)} %get-tuple-element.64.refs_4_), channel_id=1, source_target_pairs={{0,30},{2,4},{4,2},{6,8},{8,6},{10,12},{12,10},{14,16},{16,14},{18... | collective-permute-start | bytes 356360 | tf_op jit(solution)/shard_map/ppermute | solution.py:33
  (16 other events, 81.4 us)

commit v2 on v1

v2 whole, which is shorter than its diff:
```python
import functools
import jax
import numpy as np
import jax.numpy as jnp
from jax import lax
from jax.experimental import pallas as pl
from jax.experimental.pallas import tpu as pltpu
from jax.sharding import PartitionSpec as P

B = 16
H = B // 2
NSUB = 4
G = 4
HG = B // G
PLANE = B * B
CYCLES = 2
LANES = 128
TILES = B**3 // LANES
PACK = LANES // G
HEAT = 0.5
ENERGY = 2.0
FAR = -(1 << 20)
VMEM = pl.BlockSpec(memory_space=pltpu.VMEM)
SMEM = pl.BlockSpec(memory_space=pltpu.SMEM)
F32 = jnp.float32
BF16 = jnp.bfloat16


def core_swap(value):
    return lax.ppermute(value, "fld", [(0, 1), (1, 0)])


def pair_swap(value, first):
    n = lax.axis_size("blk")
    pairs = []
    for i in range(first, n + first, 2):
        a, b = i % n, (i + 1) % n
        pairs += [(a, b), (b, a)]
    return lax.ppermute(value, "blk", sorted(pairs))


def octant_sends(count):
    half = count // 2
    return [(1 + s if 1 + s < half else count - 1, half + s) for s in range(half)]


def octant_move(value, distances):
    n = lax.axis_size("blk")
    pairs = []
    for i in range(n):
        for core in range(2):
            pairs.append((2 * i + core, 2 * ((i + distances[core]) % n) + core))
    return lax.ppermute(value, ("blk", "fld"), pairs)


def tables():
    cell = np.arange(PLANE)
    j, k = cell // B, cell % B
    near = np.abs(j[:, None] - j[None, :]) + np.abs(k[:, None] - k[None, :])
    plane = (near == 1).astype(np.float32)
    side = np.zeros((LANES, PLANE), np.float32)
    line = np.arange(B)
    side[line, (B - 1) * B + line] = 1
    side[LANES - B + line, line] = 1
    place = np.zeros((2 * LANES, G * PLANE), np.float32)
    pack = np.zeros((G, PLANE, 2 * LANES), np.float32)
    far = np.zeros((2 * LANES, LANES), np.float32)
    for g in range(G):
        at = g * PACK + line
        place[at, g * PLANE + line * B] = 1
        place[LANES + at, g * PLANE + line * B + B - 1] = 1
        for depth in range(2):
            pack[g, line * B + B - 1 - depth, at + depth * B] = 1
            pack[g, line * B + depth, LANES + at + depth * B] = 1
        far[at[:-1], at[1:]] = 1
        far[at[1:], at[:-1]] = 1
        far[at + B, at] = 1
        far[LANES + at[B - 1], at[0]] = 1
        far[LANES + at[0], at[B - 1]] = 1
    return dict(
        plane=jnp.asarray(plane, BF16),
        side=jnp.asarray(side, BF16),
        place=jnp.asarray(place, BF16),
        pack=jnp.asarray(pack, BF16),
        far=jnp.asarray(far, BF16),
    )


def lane_ids():
    return lax.broadcasted_iota(jnp.int32, (8, LANES), 1)


def row_ids():
    return lax.broadcasted_iota(jnp.int32, (8, LANES), 0)


def roll(x, steps):
    steps = steps % LANES
    return x if steps == 0 else pltpu.roll(x, steps, 1)


def cols(i, jh, width=1):
    return pl.ds((2 * i + jh) * LANES, width * LANES)


def half(jh):
    return pl.ds(jh * LANES, LANES)


def rows_of(i, count=1):
    return pl.ds(8 * i, 8 * count)


def split(x):
    high = x.astype(BF16)
    return high, (x - high.astype(F32)).astype(BF16)


def product(pairs):
    total = None
    for a, b in pairs:
        term = jnp.dot(a, b, preferred_element_type=F32)
        total = term if total is None else total + term
    return total


class Links:
    def __init__(self, column, base, count, by_rows, first_slab):
        self.count = count
        self.by_rows = by_rows
        self.column = column
        self.base = base
        self.first_slab = first_slab
        self.cache = {}

    def place(self, slab, face, shift=0):
        raw = jnp.broadcast_to(self.column(slab, face), (8, LANES))
        return jnp.where(raw >= 0, raw - (self.base + shift), FAR)

    def make(self, name, slab):
        lane = lane_ids()
        if name == "j":
            return jnp.where(lane < LANES // 2, self.place(slab, 3), self.place(slab, 2))
        if name == "j_packed":
            return jnp.where(lane % B == B - 1, self.place(slab, 2), self.place(slab, 3))
        face, step = name
        return self.place(slab, face, step * self.count)

    def index(self, name, slab):
        key = (name, None if self.by_rows else slab)
        if key not in self.cache:
            where = self.make(name, slab - self.first_slab)
            if self.by_rows:
                there = (where >= 0) & (where < self.count)
                self.cache[key] = (jnp.clip(where, 0, self.count - 1), there)
            else:
                self.cache[key] = [where == q for q in range(self.count)]
        return self.cache[key]

    def read(self, name, slab, tile):
        where = self.index(name, slab)
        if self.by_rows:
            got = jnp.take_along_axis(tile(slab), where[0], axis=0, mode="promise_in_bounds")
            return jnp.where(where[1], got, 0.0)
        result = jnp.zeros((8, LANES), F32)
        for q in range(self.count):
            result = jnp.where(where[q], tile(self.first_slab + q), result)
        return result


def put_split(ref, at, lead, value, high_at, low_at):
    high, low = split(value)
    ref[lead + (at, high_at)] = high
    ref[lead + (at, low_at)] = low


def build_planes(source, slabs, planes):
    for s in range(slabs):
        for i in range(0, B, 2):
            g, h = i // HG, i % HG
            for jh in range(2):
                put_split(
                    planes,
                    rows_of(s * HG + h, 2),
                    (g,),
                    source[s, jh, rows_of(i, 2), :],
                    half(jh),
                    half(2 + jh),
                )


def build_sides(source, slabs, near, planes):
    lane = lane_ids()
    for s in range(slabs):
        for i in range(0, B, 2):
            g, h = i // HG, i % HG
            edge = []
            for n in (i, i + 1):

                def tile(q, n=n):
                    return jnp.where(
                        lane < LANES // 2,
                        source[q, 0, rows_of(n), :],
                        source[q, 1, rows_of(n), :],
                    )

                edge.append(near(s).read("j", s, tile))
            put_split(
                planes,
                rows_of(s * HG + h, 2),
                (g,),
                jnp.concatenate(edge, axis=0),
                pl.ds(2 * PLANE, LANES),
                pl.ds(2 * PLANE + LANES, LANES),
            )


def pack_faces(planes, table, used):
    pairs = []
    for g in range(G):
        pairs.append((planes[g, pl.ds(0, used), pl.ds(0, PLANE)], table[g]))
        pairs.append((planes[g, pl.ds(0, used), pl.ds(PLANE, PLANE)], table[g]))
    return product(pairs)


def laplace(source, slabs, near, up, down, below, above, mats, work, emit):
    planes, sums, ends, placed = work["planes"], work["sums"], work["ends"], work["placed"]
    used = slabs * HG * 8
    for s in range(slabs):
        for h in range(0, HG, 2):
            for side in range(2):
                pieces = []
                for n in (h, h + 1):
                    if side == 0:
                        value = near(s).read((4, 0), s, lambda q, n=n: up(q, n))
                        value = value + near(s).read((4, -1), s, lambda q, n=n: below(q, n))
                    else:
                        value = near(s).read((5, 0), s, lambda q, n=n: down(q, n))
                        value = value + near(s).read((5, 1), s, lambda q, n=n: above(q, n))
                    pieces.append(value)
                put_split(
                    ends,
                    rows_of(s * HG + h, 2),
                    (),
                    jnp.concatenate(pieces, axis=0),
                    half(side),
                    half(2 + side),
                )
    every = pl.ds(0, used)
    plane, side = mats["plane"][...], mats["side"][...]
    for g in range(G):
        sums[g, every, :] = product(
            [
                (planes[g, every, pl.ds(0, PLANE)], plane),
                (planes[g, every, pl.ds(PLANE, PLANE)], plane),
                (planes[g, every, pl.ds(2 * PLANE, LANES)], side),
                (planes[g, every, pl.ds(2 * PLANE + LANES, LANES)], side),
            ]
        )
    for g in range(G):
        table = mats["place"][:, pl.ds(g * PLANE, PLANE)]
        placed[every, pl.ds(g * PLANE, PLANE)] = product(
            [
                (ends[every, pl.ds(0, 2 * LANES)], table),
                (ends[every, pl.ds(2 * LANES, 2 * LANES)], table),
            ]
        )
    for s in range(slabs):
        for i in range(B):
            g, h = i // HG, i % HG
            at = rows_of(s * HG + h)
            for jh in range(2):
                c = source[s, jh, rows_of(i), :]
                if i > 0:
                    before = source[s, jh, rows_of(i - 1), :]
                else:
                    before = near(s).read(
                        (0, 0), s, lambda q, jh=jh: source[q, jh, rows_of(B - 1), :]
                    )
                if i < B - 1:
                    after = source[s, jh, rows_of(i + 1), :]
                else:
                    after = near(s).read((1, 0), s, lambda q, jh=jh: source[q, jh, rows_of(0), :])
                lap = (before + after) - 6.0 * c
                lap = lap + (
                    sums[g, at, half(jh)] + placed[at, pl.ds(g * PLANE + jh * LANES, LANES)]
                )
                emit(s, i, jh, c, lap)


def laplace_far(slabs, sides, mats, work, emit):
    lhs, out = work["far_lhs"], work["far_out"]
    group = lane_ids() // PACK
    for n, (links, tile, _, _) in enumerate(sides):
        for s in range(slabs):
            for h in range(0, HG, 2):
                c = jnp.concatenate([tile(s, h), tile(s, h + 1)], axis=0)
                edge = jnp.concatenate(
                    [
                        links(s).read("j_packed", s, lambda q, m=m: tile(q, m))
                        for m in (h, h + 1)
                    ],
                    axis=0,
                )
                at = rows_of((n * slabs + s) * HG + h, 2)
                put_split(lhs, at, (), c, half(0), half(2))
                put_split(lhs, at, (), edge, half(1), half(3))
    every = pl.ds(0, 2 * slabs * HG * 8)
    table = mats["far"][...]
    out[every, :] = product(
        [
            (lhs[every, pl.ds(0, 2 * LANES)], table),
            (lhs[every, pl.ds(2 * LANES, 2 * LANES)], table),
        ]
    )
    for n, (links, tile, own, own_name) in enumerate(sides):
        for s in range(slabs):
            for h in range(HG):
                c = tile(s, h)
                if h > 0:
                    before = tile(s, h - 1)
                else:
                    wrap = links(s).read((0, 0), s, lambda q: tile(q, HG - 1))
                    before = roll(jnp.where(group == G - 1, wrap, tile(s, HG - 1)), PACK)
                if h < HG - 1:
                    after = tile(s, h + 1)
                else:
                    wrap = links(s).read((1, 0), s, lambda q: tile(q, 0))
                    after = roll(jnp.where(group == 0, wrap, tile(s, 0)), -PACK)
                inner = links(s).read(own_name, s, lambda q: own(q, h))
                lap = (before + after) + inner + out[rows_of((n * slabs + s) * HG + h), :] - 6.0 * c
                emit(n, s, h, lap)


def diffuse(source, slabs, near, from_below, from_above, rate, up, down, below, above, mats, work, finish):
    first, packed = work["first"], work["packed"]
    far_first = work["far_first"]
    build_planes(source, slabs, work["planes"])
    build_sides(source, slabs, near, work["planes"])

    def keep_first(s, i, jh, c, lap):
        first[s, jh, rows_of(i), :] = rate(s) * lap

    laplace(source, slabs, near, up, down, below, above, mats, work, keep_first)

    def keep_far(n, s, h, lap):
        far_first[n, s * HG + h] = rate(s) * lap

    laplace_far(
        slabs,
        ((from_below, below, down, (5, 1)), (from_above, above, up, (4, -1))),
        mats,
        work,
        keep_far,
    )
    build_planes(first, slabs, work["planes"])
    build_sides(first, slabs, near, work["planes"])
    packed[pl.ds(0, slabs * HG * 8), :] = pack_faces(work["planes"], mats["pack"], slabs * HG * 8)

    def last(s, i, jh, c, lap):
        finish(s, i, jh, source[s, jh, rows_of(i), :] + c + 0.5 * rate(s) * lap)

    laplace(
        first,
        slabs,
        near,
        lambda s, h: packed[rows_of(s * HG + h), half(0)],
        lambda s, h: packed[rows_of(s * HG + h), half(1)],
        lambda s, h: far_first[0, s * HG + h],
        lambda s, h: far_first[1, s * HG + h],
        mats,
        work,
        last,
    )


def pick(core, a, b):
    return jnp.where(core == 0, a, b)


def spread_vector(core, own, other, row, fields):
    rows = row_ids()
    result = jnp.zeros((8, LANES), F32)
    for f in range(2 * fields):
        value = pick(core, own[row, f], other[row, f]) if f < fields else pick(
            core, other[row, f - fields], own[row, f - fields]
        )
        result = jnp.where(rows == f, value, result)
    return result


def mix_kernel(saved_f, saved_c, seed_f, par, pay, payc):
    steps, fields = saved_f.shape[0], saved_f.shape[1]
    cycles, blocks = saved_c.shape[0], saved_c.shape[2]
    for s in range(steps):
        total = par[1, 0] * saved_f[s, 0]
        for v in range(1, fields):
            total = total + par[1, v] * saved_f[s, v]
        pay[s] = total
        pay[steps + s] = saved_f[s, 0]
    pay[2 * steps] = seed_f[0]
    for c in range(cycles):
        total = par[1, 0] * saved_c[c, 0]
        for v in range(1, fields):
            total = total + par[1, v] * saved_c[c, v]
        payc[0, pl.ds(c * blocks, blocks), :] = total
        payc[1, pl.ds(c * blocks, blocks), :] = saved_c[c, 0]


def reaction_tables(mix, start, counts):
    step = HEAT / counts.astype(F32)
    state = start
    history = []
    for n in range(NSUB):
        inverse = 1.0 / state
        decay = jnp.exp(-ENERGY * inverse)
        active = n < counts
        history.append((active, inverse, decay))
        state = state + jnp.where(active, step * mix * decay, 0.0)
    passed = jnp.ones_like(start)
    weight = jnp.zeros_like(start)
    for active, inverse, decay in reversed(history):
        grown = jnp.where(active, step * decay, 0.0)
        weight = weight + grown * passed
        passed = passed * (1.0 + grown * mix * ENERGY * (inverse * inverse))
    return passed - 1.0, weight


def chem_kernel(pay, pay_o, payc, payc_o, fine_counts, coarse_counts, gain, weight, gain_c, weight_c):
    core = lax.axis_index("fld")
    steps = gain.shape[0]
    rows = row_ids()
    counts = jnp.ones((8, LANES), jnp.int32)
    for b in range(fine_counts.shape[0]):
        counts = jnp.where(rows == b, fine_counts[b], counts)
    blocks = coarse_counts.shape[0]
    entries = gain_c.shape[0]
    counts_c = jnp.ones((entries, LANES), jnp.int32)
    rows_c = lax.broadcasted_iota(jnp.int32, (entries, LANES), 0)
    for r in range(entries):
        counts_c = jnp.where(rows_c == r, coarse_counts[r % blocks], counts_c)

    def body(t, carry):
        at = pl.ds(pl.multiple_of(t * LANES, LANES), LANES)
        for s in range(steps):
            start = pick(core, pay[steps + s, :, at], pay_o[steps + s, :, at])
            a, w = reaction_tables(pay[s, :, at] + pay_o[s, :, at], start, counts)
            gain[s, :, at] = a
            weight[s, :, at] = w
        start = pick(core, payc[1, :, at], payc_o[1, :, at])
        a, w = reaction_tables(payc[0, :, at] + payc_o[0, :, at], start, counts_c)
        gain_c[:, at] = a
        weight_c[:, at] = w
        return carry

    lax.fori_loop(0, TILES, body, 0)


def octants_out(state, first_slab, children, count_f, outs):
    core = lax.axis_index("fld")
    me = lax.axis_index("blk")
    devices = lax.axis_size("blk")
    count_c = children.shape[0]
    fields = 8
    upper = lane_ids() % B // H
    found = []
    for p in range(count_c):
        for o in range(8):
            child = children[p, o]
            distance = jnp.where(child >= 0, (child // count_f - me) % devices, -1)
            found.append((distance, child, p, o))
    sends = octant_sends(count_f)
    for s, out in enumerate(outs):
        if s < len(sends):
            want = jnp.where(core == 0, sends[s][0], sends[s][1])
        else:
            want = 0
        slot = jnp.int32(0)
        label = jnp.int32(-1)
        for distance, child, p, o in found:
            hit = distance == want
            slot = jnp.where(hit, p * 8 + o, slot)
            label = jnp.where(hit, child % count_f, label)
        if s < len(sends):
            label = jnp.where((core == 0) & (sends[s][0] == count_f - 1), -1, label)
        else:
            label = jnp.where(core == 0, label, -1)
        p, a, b, c = slot // 8, slot // 4 % 2, slot // 2 % 2, slot % 2
        kept = upper == c
        for f in range(fields):
            layers = state[first_slab + p, b, pl.ds(a * (H * 8) + f, H, stride=8), :]
            out[f] = jnp.where(kept, layers, 0.0)
        out[fields] = jnp.full((H, LANES), label.astype(F32))


def keep_coarse(state, first_slab, children):
    upper = lane_ids() % B // H
    for p in range(children.shape[0]):
        for a in range(2):
            for b in range(2):
                low = jnp.where(children[p, 4 * a + 2 * b] < 0, 1.0, 0.0)
                high = jnp.where(children[p, 4 * a + 2 * b + 1] < 0, 1.0, 0.0)
                kept = jnp.where(upper == 0, low, high)
                for i in range(a * H, a * H + H):
                    at = (first_slab + p, b, rows_of(i))
                    state[at] = state[at] * kept


def seed_kernel(seed_c, seed_o, children, count_f, coarse, *rest):
    outs, stage = rest[:-1], rest[-1]
    core = lax.axis_index("fld")
    fields, count_c = seed_c.shape[0], seed_c.shape[1]
    for p in range(count_c):
        for v in range(fields):
            own = seed_c[v, pl.ds(p, 1), :]
            other = seed_o[v, pl.ds(p, 1), :]
            stage[p, pl.ds(v, 1), :] = pick(core, own, other)
            stage[p, pl.ds(fields + v, 1), :] = pick(core, other, own)
        for i in range(B):
            for jh in range(2):
                coarse[p, jh, rows_of(i), :] = stage[p, :, cols(i, jh)]
    octants_out(coarse, 0, children, count_f, outs)
    keep_coarse(coarse, 0, children)


def add_octants(messages, state, stage, fields):
    core = lax.axis_index("fld")
    slots = fields + 1
    rows = row_ids()
    lane = lane_ids()
    source = jnp.zeros((8, LANES), jnp.int32)
    for d, message in enumerate(messages):
        label = message[2 * fields].astype(jnp.int32)
        source = jnp.where(label == rows, d, source)
        for s in range(slots):
            if s == fields:
                value = message[0]
            else:
                value = message[pl.ds(core * fields + s, 1)][0]
            stage[d // 8, s, pl.ds(d % 8, H, stride=8), :] = value
    lanes_of = [((H // 2 * jh + lane // B // 2) * B + lane % B // 2) for jh in range(2)]
    groups = (len(messages) + 7) // 8
    indices = []
    for g in range(groups):
        index = source - 8 * g
        indices.append((jnp.clip(index, 0, 7), (index >= 0) & (index < 8)))
    for s in range(slots):
        for i in range(H):
            got = None
            for g in range(groups):
                part = jnp.take_along_axis(
                    stage[g, s, rows_of(i), :], indices[g][0], axis=0, mode="promise_in_bounds"
                )
                part = jnp.where(indices[g][1], part, 0.0)
                got = part if got is None else got + part
            got = 0.125 * (got + roll(got, -H))
            for jh in range(2):
                wide = jnp.take_along_axis(got, lanes_of[jh], axis=1, mode="promise_in_bounds")
                for ii in range(2):
                    at = (s, jh, rows_of(2 * i + ii))
                    state[at] = state[at] + wide


def react_fine(state, fields, par, par_o, gain, weight):
    core = lax.axis_index("fld")
    share = [par[1, s] for s in range(fields)] + [pick(core, par[1, 0], par_o[1, 0])]
    extra = jnp.where(core == 0, 1.0, 0.0)
    for i in range(B):
        for jh in range(2):
            at = cols(i, jh)
            here = (jh, rows_of(i))
            driver = state[(fields,) + here]
            heat = weight[:, at] * driver
            grown = gain[:, at] * driver
            for s in range(fields + 1):
                value = state[(s,) + here] + share[s] * heat
                if s == 0:
                    value = value + extra * grown
                if s == fields:
                    value = value + grown
                state[(s,) + here] = value


def react_coarse(state, first_slab, count_c, shares, gain, weight, first_row):
    own = jnp.where(row_ids() == 0, 1.0, 0.0)
    for p in range(count_c):
        for i in range(B):
            for jh in range(2):
                at = cols(i, jh)
                here = (first_slab + p, jh, rows_of(i))
                value = state[here]
                driver = jnp.broadcast_to(value[0:1], (8, LANES))
                heat = weight[pl.ds(first_row + p, 1), at] * driver
                grown = gain[pl.ds(first_row + p, 1), at] * driver
                state[here] = value + shares * heat + own * grown


def step_kernel(plan, names, *refs):
    r = dict(zip(names, refs))
    core = lax.axis_index("fld")
    me = lax.axis_index("blk")
    even = me % 2 == 0
    fields = plan["fields"]
    slots = fields + 1
    count_f, count_c = plan["count_f"], plan["count_c"]
    par, par_o = r["par"], r["par_o"]
    mats = {name: r[name] for name in MATS}

    if plan["slabs"]:
        slabs, arrived = plan["slabs"], plan["slabs_in"]
        own_up, own_down, far_b, far_a = (r[x] for x in ("own_up", "own_down", "far_b", "far_a"))

        @pl.when(even)
        def _():
            own_up[...] = r["sent_e"][...]
            own_down[...] = r["sent_o"][...]
            far_a[...] = r["got_e"][...]
            far_b[...] = r["got_o"][...]

        @pl.when(jnp.logical_not(even))
        def _():
            own_up[...] = r["sent_o"][...]
            own_down[...] = r["sent_e"][...]
            far_b[...] = r["got_e"][...]
            far_a[...] = r["got_o"][...]

        faces = own_up[arrived * HG]
        rate_of = [par[0, s] for s in range(fields)] + [pick(core, par[0, 0], par_o[0, 0])]
        if slabs > slots:
            rate_of += [0.5 * spread_vector(core, par, par_o, 0, fields)] * count_c

        def links_of(ref, shift):
            def column(slab, face):
                return ref[arrived * HG, :, pl.ds(face, 1)].astype(jnp.int32)

            def column_c(slab, face):
                return ref[arrived * HG, pl.ds(slab, 1), pl.ds(8 + face, 1)].astype(jnp.int32)

            fine = Links(column, (me + shift) * count_f, count_f, True, 0)
            coarse = Links(column_c, (me + shift) * count_c, count_c, False, slots)
            return lambda s: fine if s < slots else coarse

        if slabs <= slots:
            source = r["state"]
        else:
            source = r["state"]
        out = r["state_out"]
        direct = plan["final"]

        def finish(s, i, jh, value):
            if s >= slots and plan["coarse_last"]:
                r["coarse_stage"][s - slots, :, cols(i, jh)] = value
            elif direct:
                out[s, :, cols(i, jh)] = value
            else:
                out[s, jh, rows_of(i), :] = value

        diffuse(
            source,
            slabs,
            links_of(own_up, 0),
            links_of(far_b, -1),
            links_of(far_a, 1),
            lambda s: rate_of[s],
            lambda s, h: own_up[s * HG + h],
            lambda s, h: own_down[s * HG + h],
            lambda s, h: far_b[s * HG + h],
            lambda s, h: far_a[s * HG + h],
            mats,
            r,
            finish,
        )
        if plan["coarse_last"]:
            final, stage = r["coarse_final"], r["coarse_stage"]
            for p in range(count_c):
                for v in range(fields):
                    final[v, pl.ds(p, 1), :] = pick(
                        core, stage[p, pl.ds(v, 1), :], stage[p, pl.ds(fields + v, 1), :]
                    )
        if plan["send_octants"]:
            octants_out(
                out,
                slots,
                r["children"],
                count_f,
                [r[f"octant{s}"] for s in range(plan["messages"])],
            )
            keep_coarse(out, slots, r["children"])
    else:
        out = r["state_out"]
        last = r["pay"].shape[0] - 1
        for i in range(B):
            for jh in range(2):
                at = cols(i, jh)
                for s in range(fields):
                    out[s, jh, rows_of(i), :] = r["seed_f"][s, :, at]
                out[fields, jh, rows_of(i), :] = pick(
                    core, r["pay"][last, :, at], r["pay_o"][last, :, at]
                )
        for p in range(count_c):
            out[slots + p] = r["coarse"][p]
        rows = row_ids()
        lane = lane_ids()
        faces = jnp.zeros((8, LANES), F32)
        for f in range(6):
            column = r["fine_nbr"][:, pl.ds(f, 1)].astype(F32)
            faces = jnp.where(lane == f, jnp.broadcast_to(column, (8, LANES)), faces)
            for p in range(count_c):
                column = r["coarse_nbr"][pl.ds(p, 1), pl.ds(f, 1)].astype(F32)
                faces = jnp.where(
                    (lane == 8 + f) & (rows == p), jnp.broadcast_to(column, (8, LANES)), faces
                )

    if plan["add"]:
        add_octants([r[f"arrived{s}"] for s in range(plan["arrivals"])], out, r["stage"], fields)
    if plan["react"]:
        step = plan["step"]
        react_fine(out, fields, par, par_o, r["gain"].at[step], r["weight"].at[step])
        if plan["react_coarse"] is not None:
            react_coarse(
                out,
                slots,
                count_c,
                spread_vector(core, par, par_o, 1, fields),
                r["gain_c"],
                r["weight_c"],
                plan["react_coarse"] * count_c,
            )
        going = plan["slabs_out"]
        build_planes(out, going, r["planes"])
        r["packed"][pl.ds(0, going * HG * 8), :] = pack_faces(
            r["planes"], mats["pack"], going * HG * 8
        )

        def send(up, down):
            for n in range(going * HG):
                up[n] = r["packed"][rows_of(n), half(0)]
                down[n] = r["packed"][rows_of(n), half(1)]
            up[going * HG] = faces
            down[going * HG] = faces

        pl.when(even)(lambda: send(r["send_e"], r["send_o"]))
        pl.when(jnp.logical_not(even))(lambda: send(r["send_o"], r["send_e"]))


SCALARS = ("par", "par_o", "children", "fine_counts", "coarse_counts")
MATS = ("plane", "side", "place", "pack", "far")
MIB = 1024 * 1024


def call(kernel, inputs, outputs, scratch, cost=2_000_000):
    names = list(inputs) + list(outputs) + list(scratch)
    scratch = {
        name: value if isinstance(value[-1], int) is False else value + (F32,)
        for name, value in scratch.items()
    }
    size = sum(4 * np.prod(v.shape) for v in inputs.values())
    size += sum(4 * np.prod(v) for v in outputs.values())
    size += sum(4 * np.prod(v[:-1]) for v in scratch.values())
    result = pl.pallas_call(
        functools.partial(kernel, names),
        out_shape=[jax.ShapeDtypeStruct(shape, F32) for shape in outputs.values()],
        in_specs=[SMEM if name in SCALARS else VMEM for name in inputs],
        out_specs=[VMEM] * len(outputs),
        scratch_shapes=[pltpu.VMEM(value[:-1], value[-1]) for value in scratch.values()],
        compiler_params=pltpu.CompilerParams(vmem_limit_bytes=int(size) + 12 * MIB),
        cost_estimate=pl.CostEstimate(flops=cost, bytes_accessed=cost, transcendentals=0),
    )(*inputs.values())
    return dict(zip(outputs, result))


def shards(
    seed_fine,
    seed_coarse,
    saved_fine,
    saved_coarse,
    diffusion,
    species_shares,
    fine_nbr,
    coarse_nbr,
    children,
    fine_counts,
    coarse_counts,
):
    fields, count_f, cells = seed_fine.shape
    count_c = seed_coarse.shape[1]
    steps = saved_fine.shape[0]
    cycles = saved_coarse.shape[0]
    slots = fields + 1
    every = slots + count_c
    sends = octant_sends(count_f)
    messages = len(sends) + 1
    par = jnp.stack([diffusion, species_shares])
    par_o = core_swap(par)
    seed_o = core_swap(seed_coarse)
    mats = tables()

    def wrapped(kernel):
        return lambda names, *refs: kernel(*refs)

    octant_shapes = {f"octant{s}": (2 * fields + 1, H, LANES) for s in range(messages)}

    def seed_call(names, seed_c, seed_other, kids, *rest):
        seed_kernel(seed_c, seed_other, kids, count_f, *rest)

    opened = call(
        seed_call,
        dict(seed_c=seed_coarse, seed_o=seed_o, children=children),
        dict(coarse=(count_c, 2, 8 * B, LANES), **octant_shapes),
        dict(seed_stage=(count_c, 2 * fields, cells)),
    )

    def travel(made):
        landed = [octant_move(made[f"octant{s}"], d) for s, d in enumerate(sends)]
        landed.append(made[f"octant{len(sends)}"])
        return landed + [core_swap(value) for value in landed]

    arrived = travel(opened)

    paid = call(
        wrapped(mix_kernel),
        dict(saved_f=saved_fine, saved_c=saved_coarse, seed_f=seed_fine, par=par),
        dict(pay=(2 * steps + 1, count_f, cells), payc=(2, cycles * count_c, cells)),
        {},
    )
    pay, payc = paid["pay"], paid["payc"]
    pay_o, payc_o = core_swap(pay), core_swap(payc)
    made_tables = call(
        wrapped(chem_kernel),
        dict(
            pay=pay,
            pay_o=pay_o,
            payc=payc,
            payc_o=payc_o,
            fine_counts=fine_counts,
            coarse_counts=coarse_counts,
        ),
        dict(
            gain=(steps, count_f, cells),
            weight=(steps, count_f, cells),
            gain_c=(cycles * count_c, cells),
            weight_c=(cycles * count_c, cells),
        ),
        {},
    )
    chem = {name: made_tables[name] for name in ("gain", "weight")}
    chem_c = {name: made_tables[name] for name in ("gain_c", "weight_c")}

    def strip(slabs):
        return (slabs * HG + 1, 8, LANES)

    def state_shape(slabs):
        return (slabs, 2, 8 * B, LANES)

    def work(slabs_in, slabs):
        rows = slabs * HG * 8
        return dict(
            far_b=strip(slabs_in),
            far_a=strip(slabs_in),
            own_up=strip(slabs_in),
            own_down=strip(slabs_in),
            first=state_shape(slabs),
            far_first=(2, slabs * HG, 8, LANES),
            sums=(G, rows, PLANE),
            ends=(rows, 4 * LANES, BF16),
            placed=(rows, G * PLANE),
            far_lhs=(2 * rows, 4 * LANES, BF16),
            far_out=(2 * rows, LANES),
        )

    def pack_work(slabs):
        rows = slabs * HG * 8
        return dict(
            planes=(G, rows, 2 * PLANE + 2 * LANES, BF16),
            packed=(rows, 2 * LANES),
        )

    stage_work = dict(stage=((2 * messages + 7) // 8, slots, 8 * H, LANES))
    common = dict(par=par, par_o=par_o, **mats)

    def plan_of(**changes):
        plan = dict(
            fields=fields,
            count_f=count_f,
            count_c=count_c,
            messages=messages,
            arrivals=2 * messages,
            slabs_in=0,
            slabs=0,
            slabs_out=slots,
            final=False,
            coarse_last=False,
            send_octants=False,
            add=False,
            react=True,
            react_coarse=None,
            step=0,
        )
        plan.update(changes)
        return plan

    def run(plan, inputs, outputs, scratch):
        return call(functools.partial(step_kernel, plan), inputs, outputs, scratch)

    def halo(made):
        return dict(
            state=made["state_out"],
            sent_e=made["send_e"],
            sent_o=made["send_o"],
            got_e=pair_swap(made["send_e"], 0),
            got_o=pair_swap(made["send_o"], 1),
        )

    def sending(slabs):
        return dict(state_out=state_shape(slabs), send_e=strip(slabs), send_o=strip(slabs))

    def arrivals(values):
        return {f"arrived{s}": value for s, value in enumerate(values)}

    made = run(
        plan_of(add=True, react_coarse=cycles - 1, step=steps - 1, slabs_out=every),
        dict(
            common,
            **chem,
            **chem_c,
            seed_f=seed_fine,
            pay=pay,
            pay_o=pay_o,
            coarse=opened["coarse"],
            fine_nbr=fine_nbr,
            coarse_nbr=coarse_nbr,
            **arrivals(arrived),
        ),
        sending(every),
        dict(pack_work(every), **stage_work),
    )
    held = every
    coarse_final = None
    for step in reversed(range(1, steps)):
        cycle, late = step // 2, step % 2 == 1
        inputs = dict(common, **chem, **halo(made))
        scratch = dict(work(held, held), **pack_work(held))
        plan = plan_of(slabs_in=held, slabs=held, step=step - 1)
        outputs = {}
        if late and cycle > 0:
            inputs.update(chem_c, children=children)
            outputs.update(octant_shapes)
            plan.update(send_octants=True, react_coarse=cycle - 1, slabs_out=held)
        elif not late:
            inputs.update(arrivals(arrived))
            scratch.update(stage_work)
            plan.update(add=True, slabs_out=held)
            if cycle == 1:
                outputs.update(coarse_final=seed_coarse.shape)
                scratch.update(coarse_stage=(count_c, 2 * fields, cells))
                plan.update(coarse_last=True, slabs_out=slots)
        else:
            plan.update(slabs_out=held)
        held = plan["slabs_out"]
        outputs.update(sending(held))
        made = run(plan, inputs, outputs, scratch)
        if plan["send_octants"]:
            arrived = travel(made)
        if plan["coarse_last"]:
            coarse_final = made["coarse_final"]
    made = run(
        plan_of(react=False, final=True, slabs_in=held, slabs=fields),
        dict(common, **halo(made)),
        dict(state_out=seed_fine.shape),
        dict(work(held, fields), **pack_work(fields)),
    )
    return made["state_out"], coarse_final


def solution(mesh):
    return jax.shard_map(
        shards,
        mesh=mesh,
        in_specs=(
            P("fld", "blk", None),
            P("fld", "blk", None),
            P(None, "fld", "blk", None),
            P(None, "fld", "blk", None),
            P("fld"),
            P("fld"),
            P("blk", None),
            P("blk", None),
            P("blk", None),
            P("blk"),
            P("blk"),
        ),
        out_specs=(P("fld", "blk", None), P("fld", "blk", None)),
        check_vma=False,
    )
```

time: 123 us -> 88 us (0.72)
  Pallas kernels: 55.5 us -> 20.8 us
    pallas_call x8, Pallas kernels: 55.5 us -> 20.8 us  [call(): pl.pallas_call(functools.partial(kernel, names), out_shape=[jax.ShapeDtyp...]
    unnamed x20 -> x30, local copies, waits for them, and re-layouts: 3.61 us -> 3.64 us
  transfers between devices with their start and end apart: 30 -> 30, of which waited for: 15 -> 16; matrix products, arithmetic and copies ran while one was open for 0% -> 0% of each run, Pallas kernels for 3% -> 5%
where the time goes in v2:
time: 88 us; the launch traced here: 87.8 us
  waiting for transfers between devices  38.2 us (43%)
  starting transfers between devices  23.5 us (27%)
  Pallas kernels  20.8 us (24%)
  local copies, waits for them, and re-layouts  3.64 us (4%)
  between operations  0.89 us (1%)
    pallas_call x8, Pallas kernels, call(): pl.pallas_call(functools.partial(kernel, names), out_shape=[jax.ShapeDtyp...  20.8 us
    ppermute x8, waiting for transfers between devices, pair_swap(): return lax.ppermute(value, 'blk', sorted(pairs))  20.7 us
    ppermute x8, waiting for transfers between devices, octant_move(): return lax.ppermute(value, ('blk', 'fld'), pairs)  14.3 us
    ppermute x8, starting transfers between devices, octant_move(): return lax.ppermute(value, ('blk', 'fld'), pairs)  11.7 us
    ppermute x8, starting transfers between devices, pair_swap(): return lax.ppermute(value, 'blk', sorted(pairs))  8.94 us
    unnamed x30, local copies, waits for them, and re-layouts  3.64 us
    ppermute x14, waiting for transfers between devices, core_swap(): return lax.ppermute(value, 'fld', [(0, 1), (1, 0)])  3.21 us
    ppermute x14, starting transfers between devices, core_swap(): return lax.ppermute(value, 'fld', [(0, 1), (1, 0)])  2.85 us
  transfers between devices with their start and end apart: 30, of which 16 were waited for; matrix products, arithmetic and copies ran while one was open for 0% of the time, Pallas kernels for 5%

profile of v2, /device:TPU:0, one launch (start us, length us, event | category | flops | bytes accessed | tf_op | source)
XLA Modules:
  0.0 87.8 jit_solution(8310000077055899872)
XLA Ops:
  1.3 1.6 %copy-done.3 = f32[4,4,8,4096]{3,2,1,0:T(8,128)S(1)} copy-done((f32[4,4,8,4096]{3,2,1,0:T(8,128)S(1)}, f32[4,4,8,4096]{3,2,1,0:T(8,128)}, u32[]{:S(2)}) %copy-start.3) | copy-done | bytes 2097176
  6.8 2.0 %collective-permute-done.3.seed_other = f32[4,2,4096]{2,1,0:T(2,128)S(1)} collective-permute-done((f32[4,2,4096]{2,1,0:T(2,128)S(1)}, f32[4,2,4096]{2,1,0:T(2,128)S(1)}, u32[]{:S(2)}, u32[]{:S(2)}) %collective-permute-start.3) | collective-permute-done | bytes 131104 | tf_op jit(solution)/shard_map/ppermute | solution.py:30
  9.8 2.9 %collective-permute-start.4 = (f32[9,8,128]{2,1,0:T(8,128)S(1)}, f32[9,8,128]{2,1,0:T(8,128)S(1)}, u32[]{:S(2)}, u32[]{:S(2)}) collective-permute-start(f32[9,8,128]{2,1,0:T(8,128)S(1)} %get-tuple-element.39), channel_id=1, source_target_pairs={{0,2},{1,9},{2,4},{3,11},{4,6},{5,13},{6,8},{7,15},{8,10},{9,17},{... | collective-permute-start | bytes 110600 | tf_op jit(solution)/shard_map/ppermute | solution.py:53
  12.7 1.5 %collective-permute-start.5 = (f32[9,8,128]{2,1,0:T(8,128)S(1)}, f32[9,8,128]{2,1,0:T(8,128)S(1)}, u32[]{:S(2)}, u32[]{:S(2)}) collective-permute-start(f32[9,8,128]{2,1,0:T(8,128)S(1)} %get-tuple-element.40), channel_id=1, source_target_pairs={{0,4},{1,11},{2,6},{3,13},{4,8},{5,15},{6,10},{7,17},{8,12},{9,19}... | collective-permute-start | bytes 110600 | tf_op jit(solution)/shard_map/ppermute | solution.py:53
  14.2 2.4 %collective-permute-start.6 = (f32[9,8,128]{2,1,0:T(8,128)S(1)}, f32[9,8,128]{2,1,0:T(8,128)S(1)}, u32[]{:S(2)}, u32[]{:S(2)}) collective-permute-start(f32[9,8,128]{2,1,0:T(8,128)S(1)} %get-tuple-element.41), channel_id=1, source_target_pairs={{0,6},{1,13},{2,8},{3,15},{4,10},{5,17},{6,12},{7,19},{8,14},{9,21... | collective-permute-start | bytes 110600 | tf_op jit(solution)/shard_map/ppermute | solution.py:53
  16.7 2.6 %collective-permute-start.7 = (f32[9,8,128]{2,1,0:T(8,128)S(1)}, f32[9,8,128]{2,1,0:T(8,128)S(1)}, u32[]{:S(2)}, u32[]{:S(2)}) collective-permute-start(f32[9,8,128]{2,1,0:T(8,128)S(1)} %get-tuple-element.42), channel_id=1, source_target_pairs={{0,14},{1,15},{2,16},{3,17},{4,18},{5,19},{6,20},{7,21},{8,22},{9,... | collective-permute-start | bytes 110600 | tf_op jit(solution)/shard_map/ppermute | solution.py:53
  20.9 1.8 %collective-permute-done.7.refs_20_ = f32[9,8,128]{2,1,0:T(8,128)S(1)} collective-permute-done((f32[9,8,128]{2,1,0:T(8,128)S(1)}, f32[9,8,128]{2,1,0:T(8,128)S(1)}, u32[]{:S(2)}, u32[]{:S(2)}) %collective-permute-start.7) | collective-permute-done | bytes 36896 | tf_op jit(solution)/shard_map/ppermute | solution.py:53
  23.2 3.2 %shard_map.168 = (f32[4,8,4096]{2,1,0:T(8,128)S(1)}, f32[4,8,4096]{2,1,0:T(8,128)S(1)}, f32[4,4096]{1,0:T(4,128)S(1)}, f32[4,4096]{1,0:T(4,128)S(1)}) custom-call(f32[9,8,4096]{2,1,0:T(8,128)S(1)} %get-tuple-element.32.refs_0_.refs_12_, f32[9,8,4096]{2,1,0:T(8,128)S(1)} %collective-permute-done.1.refs_1_.refs_13_, ...), custom_call_target="tpu_custom_call" | custom-call | flops 2000000 | bytes 2000000 | tf_op jit(solution)/shard_map/pallas_call | solution.py:760
  26.6 1.4 %shard_map.170 = (f32[7,2,128,128]{3,2,1,0:T(8,128)S(1)}, f32[29,8,128]{2,1,0:T(8,128)S(1)}, f32[29,8,128]{2,1,0:T(8,128)S(1)}) custom-call(f32[2,4]{1,0:T(2,128)S(1)} %pad_maximum_fusion.refs_3_.refs_0_, f32[2,4]{1,0:T(2,128)S(1)} %collective-permute-done.refs_1_, bf16[256,256]{1,0:T(8,128)(2,1)S(1)} %copy-done.2, bf16[128,256]{1,0:T(8,128)(2,1)S(1)} %copy-done.7, ...), custom_call_target="tpu_custom_call" | custom-call | flops 2000000 | bytes 2000000 | tf_op jit(solution)/shard_map/pallas_call | solution.py:760
  28.0 1.6 %collective-permute-start.13 = (f32[29,8,128]{2,1,0:T(8,128)S(1)}, f32[29,8,128]{2,1,0:T(8,128)S(1)}, u32[]{:S(2)}, u32[]{:S(2)}) collective-permute-start(f32[29,8,128]{2,1,0:T(8,128)S(1)} %get-tuple-element.45.refs_10_), channel_id=1, source_target_pairs={{0,2},{2,0},{4,6},{6,4},{8,10},{10,8},{12,14},{14,12},{16,18},{18,... | collective-permute-start | bytes 356360 | tf_op jit(solution)/shard_map/ppermute | solution.py:39
  29.6 3.0 %collective-permute-start.14 = (f32[29,8,128]{2,1,0:T(8,128)S(1)}, f32[29,8,128]{2,1,0:T(8,128)S(1)}, u32[]{:S(2)}, u32[]{:S(2)}) collective-permute-start(f32[29,8,128]{2,1,0:T(8,128)S(1)} %get-tuple-element.46.refs_11_), channel_id=1, source_target_pairs={{0,30},{2,4},{4,2},{6,8},{8,6},{10,12},{12,10},{14,16},{16,14},{18... | collective-permute-start | bytes 356360 | tf_op jit(solution)/shard_map/ppermute | solution.py:39
  33.2 4.9 %collective-permute-done.14.refs_13_ = f32[29,8,128]{2,1,0:T(8,128)S(1)} collective-permute-done((f32[29,8,128]{2,1,0:T(8,128)S(1)}, f32[29,8,128]{2,1,0:T(8,128)S(1)}, u32[]{:S(2)}, u32[]{:S(2)}) %collective-permute-start.14) | collective-permute-done | bytes 118816 | tf_op jit(solution)/shard_map/ppermute | solution.py:39
  38.0 4.3 %shard_map.171 = (f32[9,8,128]{2,1,0:T(8,128)S(1)}, f32[9,8,128]{2,1,0:T(8,128)S(1)}, f32[9,8,128]{2,1,0:T(8,128)S(1)}, f32[9,8,128]{2,1,0:T(8,128)S(1)}, f32[9,...) custom-call(f32[2,4]{1,0:T(2,128)S(1)} %pad_maximum_fusion.refs_3_.r, ...), custom_call_target="tpu_custom_call" | custom-call | flops 2000000 | bytes 2000000 | tf_op jit(solution)/shard_map/pallas_call | solution.py:760
  43.2 2.4 %collective-permute-start.16 = (f32[29,8,128]{2,1,0:T(8,128)S(1)}, f32[29,8,128]{2,1,0:T(8,128)S(1)}, u32[]{:S(2)}, u32[]{:S(2)}) collective-permute-start(f32[29,8,128]{2,1,0:T(8,128)S(1)} %get-tuple-element.49.refs_11_), channel_id=1, source_target_pairs={{0,30},{2,4},{4,2},{6,8},{8,6},{10,12},{12,10},{14,16},{16,14},{18... | collective-permute-start | bytes 356360 | tf_op jit(solution)/shard_map/ppermute | solution.py:39
  45.9 1.9 %collective-permute-start.19 = (f32[9,8,128]{2,1,0:T(8,128)S(1)}, f32[9,8,128]{2,1,0:T(8,128)S(1)}, u32[]{:S(2)}, u32[]{:S(2)}) collective-permute-start(f32[9,8,128]{2,1,0:T(8,128)S(1)} %get-tuple-element.52), channel_id=1, source_target_pairs={{0,6},{1,13},{2,8},{3,15},{4,10},{5,17},{6,12},{7,19},{8,14},{9,21... | collective-permute-start | bytes 110600 | tf_op jit(solution)/shard_map/ppermute | solution.py:53
  47.9 5.7 %collective-permute-done.17.refs_14_ = f32[9,8,128]{2,1,0:T(8,128)S(1)} collective-permute-done((f32[9,8,128]{2,1,0:T(8,128)S(1)}, f32[9,8,128]{2,1,0:T(8,128)S(1)}, u32[]{:S(2)}, u32[]{:S(2)}) %collective-permute-start.17) | collective-permute-done | bytes 36896 | tf_op jit(solution)/shard_map/ppermute | solution.py:53
  54.1 5.2 %collective-permute-done.20.refs_17_ = f32[9,8,128]{2,1,0:T(8,128)S(1)} collective-permute-done((f32[9,8,128]{2,1,0:T(8,128)S(1)}, f32[9,8,128]{2,1,0:T(8,128)S(1)}, u32[]{:S(2)}, u32[]{:S(2)}) %collective-permute-start.20) | collective-permute-done | bytes 36896 | tf_op jit(solution)/shard_map/ppermute | solution.py:53
  61.1 4.3 %shard_map.172 = (f32[4,2,4096]{2,1,0:T(2,128)}, f32[5,2,128,128]{3,2,1,0:T(8,128)S(1)}, f32[21,8,128]{2,1,0:T(8,128)S(1)}, f32[21,8,128]{2,1,0:T(8,128)S(1)}) custom-call(f32[2,4]{1,0:T(2,128)S(1)} %pad_maximum_fusion.refs_3_.refs_0_, f32[2,4]{1,0:T(2,128)S(1)} %collective-permute-done.refs_1_, bf16[256,256]{1,0:T(8,128)(2,1)S(1)} %copy-done.2, ...), custom_call_target="tpu_custom_call" | custom-call | flops 2000000 | bytes 2000000 | tf_op jit(solution)/shard_map/pallas_call | solution.py:760
  65.9 4.8 %collective-permute-done.26.refs_12_ = f32[21,8,128]{2,1,0:T(8,128)S(1)} collective-permute-done((f32[21,8,128]{2,1,0:T(8,128)S(1)}, f32[21,8,128]{2,1,0:T(8,128)S(1)}, u32[]{:S(2)}, u32[]{:S(2)}) %collective-permute-start.26) | collective-permute-done | bytes 86048 | tf_op jit(solution)/shard_map/ppermute | solution.py:39
  70.8 2.8 %collective-permute-done.27.refs_13_ = f32[21,8,128]{2,1,0:T(8,128)S(1)} collective-permute-done((f32[21,8,128]{2,1,0:T(8,128)S(1)}, f32[21,8,128]{2,1,0:T(8,128)S(1)}, u32[]{:S(2)}, u32[]{:S(2)}) %collective-permute-start.27) | collective-permute-done | bytes 86048 | tf_op jit(solution)/shard_map/ppermute | solution.py:39
  73.6 3.0 %shard_map.173 = (f32[5,2,128,128]{3,2,1,0:T(8,128)S(1)}, f32[21,8,128]{2,1,0:T(8,128)S(1)}, f32[21,8,128]{2,1,0:T(8,128)S(1)}) custom-call(f32[2,4]{1,0:T(2,128)S(1)} %pad_maximum_fusion.refs_3_.refs_0_, f32[2,4]{1,0:T(2,128)S(1)} %collective-permute-done.refs_1_, bf16[256,256]{1,0:T(8,128)(2,1)S(1)} %copy-done.2, bf16[128,256]{1,0:T(8,128)(2,1)S(1)} %copy-done.7, ...), custom_call_target="tpu_custom_call" | custom-call | flops 2000000 | bytes 2000000 | tf_op jit(solution)/shard_map/pallas_call | solution.py:760
  77.1 4.2 %collective-permute-done.28.refs_10_ = f32[21,8,128]{2,1,0:T(8,128)S(1)} collective-permute-done((f32[21,8,128]{2,1,0:T(8,128)S(1)}, f32[21,8,128]{2,1,0:T(8,128)S(1)}, u32[]{:S(2)}, u32[]{:S(2)}) %collective-permute-start.28) | collective-permute-done | bytes 86048 | tf_op jit(solution)/shard_map/ppermute | solution.py:39
  81.3 3.5 %collective-permute-done.29.refs_11_ = f32[21,8,128]{2,1,0:T(8,128)S(1)} collective-permute-done((f32[21,8,128]{2,1,0:T(8,128)S(1)}, f32[21,8,128]{2,1,0:T(8,128)S(1)}, u32[]{:S(2)}, u32[]{:S(2)}) %collective-permute-start.29) | collective-permute-done | bytes 86048 | tf_op jit(solution)/shard_map/ppermute | solution.py:39
  84.8 3.0 %shard_map.174 = f32[4,8,4096]{2,1,0:T(8,128)} custom-call(f32[2,4]{1,0:T(2,128)S(1)} %pad_maximum_fusion.refs_3_.refs_0_, f32[2,4]{1,0:T(2,128)S(1)} %collective-permute-done.refs_1_, bf16[256,256]{1,0:T(8,128)(2,1)S(1)} %copy-done.2, bf16[128,256]{1,0:T(8,128)(2,1)S(1)} %copy-done.7, bf16[256,1024]{1,0:T(8,128)(2,1)S(1)} %copy-done.1, ...), custom_call_target="tpu_custom_call" | custom-call | flops 2000000 | bytes 2000000 | tf_op jit(solution)/shard_map/pallas_call | solution.py:760
  (75 shorter events, 12.8 us)
Async XLA Ops:
  5.6 17.1 %collective-permute-start.1 = (f32[9,8,4096]{2,1,0:T(8,128)S(1)}, f32[9,8,4096]{2,1,0:T(8,128)S(1)}, u32[]{:S(2)}, u32[]{:S(2)}) collective-permute-start(f32[9,8,4096]{2,1,0:T(8,128)S(1)} %get-tuple-element.32.refs_0_.refs_12_), channel_id=1, source_target_pairs={{0,1},{1,0},{2,3},{3,2},{4,5},{5,4},{6,7},{7,6},{8,9},{9,8},{10,11... | collective-permute-start | bytes 3538952 | tf_op jit(solution)/shard_map/ppermute | solution.py:30
  6.3 10.4 %collective-permute-start.2 = (f32[2,4,4096]{2,1,0:T(4,128)S(1)}, f32[2,4,4096]{2,1,0:T(4,128)S(1)}, u32[]{:S(2)}, u32[]{:S(2)}) collective-permute-start(f32[2,4,4096]{2,1,0:T(4,128)S(1)} %get-tuple-element.33.refs_2_), channel_id=1, source_target_pairs={{0,1},{1,0},{2,3},{3,2},{4,5},{5,4},{6,7},{7,6},{8,9},{9,8},{10,11... | collective-permute-start | bytes 393224 | tf_op jit(solution)/shard_map/ppermute | solution.py:30
  6.7 7.5 %collective-permute-start = (f32[2,4]{1,0:T(2,128)S(1)}, f32[2,4]{1,0:T(2,128)S(1)}, u32[]{:S(2)}, u32[]{:S(2)}) collective-permute-start(f32[2,4]{1,0:T(2,128)S(1)} %pad_maximum_fusion.refs_3_.refs_0_), channel_id=1, source_target_pairs={{0,1},{1,0},{2,3},{3,2},{4,5},{5,4},{6,7},{7,6},{8,9},{9,8},{10,11... | collective-permute-start | bytes 104 | tf_op jit(solution)/shard_map/ppermute | solution.py:30
  9.8 9.5 %collective-permute-start.4 = (f32[9,8,128]{2,1,0:T(8,128)S(1)}, f32[9,8,128]{2,1,0:T(8,128)S(1)}, u32[]{:S(2)}, u32[]{:S(2)}) collective-permute-start(f32[9,8,128]{2,1,0:T(8,128)S(1)} %get-tuple-element.39), channel_id=1, source_target_pairs={{0,2},{1,9},{2,4},{3,11},{4,6},{5,13},{6,8},{7,15},{8,10},{9,17},{... | collective-permute-start | bytes 110600 | tf_op jit(solution)/shard_map/ppermute | solution.py:53
  12.7 7.0 %collective-permute-start.5 = (f32[9,8,128]{2,1,0:T(8,128)S(1)}, f32[9,8,128]{2,1,0:T(8,128)S(1)}, u32[]{:S(2)}, u32[]{:S(2)}) collective-permute-start(f32[9,8,128]{2,1,0:T(8,128)S(1)} %get-tuple-element.40), channel_id=1, source_target_pairs={{0,4},{1,11},{2,6},{3,13},{4,8},{5,15},{6,10},{7,17},{8,12},{9,19}... | collective-permute-start | bytes 110600 | tf_op jit(solution)/shard_map/ppermute | solution.py:53
  14.2 6.7 %collective-permute-start.6 = (f32[9,8,128]{2,1,0:T(8,128)S(1)}, f32[9,8,128]{2,1,0:T(8,128)S(1)}, u32[]{:S(2)}, u32[]{:S(2)}) collective-permute-start(f32[9,8,128]{2,1,0:T(8,128)S(1)} %get-tuple-element.41), channel_id=1, source_target_pairs={{0,6},{1,13},{2,8},{3,15},{4,10},{5,17},{6,12},{7,19},{8,14},{9,21... | collective-permute-start | bytes 110600 | tf_op jit(solution)/shard_map/ppermute | solution.py:53
  16.7 6.0 %collective-permute-start.7 = (f32[9,8,128]{2,1,0:T(8,128)S(1)}, f32[9,8,128]{2,1,0:T(8,128)S(1)}, u32[]{:S(2)}, u32[]{:S(2)}) collective-permute-start(f32[9,8,128]{2,1,0:T(8,128)S(1)} %get-tuple-element.42), channel_id=1, source_target_pairs={{0,14},{1,15},{2,16},{3,17},{4,18},{5,19},{6,20},{7,21},{8,22},{9,... | collective-permute-start | bytes 110600 | tf_op jit(solution)/shard_map/ppermute | solution.py:53
  19.3 7.2 %collective-permute-start.12 = (f32[9,8,128]{2,1,0:T(8,128)S(1)}, f32[9,8,128]{2,1,0:T(8,128)S(1)}, u32[]{:S(2)}, u32[]{:S(2)}) collective-permute-start(f32[9,8,128]{2,1,0:T(8,128)S(1)} %get-tuple-element.43.refs_21_), channel_id=1, source_target_pairs={{0,1},{1,0},{2,3},{3,2},{4,5},{5,4},{6,7},{7,6},{8,9},{9,8},{10,11... | collective-permute-start | bytes 110600 | tf_op jit(solution)/shard_map/ppermute | solution.py:30
  19.7 6.7 %collective-permute-start.8 = (f32[9,8,128]{2,1,0:T(8,128)S(1)}, f32[9,8,128]{2,1,0:T(8,128)S(1)}, u32[]{:S(2)}, u32[]{:S(2)}) collective-permute-start(f32[9,8,128]{2,1,0:T(8,128)S(1)} %collective-permute-done.4.refs_17_), channel_id=1, source_target_pairs={{0,1},{1,0},{2,3},{3,2},{4,5},{5,4},{6,7},{7,6},{8,9},{9,8},{10,11... | collective-permute-start | bytes 110600 | tf_op jit(solution)/shard_map/ppermute | solution.py:30
  20.9 5.6 %collective-permute-start.9 = (f32[9,8,128]{2,1,0:T(8,128)S(1)}, f32[9,8,128]{2,1,0:T(8,128)S(1)}, u32[]{:S(2)}, u32[]{:S(2)}) collective-permute-start(f32[9,8,128]{2,1,0:T(8,128)S(1)} %collective-permute-done.5.refs_18_), channel_id=1, source_target_pairs={{0,1},{1,0},{2,3},{3,2},{4,5},{5,4},{6,7},{7,6},{8,9},{9,8},{10,11... | collective-permute-start | bytes 110600 | tf_op jit(solution)/shard_map/ppermute | solution.py:30
  28.0 5.2 %collective-permute-start.13 = (f32[29,8,128]{2,1,0:T(8,128)S(1)}, f32[29,8,128]{2,1,0:T(8,128)S(1)}, u32[]{:S(2)}, u32[]{:S(2)}) collective-permute-start(f32[29,8,128]{2,1,0:T(8,128)S(1)} %get-tuple-element.45.refs_10_), channel_id=1, source_target_pairs={{0,2},{2,0},{4,6},{6,4},{8,10},{10,8},{12,14},{14,12},{16,18},{18,... | collective-permute-start | bytes 356360 | tf_op jit(solution)/shard_map/ppermute | solution.py:39
  29.6 8.5 %collective-permute-start.14 = (f32[29,8,128]{2,1,0:T(8,128)S(1)}, f32[29,8,128]{2,1,0:T(8,128)S(1)}, u32[]{:S(2)}, u32[]{:S(2)}) collective-permute-start(f32[29,8,128]{2,1,0:T(8,128)S(1)} %get-tuple-element.46.refs_11_), channel_id=1, source_target_pairs={{0,30},{2,4},{4,2},{6,8},{8,6},{10,12},{12,10},{14,16},{16,14},{18... | collective-permute-start | bytes 356360 | tf_op jit(solution)/shard_map/ppermute | solution.py:39
  42.4 18.7 %collective-permute-start.15 = (f32[29,8,128]{2,1,0:T(8,128)S(1)}, f32[29,8,128]{2,1,0:T(8,128)S(1)}, u32[]{:S(2)}, u32[]{:S(2)}) collective-permute-start(f32[29,8,128]{2,1,0:T(8,128)S(1)} %get-tuple-element.48.refs_10_), channel_id=1, source_target_pairs={{0,2},{2,0},{4,6},{6,4},{8,10},{10,8},{12,14},{14,12},{16,18},{18,... | collective-permute-start | bytes 356360 | tf_op jit(solution)/shard_map/ppermute | solution.py:39
  43.2 17.9 %collective-permute-start.16 = (f32[29,8,128]{2,1,0:T(8,128)S(1)}, f32[29,8,128]{2,1,0:T(8,128)S(1)}, u32[]{:S(2)}, u32[]{:S(2)}) collective-permute-start(f32[29,8,128]{2,1,0:T(8,128)S(1)} %get-tuple-element.49.refs_11_), channel_id=1, source_target_pairs={{0,30},{2,4},{4,2},{6,8},{8,6},{10,12},{12,10},{14,16},{16,14},{18... | collective-permute-start | bytes 356360 | tf_op jit(solution)/shard_map/ppermute | solution.py:39
  45.6 8.0 %collective-permute-start.17 = (f32[9,8,128]{2,1,0:T(8,128)S(1)}, f32[9,8,128]{2,1,0:T(8,128)S(1)}, u32[]{:S(2)}, u32[]{:S(2)}) collective-permute-start(f32[9,8,128]{2,1,0:T(8,128)S(1)} %get-tuple-element.50), channel_id=1, source_target_pairs={{0,2},{1,9},{2,4},{3,11},{4,6},{5,13},{6,8},{7,15},{8,10},{9,17},{... | collective-permute-start | bytes 110600 | tf_op jit(solution)/shard_map/ppermute | solution.py:53
  45.6 8.0 %collective-permute-start.18 = (f32[9,8,128]{2,1,0:T(8,128)S(1)}, f32[9,8,128]{2,1,0:T(8,128)S(1)}, u32[]{:S(2)}, u32[]{:S(2)}) collective-permute-start(f32[9,8,128]{2,1,0:T(8,128)S(1)} %get-tuple-element.51), channel_id=1, source_target_pairs={{0,4},{1,11},{2,6},{3,13},{4,8},{5,15},{6,10},{7,17},{8,12},{9,19}... | collective-permute-start | bytes 110600 | tf_op jit(solution)/shard_map/ppermute | solution.py:53
  45.9 7.8 %collective-permute-start.19 = (f32[9,8,128]{2,1,0:T(8,128)S(1)}, f32[9,8,128]{2,1,0:T(8,128)S(1)}, u32[]{:S(2)}, u32[]{:S(2)}) collective-permute-start(f32[9,8,128]{2,1,0:T(8,128)S(1)} %get-tuple-element.52), channel_id=1, source_target_pairs={{0,6},{1,13},{2,8},{3,15},{4,10},{5,17},{6,12},{7,19},{8,14},{9,21... | collective-permute-start | bytes 110600 | tf_op jit(solution)/shard_map/ppermute | solution.py:53
  53.6 5.8 %collective-permute-start.20 = (f32[9,8,128]{2,1,0:T(8,128)S(1)}, f32[9,8,128]{2,1,0:T(8,128)S(1)}, u32[]{:S(2)}, u32[]{:S(2)}) collective-permute-start(f32[9,8,128]{2,1,0:T(8,128)S(1)} %get-tuple-element.53), channel_id=1, source_target_pairs={{0,14},{1,15},{2,16},{3,17},{4,18},{5,19},{6,20},{7,21},{8,22},{9,... | collective-permute-start | bytes 110600 | tf_op jit(solution)/shard_map/ppermute | solution.py:53
  53.6 5.8 %collective-permute-start.25 = (f32[9,8,128]{2,1,0:T(8,128)S(1)}, f32[9,8,128]{2,1,0:T(8,128)S(1)}, u32[]{:S(2)}, u32[]{:S(2)}) collective-permute-start(f32[9,8,128]{2,1,0:T(8,128)S(1)} %get-tuple-element.54.refs_18_), channel_id=1, source_target_pairs={{0,1},{1,0},{2,3},{3,2},{4,5},{5,4},{6,7},{7,6},{8,9},{9,8},{10,11... | collective-permute-start | bytes 110600 | tf_op jit(solution)/shard_map/ppermute | solution.py:30
  53.7 6.2 %collective-permute-start.21 = (f32[9,8,128]{2,1,0:T(8,128)S(1)}, f32[9,8,128]{2,1,0:T(8,128)S(1)}, u32[]{:S(2)}, u32[]{:S(2)}) collective-permute-start(f32[9,8,128]{2,1,0:T(8,128)S(1)} %collective-permute-done.17.refs_14_), channel_id=1, source_target_pairs={{0,1},{1,0},{2,3},{3,2},{4,5},{5,4},{6,7},{7,6},{8,9},{9,8},{10,11... | collective-permute-start | bytes 110600 | tf_op jit(solution)/shard_map/ppermute | solution.py:30
  65.4 5.4 %collective-permute-start.26 = (f32[21,8,128]{2,1,0:T(8,128)S(1)}, f32[21,8,128]{2,1,0:T(8,128)S(1)}, u32[]{:S(2)}, u32[]{:S(2)}) collective-permute-start(f32[21,8,128]{2,1,0:T(8,128)S(1)} %get-tuple-element.56.refs_10_), channel_id=1, source_target_pairs={{0,2},{2,0},{4,6},{6,4},{8,10},{10,8},{12,14},{14,12},{16,18},{18,... | collective-permute-start | bytes 258056 | tf_op jit(solution)/shard_map/ppermute | solution.py:39
  65.4 8.2 %collective-permute-start.27 = (f32[21,8,128]{2,1,0:T(8,128)S(1)}, f32[21,8,128]{2,1,0:T(8,128)S(1)}, u32[]{:S(2)}, u32[]{:S(2)}) collective-permute-start(f32[21,8,128]{2,1,0:T(8,128)S(1)} %get-tuple-element.57.refs_11_), channel_id=1, source_target_pairs={{0,30},{2,4},{4,2},{6,8},{8,6},{10,12},{12,10},{14,16},{16,14},{18... | collective-permute-start | bytes 258056 | tf_op jit(solution)/shard_map/ppermute | solution.py:39
  76.5 4.8 %collective-permute-start.28 = (f32[21,8,128]{2,1,0:T(8,128)S(1)}, f32[21,8,128]{2,1,0:T(8,128)S(1)}, u32[]{:S(2)}, u32[]{:S(2)}) collective-permute-start(f32[21,8,128]{2,1,0:T(8,128)S(1)} %get-tuple-element.59.refs_8_), channel_id=1, source_target_pairs={{0,2},{2,0},{4,6},{6,4},{8,10},{10,8},{12,14},{14,12},{16,18},{18,... | collective-permute-start | bytes 258056 | tf_op jit(solution)/shard_map/ppermute | solution.py:39
  76.6 8.1 %collective-permute-start.29 = (f32[21,8,128]{2,1,0:T(8,128)S(1)}, f32[21,8,128]{2,1,0:T(8,128)S(1)}, u32[]{:S(2)}, u32[]{:S(2)}) collective-permute-start(f32[21,8,128]{2,1,0:T(8,128)S(1)} %get-tuple-element.60.refs_9_), channel_id=1, source_target_pairs={{0,30},{2,4},{4,2},{6,8},{8,6},{10,12},{12,10},{14,16},{16,14},{18... | collective-permute-start | bytes 258056 | tf_op jit(solution)/shard_map/ppermute | solution.py:39
  (21 other events, 117.9 us)

commit v3 on v2

--- a/solution.py
+++ b/solution.py
@@ -22,6 +22,7 @@
 FAR = -(1 << 20)
 VMEM = pl.BlockSpec(memory_space=pltpu.VMEM)
 SMEM = pl.BlockSpec(memory_space=pltpu.SMEM)
+HBM = pl.BlockSpec(memory_space=pltpu.HBM)
 F32 = jnp.float32
 BF16 = jnp.bfloat16
 
@@ -30,18 +31,27 @@
     return lax.ppermute(value, "fld", [(0, 1), (1, 0)])
 
 
-def pair_swap(value, first):
+def pair_swap(value, first, ring):
     n = lax.axis_size("blk")
     pairs = []
-    for i in range(first, n + first, 2):
-        a, b = i % n, (i + 1) % n
-        pairs += [(a, b), (b, a)]
-    return lax.ppermute(value, "blk", sorted(pairs))
-
-
-def octant_sends(count):
-    half = count // 2
-    return [(1 + s if 1 + s < half else count - 1, half + s) for s in range(half)]
+    for i in range(n):
+        other = i + 1 if (i - first) % 2 == 0 else i - 1
+        for core in range(2):
+            if ring or 0 <= other < n:
+                pairs.append((2 * i + core, 2 * (other % n) + core))
+            else:
+                pairs.append((2 * i + core, 2 * i + 1 - core))
+    return lax.ppermute(value, ("blk", "fld"), pairs)
+
+
+def first_sends(count):
+    middle = count // 2
+    return list(zip(list(range(2, middle)) + [1, -1], range(middle, count)))
+
+
+def later_sends(count):
+    middle = count // 2 + 1
+    return list(zip(range(2, middle), range(middle, count)))
 
 
 def octant_move(value, distances):
@@ -382,29 +392,49 @@
     rows = row_ids()
     result = jnp.zeros((8, LANES), F32)
     for f in range(2 * fields):
-        value = pick(core, own[row, f], other[row, f]) if f < fields else pick(
-            core, other[row, f - fields], own[row, f - fields]
+        value = pick(core, own[row][f], other[row][f]) if f < fields else pick(
+            core, other[row][f - fields], own[row][f - fields]
         )
         result = jnp.where(rows == f, value, result)
     return result
 
 
-def mix_kernel(saved_f, saved_c, seed_f, par, pay, payc):
+def mix_kernel(
+    saved_f, saved_c, seed_f, seed_c, shares, pay, payc, fine, coarse, seeds,
+    fine_sem, coarse_sem, seed_sem, seeds_sem,
+):
     steps, fields = saved_f.shape[0], saved_f.shape[1]
     cycles, blocks = saved_c.shape[0], saved_c.shape[2]
+    copies = [
+        pltpu.make_async_copy(saved_f.at[s], fine.at[s], fine_sem.at[s]) for s in range(steps)
+    ]
+    copy_c = pltpu.make_async_copy(saved_c, coarse, coarse_sem)
+    copy_s = pltpu.make_async_copy(seed_f.at[0], pay.at[2 * steps], seed_sem)
+    copy_seeds = pltpu.make_async_copy(seed_c, seeds, seeds_sem)
+    copy_c.start()
+    copy_seeds.start()
+    for copy in copies:
+        copy.start()
+    copy_s.start()
+    copy_c.wait()
+    for c in range(cycles):
+        total = shares[0] * coarse[c, 0]
+        for v in range(1, fields):
+            total = total + shares[v] * coarse[c, v]
+        payc[0, pl.ds(c * blocks, blocks), :] = total
+        payc[1, pl.ds(c * blocks, blocks), :] = coarse[c, 0]
+    copy_seeds.wait()
+    for v in range(fields):
+        payc[2 + v, pl.ds(0, blocks), :] = seeds[v]
+        payc[2 + v, pl.ds(blocks, blocks), :] = seeds[v]
     for s in range(steps):
-        total = par[1, 0] * saved_f[s, 0]
+        copies[s].wait()
+        total = shares[0] * fine[s, 0]
         for v in range(1, fields):
-            total = total + par[1, v] * saved_f[s, v]
+            total = total + shares[v] * fine[s, v]
         pay[s] = total
-        pay[steps + s] = saved_f[s, 0]
-    pay[2 * steps] = seed_f[0]
-    for c in range(cycles):
-        total = par[1, 0] * saved_c[c, 0]
-        for v in range(1, fields):
-            total = total + par[1, v] * saved_c[c, v]
-        payc[0, pl.ds(c * blocks, blocks), :] = total
-        payc[1, pl.ds(c * blocks, blocks), :] = saved_c[c, 0]
+        pay[steps + s] = fine[s, 0]
+    copy_s.wait()
 
 
 def reaction_tables(mix, start, counts):
@@ -426,19 +456,13 @@
     return passed - 1.0, weight
 
 
-def chem_kernel(pay, pay_o, payc, payc_o, fine_counts, coarse_counts, gain, weight, gain_c, weight_c):
+def chem_kernel(pay, pay_o, fine_counts, gain, weight):
     core = lax.axis_index("fld")
     steps = gain.shape[0]
     rows = row_ids()
     counts = jnp.ones((8, LANES), jnp.int32)
     for b in range(fine_counts.shape[0]):
         counts = jnp.where(rows == b, fine_counts[b], counts)
-    blocks = coarse_counts.shape[0]
-    entries = gain_c.shape[0]
-    counts_c = jnp.ones((entries, LANES), jnp.int32)
-    rows_c = lax.broadcasted_iota(jnp.int32, (entries, LANES), 0)
-    for r in range(entries):
-        counts_c = jnp.where(rows_c == r, coarse_counts[r % blocks], counts_c)
 
     def body(t, carry):
         at = pl.ds(pl.multiple_of(t * LANES, LANES), LANES)
@@ -447,50 +471,66 @@
             a, w = reaction_tables(pay[s, :, at] + pay_o[s, :, at], start, counts)
             gain[s, :, at] = a
             weight[s, :, at] = w
+        return carry
+
+    lax.fori_loop(0, TILES, body, 0)
+
+
+def chem_coarse(payc, payc_o, coarse_counts, gain, weight):
+    core = lax.axis_index("fld")
+    blocks = coarse_counts.shape[0]
+    entries = gain.shape[0]
+    shape = (entries, 4 * LANES)
+    counts = jnp.ones(shape, jnp.int32)
+    rows = lax.broadcasted_iota(jnp.int32, shape, 0)
+    for r in range(entries):
+        counts = jnp.where(rows == r, coarse_counts[r % blocks], counts)
+
+    def body(t, carry):
+        at = pl.ds(pl.multiple_of(t * 4 * LANES, 4 * LANES), 4 * LANES)
         start = pick(core, payc[1, :, at], payc_o[1, :, at])
-        a, w = reaction_tables(payc[0, :, at] + payc_o[0, :, at], start, counts_c)
-        gain_c[:, at] = a
-        weight_c[:, at] = w
+        gain[:, at], weight[:, at] = reaction_tables(
+            payc[0, :, at] + payc_o[0, :, at], start, counts
+        )
         return carry
 
-    lax.fori_loop(0, TILES, body, 0)
-
-
-def octants_out(state, first_slab, children, count_f, outs):
-    core = lax.axis_index("fld")
+    lax.fori_loop(0, TILES // 4, body, 0)
+
+
+def octant_finder(children, count_f):
     me = lax.axis_index("blk")
     devices = lax.axis_size("blk")
-    count_c = children.shape[0]
-    fields = 8
-    upper = lane_ids() % B // H
     found = []
-    for p in range(count_c):
+    for p in range(children.shape[0]):
         for o in range(8):
             child = children[p, o]
-            distance = jnp.where(child >= 0, (child // count_f - me) % devices, -1)
-            found.append((distance, child, p, o))
-    sends = octant_sends(count_f)
-    for s, out in enumerate(outs):
-        if s < len(sends):
-            want = jnp.where(core == 0, sends[s][0], sends[s][1])
-        else:
-            want = 0
+            distance = jnp.where(child >= 0, (child // count_f - me) % devices, FAR)
+            found.append((distance, child, p * 8 + o))
+
+    def find(want):
         slot = jnp.int32(0)
         label = jnp.int32(-1)
-        for distance, child, p, o in found:
+        for distance, child, place in found:
             hit = distance == want
-            slot = jnp.where(hit, p * 8 + o, slot)
+            slot = jnp.where(hit, place, slot)
             label = jnp.where(hit, child % count_f, label)
-        if s < len(sends):
-            label = jnp.where((core == 0) & (sends[s][0] == count_f - 1), -1, label)
-        else:
-            label = jnp.where(core == 0, label, -1)
-        p, a, b, c = slot // 8, slot // 4 % 2, slot // 2 % 2, slot % 2
-        kept = upper == c
-        for f in range(fields):
-            layers = state[first_slab + p, b, pl.ds(a * (H * 8) + f, H, stride=8), :]
-            out[f] = jnp.where(kept, layers, 0.0)
-        out[fields] = jnp.full((H, LANES), label.astype(F32))
+        return slot, label
+
+    return find
+
+
+def write_octant(state, first_slab, found, wanted_fields, out, at):
+    slot, label = found
+    p, a, b, c = slot // 8, slot // 4 % 2, slot // 2 % 2, slot % 2
+    kept = lane_ids() % B // H == c
+    for n, f in enumerate(wanted_fields):
+        layers = state[first_slab + p, b, pl.ds(a * (H * 8) + f, H, stride=8), :]
+        out[at + n] = jnp.where(kept, layers, 0.0)
+    out[at + len(wanted_fields)] = jnp.full((H, LANES), label.astype(F32))
+
+
+def slot_fields(core, fields):
+    return [core * fields + v for v in range(fields)] + [0]
 
 
 def keep_coarse(state, first_slab, children):
@@ -506,40 +546,70 @@
                     state[at] = state[at] * kept
 
 
-def seed_kernel(seed_c, seed_o, children, count_f, coarse, *rest):
-    outs, stage = rest[:-1], rest[-1]
+def start_kernel(
+    sends, count_f, fields, payc, payc_o, children, coarse_counts, dif, shr, dif_o, shr_o,
+    fine_nbr, coarse_nbr, table, coarse, gain_c, weight_c, local, *rest
+):
     core = lax.axis_index("fld")
-    fields, count_c = seed_c.shape[0], seed_c.shape[1]
+    count_c = children.shape[0]
+    outs, (planes, packed, stage) = rest[:-3], rest[-3:]
+    up, down = outs[-2:]
     for p in range(count_c):
         for v in range(fields):
-            own = seed_c[v, pl.ds(p, 1), :]
-            other = seed_o[v, pl.ds(p, 1), :]
-            stage[p, pl.ds(v, 1), :] = pick(core, own, other)
-            stage[p, pl.ds(fields + v, 1), :] = pick(core, other, own)
+            mine = payc[2 + v, pl.ds(p, 1), :]
+            theirs = payc_o[2 + v, pl.ds(p, 1), :]
+            stage[p, pl.ds(v, 1), :] = pick(core, mine, theirs)
+            stage[p, pl.ds(fields + v, 1), :] = pick(core, theirs, mine)
         for i in range(B):
             for jh in range(2):
                 coarse[p, jh, rows_of(i), :] = stage[p, :, cols(i, jh)]
-    octants_out(coarse, 0, children, count_f, outs)
+    find = octant_finder(children, count_f)
+    for out, distances in zip(outs, sends):
+        write_octant(coarse, 0, find(pick(core, *distances)), list(range(2 * fields)), out, 0)
+    write_octant(coarse, 0, find(0), slot_fields(core, fields), local, 0)
+    chem_coarse(payc, payc_o, coarse_counts, gain_c, weight_c)
     keep_coarse(coarse, 0, children)
-
-
-def add_octants(messages, state, stage, fields):
-    core = lax.axis_index("fld")
+    react_coarse(
+        coarse,
+        0,
+        count_c,
+        spread_vector(core, (dif, shr), (dif_o, shr_o), 1, fields),
+        gain_c,
+        weight_c,
+        gain_c.shape[0] - count_c,
+    )
+    build_planes(coarse, count_c, planes)
+    packed[...] = pack_faces(planes, table, count_c * HG * 8)
+    rows = row_ids()
+    lane = lane_ids()
+    faces = jnp.zeros((8, LANES), F32)
+    for f in range(6):
+        column = fine_nbr[:, pl.ds(f, 1)].astype(F32)
+        faces = jnp.where(lane == f, jnp.broadcast_to(column, (8, LANES)), faces)
+        for p in range(count_c):
+            column = coarse_nbr[pl.ds(p, 1), pl.ds(f, 1)].astype(F32)
+            faces = jnp.where(
+                (lane == 8 + f) & (rows == p), jnp.broadcast_to(column, (8, LANES)), faces
+            )
+    base = 2 * fields + 1
+    for n in range(count_c * HG):
+        up[base + n] = packed[rows_of(n), half(0)]
+        down[base + n] = packed[rows_of(n), half(1)]
+    up[base + count_c * HG] = faces
+    down[base + count_c * HG] = faces
+
+
+def add_octants(entries, state, stage, fields):
     slots = fields + 1
     rows = row_ids()
     lane = lane_ids()
     source = jnp.zeros((8, LANES), jnp.int32)
-    for d, message in enumerate(messages):
-        label = message[2 * fields].astype(jnp.int32)
-        source = jnp.where(label == rows, d, source)
+    for d, tile in enumerate(entries):
+        source = jnp.where(tile(None).astype(jnp.int32) == rows, d, source)
         for s in range(slots):
-            if s == fields:
-                value = message[0]
-            else:
-                value = message[pl.ds(core * fields + s, 1)][0]
-            stage[d // 8, s, pl.ds(d % 8, H, stride=8), :] = value
+            stage[d // 8, s, pl.ds(d % 8, H, stride=8), :] = tile(s)
     lanes_of = [((H // 2 * jh + lane // B // 2) * B + lane % B // 2) for jh in range(2)]
-    groups = (len(messages) + 7) // 8
+    groups = (len(entries) + 7) // 8
     indices = []
     for g in range(groups):
         index = source - 8 * g
@@ -561,9 +631,22 @@
                     state[at] = state[at] + wide
 
 
+def all_fields(core, fields, ref):
+    def tile(s):
+        if s is None:
+            return ref[2 * fields]
+        return ref[0] if s == fields else ref[pl.ds(core * fields + s, 1)][0]
+
+    return tile
+
+
+def own_slots(fields, ref, at=0):
+    return lambda s: ref[at + (fields + 1 if s is None else s)]
+
+
 def react_fine(state, fields, par, par_o, gain, weight):
     core = lax.axis_index("fld")
-    share = [par[1, s] for s in range(fields)] + [pick(core, par[1, 0], par_o[1, 0])]
+    share = [par[1][s] for s in range(fields)] + [pick(core, par[1][0], par_o[1][0])]
     extra = jnp.where(core == 0, 1.0, 0.0)
     for i in range(B):
         for jh in range(2):
@@ -595,175 +678,229 @@
                 state[here] = value + shares * heat + own * grown
 
 
+def links_maker(plan, faces, shift, fine_slabs):
+    me = lax.axis_index("blk") + shift
+    count_f, count_c = plan["count_f"], plan["count_c"]
+
+    def column(slab, face):
+        return faces[:, face : face + 1].astype(jnp.int32)
+
+    def column_c(slab, face):
+        return faces[slab : slab + 1, 8 + face : 9 + face].astype(jnp.int32)
+
+    fine = Links(column, me * count_f, count_f, True, 0)
+    coarse = Links(column_c, me * count_c, count_c, False, fine_slabs)
+    return lambda s: fine if s < fine_slabs else coarse
+
+
+def strips_out(plan, r, out, faces, up_octant):
+    going = plan["slabs_out"]
+    even = lax.axis_index("blk") % 2 == 0
+    build_planes(out, going, r["planes"])
+    r["packed"][pl.ds(0, going * HG * 8), :] = pack_faces(
+        r["planes"], r["pack"], going * HG * 8
+    )
+
+    def send(up, down):
+        for n in range(going * HG):
+            up[n] = r["packed"][rows_of(n), half(0)]
+            down[n] = r["packed"][rows_of(n), half(1)]
+        at = going * HG
+        up[at] = faces
+        down[at] = faces
+        if up_octant is not None:
+            up_octant(up, at + 1)
+            for n in range(plan["fields"] + 2):
+                down[at + 1 + n] = zero_tile()
+
+    pl.when(even)(lambda: send(r["send_e"], r["send_o"]))
+    pl.when(jnp.logical_not(even))(lambda: send(r["send_o"], r["send_e"]))
+
+
+def zero_tile():
+    return jnp.zeros((8, LANES), F32)
+
+
+def open_kernel(plan, names, *refs):
+    r = dict(zip(names, refs))
+    core = lax.axis_index("fld")
+    fields = plan["fields"]
+    slots = fields + 1
+    count_f, count_c = plan["count_f"], plan["count_c"]
+    par, par_o = (r["dif"], r["shr"]), (r["dif_o"], r["shr_o"])
+    out = r["state_out"]
+    base = 2 * fields + 1
+    strip = count_c * HG
+
+    def far(ref, ref_o, n):
+        return pick(core, ref[base + n], ref_o[base + n])
+
+    last = len(plan["sends"]) - 1
+    below = [far(r[f"landed{last - 1}"], r[f"shared{last - 1}"], n) for n in range(strip + 1)]
+    above = [far(r[f"landed{last}"], r[f"shared{last}"], n) for n in range(strip + 1)]
+    own_up, own_down = r["own_up"], r["own_down"]
+    faces = own_up[base + strip]
+    rates = 0.5 * spread_vector(core, par, par_o, 0, fields)
+
+    def finish(p, i, jh, value):
+        out[slots + p, jh, rows_of(i), :] = value
+
+    diffuse(
+        r["coarse"],
+        count_c,
+        links_maker(plan, faces, 0, 0),
+        links_maker(plan, below[strip], -1, 0),
+        links_maker(plan, above[strip], 1, 0),
+        lambda s: rates,
+        lambda s, h: own_up[base + s * HG + h],
+        lambda s, h: own_down[base + s * HG + h],
+        lambda s, h: below[s * HG + h],
+        lambda s, h: above[s * HG + h],
+        r,
+        r,
+        finish,
+    )
+    find = octant_finder(r["children"], count_f)
+    for n, distances in enumerate(plan["later"]):
+        write_octant(
+            out, slots, find(pick(core, *distances)), list(range(2 * fields)), r[f"octant{n}"], 0
+        )
+    mine = slot_fields(core, fields)
+    write_octant(out, slots, find(0), mine, r["local_out"], 0)
+    near_octant = r["near_octant"]
+    write_octant(out, slots, find(1), mine, near_octant, 0)
+    keep_coarse(out, slots, r["children"])
+    react_coarse(
+        out, slots, count_c, spread_vector(core, par, par_o, 1, fields), r["gain_c"], r["weight_c"], 0
+    )
+    for i in range(B):
+        for jh in range(2):
+            at = cols(i, jh)
+            for s in range(fields):
+                out[s, jh, rows_of(i), :] = r["seed_f"][s, :, at]
+            out[fields, jh, rows_of(i), :] = pick(core, r["seed"][0, :, at], r["seed_other"][0, :, at])
+    entries = [own_slots(fields, r["local"])]
+    for n in range(last):
+        entries.append(all_fields(core, fields, r[f"landed{n}"]))
+        entries.append(all_fields(core, fields, r[f"shared{n}"]))
+    one, two = (all_fields(core, fields, r[f"{word}{last}"]) for word in ("landed", "shared"))
+    entries.append(lambda s: pick(core, two(s), one(s)))
+    add_octants(entries, out, r["stage"], fields)
+    react_fine(out, fields, par, par_o, r["gain"].at[plan["step"]], r["weight"].at[plan["step"]])
+
+    def up_octant(up, at):
+        for n in range(slots + 1):
+            up[at + n] = near_octant[n]
+
+    strips_out(plan, r, out, faces, up_octant)
+
+
 def step_kernel(plan, names, *refs):
     r = dict(zip(names, refs))
     core = lax.axis_index("fld")
-    me = lax.axis_index("blk")
-    even = me % 2 == 0
+    even = lax.axis_index("blk") % 2 == 0
     fields = plan["fields"]
     slots = fields + 1
-    count_f, count_c = plan["count_f"], plan["count_c"]
-    par, par_o = r["par"], r["par_o"]
-    mats = {name: r[name] for name in MATS}
-
-    if plan["slabs"]:
-        slabs, arrived = plan["slabs"], plan["slabs_in"]
-        own_up, own_down, far_b, far_a = (r[x] for x in ("own_up", "own_down", "far_b", "far_a"))
-
-        @pl.when(even)
-        def _():
-            own_up[...] = r["sent_e"][...]
-            own_down[...] = r["sent_o"][...]
-            far_a[...] = r["got_e"][...]
-            far_b[...] = r["got_o"][...]
-
-        @pl.when(jnp.logical_not(even))
-        def _():
-            own_up[...] = r["sent_o"][...]
-            own_down[...] = r["sent_e"][...]
-            far_b[...] = r["got_e"][...]
-            far_a[...] = r["got_o"][...]
-
-        faces = own_up[arrived * HG]
-        rate_of = [par[0, s] for s in range(fields)] + [pick(core, par[0, 0], par_o[0, 0])]
-        if slabs > slots:
-            rate_of += [0.5 * spread_vector(core, par, par_o, 0, fields)] * count_c
-
-        def links_of(ref, shift):
-            def column(slab, face):
-                return ref[arrived * HG, :, pl.ds(face, 1)].astype(jnp.int32)
-
-            def column_c(slab, face):
-                return ref[arrived * HG, pl.ds(slab, 1), pl.ds(8 + face, 1)].astype(jnp.int32)
-
-            fine = Links(column, (me + shift) * count_f, count_f, True, 0)
-            coarse = Links(column_c, (me + shift) * count_c, count_c, False, slots)
-            return lambda s: fine if s < slots else coarse
-
-        if slabs <= slots:
-            source = r["state"]
+    count_c = plan["count_c"]
+    par, par_o = (r["dif"], r["shr"]), (r["dif_o"], r["shr_o"])
+    slabs, arrived = plan["slabs"], plan["slabs_in"]
+    own_up, own_down, far_b, far_a = (r[x] for x in ("own_up", "own_down", "far_b", "far_a"))
+    used = arrived * HG + 1
+
+    def sort_strips(up, down, below, above):
+        for n in range(used):
+            own_up[n] = up[n]
+            own_down[n] = down[n]
+            far_b[n] = below[n]
+            far_a[n] = above[n]
+
+    pl.when(even)(lambda: sort_strips(r["sent_e"], r["sent_o"], r["got_o"], r["got_e"]))
+    pl.when(jnp.logical_not(even))(
+        lambda: sort_strips(r["sent_o"], r["sent_e"], r["got_e"], r["got_o"])
+    )
+    faces = own_up[arrived * HG]
+    rate_of = [par[0][s] for s in range(fields)] + [pick(core, par[0][0], par_o[0][0])]
+    if slabs > slots:
+        rate_of += [0.5 * spread_vector(core, par, par_o, 0, fields)] * count_c
+    source, out = r["state"], r["state_out"]
+
+    def finish(s, i, jh, value):
+        if s >= slots:
+            r["coarse_stage"][s - slots, :, cols(i, jh)] = value
+        elif plan["final"]:
+            out[s, :, cols(i, jh)] = value
         else:
-            source = r["state"]
-        out = r["state_out"]
-        direct = plan["final"]
-
-        def finish(s, i, jh, value):
-            if s >= slots and plan["coarse_last"]:
-                r["coarse_stage"][s - slots, :, cols(i, jh)] = value
-            elif direct:
-                out[s, :, cols(i, jh)] = value
-            else:
-                out[s, jh, rows_of(i), :] = value
-
-        diffuse(
-            source,
-            slabs,
-            links_of(own_up, 0),
-            links_of(far_b, -1),
-            links_of(far_a, 1),
-            lambda s: rate_of[s],
-            lambda s, h: own_up[s * HG + h],
-            lambda s, h: own_down[s * HG + h],
-            lambda s, h: far_b[s * HG + h],
-            lambda s, h: far_a[s * HG + h],
-            mats,
-            r,
-            finish,
-        )
-        if plan["coarse_last"]:
-            final, stage = r["coarse_final"], r["coarse_stage"]
-            for p in range(count_c):
-                for v in range(fields):
-                    final[v, pl.ds(p, 1), :] = pick(
-                        core, stage[p, pl.ds(v, 1), :], stage[p, pl.ds(fields + v, 1), :]
-                    )
-        if plan["send_octants"]:
-            octants_out(
-                out,
-                slots,
-                r["children"],
-                count_f,
-                [r[f"octant{s}"] for s in range(plan["messages"])],
-            )
-            keep_coarse(out, slots, r["children"])
-    else:
-        out = r["state_out"]
-        last = r["pay"].shape[0] - 1
-        for i in range(B):
-            for jh in range(2):
-                at = cols(i, jh)
-                for s in range(fields):
-                    out[s, jh, rows_of(i), :] = r["seed_f"][s, :, at]
-                out[fields, jh, rows_of(i), :] = pick(
-                    core, r["pay"][last, :, at], r["pay_o"][last, :, at]
+            out[s, jh, rows_of(i), :] = value
+
+    diffuse(
+        source,
+        slabs,
+        links_maker(plan, faces, 0, slots),
+        links_maker(plan, far_b[arrived * HG], -1, slots),
+        links_maker(plan, far_a[arrived * HG], 1, slots),
+        lambda s: rate_of[s],
+        lambda s, h: own_up[s * HG + h],
+        lambda s, h: own_down[s * HG + h],
+        lambda s, h: far_b[s * HG + h],
+        lambda s, h: far_a[s * HG + h],
+        r,
+        r,
+        finish,
+    )
+    if slabs > slots:
+        final, stage = r["coarse_final"], r["coarse_stage"]
+        for p in range(count_c):
+            for v in range(fields):
+                final[v, pl.ds(p, 1), :] = pick(
+                    core, stage[p, pl.ds(v, 1), :], stage[p, pl.ds(fields + v, 1), :]
                 )
-        for p in range(count_c):
-            out[slots + p] = r["coarse"][p]
-        rows = row_ids()
-        lane = lane_ids()
-        faces = jnp.zeros((8, LANES), F32)
-        for f in range(6):
-            column = r["fine_nbr"][:, pl.ds(f, 1)].astype(F32)
-            faces = jnp.where(lane == f, jnp.broadcast_to(column, (8, LANES)), faces)
-            for p in range(count_c):
-                column = r["coarse_nbr"][pl.ds(p, 1), pl.ds(f, 1)].astype(F32)
-                faces = jnp.where(
-                    (lane == 8 + f) & (rows == p), jnp.broadcast_to(column, (8, LANES)), faces
-                )
-
     if plan["add"]:
-        add_octants([r[f"arrived{s}"] for s in range(plan["arrivals"])], out, r["stage"], fields)
-    if plan["react"]:
+        near = r["near_octant"]
+
+        def take(ref):
+            for n in range(slots + 1):
+                near[n] = ref[plan["near_at"] + n]
+
+        pl.when(even)(lambda: take(r["near_o"]))
+        pl.when(jnp.logical_not(even))(lambda: take(r["near_e"]))
+        entries = [own_slots(fields, r["local"]), own_slots(fields, near)]
+        for n in range(len(plan["later"])):
+            entries.append(all_fields(core, fields, r[f"landed{n}"]))
+            entries.append(all_fields(core, fields, r[f"shared{n}"]))
+        add_octants(entries, out, r["stage"], fields)
+    if not plan["final"]:
         step = plan["step"]
         react_fine(out, fields, par, par_o, r["gain"].at[step], r["weight"].at[step])
-        if plan["react_coarse"] is not None:
-            react_coarse(
-                out,
-                slots,
-                count_c,
-                spread_vector(core, par, par_o, 1, fields),
-                r["gain_c"],
-                r["weight_c"],
-                plan["react_coarse"] * count_c,
-            )
-        going = plan["slabs_out"]
-        build_planes(out, going, r["planes"])
-        r["packed"][pl.ds(0, going * HG * 8), :] = pack_faces(
-            r["planes"], mats["pack"], going * HG * 8
-        )
-
-        def send(up, down):
-            for n in range(going * HG):
-                up[n] = r["packed"][rows_of(n), half(0)]
-                down[n] = r["packed"][rows_of(n), half(1)]
-            up[going * HG] = faces
-            down[going * HG] = faces
-
-        pl.when(even)(lambda: send(r["send_e"], r["send_o"]))
-        pl.when(jnp.logical_not(even))(lambda: send(r["send_o"], r["send_e"]))
-
-
-SCALARS = ("par", "par_o", "children", "fine_counts", "coarse_counts")
+        strips_out(plan, r, out, faces, None)
+
+
+SCALARS = ("dif", "shr", "dif_o", "shr_o", "children", "fine_counts", "coarse_counts")
 MATS = ("plane", "side", "place", "pack", "far")
 MIB = 1024 * 1024
 
 
-def call(kernel, inputs, outputs, scratch, cost=2_000_000):
+def call(kernel, inputs, outputs, scratch, hbm=(), sems=(), limit=None, cost=1000):
     names = list(inputs) + list(outputs) + list(scratch)
     scratch = {
-        name: value if isinstance(value[-1], int) is False else value + (F32,)
-        for name, value in scratch.items()
+        name: value if value[-1] is BF16 else value + (F32,) for name, value in scratch.items()
     }
-    size = sum(4 * np.prod(v.shape) for v in inputs.values())
+    size = sum(4 * np.prod(v.shape) for name, v in inputs.items() if name not in hbm)
     size += sum(4 * np.prod(v) for v in outputs.values())
     size += sum(4 * np.prod(v[:-1]) for v in scratch.values())
+
+    def spec(name):
+        if name in hbm:
+            return HBM
+        return SMEM if name in SCALARS else VMEM
+
     result = pl.pallas_call(
         functools.partial(kernel, names),
         out_shape=[jax.ShapeDtypeStruct(shape, F32) for shape in outputs.values()],
-        in_specs=[SMEM if name in SCALARS else VMEM for name in inputs],
+        in_specs=[spec(name) for name in inputs],
         out_specs=[VMEM] * len(outputs),
-        scratch_shapes=[pltpu.VMEM(value[:-1], value[-1]) for value in scratch.values()],
-        compiler_params=pltpu.CompilerParams(vmem_limit_bytes=int(size) + 12 * MIB),
+        scratch_shapes=[pltpu.VMEM(value[:-1], value[-1]) for value in scratch.values()]
+        + [pltpu.SemaphoreType.DMA(shape) for shape in sems],
+        compiler_params=pltpu.CompilerParams(vmem_limit_bytes=limit or int(size) + 12 * MIB),
         cost_estimate=pl.CostEstimate(flops=cost, bytes_accessed=cost, transcendentals=0),
     )(*inputs.values())
     return dict(zip(outputs, result))
@@ -788,77 +925,24 @@
     cycles = saved_coarse.shape[0]
     slots = fields + 1
     every = slots + count_c
-    sends = octant_sends(count_f)
-    messages = len(sends) + 1
-    par = jnp.stack([diffusion, species_shares])
-    par_o = core_swap(par)
-    seed_o = core_swap(seed_coarse)
+    sends, later = first_sends(count_f), later_sends(count_f)
     mats = tables()
-
-    def wrapped(kernel):
-        return lambda names, *refs: kernel(*refs)
-
-    octant_shapes = {f"octant{s}": (2 * fields + 1, H, LANES) for s in range(messages)}
-
-    def seed_call(names, seed_c, seed_other, kids, *rest):
-        seed_kernel(seed_c, seed_other, kids, count_f, *rest)
-
-    opened = call(
-        seed_call,
-        dict(seed_c=seed_coarse, seed_o=seed_o, children=children),
-        dict(coarse=(count_c, 2, 8 * B, LANES), **octant_shapes),
-        dict(seed_stage=(count_c, 2 * fields, cells)),
-    )
-
-    def travel(made):
-        landed = [octant_move(made[f"octant{s}"], d) for s, d in enumerate(sends)]
-        landed.append(made[f"octant{len(sends)}"])
-        return landed + [core_swap(value) for value in landed]
-
-    arrived = travel(opened)
-
-    paid = call(
-        wrapped(mix_kernel),
-        dict(saved_f=saved_fine, saved_c=saved_coarse, seed_f=seed_fine, par=par),
-        dict(pay=(2 * steps + 1, count_f, cells), payc=(2, cycles * count_c, cells)),
-        {},
-    )
-    pay, payc = paid["pay"], paid["payc"]
-    pay_o, payc_o = core_swap(pay), core_swap(payc)
-    made_tables = call(
-        wrapped(chem_kernel),
-        dict(
-            pay=pay,
-            pay_o=pay_o,
-            payc=payc,
-            payc_o=payc_o,
-            fine_counts=fine_counts,
-            coarse_counts=coarse_counts,
-        ),
-        dict(
-            gain=(steps, count_f, cells),
-            weight=(steps, count_f, cells),
-            gain_c=(cycles * count_c, cells),
-            weight_c=(cycles * count_c, cells),
-        ),
-        {},
-    )
-    chem = {name: made_tables[name] for name in ("gain", "weight")}
-    chem_c = {name: made_tables[name] for name in ("gain_c", "weight_c")}
-
-    def strip(slabs):
-        return (slabs * HG + 1, 8, LANES)
+    octant_shape = (2 * fields + 1, H, LANES)
+    slots_shape = (slots + 1, H, LANES)
+    loaded_shape = (2 * fields + 1 + count_c * HG + 1, 8, LANES)
+
+    def plain(kernel, *fixed):
+        return lambda names, *refs: kernel(*fixed, *refs)
+
+    def strip(slabs, more=0):
+        return (slabs * HG + 1 + more, 8, LANES)
 
     def state_shape(slabs):
         return (slabs, 2, 8 * B, LANES)
 
-    def work(slabs_in, slabs):
+    def work(slabs):
         rows = slabs * HG * 8
         return dict(
-            far_b=strip(slabs_in),
-            far_a=strip(slabs_in),
-            own_up=strip(slabs_in),
-            own_down=strip(slabs_in),
             first=state_shape(slabs),
             far_first=(2, slabs * HG, 8, LANES),
             sums=(G, rows, PLANE),
@@ -868,6 +952,9 @@
             far_out=(2 * rows, LANES),
         )
 
+    def strip_work(slabs):
+        return {name: strip(slabs) for name in ("far_b", "far_a", "own_up", "own_down")}
+
     def pack_work(slabs):
         rows = slabs * HG * 8
         return dict(
@@ -875,99 +962,159 @@
             packed=(rows, 2 * LANES),
         )
 
-    stage_work = dict(stage=((2 * messages + 7) // 8, slots, 8 * H, LANES))
-    common = dict(par=par, par_o=par_o, **mats)
-
-    def plan_of(**changes):
-        plan = dict(
-            fields=fields,
-            count_f=count_f,
-            count_c=count_c,
-            messages=messages,
-            arrivals=2 * messages,
-            slabs_in=0,
-            slabs=0,
-            slabs_out=slots,
-            final=False,
-            coarse_last=False,
-            send_octants=False,
-            add=False,
-            react=True,
-            react_coarse=None,
-            step=0,
-        )
-        plan.update(changes)
-        return plan
-
-    def run(plan, inputs, outputs, scratch):
-        return call(functools.partial(step_kernel, plan), inputs, outputs, scratch)
-
-    def halo(made):
-        return dict(
-            state=made["state_out"],
-            sent_e=made["send_e"],
-            sent_o=made["send_o"],
-            got_e=pair_swap(made["send_e"], 0),
-            got_o=pair_swap(made["send_o"], 1),
-        )
-
-    def sending(slabs):
-        return dict(state_out=state_shape(slabs), send_e=strip(slabs), send_o=strip(slabs))
-
-    def arrivals(values):
-        return {f"arrived{s}": value for s, value in enumerate(values)}
-
-    made = run(
-        plan_of(add=True, react_coarse=cycles - 1, step=steps - 1, slabs_out=every),
+    def after(value, *before):
+        return lax.optimization_barrier((value, before))[0]
+
+    stage_work = dict(stage=(1, slots, 8 * H, LANES))
+    dif_o, shr_o = core_swap(diffusion), core_swap(species_shares)
+    par = dict(dif=diffusion, shr=species_shares, dif_o=dif_o, shr_o=shr_o)
+
+    paid = call(
+        plain(mix_kernel),
         dict(
-            common,
-            **chem,
-            **chem_c,
+            saved_f=saved_fine,
+            saved_c=saved_coarse,
             seed_f=seed_fine,
-            pay=pay,
-            pay_o=pay_o,
-            coarse=opened["coarse"],
+            seed_c=seed_coarse,
+            shr=species_shares,
+        ),
+        dict(
+            pay=(2 * steps + 1, count_f, cells), payc=(2 + fields, cycles * count_c, cells)
+        ),
+        dict(fine=saved_fine.shape, coarse=saved_coarse.shape, seeds=seed_coarse.shape),
+        hbm=("saved_f", "saved_c", "seed_f", "seed_c"),
+        sems=((steps,), (), (), ()),
+        limit=60 * MIB,
+    )
+    pay, payc = paid["pay"], paid["payc"]
+    payc_o, pay_o = core_swap(payc), core_swap(pay)
+
+    loaded = [f"octant{n}" for n in range(len(sends) - 2)] + ["up", "down"]
+    started = call(
+        plain(start_kernel, sends, count_f, fields),
+        dict(
+            payc=payc,
+            payc_o=payc_o,
+            children=children,
+            coarse_counts=coarse_counts,
+            **par,
             fine_nbr=fine_nbr,
             coarse_nbr=coarse_nbr,
-            **arrivals(arrived),
+            pack=mats["pack"],
         ),
-        sending(every),
-        dict(pack_work(every), **stage_work),
-    )
-    held = every
-    coarse_final = None
-    for step in reversed(range(1, steps)):
-        cycle, late = step // 2, step % 2 == 1
-        inputs = dict(common, **chem, **halo(made))
-        scratch = dict(work(held, held), **pack_work(held))
-        plan = plan_of(slabs_in=held, slabs=held, step=step - 1)
-        outputs = {}
-        if late and cycle > 0:
-            inputs.update(chem_c, children=children)
-            outputs.update(octant_shapes)
-            plan.update(send_octants=True, react_coarse=cycle - 1, slabs_out=held)
-        elif not late:
-            inputs.update(arrivals(arrived))
-            scratch.update(stage_work)
-            plan.update(add=True, slabs_out=held)
-            if cycle == 1:
-                outputs.update(coarse_final=seed_coarse.shape)
-                scratch.update(coarse_stage=(count_c, 2 * fields, cells))
-                plan.update(coarse_last=True, slabs_out=slots)
-        else:
-            plan.update(slabs_out=held)
-        held = plan["slabs_out"]
-        outputs.update(sending(held))
-        made = run(plan, inputs, outputs, scratch)
-        if plan["send_octants"]:
-            arrived = travel(made)
-        if plan["coarse_last"]:
-            coarse_final = made["coarse_final"]
+        dict(
+            coarse=state_shape(count_c),
+            gain_c=(cycles * count_c, cells),
+            weight_c=(cycles * count_c, cells),
+            local=slots_shape,
+            **{name: loaded_shape if name in ("up", "down") else octant_shape for name in loaded},
+        ),
+        dict(pack_work(count_c), coarse_stage=(count_c, 2 * fields, cells)),
+    )
+    landed = [octant_move(started[name], d) for name, d in zip(loaded, sends)]
+    chem = call(
+        plain(chem_kernel),
+        dict(pay=pay, pay_o=pay_o, fine_counts=fine_counts),
+        dict(gain=(steps, count_f, cells), weight=(steps, count_f, cells)),
+        {},
+    )
+    landed, chem = lax.optimization_barrier((landed, chem))
+    shared = [core_swap(value) for value in landed]
+
+    def named(word, values):
+        return {f"{word}{n}": value for n, value in enumerate(values)}
+
+    plan = dict(
+        fields=fields,
+        count_f=count_f,
+        count_c=count_c,
+        sends=sends,
+        later=later,
+        slabs_in=every,
+        slabs=every,
+        slabs_out=slots,
+        final=False,
+        add=False,
+        near_at=every * HG + 1,
+    )
+
+    def run(kernel, changes, inputs, outputs, scratch):
+        return call(
+            functools.partial(kernel, dict(plan, **changes)),
+            dict(par, **mats, **inputs),
+            outputs,
+            scratch,
+        )
+
+    def halo(made, ring=False):
+        got_o = pair_swap(made["send_o"], 1, ring)
+        got_e = pair_swap(made["send_e"], 0, ring)
+        return dict(sent_o=made["send_o"], got_o=got_o, sent_e=made["send_e"], got_e=got_e)
+
+    def sending(slabs, more=0):
+        return dict(
+            state_out=state_shape(slabs), send_e=strip(slabs, more), send_o=strip(slabs, more)
+        )
+
     made = run(
-        plan_of(react=False, final=True, slabs_in=held, slabs=fields),
-        dict(common, **halo(made)),
+        open_kernel,
+        dict(slabs_out=every, step=steps - 1),
+        dict(
+            chem,
+            gain_c=started["gain_c"],
+            weight_c=started["weight_c"],
+            children=children,
+            coarse=started["coarse"],
+            own_up=started["up"],
+            own_down=started["down"],
+            seed_f=seed_fine,
+            seed=pay[2 * steps :],
+            seed_other=pay_o[2 * steps :],
+            local=started["local"],
+            **named("landed", landed),
+            **named("shared", shared),
+        ),
+        dict(
+            sending(every, slots + 1),
+            local_out=slots_shape,
+            **named("octant", [octant_shape] * len(later)),
+        ),
+        dict(work(count_c), **pack_work(every), **stage_work, near_octant=slots_shape),
+    )
+    first_halo = halo(made, True)
+    local = made["local_out"]
+    landed = [octant_move(made[f"octant{n}"], d) for n, d in enumerate(later)]
+    landed, first_halo = lax.optimization_barrier((landed, first_halo))
+    shared = [core_swap(value) for value in landed]
+    made = run(
+        step_kernel,
+        dict(step=steps - 2),
+        dict(chem, state=made["state_out"], **first_halo),
+        dict(sending(slots), coarse_final=seed_coarse.shape),
+        dict(
+            work(every),
+            **strip_work(every),
+            **pack_work(every),
+            coarse_stage=(count_c, 2 * fields, cells),
+        ),
+    )
+    coarse_final = made["coarse_final"]
+    for step in reversed(range(steps - 2)):
+        inputs = dict(chem, state=made["state_out"], **halo(made))
+        scratch = dict(work(slots), **strip_work(slots), **pack_work(slots))
+        changes = dict(step=step, slabs_in=slots, slabs=slots)
+        if step == steps - 3:
+            inputs.update(named("landed", landed), **named("shared", shared), local=local)
+            inputs.update(near_e=first_halo["got_e"], near_o=first_halo["got_o"])
+            scratch.update(stage_work, near_octant=slots_shape)
+            changes.update(add=True)
+        made = run(step_kernel, changes, inputs, sending(slots), scratch)
+    made = run(
+        step_kernel,
+        dict(final=True, slabs_in=slots, slabs=fields),
+        dict(state=made["state_out"], **halo(made)),
         dict(state_out=seed_fine.shape),
-        dict(work(held, fields), **pack_work(fields)),
+        dict(work(fields), **strip_work(slots), **pack_work(fields)),
     )
     return made["state_out"], coarse_final
 

time: 88 us -> 76.1 us (0.86)
  waiting for transfers between devices: 38.2 us -> 23.4 us
  Pallas kernels: 20.8 us -> 25.5 us
  local copies, waits for them, and re-layouts: 3.64 us -> 1.07 us
  starting transfers between devices: 23.5 us -> 25 us
    ppermute x8, waiting for transfers between devices: 20.7 us -> 10.9 us  [pair_swap(): return lax.ppermute(value, ('blk', 'fld'), pairs)]
    ppermute x8 -> x7, waiting for transfers between devices: 14.3 us -> 8.13 us  [octant_move(): return lax.ppermute(value, ('blk', 'fld'), pairs)]
    pallas_call x8, Pallas kernels: 20.8 us -> 25.5 us  [call(): pl.pallas_call(functools.partial(kernel, names), out_shape=[jax.ShapeDtyp...]
    ppermute x8, starting transfers between devices: 8.94 us -> 11.9 us  [pair_swap(): return lax.ppermute(value, ('blk', 'fld'), pairs)]
    unnamed x30, local copies, waits for them, and re-layouts: 3.64 us -> 1.05 us
    ppermute x8 -> x7, starting transfers between devices: 11.7 us -> 9.75 us  [octant_move(): return lax.ppermute(value, ('blk', 'fld'), pairs)]
    ppermute x14 -> x11, waiting for transfers between devices: 3.21 us -> 4.36 us  [core_swap(): return lax.ppermute(value, 'fld', [(0, 1), (1, 0)])]
    ppermute x14 -> x11, starting transfers between devices: 2.85 us -> 3.35 us  [core_swap(): return lax.ppermute(value, 'fld', [(0, 1), (1, 0)])]
  transfers between devices with their start and end apart: 30 -> 26, of which waited for: 16 -> 14; matrix products, arithmetic and copies ran while one was open for 0% -> 0% of each run, Pallas kernels for 5% -> 7%
where the time goes in v3:
time: 76.1 us; the launch traced here: 75.9 us
  Pallas kernels  25.5 us (34%)
  starting transfers between devices  25 us (33%)
  waiting for transfers between devices  23.4 us (31%)
  local copies, waits for them, and re-layouts  1.07 us (1%)
  between operations  0.89 us (1%)
    pallas_call x8, Pallas kernels, call(): pl.pallas_call(functools.partial(kernel, names), out_shape=[jax.ShapeDtyp...  25.5 us
    ppermute x8, starting transfers between devices, pair_swap(): return lax.ppermute(value, ('blk', 'fld'), pairs)  11.9 us
    ppermute x8, waiting for transfers between devices, pair_swap(): return lax.ppermute(value, ('blk', 'fld'), pairs)  10.9 us
    ppermute x7, starting transfers between devices, octant_move(): return lax.ppermute(value, ('blk', 'fld'), pairs)  9.75 us
    ppermute x7, waiting for transfers between devices, octant_move(): return lax.ppermute(value, ('blk', 'fld'), pairs)  8.13 us
    ppermute x11, waiting for transfers between devices, core_swap(): return lax.ppermute(value, 'fld', [(0, 1), (1, 0)])  4.36 us
    ppermute x11, starting transfers between devices, core_swap(): return lax.ppermute(value, 'fld', [(0, 1), (1, 0)])  3.35 us
  transfers between devices with their start and end apart: 26, of which 14 were waited for; matrix products, arithmetic and copies ran while one was open for 0% of the time, Pallas kernels for 7%

profile of v3, /device:TPU:0, one launch (start us, length us, event | category | flops | bytes accessed | tf_op | source)
XLA Modules:
  0.0 75.9 jit_solution(2646831118416409976)
XLA Ops:
  0.7 3.7 %shard_map.167 = (f32[9,8,4096]{2,1,0:T(8,128)}, f32[6,4,4096]{2,1,0:T(4,128)}) custom-call(f32[4,4,8,4096]{3,2,1,0:T(8,128)} %refs_0_.6, f32[2,4,2,4096]{3,2,1,0:T(2,128)} %refs_1_.6, f32[4,8,4096]{2,1,0:T(8,128)} %refs_17_.1, f32[4,2,4096]{2,1,0:T(2,128)} %refs_3_.2, f32[4]{0:T(128)} %refs_1_.11), custom_call_target="tpu_custom_call" | custom-call | flops 1000 | bytes 1000 | tf_op jit(solution)/shard_map/pallas_call | solution.py:896
  5.5 2.4 %collective-permute-done.refs_6_.refs_2_ = f32[4]{0:T(128)S(1)} collective-permute-done((f32[4]{0:T(128)S(1)}, f32[4]{0:T(128)S(1)}, u32[]{:S(2)}, u32[]{:S(2)}) %collective-permute-start) | collective-permute-done | bytes 48 | tf_op jit(solution)/shard_map/ppermute | solution.py:31
  9.2 2.0 %shard_map.168 = (f32[2,2,128,128]{3,2,1,0:T(8,128)S(1)}, f32[4,4096]{1,0:T(4,128)S(1)}, f32[4,4096]{1,0:T(4,128)S(1)}, f32[6,8,128]{2,1,0:T(8,128)S(1)}, f32[9,...) custom-call(f32[6,4,4096]{2,1,0:T(4,128)S(1)} %copy-done.7, ...), custom_call_target="tpu_custom_call" | custom-call | flops 1000 | bytes 1000 | tf_op jit(solution)/shard_map/pallas_call | solution.py:896
  11.2 2.9 %collective-permute-start.5 = (f32[18,8,128]{2,1,0:T(8,128)S(1)}, f32[18,8,128]{2,1,0:T(8,128)S(1)}, u32[]{:S(2)}, u32[]{:S(2)}) collective-permute-start(f32[18,8,128]{2,1,0:T(8,128)S(1)} %get-tuple-element.47.refs_15_), channel_id=1, source_target_pairs={{0,2},{1,13},{2,4},{3,15},{4,6},{5,17},{6,8},{7,19},{8,10},{9,21},... | collective-permute-start | bytes 221192 | tf_op jit(solution)/shard_map/ppermute | solution.py:63
  14.1 4.1 %collective-permute-start.6 = (f32[18,8,128]{2,1,0:T(8,128)S(1)}, f32[18,8,128]{2,1,0:T(8,128)S(1)}, u32[]{:S(2)}, u32[]{:S(2)}) collective-permute-start(f32[18,8,128]{2,1,0:T(8,128)S(1)} %get-tuple-element.48.refs_16_), channel_id=1, source_target_pairs={{0,30},{1,15},{2,0},{3,17},{4,2},{5,19},{6,4},{7,21},{8,6},{9,23},... | collective-permute-start | bytes 221192 | tf_op jit(solution)/shard_map/ppermute | solution.py:63
  18.7 3.2 %shard_map.169 = (f32[4,8,4096]{2,1,0:T(8,128)S(1)}, f32[4,8,4096]{2,1,0:T(8,128)S(1)}) custom-call(f32[9,8,4096]{2,1,0:T(8,128)S(1)} %copy-done.6, f32[9,8,4096]{2,1,0:T(8,128)S(1)} %collective-permute-done.7.refs_1_, s32[8]{0:T(128)S(1)} %copy-done.14), custom_call_target="tpu_custom_call" | custom-call | flops 1000 | bytes 1000 | tf_op jit(solution)/shard_map/pallas_call | solution.py:896
  21.9 2.9 %collective-permute-done.3.refs_21_ = f32[9,8,128]{2,1,0:T(8,128)S(1)} collective-permute-done((f32[9,8,128]{2,1,0:T(8,128)S(1)}, f32[9,8,128]{2,1,0:T(8,128)S(1)}, u32[]{:S(2)}, u32[]{:S(2)}) %collective-permute-start.3) | collective-permute-done | bytes 36896 | tf_op jit(solution)/shard_map/ppermute | solution.py:63
  27.3 2.9 %shard_map.170 = (f32[7,2,128,128]{3,2,1,0:T(8,128)S(1)}, f32[35,8,128]{2,1,0:T(8,128)S(1)}, f32[35,8,128]{2,1,0:T(8,128)S(1)}, f32[6,8,128]{2,1,0:T(8,128)S(1)}...) custom-call(f32[4]{0:T(128)S(1)} %copy-done.9, f32[4]{0:T(128)S(1)} %copy-done.8, ...), custom_call_target="tpu_custom_call" | custom-call | flops 1000 | bytes 1000 | tf_op jit(solution)/shard_map/pallas_call | solution.py:896
  30.2 1.4 %collective-permute-start.15 = (f32[35,8,128]{2,1,0:T(8,128)S(1)}, f32[35,8,128]{2,1,0:T(8,128)S(1)}, u32[]{:S(2)}, u32[]{:S(2)}) collective-permute-start(f32[35,8,128]{2,1,0:T(8,128)S(1)} %get-tuple-element.70.refs_14_), channel_id=1, source_target_pairs={{0,2},{1,3},{2,0},{3,1},{4,6},{5,7},{6,4},{7,5},{8,10},{9,11},{10,... | collective-permute-start | bytes 430088 | tf_op jit(solution)/shard_map/ppermute | solution.py:44
  31.6 2.8 %collective-permute-start.16 = (f32[35,8,128]{2,1,0:T(8,128)S(1)}, f32[35,8,128]{2,1,0:T(8,128)S(1)}, u32[]{:S(2)}, u32[]{:S(2)}) collective-permute-start(f32[35,8,128]{2,1,0:T(8,128)S(1)} %get-tuple-element.71.refs_15_), channel_id=1, source_target_pairs={{0,30},{1,31},{2,4},{3,5},{4,2},{5,3},{6,8},{7,9},{8,6},{9,7},{10,... | collective-permute-start | bytes 430088 | tf_op jit(solution)/shard_map/ppermute | solution.py:44
  34.5 1.0 %collective-permute-start.13 = (f32[9,8,128]{2,1,0:T(8,128)S(1)}, f32[9,8,128]{2,1,0:T(8,128)S(1)}, u32[]{:S(2)}, u32[]{:S(2)}) collective-permute-start(f32[9,8,128]{2,1,0:T(8,128)S(1)} %get-tuple-element.64), channel_id=1, source_target_pairs={{0,6},{1,13},{2,8},{3,15},{4,10},{5,17},{6,12},{7,19},{8,14},{9,21... | collective-permute-start | bytes 110600 | tf_op jit(solution)/shard_map/ppermute | solution.py:63
  35.5 1.3 %collective-permute-start.14 = (f32[9,8,128]{2,1,0:T(8,128)S(1)}, f32[9,8,128]{2,1,0:T(8,128)S(1)}, u32[]{:S(2)}, u32[]{:S(2)}) collective-permute-start(f32[9,8,128]{2,1,0:T(8,128)S(1)} %get-tuple-element.65), channel_id=1, source_target_pairs={{0,8},{1,15},{2,10},{3,17},{4,12},{5,19},{6,14},{7,21},{8,16},{9,2... | collective-permute-start | bytes 110600 | tf_op jit(solution)/shard_map/ppermute | solution.py:63
  36.8 4.7 %collective-permute-done.12.refs_16_ = f32[9,8,128]{2,1,0:T(8,128)S(1)} collective-permute-done((f32[9,8,128]{2,1,0:T(8,128)S(1)}, f32[9,8,128]{2,1,0:T(8,128)S(1)}, u32[]{:S(2)}, u32[]{:S(2)}) %collective-permute-start.12) | collective-permute-done | bytes 36896 | tf_op jit(solution)/shard_map/ppermute | solution.py:63
  42.0 4.2 %shard_map.171 = (f32[5,2,128,128]{3,2,1,0:T(8,128)S(1)}, f32[21,8,128]{2,1,0:T(8,128)S(1)}, f32[21,8,128]{2,1,0:T(8,128)S(1)}, f32[4,2,4096]{2,1,0:T(2,128)}) custom-call(f32[4]{0:T(128)S(1)} %copy-done.9, f32[4]{0:T(128)S(1)} %copy-done.8, f32[4]{0:T(128)S(1)} %collective-permute-done.refs_6_.refs_2_, f32[4]{0:T(128)S(1)} %collective-permute-done.1.refs_7_.refs_3_, ...), custom_call_target="tpu_custom_call" | custom-call | flops 1000 | bytes 1000 | tf_op jit(solution)/shard_map/pallas_call | solution.py:896
  46.2 1.6 %collective-permute-start.17 = (f32[21,8,128]{2,1,0:T(8,128)S(1)}, f32[21,8,128]{2,1,0:T(8,128)S(1)}, u32[]{:S(2)}, u32[]{:S(2)}) collective-permute-start(f32[21,8,128]{2,1,0:T(8,128)S(1)} %get-tuple-element.73.refs_12_), channel_id=1, source_target_pairs={{0,1},{1,0},{2,4},{3,5},{4,2},{5,3},{6,8},{7,9},{8,6},{9,7},{10,12... | collective-permute-start | bytes 258056 | tf_op jit(solution)/shard_map/ppermute | solution.py:44
  47.8 1.5 %collective-permute-start.18 = (f32[21,8,128]{2,1,0:T(8,128)S(1)}, f32[21,8,128]{2,1,0:T(8,128)S(1)}, u32[]{:S(2)}, u32[]{:S(2)}) collective-permute-start(f32[21,8,128]{2,1,0:T(8,128)S(1)} %get-tuple-element.74.refs_14_), channel_id=1, source_target_pairs={{0,2},{1,3},{2,0},{3,1},{4,6},{5,7},{6,4},{7,5},{8,10},{9,11},{10,... | collective-permute-start | bytes 258056 | tf_op jit(solution)/shard_map/ppermute | solution.py:44
  51.4 2.8 %collective-permute-done.18.refs_15_ = f32[21,8,128]{2,1,0:T(8,128)S(1)} collective-permute-done((f32[21,8,128]{2,1,0:T(8,128)S(1)}, f32[21,8,128]{2,1,0:T(8,128)S(1)}, u32[]{:S(2)}, u32[]{:S(2)}) %collective-permute-start.18) | collective-permute-done | bytes 86048 | tf_op jit(solution)/shard_map/ppermute | solution.py:44
  54.2 3.3 %shard_map.172 = (f32[5,2,128,128]{3,2,1,0:T(8,128)S(1)}, f32[21,8,128]{2,1,0:T(8,128)S(1)}, f32[21,8,128]{2,1,0:T(8,128)S(1)}) custom-call(f32[4]{0:T(128)S(1)} %copy-done.9, f32[4]{0:T(128)S(1)} %copy-done.8, f32[4]{0:T(128)S(1)} %collective-permute-done.refs_6_.refs_2_, f32[4]{0:T(128)S(1)} %collective-permute-done.1.refs_7_.refs_3_, ...), custom_call_target="tpu_custom_call" | custom-call | flops 1000 | bytes 1000 | tf_op jit(solution)/shard_map/pallas_call | solution.py:896
  57.8 1.5 %collective-permute-start.23 = (f32[21,8,128]{2,1,0:T(8,128)S(1)}, f32[21,8,128]{2,1,0:T(8,128)S(1)}, u32[]{:S(2)}, u32[]{:S(2)}) collective-permute-start(f32[21,8,128]{2,1,0:T(8,128)S(1)} %get-tuple-element.81.refs_14_), channel_id=1, source_target_pairs={{0,2},{1,3},{2,0},{3,1},{4,6},{5,7},{6,4},{7,5},{8,10},{9,11},{10,... | collective-permute-start | bytes 258056 | tf_op jit(solution)/shard_map/ppermute | solution.py:44
  59.3 4.3 %collective-permute-done.23.refs_15_ = f32[21,8,128]{2,1,0:T(8,128)S(1)} collective-permute-done((f32[21,8,128]{2,1,0:T(8,128)S(1)}, f32[21,8,128]{2,1,0:T(8,128)S(1)}, u32[]{:S(2)}, u32[]{:S(2)}) %collective-permute-start.23) | collective-permute-done | bytes 86048 | tf_op jit(solution)/shard_map/ppermute | solution.py:44
  63.5 3.1 %shard_map.173 = (f32[5,2,128,128]{3,2,1,0:T(8,128)S(1)}, f32[21,8,128]{2,1,0:T(8,128)S(1)}, f32[21,8,128]{2,1,0:T(8,128)S(1)}) custom-call(f32[4]{0:T(128)S(1)} %copy-done.9, f32[4]{0:T(128)S(1)} %copy-done.8, f32[4]{0:T(128)S(1)} %collective-permute-done.refs_6_.refs_2_, f32[4]{0:T(128)S(1)} %collective-permute-done.1.refs_7_.refs_3_, ...), custom_call_target="tpu_custom_call" | custom-call | flops 1000 | bytes 1000 | tf_op jit(solution)/shard_map/pallas_call | solution.py:896
  66.7 2.7 %collective-permute-start.25 = (f32[21,8,128]{2,1,0:T(8,128)S(1)}, f32[21,8,128]{2,1,0:T(8,128)S(1)}, u32[]{:S(2)}, u32[]{:S(2)}) collective-permute-start(f32[21,8,128]{2,1,0:T(8,128)S(1)} %get-tuple-element.84.refs_12_), channel_id=1, source_target_pairs={{0,2},{1,3},{2,0},{3,1},{4,6},{5,7},{6,4},{7,5},{8,10},{9,11},{10,... | collective-permute-start | bytes 258056 | tf_op jit(solution)/shard_map/ppermute | solution.py:44
  69.5 3.4 %collective-permute-done.25.refs_13_ = f32[21,8,128]{2,1,0:T(8,128)S(1)} collective-permute-done((f32[21,8,128]{2,1,0:T(8,128)S(1)}, f32[21,8,128]{2,1,0:T(8,128)S(1)}, u32[]{:S(2)}, u32[]{:S(2)}) %collective-permute-start.25) | collective-permute-done | bytes 86048 | tf_op jit(solution)/shard_map/ppermute | solution.py:44
  72.9 3.0 %shard_map.174 = f32[4,8,4096]{2,1,0:T(8,128)} custom-call(f32[4]{0:T(128)S(1)} %copy-done.9, f32[4]{0:T(128)S(1)} %copy-done.8, f32[4]{0:T(128)S(1)} %collective-permute-done.refs_6_.refs_2_, f32[4]{0:T(128)S(1)} %collective-permute-done.1.refs_7_.refs_3_, bf16[256,256]{1,0:T(8,128)(2,1)S(1)} %copy-done.2, bf16[128,256]{1,0:T(8,128)(2,1)S(1)} %copy-done.5, ...), custom_call_target="tpu_custom_call" | custom-call | flops 1000 | bytes 1000 | tf_op jit(solution)/shard_map/pallas_call | solution.py:896
  (68 shorter events, 8.1 us)
Async XLA Ops:
  4.4 14.3 %collective-permute-start.7 = (f32[9,8,4096]{2,1,0:T(8,128)}, f32[9,8,4096]{2,1,0:T(8,128)S(1)}, u32[]{:S(2)}, u32[]{:S(2)}) collective-permute-start(f32[9,8,4096]{2,1,0:T(8,128)} %get-tuple-element.49.refs_0_), channel_id=1, source_target_pairs={{0,1},{1,0},{2,3},{3,2},{4,5},{5,4},{6,7},{7,6},{8,9},{9,8},{10,11... | collective-permute-start | bytes 3538952 | tf_op jit(solution)/shard_map/ppermute | solution.py:31
  4.9 3.2 %collective-permute-start.2 = (f32[6,4,4096]{2,1,0:T(4,128)}, f32[6,4,4096]{2,1,0:T(4,128)S(1)}, u32[]{:S(2)}, u32[]{:S(2)}) collective-permute-start(f32[6,4,4096]{2,1,0:T(4,128)} %get-tuple-element.44.refs_0_), channel_id=1, source_target_pairs={{0,1},{1,0},{2,3},{3,2},{4,5},{5,4},{6,7},{7,6},{8,9},{9,8},{10,11... | collective-permute-start | bytes 1179656 | tf_op jit(solution)/shard_map/ppermute | solution.py:31
  5.0 3.0 %collective-permute-start.1 = (f32[4]{0:T(128)S(1)}, f32[4]{0:T(128)S(1)}, u32[]{:S(2)}, u32[]{:S(2)}) collective-permute-start(f32[4]{0:T(128)S(1)} %copy-done.8), channel_id=1, source_target_pairs={{0,1},{1,0},{2,3},{3,2},{4,5},{5,4},{6,7},{7,6},{8,9},{9,8},{10,11... | collective-permute-start | bytes 56 | tf_op jit(solution)/shard_map/ppermute | solution.py:31
  5.4 2.5 %collective-permute-start = (f32[4]{0:T(128)S(1)}, f32[4]{0:T(128)S(1)}, u32[]{:S(2)}, u32[]{:S(2)}) collective-permute-start(f32[4]{0:T(128)S(1)} %copy-done.9), channel_id=1, source_target_pairs={{0,1},{1,0},{2,3},{3,2},{4,5},{5,4},{6,7},{7,6},{8,9},{9,8},{10,11... | collective-permute-start | bytes 56 | tf_op jit(solution)/shard_map/ppermute | solution.py:31
  11.2 14.1 %collective-permute-start.5 = (f32[18,8,128]{2,1,0:T(8,128)S(1)}, f32[18,8,128]{2,1,0:T(8,128)S(1)}, u32[]{:S(2)}, u32[]{:S(2)}) collective-permute-start(f32[18,8,128]{2,1,0:T(8,128)S(1)} %get-tuple-element.47.refs_15_), channel_id=1, source_target_pairs={{0,2},{1,13},{2,4},{3,15},{4,6},{5,17},{6,8},{7,19},{8,10},{9,21},... | collective-permute-start | bytes 221192 | tf_op jit(solution)/shard_map/ppermute | solution.py:63
  14.1 11.2 %collective-permute-start.6 = (f32[18,8,128]{2,1,0:T(8,128)S(1)}, f32[18,8,128]{2,1,0:T(8,128)S(1)}, u32[]{:S(2)}, u32[]{:S(2)}) collective-permute-start(f32[18,8,128]{2,1,0:T(8,128)S(1)} %get-tuple-element.48.refs_16_), channel_id=1, source_target_pairs={{0,30},{1,15},{2,0},{3,17},{4,2},{5,19},{6,4},{7,21},{8,6},{9,23},... | collective-permute-start | bytes 221192 | tf_op jit(solution)/shard_map/ppermute | solution.py:63
  18.2 6.7 %collective-permute-start.3 = (f32[9,8,128]{2,1,0:T(8,128)S(1)}, f32[9,8,128]{2,1,0:T(8,128)S(1)}, u32[]{:S(2)}, u32[]{:S(2)}) collective-permute-start(f32[9,8,128]{2,1,0:T(8,128)S(1)} %get-tuple-element.45), channel_id=1, source_target_pairs={{0,4},{1,9},{2,6},{3,11},{4,8},{5,13},{6,10},{7,15},{8,12},{9,17},... | collective-permute-start | bytes 110600 | tf_op jit(solution)/shard_map/ppermute | solution.py:63
  18.2 7.1 %collective-permute-start.4 = (f32[9,8,128]{2,1,0:T(8,128)S(1)}, f32[9,8,128]{2,1,0:T(8,128)S(1)}, u32[]{:S(2)}, u32[]{:S(2)}) collective-permute-start(f32[9,8,128]{2,1,0:T(8,128)S(1)} %get-tuple-element.46), channel_id=1, source_target_pairs={{0,6},{1,11},{2,8},{3,13},{4,10},{5,15},{6,12},{7,17},{8,14},{9,19... | collective-permute-start | bytes 110600 | tf_op jit(solution)/shard_map/ppermute | solution.py:63
  25.3 1.9 %collective-permute-start.10 = (f32[18,8,128]{2,1,0:T(8,128)S(1)}, f32[18,8,128]{2,1,0:T(8,128)S(1)}, u32[]{:S(2)}, u32[]{:S(2)}) collective-permute-start(f32[18,8,128]{2,1,0:T(8,128)S(1)} %collective-permute-done.5.refs_23_), channel_id=1, source_target_pairs={{0,1},{1,0},{2,3},{3,2},{4,5},{5,4},{6,7},{7,6},{8,9},{9,8},{10,11... | collective-permute-start | bytes 221192 | tf_op jit(solution)/shard_map/ppermute | solution.py:31
  25.3 1.9 %collective-permute-start.11 = (f32[18,8,128]{2,1,0:T(8,128)S(1)}, f32[18,8,128]{2,1,0:T(8,128)S(1)}, u32[]{:S(2)}, u32[]{:S(2)}) collective-permute-start(f32[18,8,128]{2,1,0:T(8,128)S(1)} %collective-permute-done.6.refs_24_), channel_id=1, source_target_pairs={{0,1},{1,0},{2,3},{3,2},{4,5},{5,4},{6,7},{7,6},{8,9},{9,8},{10,11... | collective-permute-start | bytes 221192 | tf_op jit(solution)/shard_map/ppermute | solution.py:31
  25.9 1.3 %collective-permute-start.9 = (f32[9,8,128]{2,1,0:T(8,128)S(1)}, f32[9,8,128]{2,1,0:T(8,128)S(1)}, u32[]{:S(2)}, u32[]{:S(2)}) collective-permute-start(f32[9,8,128]{2,1,0:T(8,128)S(1)} %collective-permute-done.4.refs_22_), channel_id=1, source_target_pairs={{0,1},{1,0},{2,3},{3,2},{4,5},{5,4},{6,7},{7,6},{8,9},{9,8},{10,11... | collective-permute-start | bytes 110600 | tf_op jit(solution)/shard_map/ppermute | solution.py:31
  30.2 11.3 %collective-permute-start.15 = (f32[35,8,128]{2,1,0:T(8,128)S(1)}, f32[35,8,128]{2,1,0:T(8,128)S(1)}, u32[]{:S(2)}, u32[]{:S(2)}) collective-permute-start(f32[35,8,128]{2,1,0:T(8,128)S(1)} %get-tuple-element.70.refs_14_), channel_id=1, source_target_pairs={{0,2},{1,3},{2,0},{3,1},{4,6},{5,7},{6,4},{7,5},{8,10},{9,11},{10,... | collective-permute-start | bytes 430088 | tf_op jit(solution)/shard_map/ppermute | solution.py:44
  31.6 10.3 %collective-permute-start.16 = (f32[35,8,128]{2,1,0:T(8,128)S(1)}, f32[35,8,128]{2,1,0:T(8,128)S(1)}, u32[]{:S(2)}, u32[]{:S(2)}) collective-permute-start(f32[35,8,128]{2,1,0:T(8,128)S(1)} %get-tuple-element.71.refs_15_), channel_id=1, source_target_pairs={{0,30},{1,31},{2,4},{3,5},{4,2},{5,3},{6,8},{7,9},{8,6},{9,7},{10,... | collective-permute-start | bytes 430088 | tf_op jit(solution)/shard_map/ppermute | solution.py:44
  34.5 7.0 %collective-permute-start.12 = (f32[9,8,128]{2,1,0:T(8,128)S(1)}, f32[9,8,128]{2,1,0:T(8,128)S(1)}, u32[]{:S(2)}, u32[]{:S(2)}) collective-permute-start(f32[9,8,128]{2,1,0:T(8,128)S(1)} %get-tuple-element.63), channel_id=1, source_target_pairs={{0,4},{1,11},{2,6},{3,13},{4,8},{5,15},{6,10},{7,17},{8,12},{9,19}... | collective-permute-start | bytes 110600 | tf_op jit(solution)/shard_map/ppermute | solution.py:63
  34.5 7.0 %collective-permute-start.13 = (f32[9,8,128]{2,1,0:T(8,128)S(1)}, f32[9,8,128]{2,1,0:T(8,128)S(1)}, u32[]{:S(2)}, u32[]{:S(2)}) collective-permute-start(f32[9,8,128]{2,1,0:T(8,128)S(1)} %get-tuple-element.64), channel_id=1, source_target_pairs={{0,6},{1,13},{2,8},{3,15},{4,10},{5,17},{6,12},{7,19},{8,14},{9,21... | collective-permute-start | bytes 110600 | tf_op jit(solution)/shard_map/ppermute | solution.py:63
  35.5 6.0 %collective-permute-start.14 = (f32[9,8,128]{2,1,0:T(8,128)S(1)}, f32[9,8,128]{2,1,0:T(8,128)S(1)}, u32[]{:S(2)}, u32[]{:S(2)}) collective-permute-start(f32[9,8,128]{2,1,0:T(8,128)S(1)} %get-tuple-element.65), channel_id=1, source_target_pairs={{0,8},{1,15},{2,10},{3,17},{4,12},{5,19},{6,14},{7,21},{8,16},{9,2... | collective-permute-start | bytes 110600 | tf_op jit(solution)/shard_map/ppermute | solution.py:63
  46.2 5.2 %collective-permute-start.17 = (f32[21,8,128]{2,1,0:T(8,128)S(1)}, f32[21,8,128]{2,1,0:T(8,128)S(1)}, u32[]{:S(2)}, u32[]{:S(2)}) collective-permute-start(f32[21,8,128]{2,1,0:T(8,128)S(1)} %get-tuple-element.73.refs_12_), channel_id=1, source_target_pairs={{0,1},{1,0},{2,4},{3,5},{4,2},{5,3},{6,8},{7,9},{8,6},{9,7},{10,12... | collective-permute-start | bytes 258056 | tf_op jit(solution)/shard_map/ppermute | solution.py:44
  47.8 6.4 %collective-permute-start.18 = (f32[21,8,128]{2,1,0:T(8,128)S(1)}, f32[21,8,128]{2,1,0:T(8,128)S(1)}, u32[]{:S(2)}, u32[]{:S(2)}) collective-permute-start(f32[21,8,128]{2,1,0:T(8,128)S(1)} %get-tuple-element.74.refs_14_), channel_id=1, source_target_pairs={{0,2},{1,3},{2,0},{3,1},{4,6},{5,7},{6,4},{7,5},{8,10},{9,11},{10,... | collective-permute-start | bytes 258056 | tf_op jit(solution)/shard_map/ppermute | solution.py:44
  49.3 1.6 %collective-permute-start.19 = (f32[9,8,128]{2,1,0:T(8,128)S(1)}, f32[9,8,128]{2,1,0:T(8,128)S(1)}, u32[]{:S(2)}, u32[]{:S(2)}) collective-permute-start(f32[9,8,128]{2,1,0:T(8,128)S(1)} %collective-permute-done.12.refs_16_), channel_id=1, source_target_pairs={{0,1},{1,0},{2,3},{3,2},{4,5},{5,4},{6,7},{7,6},{8,9},{9,8},{10,11... | collective-permute-start | bytes 110600 | tf_op jit(solution)/shard_map/ppermute | solution.py:31
  50.1 1.4 %collective-permute-start.21 = (f32[9,8,128]{2,1,0:T(8,128)S(1)}, f32[9,8,128]{2,1,0:T(8,128)S(1)}, u32[]{:S(2)}, u32[]{:S(2)}) collective-permute-start(f32[9,8,128]{2,1,0:T(8,128)S(1)} %collective-permute-done.14.refs_18_), channel_id=1, source_target_pairs={{0,1},{1,0},{2,3},{3,2},{4,5},{5,4},{6,7},{7,6},{8,9},{9,8},{10,11... | collective-permute-start | bytes 110600 | tf_op jit(solution)/shard_map/ppermute | solution.py:31
  57.6 1.7 %collective-permute-start.22 = (f32[21,8,128]{2,1,0:T(8,128)S(1)}, f32[21,8,128]{2,1,0:T(8,128)S(1)}, u32[]{:S(2)}, u32[]{:S(2)}) collective-permute-start(f32[21,8,128]{2,1,0:T(8,128)S(1)} %get-tuple-element.80.refs_12_), channel_id=1, source_target_pairs={{0,1},{1,0},{2,4},{3,5},{4,2},{5,3},{6,8},{7,9},{8,6},{9,7},{10,12... | collective-permute-start | bytes 258056 | tf_op jit(solution)/shard_map/ppermute | solution.py:44
  57.8 5.7 %collective-permute-start.23 = (f32[21,8,128]{2,1,0:T(8,128)S(1)}, f32[21,8,128]{2,1,0:T(8,128)S(1)}, u32[]{:S(2)}, u32[]{:S(2)}) collective-permute-start(f32[21,8,128]{2,1,0:T(8,128)S(1)} %get-tuple-element.81.refs_14_), channel_id=1, source_target_pairs={{0,2},{1,3},{2,0},{3,1},{4,6},{5,7},{6,4},{7,5},{8,10},{9,11},{10,... | collective-permute-start | bytes 258056 | tf_op jit(solution)/shard_map/ppermute | solution.py:44
  66.7 2.8 %collective-permute-start.24 = (f32[21,8,128]{2,1,0:T(8,128)S(1)}, f32[21,8,128]{2,1,0:T(8,128)S(1)}, u32[]{:S(2)}, u32[]{:S(2)}) collective-permute-start(f32[21,8,128]{2,1,0:T(8,128)S(1)} %get-tuple-element.83.refs_10_), channel_id=1, source_target_pairs={{0,1},{1,0},{2,4},{3,5},{4,2},{5,3},{6,8},{7,9},{8,6},{9,7},{10,12... | collective-permute-start | bytes 258056 | tf_op jit(solution)/shard_map/ppermute | solution.py:44
  66.7 6.1 %collective-permute-start.25 = (f32[21,8,128]{2,1,0:T(8,128)S(1)}, f32[21,8,128]{2,1,0:T(8,128)S(1)}, u32[]{:S(2)}, u32[]{:S(2)}) collective-permute-start(f32[21,8,128]{2,1,0:T(8,128)S(1)} %get-tuple-element.84.refs_12_), channel_id=1, source_target_pairs={{0,2},{1,3},{2,0},{3,1},{4,6},{5,7},{6,4},{7,5},{8,10},{9,11},{10,... | collective-permute-start | bytes 258056 | tf_op jit(solution)/shard_map/ppermute | solution.py:44
  (17 other events, 127.7 us)

commit v4 on v3

--- a/solution.py
+++ b/solution.py
@@ -1,4 +1,5 @@
 import functools
+from types import SimpleNamespace
 import jax
 import numpy as np
 import jax.numpy as jnp
@@ -72,13 +73,10 @@
     line = np.arange(B)
     side[line, (B - 1) * B + line] = 1
     side[LANES - B + line, line] = 1
-    place = np.zeros((2 * LANES, G * PLANE), np.float32)
     pack = np.zeros((G, PLANE, 2 * LANES), np.float32)
     far = np.zeros((2 * LANES, LANES), np.float32)
     for g in range(G):
         at = g * PACK + line
-        place[at, g * PLANE + line * B] = 1
-        place[LANES + at, g * PLANE + line * B + B - 1] = 1
         for depth in range(2):
             pack[g, line * B + B - 1 - depth, at + depth * B] = 1
             pack[g, line * B + depth, LANES + at + depth * B] = 1
@@ -87,7 +85,8 @@
         far[at + B, at] = 1
         far[LANES + at[B - 1], at[0]] = 1
         far[LANES + at[0], at[B - 1]] = 1
-    return dict(
+    place = np.concatenate([pack[g].T for g in range(G)], axis=1)
+    return SimpleNamespace(
         plane=jnp.asarray(plane, BF16),
         side=jnp.asarray(side, BF16),
         place=jnp.asarray(place, BF16),
@@ -233,21 +232,44 @@
     return product(pairs)
 
 
+def outer_lanes():
+    return lane_ids() // B % 2 == 0
+
+
+def place_ends(ends, placed, used, mats):
+    every = pl.ds(0, used)
+    for g in range(G):
+        table = mats.place[:, pl.ds(g * PLANE, PLANE)]
+        placed[every, pl.ds(g * PLANE, PLANE)] = product(
+            [
+                (ends[every, pl.ds(0, 2 * LANES)], table),
+                (ends[every, pl.ds(2 * LANES, 2 * LANES)], table),
+            ]
+        )
+
+
+def placed_tile(placed, s, i, jh):
+    return placed[rows_of(s * HG + i % HG), pl.ds(i // HG * PLANE + jh * LANES, LANES)]
+
+
 def laplace(source, slabs, near, up, down, below, above, mats, work, emit):
-    planes, sums, ends, placed = work["planes"], work["sums"], work["ends"], work["placed"]
+    planes, sums, ends, placed = work.planes, work.sums, work.ends, work.placed
     used = slabs * HG * 8
+    outer = outer_lanes()
     for s in range(slabs):
         for h in range(0, HG, 2):
             for side in range(2):
                 pieces = []
                 for n in (h, h + 1):
                     if side == 0:
+                        value = near(s).read((5, 0), s, lambda q, n=n: down(q, n))
+                        if above is not None:
+                            value = value + near(s).read((5, 1), s, lambda q, n=n: above(q, n))
+                    else:
                         value = near(s).read((4, 0), s, lambda q, n=n: up(q, n))
-                        value = value + near(s).read((4, -1), s, lambda q, n=n: below(q, n))
-                    else:
-                        value = near(s).read((5, 0), s, lambda q, n=n: down(q, n))
-                        value = value + near(s).read((5, 1), s, lambda q, n=n: above(q, n))
-                    pieces.append(value)
+                        if below is not None:
+                            value = value + near(s).read((4, -1), s, lambda q, n=n: below(q, n))
+                    pieces.append(jnp.where(outer, value, 0.0))
                 put_split(
                     ends,
                     rows_of(s * HG + h, 2),
@@ -257,7 +279,7 @@
                     half(2 + side),
                 )
     every = pl.ds(0, used)
-    plane, side = mats["plane"][...], mats["side"][...]
+    plane, side = mats.plane[...], mats.side[...]
     for g in range(G):
         sums[g, every, :] = product(
             [
@@ -267,14 +289,7 @@
                 (planes[g, every, pl.ds(2 * PLANE + LANES, LANES)], side),
             ]
         )
-    for g in range(G):
-        table = mats["place"][:, pl.ds(g * PLANE, PLANE)]
-        placed[every, pl.ds(g * PLANE, PLANE)] = product(
-            [
-                (ends[every, pl.ds(0, 2 * LANES)], table),
-                (ends[every, pl.ds(2 * LANES, 2 * LANES)], table),
-            ]
-        )
+    place_ends(ends, placed, used, mats)
     for s in range(slabs):
         for i in range(B):
             g, h = i // HG, i % HG
@@ -299,7 +314,7 @@
 
 
 def laplace_far(slabs, sides, mats, work, emit):
-    lhs, out = work["far_lhs"], work["far_out"]
+    lhs, out = work.far_lhs, work.far_out
     group = lane_ids() // PACK
     for n, (links, tile, _, _) in enumerate(sides):
         for s in range(slabs):
@@ -316,7 +331,7 @@
                 put_split(lhs, at, (), c, half(0), half(2))
                 put_split(lhs, at, (), edge, half(1), half(3))
     every = pl.ds(0, 2 * slabs * HG * 8)
-    table = mats["far"][...]
+    table = mats.far[...]
     out[every, :] = product(
         [
             (lhs[every, pl.ds(0, 2 * LANES)], table),
@@ -337,16 +352,18 @@
                 else:
                     wrap = links(s).read((1, 0), s, lambda q: tile(q, 0))
                     after = roll(jnp.where(group == 0, wrap, tile(s, 0)), -PACK)
-                inner = links(s).read(own_name, s, lambda q: own(q, h))
-                lap = (before + after) + inner + out[rows_of((n * slabs + s) * HG + h), :] - 6.0 * c
+                lap = (before + after) + out[rows_of((n * slabs + s) * HG + h), :] - 6.0 * c
+                if own is not None:
+                    lap = lap + links(s).read(own_name, s, lambda q: own(q, h))
                 emit(n, s, h, lap)
 
 
 def diffuse(source, slabs, near, from_below, from_above, rate, up, down, below, above, mats, work, finish):
-    first, packed = work["first"], work["packed"]
-    far_first = work["far_first"]
-    build_planes(source, slabs, work["planes"])
-    build_sides(source, slabs, near, work["planes"])
+    first, packed = work.first, work.packed
+    alone = below is None
+    far_first = None if alone else work.far_first
+    build_planes(source, slabs, work.planes)
+    build_sides(source, slabs, near, work.planes)
 
     def keep_first(s, i, jh, c, lap):
         first[s, jh, rows_of(i), :] = rate(s) * lap
@@ -356,16 +373,17 @@
     def keep_far(n, s, h, lap):
         far_first[n, s * HG + h] = rate(s) * lap
 
-    laplace_far(
-        slabs,
-        ((from_below, below, down, (5, 1)), (from_above, above, up, (4, -1))),
-        mats,
-        work,
-        keep_far,
-    )
-    build_planes(first, slabs, work["planes"])
-    build_sides(first, slabs, near, work["planes"])
-    packed[pl.ds(0, slabs * HG * 8), :] = pack_faces(work["planes"], mats["pack"], slabs * HG * 8)
+    if not alone:
+        laplace_far(
+            slabs,
+            ((from_below, below, down, (5, 1)), (from_above, above, up, (4, -1))),
+            mats,
+            work,
+            keep_far,
+        )
+    build_planes(first, slabs, work.planes)
+    build_sides(first, slabs, near, work.planes)
+    packed[pl.ds(0, slabs * HG * 8), :] = pack_faces(work.planes, mats.pack, slabs * HG * 8)
 
     def last(s, i, jh, c, lap):
         finish(s, i, jh, source[s, jh, rows_of(i), :] + c + 0.5 * rate(s) * lap)
@@ -376,12 +394,16 @@
         near,
         lambda s, h: packed[rows_of(s * HG + h), half(0)],
         lambda s, h: packed[rows_of(s * HG + h), half(1)],
-        lambda s, h: far_first[0, s * HG + h],
-        lambda s, h: far_first[1, s * HG + h],
+        None if alone else lambda s, h: far_first[0, s * HG + h],
+        None if alone else lambda s, h: far_first[1, s * HG + h],
         mats,
         work,
         last,
     )
+
+
+def numbered(word, n):
+    return word + str(n)
 
 
 def pick(core, a, b):
@@ -456,7 +478,7 @@
     return passed - 1.0, weight
 
 
-def chem_kernel(pay, pay_o, fine_counts, gain, weight):
+def chem_kernel(pay, pay_o, fine_counts, pack, gain, weight, edges, planes):
     core = lax.axis_index("fld")
     steps = gain.shape[0]
     rows = row_ids()
@@ -474,6 +496,19 @@
         return carry
 
     lax.fori_loop(0, TILES, body, 0)
+    for n, table in enumerate((gain, weight)):
+        for s in range(steps - 1):
+            for i in range(0, B, 2):
+                for jh in range(2):
+                    put_split(
+                        planes,
+                        rows_of((n * (steps - 1) + s) * HG + i % HG, 2),
+                        (i // HG,),
+                        jnp.concatenate([table[s, :, cols(i, jh)], table[s, :, cols(i + 1, jh)]], axis=0),
+                        half(jh),
+                        half(2 + jh),
+                    )
+    edges[...] = pack_faces(planes, pack, edges.shape[0])
 
 
 def chem_coarse(payc, payc_o, coarse_counts, gain, weight):
@@ -546,13 +581,25 @@
                     state[at] = state[at] * kept
 
 
+def fill_pack(table):
+    cell = lax.broadcasted_iota(jnp.int32, (PLANE, 2 * LANES), 0)
+    place = lax.broadcasted_iota(jnp.int32, (PLANE, 2 * LANES), 1)
+    depth = place // B % 2
+    layer = jnp.where(place < LANES, B - 1 - depth, depth)
+    match = jnp.where(cell == place % B * B + layer, 1.0, 0.0)
+    group = place % LANES // PACK
+    for g in range(G):
+        table[g] = jnp.where(group == g, match, 0.0).astype(BF16)
+
+
 def start_kernel(
     sends, count_f, fields, payc, payc_o, children, coarse_counts, dif, shr, dif_o, shr_o,
-    fine_nbr, coarse_nbr, table, coarse, gain_c, weight_c, local, *rest
+    fine_nbr, coarse_nbr, coarse, gain_c, weight_c, local, *rest
 ):
     core = lax.axis_index("fld")
     count_c = children.shape[0]
-    outs, (planes, packed, stage) = rest[:-3], rest[-3:]
+    outs, (planes, packed, table, stage) = rest[:-4], rest[-4:]
+    fill_pack(table)
     up, down = outs[-2:]
     for p in range(count_c):
         for v in range(fields):
@@ -680,7 +727,7 @@
 
 def links_maker(plan, faces, shift, fine_slabs):
     me = lax.axis_index("blk") + shift
-    count_f, count_c = plan["count_f"], plan["count_c"]
+    count_f, count_c = plan.count_f, plan.count_c
 
     def column(slab, face):
         return faces[:, face : face + 1].astype(jnp.int32)
@@ -694,27 +741,27 @@
 
 
 def strips_out(plan, r, out, faces, up_octant):
-    going = plan["slabs_out"]
+    going = plan.slabs_out
     even = lax.axis_index("blk") % 2 == 0
-    build_planes(out, going, r["planes"])
-    r["packed"][pl.ds(0, going * HG * 8), :] = pack_faces(
-        r["planes"], r["pack"], going * HG * 8
+    build_planes(out, going, r.planes)
+    r.packed[pl.ds(0, going * HG * 8), :] = pack_faces(
+        r.planes, r.pack, going * HG * 8
     )
 
     def send(up, down):
         for n in range(going * HG):
-            up[n] = r["packed"][rows_of(n), half(0)]
-            down[n] = r["packed"][rows_of(n), half(1)]
+            up[n] = r.packed[rows_of(n), half(0)]
+            down[n] = r.packed[rows_of(n), half(1)]
         at = going * HG
         up[at] = faces
         down[at] = faces
         if up_octant is not None:
             up_octant(up, at + 1)
-            for n in range(plan["fields"] + 2):
+            for n in range(plan.fields + 2):
                 down[at + 1 + n] = zero_tile()
 
-    pl.when(even)(lambda: send(r["send_e"], r["send_o"]))
-    pl.when(jnp.logical_not(even))(lambda: send(r["send_o"], r["send_e"]))
+    pl.when(even)(lambda: send(r.send_e, r.send_o))
+    pl.when(jnp.logical_not(even))(lambda: send(r.send_o, r.send_e))
 
 
 def zero_tile():
@@ -722,23 +769,23 @@
 
 
 def open_kernel(plan, names, *refs):
-    r = dict(zip(names, refs))
+    r = SimpleNamespace(**dict(zip(names, refs)))
     core = lax.axis_index("fld")
-    fields = plan["fields"]
+    fields = plan.fields
     slots = fields + 1
-    count_f, count_c = plan["count_f"], plan["count_c"]
-    par, par_o = (r["dif"], r["shr"]), (r["dif_o"], r["shr_o"])
-    out = r["state_out"]
+    count_f, count_c = plan.count_f, plan.count_c
+    par, par_o = (r.dif, r.shr), (r.dif_o, r.shr_o)
+    out = r.state_out
     base = 2 * fields + 1
     strip = count_c * HG
 
     def far(ref, ref_o, n):
         return pick(core, ref[base + n], ref_o[base + n])
 
-    last = len(plan["sends"]) - 1
-    below = [far(r[f"landed{last - 1}"], r[f"shared{last - 1}"], n) for n in range(strip + 1)]
-    above = [far(r[f"landed{last}"], r[f"shared{last}"], n) for n in range(strip + 1)]
-    own_up, own_down = r["own_up"], r["own_down"]
+    last = len(plan.sends) - 1
+    below = [far(getattr(r, numbered("landed", last - 1)), getattr(r, numbered("shared", last - 1)), n) for n in range(strip + 1)]
+    above = [far(getattr(r, numbered("landed", last)), getattr(r, numbered("shared", last)), n) for n in range(strip + 1)]
+    own_up, own_down = r.own_up, r.own_down
     faces = own_up[base + strip]
     rates = 0.5 * spread_vector(core, par, par_o, 0, fields)
 
@@ -746,7 +793,7 @@
         out[slots + p, jh, rows_of(i), :] = value
 
     diffuse(
-        r["coarse"],
+        r.coarse,
         count_c,
         links_maker(plan, faces, 0, 0),
         links_maker(plan, below[strip], -1, 0),
@@ -760,33 +807,33 @@
         r,
         finish,
     )
-    find = octant_finder(r["children"], count_f)
-    for n, distances in enumerate(plan["later"]):
+    find = octant_finder(r.children, count_f)
+    for n, distances in enumerate(plan.later):
         write_octant(
-            out, slots, find(pick(core, *distances)), list(range(2 * fields)), r[f"octant{n}"], 0
+            out, slots, find(pick(core, *distances)), list(range(2 * fields)), getattr(r, numbered("octant", n)), 0
         )
     mine = slot_fields(core, fields)
-    write_octant(out, slots, find(0), mine, r["local_out"], 0)
-    near_octant = r["near_octant"]
+    write_octant(out, slots, find(0), mine, r.local_out, 0)
+    near_octant = r.near_octant
     write_octant(out, slots, find(1), mine, near_octant, 0)
-    keep_coarse(out, slots, r["children"])
+    keep_coarse(out, slots, r.children)
     react_coarse(
-        out, slots, count_c, spread_vector(core, par, par_o, 1, fields), r["gain_c"], r["weight_c"], 0
+        out, slots, count_c, spread_vector(core, par, par_o, 1, fields), r.gain_c, r.weight_c, 0
     )
     for i in range(B):
         for jh in range(2):
             at = cols(i, jh)
             for s in range(fields):
-                out[s, jh, rows_of(i), :] = r["seed_f"][s, :, at]
-            out[fields, jh, rows_of(i), :] = pick(core, r["seed"][0, :, at], r["seed_other"][0, :, at])
-    entries = [own_slots(fields, r["local"])]
+                out[s, jh, rows_of(i), :] = r.seed_f[s, :, at]
+            out[fields, jh, rows_of(i), :] = pick(core, r.seed[0, :, at], r.seed_other[0, :, at])
+    entries = [own_slots(fields, r.local)]
     for n in range(last):
-        entries.append(all_fields(core, fields, r[f"landed{n}"]))
-        entries.append(all_fields(core, fields, r[f"shared{n}"]))
-    one, two = (all_fields(core, fields, r[f"{word}{last}"]) for word in ("landed", "shared"))
+        entries.append(all_fields(core, fields, getattr(r, numbered("landed", n))))
+        entries.append(all_fields(core, fields, getattr(r, numbered("shared", n))))
+    one, two = (all_fields(core, fields, getattr(r, numbered(word, last))) for word in ("landed", "shared"))
     entries.append(lambda s: pick(core, two(s), one(s)))
-    add_octants(entries, out, r["stage"], fields)
-    react_fine(out, fields, par, par_o, r["gain"].at[plan["step"]], r["weight"].at[plan["step"]])
+    add_octants(entries, out, r.stage, fields)
+    react_fine(out, fields, par, par_o, r.gain.at[plan.step], r.weight.at[plan.step])
 
     def up_octant(up, at):
         for n in range(slots + 1):
@@ -795,88 +842,218 @@
     strips_out(plan, r, out, faces, up_octant)
 
 
-def step_kernel(plan, names, *refs):
-    r = dict(zip(names, refs))
+def rates_of(plan, r):
     core = lax.axis_index("fld")
+    par, par_o = (r.dif, r.shr), (r.dif_o, r.shr_o)
+    fields = plan.fields
+    rates = [par[0][s] for s in range(fields)] + [pick(core, par[0][0], par_o[0][0])]
+    return rates + [0.5 * spread_vector(core, par, par_o, 0, fields)] * plan.count_c
+
+
+def by_parity(action, r):
     even = lax.axis_index("blk") % 2 == 0
-    fields = plan["fields"]
+    pl.when(even)(lambda: action(r.sent_e, r.sent_o, r.got_o, r.got_e))
+    pl.when(jnp.logical_not(even))(lambda: action(r.sent_o, r.sent_e, r.got_e, r.got_o))
+
+
+def bulk_kernel(plan, names, *refs):
+    r = SimpleNamespace(**dict(zip(names, refs)))
+    core = lax.axis_index("fld")
+    fields = plan.fields
     slots = fields + 1
-    count_c = plan["count_c"]
-    par, par_o = (r["dif"], r["shr"]), (r["dif_o"], r["shr_o"])
-    slabs, arrived = plan["slabs"], plan["slabs_in"]
-    own_up, own_down, far_b, far_a = (r[x] for x in ("own_up", "own_down", "far_b", "far_a"))
-    used = arrived * HG + 1
+    count_c = plan.count_c
+    par, par_o = (r.dif, r.shr), (r.dif_o, r.shr_o)
+    slabs, arrived = plan.slabs, plan.slabs_in
+    own_up, own_down = r.own_up, r.own_down
 
     def sort_strips(up, down, below, above):
-        for n in range(used):
+        for n in range(arrived * HG + 1):
+            own_up[n] = up[n]
+            own_down[n] = down[n]
+
+    even = lax.axis_index("blk") % 2 == 0
+    pl.when(even)(lambda: sort_strips(r.sent_e, r.sent_o, None, None))
+    pl.when(jnp.logical_not(even))(lambda: sort_strips(r.sent_o, r.sent_e, None, None))
+    faces = own_up[arrived * HG]
+    source, out = r.state, r.state_out
+    if plan.late:
+        late = plan.late * HG * 8
+        high, low = split(r.late[pl.ds(0, late), :])
+        r.ends[pl.ds(0, late), pl.ds(0, 2 * LANES)] = high
+        r.ends[pl.ds(0, late), pl.ds(2 * LANES, 2 * LANES)] = low
+        place_ends(r.ends, r.placed, late, r)
+        source = r.whole
+        for i in range(B):
+            for jh in range(2):
+                for s in range(slabs):
+                    source[s, jh, rows_of(i), :] = r.state[s, jh, rows_of(i), :] + placed_tile(
+                        r.placed, s, i, jh
+                    )
+                for p in range(plan.late - slots):
+                    r.coarse_stage[p, :, cols(i, jh)] = r.coarse[p, jh, rows_of(i), :] + placed_tile(
+                        r.placed, slots + p, i, jh
+                    )
+        for p in range(plan.late - slots):
+            for v in range(fields):
+                r.coarse_final[v, pl.ds(p, 1), :] = pick(
+                    core,
+                    r.coarse_stage[p, pl.ds(v, 1), :],
+                    r.coarse_stage[p, pl.ds(fields + v, 1), :],
+                )
+
+    def finish(s, i, jh, value):
+        if s >= slots:
+            r.coarse_out[s - slots, jh, rows_of(i), :] = value
+        else:
+            out[s, jh, rows_of(i), :] = value
+
+    rates = rates_of(plan, r)
+    diffuse(
+        source,
+        slabs,
+        links_maker(plan, faces, 0, slots),
+        None,
+        None,
+        lambda s: rates[s],
+        lambda s, h: own_up[s * HG + h],
+        lambda s, h: own_down[s * HG + h],
+        None,
+        None,
+        r,
+        r,
+        finish,
+    )
+    if plan.add:
+        near = r.near_octant
+
+        def take(ref):
+            for n in range(slots + 1):
+                near[n] = ref[plan.near_at + n]
+
+        pl.when(even)(lambda: take(r.near_o))
+        pl.when(jnp.logical_not(even))(lambda: take(r.near_e))
+        entries = [own_slots(fields, r.local), own_slots(fields, near)]
+        for n in range(len(plan.later)):
+            entries.append(all_fields(core, fields, getattr(r, numbered("landed", n))))
+            entries.append(all_fields(core, fields, getattr(r, numbered("shared", n))))
+        add_octants(entries, out, r.stage, fields)
+    if not plan.final:
+        step = plan.step
+        react_fine(out, fields, par, par_o, r.gain.at[step], r.weight.at[step])
+        build_planes(out, slots, r.planes)
+        r.faces_out[...] = pack_faces(r.planes, r.pack, slots * HG * 8)
+
+
+def edge_kernel(plan, names, *refs):
+    r = SimpleNamespace(**dict(zip(names, refs)))
+    core = lax.axis_index("fld")
+    fields = plan.fields
+    slots = fields + 1
+    par, par_o = (r.dif, r.shr), (r.dif_o, r.shr_o)
+    slabs, arrived = plan.slabs, plan.slabs_in
+    own_up, own_down, far_b, far_a = r.own_up, r.own_down, r.far_b, r.far_a
+
+    def sort_strips(up, down, below, above):
+        for n in range(arrived * HG + 1):
             own_up[n] = up[n]
             own_down[n] = down[n]
             far_b[n] = below[n]
             far_a[n] = above[n]
 
-    pl.when(even)(lambda: sort_strips(r["sent_e"], r["sent_o"], r["got_o"], r["got_e"]))
-    pl.when(jnp.logical_not(even))(
-        lambda: sort_strips(r["sent_o"], r["sent_e"], r["got_e"], r["got_o"])
-    )
+    by_parity(sort_strips, r)
     faces = own_up[arrived * HG]
-    rate_of = [par[0][s] for s in range(fields)] + [pick(core, par[0][0], par_o[0][0])]
-    if slabs > slots:
-        rate_of += [0.5 * spread_vector(core, par, par_o, 0, fields)] * count_c
-    source, out = r["state"], r["state_out"]
-
-    def finish(s, i, jh, value):
-        if s >= slots:
-            r["coarse_stage"][s - slots, :, cols(i, jh)] = value
-        elif plan["final"]:
-            out[s, :, cols(i, jh)] = value
-        else:
-            out[s, jh, rows_of(i), :] = value
-
-    diffuse(
-        source,
+    rates = rates_of(plan, r)
+    near = links_maker(plan, faces, 0, slots)
+    from_below = links_maker(plan, far_b[arrived * HG], -1, slots)
+    from_above = links_maker(plan, far_a[arrived * HG], 1, slots)
+    outer = outer_lanes()
+    delta, far_first, lateral, late = r.delta, r.far_first, r.lateral, r.late
+
+    def at_tile(ref):
+        return lambda s, h: ref[s * HG + h]
+
+    for s in range(slabs):
+        for h in range(HG):
+            for n, (name, ref) in enumerate((((5, 1), far_a), ((4, -1), far_b))):
+                ghost = near(s).read(name, s, lambda q, ref=ref: ref[q * HG + h])
+                delta[n, s * HG + h] = jnp.where(outer, rates[s] * ghost, 0.0)
+
+    def keep_far(n, s, h, lap):
+        far_first[n, s * HG + h] = rates[s] * lap
+
+    def keep_lateral(n, s, h, lap):
+        lateral[n, s * HG + h] = lap
+
+    laplace_far(
         slabs,
-        links_maker(plan, faces, 0, slots),
-        links_maker(plan, far_b[arrived * HG], -1, slots),
-        links_maker(plan, far_a[arrived * HG], 1, slots),
-        lambda s: rate_of[s],
-        lambda s, h: own_up[s * HG + h],
-        lambda s, h: own_down[s * HG + h],
-        lambda s, h: far_b[s * HG + h],
-        lambda s, h: far_a[s * HG + h],
+        (
+            (from_below, at_tile(far_b), at_tile(own_down), (5, 1)),
+            (from_above, at_tile(far_a), at_tile(own_up), (4, -1)),
+        ),
         r,
         r,
-        finish,
-    )
-    if slabs > slots:
-        final, stage = r["coarse_final"], r["coarse_stage"]
-        for p in range(count_c):
-            for v in range(fields):
-                final[v, pl.ds(p, 1), :] = pick(
-                    core, stage[p, pl.ds(v, 1), :], stage[p, pl.ds(fields + v, 1), :]
-                )
-    if plan["add"]:
-        near = r["near_octant"]
-
-        def take(ref):
-            for n in range(slots + 1):
-                near[n] = ref[plan["near_at"] + n]
-
-        pl.when(even)(lambda: take(r["near_o"]))
-        pl.when(jnp.logical_not(even))(lambda: take(r["near_e"]))
-        entries = [own_slots(fields, r["local"]), own_slots(fields, near)]
-        for n in range(len(plan["later"])):
-            entries.append(all_fields(core, fields, r[f"landed{n}"]))
-            entries.append(all_fields(core, fields, r[f"shared{n}"]))
-        add_octants(entries, out, r["stage"], fields)
-    if not plan["final"]:
-        step = plan["step"]
-        react_fine(out, fields, par, par_o, r["gain"].at[step], r["weight"].at[step])
-        strips_out(plan, r, out, faces, None)
+        keep_far,
+    )
+    laplace_far(
+        slabs,
+        ((near, at_tile(delta.at[0]), None, None), (near, at_tile(delta.at[1]), None, None)),
+        r,
+        SimpleNamespace(far_lhs=r.far_lhs2, far_out=r.far_out2),
+        keep_lateral,
+    )
+    share = [par[1][s] for s in range(fields)] + [pick(core, par[1][0], par_o[1][0])]
+    extra = jnp.where(core == 0, 1.0, 0.0)
+    for n, (name, other) in enumerate((((5, 1), 1), ((4, -1), 0))):
+        for h in range(HG):
+            added = []
+            for s in range(slabs):
+                at = s * HG + h
+                ghost = near(s).read(name, s, lambda q: far_first[other, q * HG + h])
+                value = delta[n, at]
+                more = 0.5 * rates[s]
+                inner = more * roll(value, B)
+                value = value + more * (lateral[n, at] + ghost)
+                added.append(jnp.where(outer, value, inner))
+            if not plan.final:
+                gain = r.edges[rows_of(plan.step * HG + h), half(n)]
+                weight = r.edges[rows_of((plan.steps + plan.step) * HG + h), half(n)]
+                driver = added[fields]
+                heat, grown = weight * driver, gain * driver
+                for s in range(slots):
+                    added[s] = added[s] + share[s] * heat
+                added[0] = added[0] + extra * grown
+                added[fields] = added[fields] + grown
+            for s in range(slabs):
+                late[rows_of(s * HG + h), half(n)] = added[s]
+    if plan.final:
+        high, low = split(late[...])
+        r.ends[:, pl.ds(0, 2 * LANES)] = high
+        r.ends[:, pl.ds(2 * LANES, 2 * LANES)] = low
+        place_ends(r.ends, r.placed, slabs * HG * 8, r)
+        for s in range(slabs):
+            for i in range(B):
+                for jh in range(2):
+                    r.state_out[s, :, cols(i, jh)] = r.state[s, jh, rows_of(i), :] + placed_tile(
+                        r.placed, s, i, jh
+                    )
+        return
+
+    def send(up, down):
+        for n in range(slots * HG):
+            up[n] = r.faces_in[rows_of(n), half(0)] + late[rows_of(n), half(0)]
+            down[n] = r.faces_in[rows_of(n), half(1)] + late[rows_of(n), half(1)]
+        up[slots * HG] = faces
+        down[slots * HG] = faces
+
+    even = lax.axis_index("blk") % 2 == 0
+    pl.when(even)(lambda: send(r.send_e, r.send_o))
+    pl.when(jnp.logical_not(even))(lambda: send(r.send_o, r.send_e))
 
 
 SCALARS = ("dif", "shr", "dif_o", "shr_o", "children", "fine_counts", "coarse_counts")
 MATS = ("plane", "side", "place", "pack", "far")
 MIB = 1024 * 1024
+LIMIT = 60
 
 
 def call(kernel, inputs, outputs, scratch, hbm=(), sems=(), limit=None, cost=1000):
@@ -903,7 +1080,7 @@
         compiler_params=pltpu.CompilerParams(vmem_limit_bytes=limit or int(size) + 12 * MIB),
         cost_estimate=pl.CostEstimate(flops=cost, bytes_accessed=cost, transcendentals=0),
     )(*inputs.values())
-    return dict(zip(outputs, result))
+    return SimpleNamespace(**dict(zip(outputs, result)))
 
 
 def shards(
@@ -967,8 +1144,6 @@
 
     stage_work = dict(stage=(1, slots, 8 * H, LANES))
     dif_o, shr_o = core_swap(diffusion), core_swap(species_shares)
-    par = dict(dif=diffusion, shr=species_shares, dif_o=dif_o, shr_o=shr_o)
-
     paid = call(
         plain(mix_kernel),
         dict(
@@ -984,12 +1159,15 @@
         dict(fine=saved_fine.shape, coarse=saved_coarse.shape, seeds=seed_coarse.shape),
         hbm=("saved_f", "saved_c", "seed_f", "seed_c"),
         sems=((steps,), (), (), ()),
-        limit=60 * MIB,
-    )
-    pay, payc = paid["pay"], paid["payc"]
-    payc_o, pay_o = core_swap(payc), core_swap(pay)
-
-    loaded = [f"octant{n}" for n in range(len(sends) - 2)] + ["up", "down"]
+        limit=LIMIT * MIB,
+    )
+    payc = paid.payc
+    payc_o = core_swap(payc)
+    pay, payc_o, dif_o, shr_o = lax.optimization_barrier((paid.pay, payc_o, dif_o, shr_o))
+    par = dict(dif=diffusion, shr=species_shares, dif_o=dif_o, shr_o=shr_o)
+    pay_o = core_swap(pay)
+
+    loaded = [numbered("octant", n) for n in range(len(sends) - 2)] + ["up", "down"]
     started = call(
         plain(start_kernel, sends, count_f, fields),
         dict(
@@ -1000,7 +1178,6 @@
             **par,
             fine_nbr=fine_nbr,
             coarse_nbr=coarse_nbr,
-            pack=mats["pack"],
         ),
         dict(
             coarse=state_shape(count_c),
@@ -1009,20 +1186,30 @@
             local=slots_shape,
             **{name: loaded_shape if name in ("up", "down") else octant_shape for name in loaded},
         ),
-        dict(pack_work(count_c), coarse_stage=(count_c, 2 * fields, cells)),
-    )
-    landed = [octant_move(started[name], d) for name, d in zip(loaded, sends)]
+        dict(
+            pack_work(count_c),
+            table=(G, PLANE, 2 * LANES, BF16),
+            coarse_stage=(count_c, 2 * fields, cells),
+        ),
+    )
+    landed = [octant_move(getattr(started, name), d) for name, d in zip(loaded, sends)]
     chem = call(
         plain(chem_kernel),
-        dict(pay=pay, pay_o=pay_o, fine_counts=fine_counts),
-        dict(gain=(steps, count_f, cells), weight=(steps, count_f, cells)),
-        {},
-    )
-    landed, chem = lax.optimization_barrier((landed, chem))
+        dict(pay=pay, pay_o=pay_o, fine_counts=fine_counts, pack=mats.pack),
+        dict(
+            gain=(steps, count_f, cells),
+            weight=(steps, count_f, cells),
+            edges=(2 * (steps - 1) * HG * 8, 2 * LANES),
+        ),
+        dict(planes=pack_work(2 * (steps - 1))["planes"]),
+    )
+    landed, (chem.gain, chem.weight, chem.edges) = lax.optimization_barrier(
+        (landed, (chem.gain, chem.weight, chem.edges))
+    )
     shared = [core_swap(value) for value in landed]
 
     def named(word, values):
-        return {f"{word}{n}": value for n, value in enumerate(values)}
+        return {numbered(word, n): value for n, value in enumerate(values)}
 
     plan = dict(
         fields=fields,
@@ -1036,20 +1223,22 @@
         final=False,
         add=False,
         near_at=every * HG + 1,
+        late=0,
+        steps=steps,
     )
 
     def run(kernel, changes, inputs, outputs, scratch):
         return call(
-            functools.partial(kernel, dict(plan, **changes)),
-            dict(par, **mats, **inputs),
+            functools.partial(kernel, SimpleNamespace(**{**plan, **changes})),
+            dict(par, **vars(mats), **inputs),
             outputs,
             scratch,
         )
 
     def halo(made, ring=False):
-        got_o = pair_swap(made["send_o"], 1, ring)
-        got_e = pair_swap(made["send_e"], 0, ring)
-        return dict(sent_o=made["send_o"], got_o=got_o, sent_e=made["send_e"], got_e=got_e)
+        got_o = pair_swap(made.send_o, 1, ring)
+        got_e = pair_swap(made.send_e, 0, ring)
+        return dict(sent_o=made.send_o, got_o=got_o, sent_e=made.send_e, got_e=got_e)
 
     def sending(slabs, more=0):
         return dict(
@@ -1060,17 +1249,17 @@
         open_kernel,
         dict(slabs_out=every, step=steps - 1),
         dict(
-            chem,
-            gain_c=started["gain_c"],
-            weight_c=started["weight_c"],
+            vars(chem),
+            gain_c=started.gain_c,
+            weight_c=started.weight_c,
             children=children,
-            coarse=started["coarse"],
-            own_up=started["up"],
-            own_down=started["down"],
+            coarse=started.coarse,
+            own_up=started.up,
+            own_down=started.down,
             seed_f=seed_fine,
             seed=pay[2 * steps :],
             seed_other=pay_o[2 * steps :],
-            local=started["local"],
+            local=started.local,
             **named("landed", landed),
             **named("shared", shared),
         ),
@@ -1082,41 +1271,82 @@
         dict(work(count_c), **pack_work(every), **stage_work, near_octant=slots_shape),
     )
     first_halo = halo(made, True)
-    local = made["local_out"]
-    landed = [octant_move(made[f"octant{n}"], d) for n, d in enumerate(later)]
-    landed, first_halo = lax.optimization_barrier((landed, first_halo))
+    landed = [octant_move(getattr(made, numbered("octant", n)), d) for n, d in enumerate(later)]
+    landed, arrived_halo = lax.optimization_barrier((landed, first_halo))
     shared = [core_swap(value) for value in landed]
-    made = run(
-        step_kernel,
-        dict(step=steps - 2),
-        dict(chem, state=made["state_out"], **first_halo),
-        dict(sending(slots), coarse_final=seed_coarse.shape),
-        dict(
-            work(every),
-            **strip_work(every),
-            **pack_work(every),
-            coarse_stage=(count_c, 2 * fields, cells),
-        ),
-    )
-    coarse_final = made["coarse_final"]
-    for step in reversed(range(steps - 2)):
-        inputs = dict(chem, state=made["state_out"], **halo(made))
-        scratch = dict(work(slots), **strip_work(slots), **pack_work(slots))
-        changes = dict(step=step, slabs_in=slots, slabs=slots)
+
+    def edge_work(slabs):
+        rows = slabs * HG * 8
+        packed = (2, slabs * HG, 8, LANES)
+        return dict(
+            delta=packed,
+            far_first=packed,
+            lateral=packed,
+            far_lhs=(2 * rows, 4 * LANES, BF16),
+            far_out=(2 * rows, LANES),
+            far_lhs2=(2 * rows, 4 * LANES, BF16),
+            far_out2=(2 * rows, LANES),
+        )
+
+    def place_work(slabs):
+        rows = slabs * HG * 8
+        return dict(ends=(rows, 4 * LANES, BF16), placed=(rows, G * PLANE))
+
+    def own_strips(slabs):
+        return dict(own_up=strip(slabs), own_down=strip(slabs))
+
+    state, flown, held = made.state_out, arrived_halo, every
+    local = made.local_out
+    sent = dict(sent_e=made.send_e, sent_o=made.send_o)
+    late, coarse, coarse_final = None, None, None
+    for step in reversed(range(-1, steps - 1)):
+        final = step < 0
+        slabs = fields if final else held
+        changes = dict(step=step, steps=steps - 1, slabs_in=held, slabs=slabs, final=final)
+        inputs = dict(state=state, **sent)
+        outputs = dict(state_out=state_shape(min(slabs, slots)))
+        scratch = dict(work(slabs), **own_strips(held), **pack_work(slabs))
+        if not final:
+            inputs.update(gain=chem.gain, weight=chem.weight)
+            outputs.update(faces_out=(slots * HG * 8, 2 * LANES))
+        if held > slots:
+            outputs.update(coarse_out=state_shape(count_c))
+        if late is not None:
+            before = every if coarse is not None else slabs
+            inputs.update(late=late)
+            scratch.update(whole=state_shape(slabs), **place_work(max(before, slabs)))
+            changes.update(late=before)
+            if coarse is not None:
+                inputs.update(coarse=coarse)
+                outputs.update(coarse_final=seed_coarse.shape)
+                scratch.update(coarse_stage=(count_c, 2 * fields, cells))
         if step == steps - 3:
             inputs.update(named("landed", landed), **named("shared", shared), local=local)
-            inputs.update(near_e=first_halo["got_e"], near_o=first_halo["got_o"])
+            inputs.update(near_e=arrived_halo["got_e"], near_o=arrived_halo["got_o"])
             scratch.update(stage_work, near_octant=slots_shape)
             changes.update(add=True)
-        made = run(step_kernel, changes, inputs, sending(slots), scratch)
-    made = run(
-        step_kernel,
-        dict(final=True, slabs_in=slots, slabs=fields),
-        dict(state=made["state_out"], **halo(made)),
-        dict(state_out=seed_fine.shape),
-        dict(work(fields), **strip_work(slots), **pack_work(fields)),
-    )
-    return made["state_out"], coarse_final
+        bulk = run(bulk_kernel, changes, inputs, outputs, scratch)
+        if coarse is not None:
+            coarse_final = bulk.coarse_final
+        coarse = bulk.coarse_out if held > slots else None
+        inputs = dict(flown)
+        scratch = dict(edge_work(slabs), **strip_work(held))
+        if final:
+            inputs.update(state=bulk.state_out)
+            outputs = dict(state_out=seed_fine.shape)
+            scratch.update(late=(slabs * HG * 8, 2 * LANES), **place_work(slabs))
+        else:
+            inputs.update(edges=chem.edges, faces_in=bulk.faces_out)
+            outputs = dict(
+                late=(slabs * HG * 8, 2 * LANES), send_e=strip(slots), send_o=strip(slots)
+            )
+        made = run(edge_kernel, changes, inputs, outputs, scratch)
+        if final:
+            break
+        state, late, held = bulk.state_out, made.late, slots
+        flown = halo(made)
+        sent = dict(sent_e=made.send_e, sent_o=made.send_o)
+    return made.state_out, coarse_final
 
 
 def solution(mesh):

time: 76.1 us -> 67.7 us (0.89)
  waiting for transfers between devices: 23.4 us -> 9.3 us
  Pallas kernels: 25.5 us -> 30.1 us
  local copies, waits for them, and re-layouts: 1.07 us -> 2.33 us
    ppermute x8, waiting for transfers between devices: 10.9 us -> 3.3 us  [pair_swap(): return lax.ppermute(value, ('blk', 'fld'), pairs)]
    ppermute x7, waiting for transfers between devices: 8.13 us -> 2.91 us  [octant_move(): return lax.ppermute(value, ('blk', 'fld'), pairs)]
    pallas_call x8 -> x12, Pallas kernels: 25.5 us -> 30.1 us  [call(): pl.pallas_call(functools.partial(kernel, names), out_shape=[jax.ShapeDtyp...]
    ppermute x7, starting transfers between devices: 9.75 us -> 11 us  [octant_move(): return lax.ppermute(value, ('blk', 'fld'), pairs)]
    ppermute x8, starting transfers between devices: 11.9 us -> 10.6 us  [pair_swap(): return lax.ppermute(value, ('blk', 'fld'), pairs)]
    ppermute x11, waiting for transfers between devices: 4.36 us -> 3.09 us  [core_swap(): return lax.ppermute(value, 'fld', [(0, 1), (1, 0)])]
    unnamed x30, local copies, waits for them, and re-layouts: 1.05 us -> 2.31 us
  transfers between devices with their start and end apart: 26 -> 26, of which waited for: 14 -> 12; matrix products, arithmetic and copies ran while one was open for 0% -> 0% of each run, Pallas kernels for 7% -> 27%
where the time goes in v4:
time: 67.7 us; the launch traced here: 67.3 us
  Pallas kernels  30.1 us (44%)
  starting transfers between devices  24.6 us (36%)
  waiting for transfers between devices  9.3 us (14%)
  local copies, waits for them, and re-layouts  2.33 us (3%)
  between operations  0.94 us (1%)
    pallas_call x12, Pallas kernels, call(): pl.pallas_call(functools.partial(kernel, names), out_shape=[jax.ShapeDtyp...  30.1 us
    ppermute x7, starting transfers between devices, octant_move(): return lax.ppermute(value, ('blk', 'fld'), pairs)  11 us
    ppermute x8, starting transfers between devices, pair_swap(): return lax.ppermute(value, ('blk', 'fld'), pairs)  10.6 us
    ppermute x8, waiting for transfers between devices, pair_swap(): return lax.ppermute(value, ('blk', 'fld'), pairs)  3.3 us
    ppermute x11, waiting for transfers between devices, core_swap(): return lax.ppermute(value, 'fld', [(0, 1), (1, 0)])  3.09 us
    ppermute x11, starting transfers between devices, core_swap(): return lax.ppermute(value, 'fld', [(0, 1), (1, 0)])  2.95 us
    ppermute x7, waiting for transfers between devices, octant_move(): return lax.ppermute(value, ('blk', 'fld'), pairs)  2.91 us
    unnamed x30, local copies, waits for them, and re-layouts  2.31 us
  transfers between devices with their start and end apart: 26, of which 12 were waited for; matrix products, arithmetic and copies ran while one was open for 0% of the time, Pallas kernels for 27%

profile of v4, /device:TPU:0, one launch (start us, length us, event | category | flops | bytes accessed | tf_op | source)
XLA Modules:
  0.0 67.3 jit_solution(13918949970613643371)
XLA Ops:
  0.7 3.7 %shard_map.167 = (f32[9,8,4096]{2,1,0:T(8,128)}, f32[6,4,4096]{2,1,0:T(4,128)}) custom-call(f32[4,4,8,4096]{3,2,1,0:T(8,128)} %refs_0_.10, f32[2,4,2,4096]{3,2,1,0:T(2,128)} %refs_1_.10, f32[4,8,4096]{2,1,0:T(8,128)} %refs_18_.1, f32[4,2,4096]{2,1,0:T(2,128)} %refs_3_.3, f32[4]{0:T(128)} %refs_1_.19), custom_call_target="tpu_custom_call" | custom-call | flops 1000 | bytes 1000 | tf_op jit(solution)/shard_map/pallas_call | solution.py:1073
  7.9 2.0 %shard_map.168 = (f32[2,2,128,128]{3,2,1,0:T(8,128)S(1)}, f32[4,4096]{1,0:T(4,128)S(1)}, f32[4,4096]{1,0:T(4,128)S(1)}, f32[6,8,128]{2,1,0:T(8,128)S(1)}, f32[9,...) custom-call(f32[6,4,4096]{2,1,0:T(4,128)S(1)} %copy-done.7, ...), custom_call_target="tpu_custom_call" | custom-call | flops 1000 | bytes 1000 | tf_op jit(solution)/shard_map/pallas_call | solution.py:1073
  9.9 2.7 %collective-permute-start.5 = (f32[18,8,128]{2,1,0:T(8,128)S(1)}, f32[18,8,128]{2,1,0:T(8,128)S(1)}, u32[]{:S(2)}, u32[]{:S(2)}) collective-permute-start(f32[18,8,128]{2,1,0:T(8,128)S(1)} %get-tuple-element.64.refs_16_), channel_id=1, source_target_pairs={{0,2},{1,13},{2,4},{3,15},{4,6},{5,17},{6,8},{7,19},{8,10},{9,21},... | collective-permute-start | bytes 221192 | tf_op jit(solution)/shard_map/ppermute | solution.py:64
  12.6 4.1 %collective-permute-start.6 = (f32[18,8,128]{2,1,0:T(8,128)S(1)}, f32[18,8,128]{2,1,0:T(8,128)S(1)}, u32[]{:S(2)}, u32[]{:S(2)}) collective-permute-start(f32[18,8,128]{2,1,0:T(8,128)S(1)} %get-tuple-element.65.refs_17_), channel_id=1, source_target_pairs={{0,30},{1,15},{2,0},{3,17},{4,2},{5,19},{6,4},{7,21},{8,6},{9,23},... | collective-permute-start | bytes 221192 | tf_op jit(solution)/shard_map/ppermute | solution.py:64
  17.2 1.3 %copy-done.6 = f32[9,8,4096]{2,1,0:T(8,128)S(1)} copy-done((f32[9,8,4096]{2,1,0:T(8,128)S(1)}, f32[9,8,4096]{2,1,0:T(8,128)}, u32[]{:S(2)}) %copy-start.6) | copy-done | bytes 1179672
  18.4 3.6 %shard_map.169 = (f32[4,8,4096]{2,1,0:T(8,128)S(1)}, f32[4,8,4096]{2,1,0:T(8,128)S(1)}, f32[192,256]{1,0:T(8,128)S(1)}) custom-call(f32[9,8,4096]{2,1,0:T(8,128)S(1)} %copy-done.6, f32[9,8,4096]{2,1,0:T(8,128)S(1)} %collective-permute-done.7.refs_1_, s32[8]{0:T(128)S(1)} %copy-done.13, bf16[4,256,256]{2,1,0:T(8,128)(2,1)S(1)} %copy-done), custom_call_target="tpu_custom_call" | custom-call | flops 1000 | bytes 1000 | tf_op jit(solution)/shard_map/pallas_call | solution.py:1073
  22.1 1.4 %collective-permute-done.3.refs_22_ = f32[9,8,128]{2,1,0:T(8,128)S(1)} collective-permute-done((f32[9,8,128]{2,1,0:T(8,128)S(1)}, f32[9,8,128]{2,1,0:T(8,128)S(1)}, u32[]{:S(2)}, u32[]{:S(2)}) %collective-permute-start.3) | collective-permute-done | bytes 36896 | tf_op jit(solution)/shard_map/ppermute | solution.py:64
  25.5 2.8 %shard_map.170 = (f32[7,2,128,128]{3,2,1,0:T(8,128)S(1)}, f32[35,8,128]{2,1,0:T(8,128)S(1)}, f32[35,8,128]{2,1,0:T(8,128)S(1)}, f32[6,8,128]{2,1,0:T(8,128)S(1)}...) custom-call(f32[4]{0:T(128)S(1)} %copy-done.9, f32[4]{0:T(128)S(1)} %copy-done.8, ...), custom_call_target="tpu_custom_call" | custom-call | flops 1000 | bytes 1000 | tf_op jit(solution)/shard_map/pallas_call | solution.py:1073
  28.3 1.8 %collective-permute-start.15 = (f32[35,8,128]{2,1,0:T(8,128)S(1)}, f32[35,8,128]{2,1,0:T(8,128)S(1)}, u32[]{:S(2)}, u32[]{:S(2)}) collective-permute-start(f32[35,8,128]{2,1,0:T(8,128)S(1)} %get-tuple-element.88.refs_10_.refs_11_), channel_id=1, source_target_pairs={{0,2},{1,3},{2,0},{3,1},{4,6},{5,7},{6,4},{7,5},{8,10},{9,11},{10,... | collective-permute-start | bytes 430088 | tf_op jit(solution)/shard_map/ppermute | solution.py:45
  30.1 2.9 %collective-permute-start.16 = (f32[35,8,128]{2,1,0:T(8,128)S(1)}, f32[35,8,128]{2,1,0:T(8,128)S(1)}, u32[]{:S(2)}, u32[]{:S(2)}) collective-permute-start(f32[35,8,128]{2,1,0:T(8,128)S(1)} %get-tuple-element.89.refs_11_.refs_12_), channel_id=1, source_target_pairs={{0,30},{1,31},{2,4},{3,5},{4,2},{5,3},{6,8},{7,9},{8,6},{9,7},{10,... | collective-permute-start | bytes 430088 | tf_op jit(solution)/shard_map/ppermute | solution.py:45
  33.0 2.8 %collective-permute-start.13 = (f32[9,8,128]{2,1,0:T(8,128)S(1)}, f32[9,8,128]{2,1,0:T(8,128)S(1)}, u32[]{:S(2)}, u32[]{:S(2)}) collective-permute-start(f32[9,8,128]{2,1,0:T(8,128)S(1)} %get-tuple-element.82), channel_id=1, source_target_pairs={{0,6},{1,13},{2,8},{3,15},{4,10},{5,17},{6,12},{7,19},{8,14},{9,21... | collective-permute-start | bytes 110600 | tf_op jit(solution)/shard_map/ppermute | solution.py:64
  36.8 3.3 %shard_map.171 = (f32[5,2,128,128]{3,2,1,0:T(8,128)S(1)}, f32[160,256]{1,0:T(8,128)S(1)}, f32[2,2,128,128]{3,2,1,0:T(8,128)S(1)}) custom-call(f32[4]{0:T(128)S(1)} %copy-done.9, f32[4]{0:T(128)S(1)} %copy-done.8, f32[4]{0:T(128)S(1)} %collective-permute-done.1.refs_6_.refs_2_, f32[4]{0:T(128)S(1)} %collective-permute-done.2.refs_7_.refs_3_, ...), custom_call_target="tpu_custom_call" | custom-call | flops 1000 | bytes 1000 | tf_op jit(solution)/shard_map/pallas_call | solution.py:1073
  40.1 1.4 %collective-permute-done.14.refs_18_ = f32[9,8,128]{2,1,0:T(8,128)S(1)} collective-permute-done((f32[9,8,128]{2,1,0:T(8,128)S(1)}, f32[9,8,128]{2,1,0:T(8,128)S(1)}, u32[]{:S(2)}, u32[]{:S(2)}) %collective-permute-start.14) | collective-permute-done | bytes 36896 | tf_op jit(solution)/shard_map/ppermute | solution.py:64
  41.5 1.3 %shard_map.172 = (f32[224,256]{1,0:T(8,128)S(1)}, f32[21,8,128]{2,1,0:T(8,128)S(1)}, f32[21,8,128]{2,1,0:T(8,128)S(1)}) custom-call(f32[4]{0:T(128)S(1)} %copy-done.9, f32[4]{0:T(128)S(1)} %copy-done.8, f32[4]{0:T(128)S(1)} %collective-permute-done.1.refs_6_.refs_2_, f32[4]{0:T(128)S(1)} %collective-permute-done.2.refs_7_.refs_3_, ...), custom_call_target="tpu_custom_call" | custom-call | flops 1000 | bytes 1000 | tf_op jit(solution)/shard_map/pallas_call | solution.py:1073
  43.4 2.4 %collective-permute-start.18 = (f32[21,8,128]{2,1,0:T(8,128)S(1)}, f32[21,8,128]{2,1,0:T(8,128)S(1)}, u32[]{:S(2)}, u32[]{:S(2)}) collective-permute-start(f32[21,8,128]{2,1,0:T(8,128)S(1)} %get-tuple-element.93.refs_10_.refs_11_), channel_id=1, source_target_pairs={{0,2},{1,3},{2,0},{3,1},{4,6},{5,7},{6,4},{7,5},{8,10},{9,11},{10,... | collective-permute-start | bytes 258056 | tf_op jit(solution)/shard_map/ppermute | solution.py:45
  47.6 3.8 %shard_map.173 = (f32[5,2,128,128]{3,2,1,0:T(8,128)S(1)}, f32[160,256]{1,0:T(8,128)S(1)}, f32[4,2,4096]{2,1,0:T(2,128)}) custom-call(f32[4]{0:T(128)S(1)} %copy-done.9, f32[4]{0:T(128)S(1)} %copy-done.8, f32[4]{0:T(128)S(1)} %collective-permute-done.1.refs_6_.refs_2_, f32[4]{0:T(128)S(1)} %collective-permute-done.2.refs_7_.refs_3_, ...), custom_call_target="tpu_custom_call" | custom-call | flops 1000 | bytes 1000 | tf_op jit(solution)/shard_map/pallas_call | solution.py:1073
  51.4 1.1 %shard_map.174 = (f32[160,256]{1,0:T(8,128)S(1)}, f32[21,8,128]{2,1,0:T(8,128)S(1)}, f32[21,8,128]{2,1,0:T(8,128)S(1)}) custom-call(f32[4]{0:T(128)S(1)} %copy-done.9, f32[4]{0:T(128)S(1)} %copy-done.8, f32[4]{0:T(128)S(1)} %collective-permute-done.1.refs_6_.refs_2_, f32[4]{0:T(128)S(1)} %collective-permute-done.2.refs_7_.refs_3_, ...), custom_call_target="tpu_custom_call" | custom-call | flops 1000 | bytes 1000 | tf_op jit(solution)/shard_map/pallas_call | solution.py:1073
  53.4 3.1 %shard_map.175 = (f32[5,2,128,128]{3,2,1,0:T(8,128)S(1)}, f32[160,256]{1,0:T(8,128)S(1)}) custom-call(f32[4]{0:T(128)S(1)} %copy-done.9, f32[4]{0:T(128)S(1)} %copy-done.8, f32[4]{0:T(128)S(1)} %collective-permute-done.1.refs_6_.refs_2_, f32[4]{0:T(128)S(1)} %collective-permute-done.2.refs_7_.refs_3_, bf16[256,256]{1,0:T(8,128)(2,1)S(1)} %copy-done.2, ...), custom_call_target="tpu_custom_call" | custom-call | flops 1000 | bytes 1000 | tf_op jit(solution)/shard_map/pallas_call | solution.py:1073
  56.5 1.5 %collective-permute-done.23.refs_12_ = f32[21,8,128]{2,1,0:T(8,128)S(1)} collective-permute-done((f32[21,8,128]{2,1,0:T(8,128)S(1)}, f32[21,8,128]{2,1,0:T(8,128)S(1)}, u32[]{:S(2)}, u32[]{:S(2)}) %collective-permute-start.23) | collective-permute-done | bytes 86048 | tf_op jit(solution)/shard_map/ppermute | solution.py:45
  58.0 1.1 %shard_map.176 = (f32[160,256]{1,0:T(8,128)S(1)}, f32[21,8,128]{2,1,0:T(8,128)S(1)}, f32[21,8,128]{2,1,0:T(8,128)S(1)}) custom-call(f32[4]{0:T(128)S(1)} %copy-done.9, f32[4]{0:T(128)S(1)} %copy-done.8, f32[4]{0:T(128)S(1)} %collective-permute-done.1.refs_6_.refs_2_, f32[4]{0:T(128)S(1)} %collective-permute-done.2.refs_7_.refs_3_, ...), custom_call_target="tpu_custom_call" | custom-call | flops 1000 | bytes 1000 | tf_op jit(solution)/shard_map/pallas_call | solution.py:1073
  59.2 2.0 %collective-permute-start.25 = (f32[21,8,128]{2,1,0:T(8,128)S(1)}, f32[21,8,128]{2,1,0:T(8,128)S(1)}, u32[]{:S(2)}, u32[]{:S(2)}) collective-permute-start(f32[21,8,128]{2,1,0:T(8,128)S(1)} %get-tuple-element.108.refs_10_.refs_11_), channel_id=1, source_target_pairs={{0,2},{1,3},{2,0},{3,1},{4,6},{5,7},{6,4},{7,5},{8,10},{9,11},{10,... | collective-permute-start | bytes 258056 | tf_op jit(solution)/shard_map/ppermute | solution.py:45
  61.2 2.2 %shard_map.177.refs_13_ = f32[4,2,128,128]{3,2,1,0:T(8,128)S(1)} custom-call(f32[4]{0:T(128)S(1)} %copy-done.9, f32[4]{0:T(128)S(1)} %copy-done.8, f32[4]{0:T(128)S(1)} %collective-permute-done.1.refs_6_.refs_2_, f32[4]{0:T(128)S(1)} %collective-permute-done.2.refs_7_.refs_3_, bf16[256,256]{1,0:T(8,128)(2,1)S(1)} %copy-done.2, ...), custom_call_target="tpu_custom_call" | custom-call | flops 1000 | bytes 1000 | tf_op jit(solution)/shard_map/pallas_call | solution.py:1073
  63.5 1.8 %collective-permute-done.25.refs_12_ = f32[21,8,128]{2,1,0:T(8,128)S(1)} collective-permute-done((f32[21,8,128]{2,1,0:T(8,128)S(1)}, f32[21,8,128]{2,1,0:T(8,128)S(1)}, u32[]{:S(2)}, u32[]{:S(2)}) %collective-permute-start.25) | collective-permute-done | bytes 86048 | tf_op jit(solution)/shard_map/ppermute | solution.py:45
  65.2 2.1 %shard_map.178 = f32[4,8,4096]{2,1,0:T(8,128)} custom-call(f32[4]{0:T(128)S(1)} %copy-done.9, f32[4]{0:T(128)S(1)} %copy-done.8, f32[4]{0:T(128)S(1)} %collective-permute-done.1.refs_6_.refs_2_, f32[4]{0:T(128)S(1)} %collective-permute-done.2.refs_7_.refs_3_, bf16[256,256]{1,0:T(8,128)(2,1)S(1)} %copy-done.2, bf16[128,256]{1,0:T(8,128)(2,1)S(1)} %copy-done.4, ...), custom_call_target="tpu_custom_call" | custom-call | flops 1000 | bytes 1000 | tf_op jit(solution)/shard_map/pallas_call | solution.py:1073
  (72 shorter events, 10.3 us)
Async XLA Ops:
  4.4 2.1 %collective-permute-start = (f32[6,4,4096]{2,1,0:T(4,128)}, f32[6,4,4096]{2,1,0:T(4,128)S(1)}, u32[]{:S(2)}, u32[]{:S(2)}) collective-permute-start(f32[6,4,4096]{2,1,0:T(4,128)} %get-tuple-element.58.refs_0_), channel_id=1, source_target_pairs={{0,1},{1,0},{2,3},{3,2},{4,5},{5,4},{6,7},{7,6},{8,9},{9,8},{10,11... | collective-permute-start | bytes 1179656 | tf_op jit(solution)/shard_map/ppermute | solution.py:32
  4.9 1.4 %collective-permute-start.2 = (f32[4]{0:T(128)S(1)}, f32[4]{0:T(128)S(1)}, u32[]{:S(2)}, u32[]{:S(2)}) collective-permute-start(f32[4]{0:T(128)S(1)} %copy-done.8), channel_id=1, source_target_pairs={{0,1},{1,0},{2,3},{3,2},{4,5},{5,4},{6,7},{7,6},{8,9},{9,8},{10,11... | collective-permute-start | bytes 56 | tf_op jit(solution)/shard_map/ppermute | solution.py:32
  5.0 1.3 %collective-permute-start.1 = (f32[4]{0:T(128)S(1)}, f32[4]{0:T(128)S(1)}, u32[]{:S(2)}, u32[]{:S(2)}) collective-permute-start(f32[4]{0:T(128)S(1)} %copy-done.9), channel_id=1, source_target_pairs={{0,1},{1,0},{2,3},{3,2},{4,5},{5,4},{6,7},{7,6},{8,9},{9,8},{10,11... | collective-permute-start | bytes 56 | tf_op jit(solution)/shard_map/ppermute | solution.py:32
  6.5 10.7 %collective-permute-start.7 = (f32[9,8,4096]{2,1,0:T(8,128)}, f32[9,8,4096]{2,1,0:T(8,128)S(1)}, u32[]{:S(2)}, u32[]{:S(2)}) collective-permute-start(f32[9,8,4096]{2,1,0:T(8,128)} %get-tuple-element.66.refs_0_), channel_id=1, source_target_pairs={{0,1},{1,0},{2,3},{3,2},{4,5},{5,4},{6,7},{7,6},{8,9},{9,8},{10,11... | collective-permute-start | bytes 3538952 | tf_op jit(solution)/shard_map/ppermute | solution.py:32
  9.9 13.6 %collective-permute-start.5 = (f32[18,8,128]{2,1,0:T(8,128)S(1)}, f32[18,8,128]{2,1,0:T(8,128)S(1)}, u32[]{:S(2)}, u32[]{:S(2)}) collective-permute-start(f32[18,8,128]{2,1,0:T(8,128)S(1)} %get-tuple-element.64.refs_16_), channel_id=1, source_target_pairs={{0,2},{1,13},{2,4},{3,15},{4,6},{5,17},{6,8},{7,19},{8,10},{9,21},... | collective-permute-start | bytes 221192 | tf_op jit(solution)/shard_map/ppermute | solution.py:64
  12.6 11.0 %collective-permute-start.6 = (f32[18,8,128]{2,1,0:T(8,128)S(1)}, f32[18,8,128]{2,1,0:T(8,128)S(1)}, u32[]{:S(2)}, u32[]{:S(2)}) collective-permute-start(f32[18,8,128]{2,1,0:T(8,128)S(1)} %get-tuple-element.65.refs_17_), channel_id=1, source_target_pairs={{0,30},{1,15},{2,0},{3,17},{4,2},{5,19},{6,4},{7,21},{8,6},{9,23},... | collective-permute-start | bytes 221192 | tf_op jit(solution)/shard_map/ppermute | solution.py:64
  16.6 6.8 %collective-permute-start.3 = (f32[9,8,128]{2,1,0:T(8,128)S(1)}, f32[9,8,128]{2,1,0:T(8,128)S(1)}, u32[]{:S(2)}, u32[]{:S(2)}) collective-permute-start(f32[9,8,128]{2,1,0:T(8,128)S(1)} %get-tuple-element.62), channel_id=1, source_target_pairs={{0,4},{1,9},{2,6},{3,11},{4,8},{5,13},{6,10},{7,15},{8,12},{9,17},... | collective-permute-start | bytes 110600 | tf_op jit(solution)/shard_map/ppermute | solution.py:64
  16.7 6.9 %collective-permute-start.4 = (f32[9,8,128]{2,1,0:T(8,128)S(1)}, f32[9,8,128]{2,1,0:T(8,128)S(1)}, u32[]{:S(2)}, u32[]{:S(2)}) collective-permute-start(f32[9,8,128]{2,1,0:T(8,128)S(1)} %get-tuple-element.63), channel_id=1, source_target_pairs={{0,6},{1,11},{2,8},{3,13},{4,10},{5,15},{6,12},{7,17},{8,14},{9,19... | collective-permute-start | bytes 110600 | tf_op jit(solution)/shard_map/ppermute | solution.py:64
  23.6 1.9 %collective-permute-start.10 = (f32[18,8,128]{2,1,0:T(8,128)S(1)}, f32[18,8,128]{2,1,0:T(8,128)S(1)}, u32[]{:S(2)}, u32[]{:S(2)}) collective-permute-start(f32[18,8,128]{2,1,0:T(8,128)S(1)} %collective-permute-done.5.refs_24_), channel_id=1, source_target_pairs={{0,1},{1,0},{2,3},{3,2},{4,5},{5,4},{6,7},{7,6},{8,9},{9,8},{10,11... | collective-permute-start | bytes 221192 | tf_op jit(solution)/shard_map/ppermute | solution.py:32
  23.6 1.9 %collective-permute-start.11 = (f32[18,8,128]{2,1,0:T(8,128)S(1)}, f32[18,8,128]{2,1,0:T(8,128)S(1)}, u32[]{:S(2)}, u32[]{:S(2)}) collective-permute-start(f32[18,8,128]{2,1,0:T(8,128)S(1)} %collective-permute-done.6.refs_25_), channel_id=1, source_target_pairs={{0,1},{1,0},{2,3},{3,2},{4,5},{5,4},{6,7},{7,6},{8,9},{9,8},{10,11... | collective-permute-start | bytes 221192 | tf_op jit(solution)/shard_map/ppermute | solution.py:32
  24.2 1.3 %collective-permute-start.9 = (f32[9,8,128]{2,1,0:T(8,128)S(1)}, f32[9,8,128]{2,1,0:T(8,128)S(1)}, u32[]{:S(2)}, u32[]{:S(2)}) collective-permute-start(f32[9,8,128]{2,1,0:T(8,128)S(1)} %collective-permute-done.4.refs_23_), channel_id=1, source_target_pairs={{0,1},{1,0},{2,3},{3,2},{4,5},{5,4},{6,7},{7,6},{8,9},{9,8},{10,11... | collective-permute-start | bytes 110600 | tf_op jit(solution)/shard_map/ppermute | solution.py:32
  28.3 13.2 %collective-permute-start.15 = (f32[35,8,128]{2,1,0:T(8,128)S(1)}, f32[35,8,128]{2,1,0:T(8,128)S(1)}, u32[]{:S(2)}, u32[]{:S(2)}) collective-permute-start(f32[35,8,128]{2,1,0:T(8,128)S(1)} %get-tuple-element.88.refs_10_.refs_11_), channel_id=1, source_target_pairs={{0,2},{1,3},{2,0},{3,1},{4,6},{5,7},{6,4},{7,5},{8,10},{9,11},{10,... | collective-permute-start | bytes 430088 | tf_op jit(solution)/shard_map/ppermute | solution.py:45
  30.1 11.4 %collective-permute-start.16 = (f32[35,8,128]{2,1,0:T(8,128)S(1)}, f32[35,8,128]{2,1,0:T(8,128)S(1)}, u32[]{:S(2)}, u32[]{:S(2)}) collective-permute-start(f32[35,8,128]{2,1,0:T(8,128)S(1)} %get-tuple-element.89.refs_11_.refs_12_), channel_id=1, source_target_pairs={{0,30},{1,31},{2,4},{3,5},{4,2},{5,3},{6,8},{7,9},{8,6},{9,7},{10,... | collective-permute-start | bytes 430088 | tf_op jit(solution)/shard_map/ppermute | solution.py:45
  33.0 7.1 %collective-permute-start.12 = (f32[9,8,128]{2,1,0:T(8,128)S(1)}, f32[9,8,128]{2,1,0:T(8,128)S(1)}, u32[]{:S(2)}, u32[]{:S(2)}) collective-permute-start(f32[9,8,128]{2,1,0:T(8,128)S(1)} %get-tuple-element.81), channel_id=1, source_target_pairs={{0,4},{1,11},{2,6},{3,13},{4,8},{5,15},{6,10},{7,17},{8,12},{9,19}... | collective-permute-start | bytes 110600 | tf_op jit(solution)/shard_map/ppermute | solution.py:64
  33.0 7.1 %collective-permute-start.13 = (f32[9,8,128]{2,1,0:T(8,128)S(1)}, f32[9,8,128]{2,1,0:T(8,128)S(1)}, u32[]{:S(2)}, u32[]{:S(2)}) collective-permute-start(f32[9,8,128]{2,1,0:T(8,128)S(1)} %get-tuple-element.82), channel_id=1, source_target_pairs={{0,6},{1,13},{2,8},{3,15},{4,10},{5,17},{6,12},{7,19},{8,14},{9,21... | collective-permute-start | bytes 110600 | tf_op jit(solution)/shard_map/ppermute | solution.py:64
  35.8 5.8 %collective-permute-start.14 = (f32[9,8,128]{2,1,0:T(8,128)S(1)}, f32[9,8,128]{2,1,0:T(8,128)S(1)}, u32[]{:S(2)}, u32[]{:S(2)}) collective-permute-start(f32[9,8,128]{2,1,0:T(8,128)S(1)} %get-tuple-element.83), channel_id=1, source_target_pairs={{0,8},{1,15},{2,10},{3,17},{4,12},{5,19},{6,14},{7,21},{8,16},{9,2... | collective-permute-start | bytes 110600 | tf_op jit(solution)/shard_map/ppermute | solution.py:64
  42.8 8.6 %collective-permute-start.17 = (f32[21,8,128]{2,1,0:T(8,128)S(1)}, f32[21,8,128]{2,1,0:T(8,128)S(1)}, u32[]{:S(2)}, u32[]{:S(2)}) collective-permute-start(f32[21,8,128]{2,1,0:T(8,128)S(1)} %get-tuple-element.92.refs_11_.refs_9_), channel_id=1, source_target_pairs={{0,1},{1,0},{2,4},{3,5},{4,2},{5,3},{6,8},{7,9},{8,6},{9,7},{10,12... | collective-permute-start | bytes 258056 | tf_op jit(solution)/shard_map/ppermute | solution.py:45
  43.4 8.0 %collective-permute-start.18 = (f32[21,8,128]{2,1,0:T(8,128)S(1)}, f32[21,8,128]{2,1,0:T(8,128)S(1)}, u32[]{:S(2)}, u32[]{:S(2)}) collective-permute-start(f32[21,8,128]{2,1,0:T(8,128)S(1)} %get-tuple-element.93.refs_10_.refs_11_), channel_id=1, source_target_pairs={{0,2},{1,3},{2,0},{3,1},{4,6},{5,7},{6,4},{7,5},{8,10},{9,11},{10,... | collective-permute-start | bytes 258056 | tf_op jit(solution)/shard_map/ppermute | solution.py:45
  45.9 1.2 %collective-permute-start.19 = (f32[9,8,128]{2,1,0:T(8,128)S(1)}, f32[9,8,128]{2,1,0:T(8,128)S(1)}, u32[]{:S(2)}, u32[]{:S(2)}) collective-permute-start(f32[9,8,128]{2,1,0:T(8,128)S(1)} %collective-permute-done.12.refs_16_), channel_id=1, source_target_pairs={{0,1},{1,0},{2,3},{3,2},{4,5},{5,4},{6,7},{7,6},{8,9},{9,8},{10,11... | collective-permute-start | bytes 110600 | tf_op jit(solution)/shard_map/ppermute | solution.py:32
  45.9 1.4 %collective-permute-start.20 = (f32[9,8,128]{2,1,0:T(8,128)S(1)}, f32[9,8,128]{2,1,0:T(8,128)S(1)}, u32[]{:S(2)}, u32[]{:S(2)}) collective-permute-start(f32[9,8,128]{2,1,0:T(8,128)S(1)} %collective-permute-done.13.refs_17_), channel_id=1, source_target_pairs={{0,1},{1,0},{2,3},{3,2},{4,5},{5,4},{6,7},{7,6},{8,9},{9,8},{10,11... | collective-permute-start | bytes 110600 | tf_op jit(solution)/shard_map/ppermute | solution.py:32
  52.6 4.0 %collective-permute-start.22 = (f32[21,8,128]{2,1,0:T(8,128)S(1)}, f32[21,8,128]{2,1,0:T(8,128)S(1)}, u32[]{:S(2)}, u32[]{:S(2)}) collective-permute-start(f32[21,8,128]{2,1,0:T(8,128)S(1)} %get-tuple-element.102.refs_11_.refs_9_), channel_id=1, source_target_pairs={{0,1},{1,0},{2,4},{3,5},{4,2},{5,3},{6,8},{7,9},{8,6},{9,7},{10,12... | collective-permute-start | bytes 258056 | tf_op jit(solution)/shard_map/ppermute | solution.py:45
  52.8 5.2 %collective-permute-start.23 = (f32[21,8,128]{2,1,0:T(8,128)S(1)}, f32[21,8,128]{2,1,0:T(8,128)S(1)}, u32[]{:S(2)}, u32[]{:S(2)}) collective-permute-start(f32[21,8,128]{2,1,0:T(8,128)S(1)} %get-tuple-element.103.refs_10_.refs_11_), channel_id=1, source_target_pairs={{0,2},{1,3},{2,0},{3,1},{4,6},{5,7},{6,4},{7,5},{8,10},{9,11},{10,... | collective-permute-start | bytes 258056 | tf_op jit(solution)/shard_map/ppermute | solution.py:45
  59.2 4.3 %collective-permute-start.24 = (f32[21,8,128]{2,1,0:T(8,128)S(1)}, f32[21,8,128]{2,1,0:T(8,128)S(1)}, u32[]{:S(2)}, u32[]{:S(2)}) collective-permute-start(f32[21,8,128]{2,1,0:T(8,128)S(1)} %get-tuple-element.107.refs_11_.refs_9_), channel_id=1, source_target_pairs={{0,1},{1,0},{2,4},{3,5},{4,2},{5,3},{6,8},{7,9},{8,6},{9,7},{10,12... | collective-permute-start | bytes 258056 | tf_op jit(solution)/shard_map/ppermute | solution.py:45
  59.2 6.0 %collective-permute-start.25 = (f32[21,8,128]{2,1,0:T(8,128)S(1)}, f32[21,8,128]{2,1,0:T(8,128)S(1)}, u32[]{:S(2)}, u32[]{:S(2)}) collective-permute-start(f32[21,8,128]{2,1,0:T(8,128)S(1)} %get-tuple-element.108.refs_10_.refs_11_), channel_id=1, source_target_pairs={{0,2},{1,3},{2,0},{3,1},{4,6},{5,7},{6,4},{7,5},{8,10},{9,11},{10,... | collective-permute-start | bytes 258056 | tf_op jit(solution)/shard_map/ppermute | solution.py:45
  (17 other events, 115.2 us)

commit v5 on v4

--- a/solution.py
+++ b/solution.py
@@ -18,6 +18,7 @@
 LANES = 128
 TILES = B**3 // LANES
 PACK = LANES // G
+CHEM = 4
 HEAT = 0.5
 ENERGY = 2.0
 FAR = -(1 << 20)
@@ -421,34 +422,11 @@
     return result
 
 
-def mix_kernel(
-    saved_f, saved_c, seed_f, seed_c, shares, pay, payc, fine, coarse, seeds,
-    fine_sem, coarse_sem, seed_sem, seeds_sem,
-):
+def mix_fine(saved_f, shares, pay, fine, sems):
     steps, fields = saved_f.shape[0], saved_f.shape[1]
-    cycles, blocks = saved_c.shape[0], saved_c.shape[2]
-    copies = [
-        pltpu.make_async_copy(saved_f.at[s], fine.at[s], fine_sem.at[s]) for s in range(steps)
-    ]
-    copy_c = pltpu.make_async_copy(saved_c, coarse, coarse_sem)
-    copy_s = pltpu.make_async_copy(seed_f.at[0], pay.at[2 * steps], seed_sem)
-    copy_seeds = pltpu.make_async_copy(seed_c, seeds, seeds_sem)
-    copy_c.start()
-    copy_seeds.start()
+    copies = [pltpu.make_async_copy(saved_f.at[s], fine.at[s], sems.at[s]) for s in range(steps)]
     for copy in copies:
         copy.start()
-    copy_s.start()
-    copy_c.wait()
-    for c in range(cycles):
-        total = shares[0] * coarse[c, 0]
-        for v in range(1, fields):
-            total = total + shares[v] * coarse[c, v]
-        payc[0, pl.ds(c * blocks, blocks), :] = total
-        payc[1, pl.ds(c * blocks, blocks), :] = coarse[c, 0]
-    copy_seeds.wait()
-    for v in range(fields):
-        payc[2 + v, pl.ds(0, blocks), :] = seeds[v]
-        payc[2 + v, pl.ds(blocks, blocks), :] = seeds[v]
     for s in range(steps):
         copies[s].wait()
         total = shares[0] * fine[s, 0]
@@ -456,55 +434,75 @@
             total = total + shares[v] * fine[s, v]
         pay[s] = total
         pay[steps + s] = fine[s, 0]
-    copy_s.wait()
-
-
-def reaction_tables(mix, start, counts):
+
+
+def mix_coarse(saved_c, seed_c, shares, after, payc):
+    fields, blocks = saved_c.shape[1], saved_c.shape[2]
+    for c in range(saved_c.shape[0]):
+        total = shares[0] * saved_c[c, 0]
+        for v in range(1, fields):
+            total = total + shares[v] * saved_c[c, v]
+        payc[0, pl.ds(c * blocks, blocks), :] = total
+        payc[1, pl.ds(c * blocks, blocks), :] = saved_c[c, 0]
+    for v in range(fields):
+        payc[2 + v, pl.ds(0, blocks), :] = seed_c[v]
+        payc[2 + v, pl.ds(blocks, blocks), :] = seed_c[v]
+
+
+def substeps(counts):
     step = HEAT / counts.astype(F32)
+    return [jnp.where(n < counts, step, 0.0) for n in range(NSUB)]
+
+
+def reaction_tables(mix, start, steps):
     state = start
     history = []
-    for n in range(NSUB):
+    for step in steps:
         inverse = 1.0 / state
         decay = jnp.exp(-ENERGY * inverse)
-        active = n < counts
-        history.append((active, inverse, decay))
-        state = state + jnp.where(active, step * mix * decay, 0.0)
+        rise = step * mix * decay
+        history.append((step * decay, rise * (inverse * inverse)))
+        state = state + rise
     passed = jnp.ones_like(start)
     weight = jnp.zeros_like(start)
-    for active, inverse, decay in reversed(history):
-        grown = jnp.where(active, step * decay, 0.0)
+    for grown, slope in reversed(history):
         weight = weight + grown * passed
-        passed = passed * (1.0 + grown * mix * ENERGY * (inverse * inverse))
+        passed = passed + passed * (ENERGY * slope)
     return passed - 1.0, weight
 
 
-def chem_kernel(pay, pay_o, fine_counts, pack, gain, weight, edges, planes):
+def chem_kernel(which, pay, pay_o, fine_counts, pack, after, gain, weight, edges, planes):
     core = lax.axis_index("fld")
-    steps = gain.shape[0]
-    rows = row_ids()
-    counts = jnp.ones((8, LANES), jnp.int32)
+    every = pay.shape[0] // 2
+    shape = (8, CHEM * LANES)
+    rows = lax.broadcasted_iota(jnp.int32, shape, 0)
+    counts = jnp.ones(shape, jnp.int32)
     for b in range(fine_counts.shape[0]):
         counts = jnp.where(rows == b, fine_counts[b], counts)
+    lengths = substeps(counts)
 
     def body(t, carry):
-        at = pl.ds(pl.multiple_of(t * LANES, LANES), LANES)
-        for s in range(steps):
-            start = pick(core, pay[steps + s, :, at], pay_o[steps + s, :, at])
-            a, w = reaction_tables(pay[s, :, at] + pay_o[s, :, at], start, counts)
-            gain[s, :, at] = a
-            weight[s, :, at] = w
+        at = pl.ds(pl.multiple_of(t * CHEM * LANES, CHEM * LANES), CHEM * LANES)
+        for n, s in enumerate(which):
+            start = pick(core, pay[every + s, :, at], pay_o[every + s, :, at])
+            a, w = reaction_tables(pay[s, :, at] + pay_o[s, :, at], start, lengths)
+            gain[n, :, at] = a
+            weight[n, :, at] = w
         return carry
 
-    lax.fori_loop(0, TILES, body, 0)
-    for n, table in enumerate((gain, weight)):
-        for s in range(steps - 1):
+    lax.fori_loop(0, TILES // CHEM, body, 0)
+    later = [n for n, s in enumerate(which) if s < every - 1]
+    for m, table in enumerate((gain, weight)):
+        for order, n in enumerate(later):
             for i in range(0, B, 2):
                 for jh in range(2):
                     put_split(
                         planes,
-                        rows_of((n * (steps - 1) + s) * HG + i % HG, 2),
+                        rows_of((m * len(later) + order) * HG + i % HG, 2),
                         (i // HG,),
-                        jnp.concatenate([table[s, :, cols(i, jh)], table[s, :, cols(i + 1, jh)]], axis=0),
+                        jnp.concatenate(
+                            [table[n, :, cols(i, jh)], table[n, :, cols(i + 1, jh)]], axis=0
+                        ),
                         half(jh),
                         half(2 + jh),
                     )
@@ -520,12 +518,13 @@
     rows = lax.broadcasted_iota(jnp.int32, shape, 0)
     for r in range(entries):
         counts = jnp.where(rows == r, coarse_counts[r % blocks], counts)
+    lengths = substeps(counts)
 
     def body(t, carry):
         at = pl.ds(pl.multiple_of(t * 4 * LANES, 4 * LANES), 4 * LANES)
         start = pick(core, payc[1, :, at], payc_o[1, :, at])
         gain[:, at], weight[:, at] = reaction_tables(
-            payc[0, :, at] + payc_o[0, :, at], start, counts
+            payc[0, :, at] + payc_o[0, :, at], start, lengths
         )
         return carry
 
@@ -825,7 +824,7 @@
             at = cols(i, jh)
             for s in range(fields):
                 out[s, jh, rows_of(i), :] = r.seed_f[s, :, at]
-            out[fields, jh, rows_of(i), :] = pick(core, r.seed[0, :, at], r.seed_other[0, :, at])
+            out[fields, jh, rows_of(i), :] = pick(core, r.seed_f[0, :, at], r.seed_other[0, :, at])
     entries = [own_slots(fields, r.local)]
     for n in range(last):
         entries.append(all_fields(core, fields, getattr(r, numbered("landed", n))))
@@ -854,6 +853,14 @@
     even = lax.axis_index("blk") % 2 == 0
     pl.when(even)(lambda: action(r.sent_e, r.sent_o, r.got_o, r.got_e))
     pl.when(jnp.logical_not(even))(lambda: action(r.sent_o, r.sent_e, r.got_e, r.got_o))
+
+
+def react_bulk(plan, r, out):
+    slots = plan.fields + 1
+    par, par_o = (r.dif, r.shr), (r.dif_o, r.shr_o)
+    react_fine(out, plan.fields, par, par_o, r.gain.at[plan.step], r.weight.at[plan.step])
+    build_planes(out, slots, r.planes)
+    r.faces_out[...] = pack_faces(r.planes, r.pack, slots * HG * 8)
 
 
 def bulk_kernel(plan, names, *refs):
@@ -923,28 +930,36 @@
         r,
         finish,
     )
-    if plan.add:
-        near = r.near_octant
-
-        def take(ref):
-            for n in range(slots + 1):
-                near[n] = ref[plan.near_at + n]
-
-        pl.when(even)(lambda: take(r.near_o))
-        pl.when(jnp.logical_not(even))(lambda: take(r.near_e))
-        entries = [own_slots(fields, r.local), own_slots(fields, near)]
-        for n in range(len(plan.later)):
-            entries.append(all_fields(core, fields, getattr(r, numbered("landed", n))))
-            entries.append(all_fields(core, fields, getattr(r, numbered("shared", n))))
-        add_octants(entries, out, r.stage, fields)
-    if not plan.final:
-        step = plan.step
-        react_fine(out, fields, par, par_o, r.gain.at[step], r.weight.at[step])
-        build_planes(out, slots, r.planes)
-        r.faces_out[...] = pack_faces(r.planes, r.pack, slots * HG * 8)
+    if not plan.final and not plan.pause:
+        react_bulk(plan, r, out)
+
+
+def resume_kernel(plan, names, *refs):
+    r = SimpleNamespace(**dict(zip(names, refs)))
+    core = lax.axis_index("fld")
+    even = lax.axis_index("blk") % 2 == 0
+    fields = plan.fields
+    slots = fields + 1
+    out = r.state_out
+    out[...] = r.state[...]
+    near = r.near_octant
+
+    def take(ref):
+        for n in range(slots + 1):
+            near[n] = ref[plan.near_at + n]
+
+    pl.when(even)(lambda: take(r.near_o))
+    pl.when(jnp.logical_not(even))(lambda: take(r.near_e))
+    entries = [own_slots(fields, r.local), own_slots(fields, near)]
+    for n in range(len(plan.later)):
+        entries.append(all_fields(core, fields, getattr(r, numbered("landed", n))))
+        entries.append(own_slots(fields, r.shared, n * (slots + 1)))
+    add_octants(entries, out, r.stage, fields)
+    react_bulk(plan, r, out)
 
 
 def edge_kernel(plan, names, *refs):
+    sems = refs[-1]
     r = SimpleNamespace(**dict(zip(names, refs)))
     core = lax.axis_index("fld")
     fields = plan.fields
@@ -961,6 +976,12 @@
             far_a[n] = above[n]
 
     by_parity(sort_strips, r)
+    if plan.share:
+        for n in range(len(plan.later)):
+            tile = all_fields(1 - core, fields, getattr(r, numbered("landed", n)))
+            for s in range(slots):
+                r.shared[n * (slots + 1) + s] = tile(s)
+            r.shared[n * (slots + 1) + slots] = tile(None)
     faces = own_up[arrived * HG]
     rates = rates_of(plan, r)
     near = links_maker(plan, faces, 0, slots)
@@ -1016,7 +1037,7 @@
                 added.append(jnp.where(outer, value, inner))
             if not plan.final:
                 gain = r.edges[rows_of(plan.step * HG + h), half(n)]
-                weight = r.edges[rows_of((plan.steps + plan.step) * HG + h), half(n)]
+                weight = r.edges[rows_of((plan.packed + plan.step) * HG + h), half(n)]
                 driver = added[fields]
                 heat, grown = weight * driver, gain * driver
                 for s in range(slots):
@@ -1030,12 +1051,17 @@
         r.ends[:, pl.ds(0, 2 * LANES)] = high
         r.ends[:, pl.ds(2 * LANES, 2 * LANES)] = low
         place_ends(r.ends, r.placed, slabs * HG * 8, r)
+        copies = []
         for s in range(slabs):
             for i in range(B):
                 for jh in range(2):
-                    r.state_out[s, :, cols(i, jh)] = r.state[s, jh, rows_of(i), :] + placed_tile(
+                    r.result[s, :, cols(i, jh)] = r.state[s, jh, rows_of(i), :] + placed_tile(
                         r.placed, s, i, jh
                     )
+            copies.append(pltpu.make_async_copy(r.result.at[s], r.state_out.at[s], sems.at[s]))
+            copies[s].start()
+        for copy in copies:
+            copy.wait()
         return
 
     def send(up, down):
@@ -1053,7 +1079,7 @@
 SCALARS = ("dif", "shr", "dif_o", "shr_o", "children", "fine_counts", "coarse_counts")
 MATS = ("plane", "side", "place", "pack", "far")
 MIB = 1024 * 1024
-LIMIT = 60
+LIMIT = 51
 
 
 def call(kernel, inputs, outputs, scratch, hbm=(), sems=(), limit=None, cost=1000):
@@ -1074,7 +1100,7 @@
         functools.partial(kernel, names),
         out_shape=[jax.ShapeDtypeStruct(shape, F32) for shape in outputs.values()],
         in_specs=[spec(name) for name in inputs],
-        out_specs=[VMEM] * len(outputs),
+        out_specs=[spec(name) for name in outputs],
         scratch_shapes=[pltpu.VMEM(value[:-1], value[-1]) for value in scratch.values()]
         + [pltpu.SemaphoreType.DMA(shape) for shape in sems],
         compiler_params=pltpu.CompilerParams(vmem_limit_bytes=limit or int(size) + 12 * MIB),
@@ -1144,28 +1170,28 @@
 
     stage_work = dict(stage=(1, slots, 8 * H, LANES))
     dif_o, shr_o = core_swap(diffusion), core_swap(species_shares)
-    paid = call(
-        plain(mix_kernel),
-        dict(
-            saved_f=saved_fine,
-            saved_c=saved_coarse,
-            seed_f=seed_fine,
-            seed_c=seed_coarse,
-            shr=species_shares,
-        ),
-        dict(
-            pay=(2 * steps + 1, count_f, cells), payc=(2 + fields, cycles * count_c, cells)
-        ),
-        dict(fine=saved_fine.shape, coarse=saved_coarse.shape, seeds=seed_coarse.shape),
-        hbm=("saved_f", "saved_c", "seed_f", "seed_c"),
-        sems=((steps,), (), (), ()),
+    pay = call(
+        plain(mix_fine),
+        dict(saved_f=saved_fine, shr=species_shares),
+        dict(pay=(2 * steps, count_f, cells)),
+        dict(fine=saved_fine.shape),
+        hbm=("saved_f",),
+        sems=((steps,),),
         limit=LIMIT * MIB,
-    )
-    payc = paid.payc
+    ).pay
+    payc = call(
+        plain(mix_coarse),
+        dict(saved_c=saved_coarse, seed_c=seed_coarse, shr=species_shares, after=pay),
+        dict(payc=(2 + fields, cycles * count_c, cells)),
+        {},
+        hbm=("after",),
+    ).payc
     payc_o = core_swap(payc)
-    pay, payc_o, dif_o, shr_o = lax.optimization_barrier((paid.pay, payc_o, dif_o, shr_o))
+    pay, sown, payc_o, dif_o, shr_o = lax.optimization_barrier(
+        (pay, seed_fine, payc_o, dif_o, shr_o)
+    )
     par = dict(dif=diffusion, shr=species_shares, dif_o=dif_o, shr_o=shr_o)
-    pay_o = core_swap(pay)
+    pay_o, seed_o = core_swap(pay), core_swap(sown)
 
     loaded = [numbered("octant", n) for n in range(len(sends) - 2)] + ["up", "down"]
     started = call(
@@ -1193,16 +1219,21 @@
         ),
     )
     landed = [octant_move(getattr(started, name), d) for name, d in zip(loaded, sends)]
-    chem = call(
-        plain(chem_kernel),
-        dict(pay=pay, pay_o=pay_o, fine_counts=fine_counts, pack=mats.pack),
-        dict(
-            gain=(steps, count_f, cells),
-            weight=(steps, count_f, cells),
-            edges=(2 * (steps - 1) * HG * 8, 2 * LANES),
-        ),
-        dict(planes=pack_work(2 * (steps - 1))["planes"]),
-    )
+    def chem_of(which, before):
+        packed = 2 * sum(step < steps - 1 for step in which)
+        return call(
+            plain(chem_kernel, which),
+            dict(pay=pay, pay_o=pay_o, fine_counts=fine_counts, pack=mats.pack, after=before),
+            dict(
+                gain=(len(which), count_f, cells),
+                weight=(len(which), count_f, cells),
+                edges=(packed * HG * 8, 2 * LANES),
+            ),
+            dict(planes=pack_work(packed)["planes"]),
+            hbm=("after",),
+        )
+
+    chem = chem_of(tuple(range(steps)), payc)
     landed, (chem.gain, chem.weight, chem.edges) = lax.optimization_barrier(
         (landed, (chem.gain, chem.weight, chem.edges))
     )
@@ -1224,15 +1255,18 @@
         add=False,
         near_at=every * HG + 1,
         late=0,
-        steps=steps,
-    )
-
-    def run(kernel, changes, inputs, outputs, scratch):
+        share=False,
+        pause=False,
+        packed=0,
+    )
+
+    def run(kernel, changes, inputs, outputs, scratch, **more):
         return call(
             functools.partial(kernel, SimpleNamespace(**{**plan, **changes})),
             dict(par, **vars(mats), **inputs),
             outputs,
             scratch,
+            **more,
         )
 
     def halo(made, ring=False):
@@ -1249,7 +1283,8 @@
         open_kernel,
         dict(slabs_out=every, step=steps - 1),
         dict(
-            vars(chem),
+            gain=chem.gain,
+            weight=chem.weight,
             gain_c=started.gain_c,
             weight_c=started.weight_c,
             children=children,
@@ -1257,8 +1292,7 @@
             own_up=started.up,
             own_down=started.down,
             seed_f=seed_fine,
-            seed=pay[2 * steps :],
-            seed_other=pay_o[2 * steps :],
+            seed_other=seed_o,
             local=started.local,
             **named("landed", landed),
             **named("shared", shared),
@@ -1273,7 +1307,6 @@
     first_halo = halo(made, True)
     landed = [octant_move(getattr(made, numbered("octant", n)), d) for n, d in enumerate(later)]
     landed, arrived_halo = lax.optimization_barrier((landed, first_halo))
-    shared = [core_swap(value) for value in landed]
 
     def edge_work(slabs):
         rows = slabs * HG * 8
@@ -1302,7 +1335,8 @@
     for step in reversed(range(-1, steps - 1)):
         final = step < 0
         slabs = fields if final else held
-        changes = dict(step=step, steps=steps - 1, slabs_in=held, slabs=slabs, final=final)
+        changes = dict(step=step, packed=steps - 1)
+        changes.update(slabs_in=held, slabs=slabs, final=final)
         inputs = dict(state=state, **sent)
         outputs = dict(state_out=state_shape(min(slabs, slots)))
         scratch = dict(work(slabs), **own_strips(held), **pack_work(slabs))
@@ -1320,12 +1354,31 @@
                 inputs.update(coarse=coarse)
                 outputs.update(coarse_final=seed_coarse.shape)
                 scratch.update(coarse_stage=(count_c, 2 * fields, cells))
-        if step == steps - 3:
-            inputs.update(named("landed", landed), **named("shared", shared), local=local)
-            inputs.update(near_e=arrived_halo["got_e"], near_o=arrived_halo["got_o"])
-            scratch.update(stage_work, near_octant=slots_shape)
-            changes.update(add=True)
+        paused = step == steps - 3
+        if paused:
+            for name in ("gain", "weight"):
+                inputs.pop(name)
+            outputs.pop("faces_out")
+            changes.update(pause=True)
         bulk = run(bulk_kernel, changes, inputs, outputs, scratch)
+        if paused:
+            whole = run(
+                resume_kernel,
+                changes,
+                dict(
+                    state=bulk.state_out,
+                    gain=chem.gain,
+                    weight=chem.weight,
+                    near_e=arrived_halo["got_e"],
+                    near_o=arrived_halo["got_o"],
+                    local=local,
+                    shared=shared,
+                    **named("landed", landed),
+                ),
+                dict(state_out=state_shape(slots), faces_out=(slots * HG * 8, 2 * LANES)),
+                dict(pack_work(slots), **stage_work, near_octant=slots_shape),
+            )
+            bulk.state_out, bulk.faces_out = whole.state_out, whole.faces_out
         if coarse is not None:
             coarse_final = bulk.coarse_final
         coarse = bulk.coarse_out if held > slots else None
@@ -1334,13 +1387,22 @@
         if final:
             inputs.update(state=bulk.state_out)
             outputs = dict(state_out=seed_fine.shape)
-            scratch.update(late=(slabs * HG * 8, 2 * LANES), **place_work(slabs))
+            scratch.update(
+                late=(slabs * HG * 8, 2 * LANES), result=seed_fine.shape, **place_work(slabs)
+            )
         else:
             inputs.update(edges=chem.edges, faces_in=bulk.faces_out)
             outputs = dict(
                 late=(slabs * HG * 8, 2 * LANES), send_e=strip(slots), send_o=strip(slots)
             )
-        made = run(edge_kernel, changes, inputs, outputs, scratch)
+        if step == steps - 2:
+            inputs.update(named("landed", landed))
+            outputs.update(shared=(len(later) * (slots + 1), 8, LANES))
+            changes.update(share=True)
+        more = dict(hbm=("state_out",), sems=((fields,),)) if final else {}
+        made = run(edge_kernel, changes, inputs, outputs, scratch, **more)
+        if step == steps - 2:
+            shared = core_swap(made.shared)
         if final:
             break
         state, late, held = bulk.state_out, made.late, slots

time: 67.7 us -> 65.6 us (0.969)
  waiting for transfers between devices: 9.3 us -> 11.2 us
  Pallas kernels: 30.1 us -> 28.4 us
  local copies, waits for them, and re-layouts: 2.33 us -> 0.8 us
  starting transfers between devices: 24.6 us -> 23.8 us
    ppermute x7, waiting for transfers between devices: 2.91 us -> 6.67 us  [octant_move(): return lax.ppermute(value, ('blk', 'fld'), pairs)]
    ppermute x7, starting transfers between devices: 11 us -> 8.83 us  [octant_move(): return lax.ppermute(value, ('blk', 'fld'), pairs)]
    pallas_call x12 -> x14, Pallas kernels: 30.1 us -> 28.4 us  [call(): pl.pallas_call(functools.partial(kernel, names), out_shape=[jax.ShapeDtyp...]
    unnamed x30, local copies, waits for them, and re-layouts: 2.31 us -> 0.8 us
    ppermute x11 -> x10, waiting for transfers between devices: 3.09 us -> 1.72 us  [core_swap(): return lax.ppermute(value, 'fld', [(0, 1), (1, 0)])]
    ppermute x8, starting transfers between devices: 10.6 us -> 11.7 us  [pair_swap(): return lax.ppermute(value, ('blk', 'fld'), pairs)]
    ppermute x11 -> x10, starting transfers between devices: 2.95 us -> 3.28 us  [core_swap(): return lax.ppermute(value, 'fld', [(0, 1), (1, 0)])]
  transfers between devices with their start and end apart: 26 -> 25, of which waited for: 12 -> 9; matrix products, arithmetic and copies ran while one was open for 0% -> 0% of each run, Pallas kernels for 27% -> 26%
where the time goes in v5:
time: 65.6 us; the launch traced here: 65.4 us
  Pallas kernels  28.4 us (43%)
  starting transfers between devices  23.8 us (36%)
  waiting for transfers between devices  11.2 us (17%)
  between operations  1.11 us (2%)
  local copies, waits for them, and re-layouts  0.8 us (1%)
    pallas_call x14, Pallas kernels, call(): pl.pallas_call(functools.partial(kernel, names), out_shape=[jax.ShapeDtyp...  28.4 us
    ppermute x8, starting transfers between devices, pair_swap(): return lax.ppermute(value, ('blk', 'fld'), pairs)  11.7 us
    ppermute x7, starting transfers between devices, octant_move(): return lax.ppermute(value, ('blk', 'fld'), pairs)  8.83 us
    ppermute x7, waiting for transfers between devices, octant_move(): return lax.ppermute(value, ('blk', 'fld'), pairs)  6.67 us
    ppermute x10, starting transfers between devices, core_swap(): return lax.ppermute(value, 'fld', [(0, 1), (1, 0)])  3.28 us
    ppermute x8, waiting for transfers between devices, pair_swap(): return lax.ppermute(value, ('blk', 'fld'), pairs)  2.86 us
    ppermute x10, waiting for transfers between devices, core_swap(): return lax.ppermute(value, 'fld', [(0, 1), (1, 0)])  1.72 us
  transfers between devices with their start and end apart: 25, of which 9 were waited for; matrix products, arithmetic and copies ran while one was open for 0% of the time, Pallas kernels for 26%

profile of v5, /device:TPU:0, one launch (start us, length us, event | category | flops | bytes accessed | tf_op | source)
XLA Modules:
  0.0 65.4 jit_solution(872949568265266223)
XLA Ops:
  1.4 2.1 %shard_map.167.refs_3_.refs_0_ = f32[8,8,4096]{2,1,0:T(8,128)S(1)} custom-call(f32[4,4,8,4096]{3,2,1,0:T(8,128)} %refs_0_.12, f32[4]{0:T(128)S(1)} %copy-done.8), custom_call_target="tpu_custom_call" | custom-call | flops 1000 | bytes 1000 | tf_op jit(solution)/shard_map/pallas_call | solution.py:1099
  6.7 2.0 %shard_map.169 = (f32[2,2,128,128]{3,2,1,0:T(8,128)S(1)}, f32[4,4096]{1,0:T(4,128)S(1)}, f32[4,4096]{1,0:T(4,128)S(1)}, f32[6,8,128]{2,1,0:T(8,128)S(1)}, f32[9,...) custom-call(f32[6,4,4096]{2,1,0:T(4,128)S(1)} %shard_map.168.refs_0_.refs_, ...), custom_call_target="tpu_custom_call" | custom-call | flops 1000 | bytes 1000 | tf_op jit(solution)/shard_map/pallas_call | solution.py:1099
  8.7 2.9 %collective-permute-start.5 = (f32[18,8,128]{2,1,0:T(8,128)S(1)}, f32[18,8,128]{2,1,0:T(8,128)S(1)}, u32[]{:S(2)}, u32[]{:S(2)}) collective-permute-start(f32[18,8,128]{2,1,0:T(8,128)S(1)} %get-tuple-element.63.refs_15_), channel_id=1, source_target_pairs={{0,2},{1,13},{2,4},{3,15},{4,6},{5,17},{6,8},{7,19},{8,10},{9,21},... | collective-permute-start | bytes 221192 | tf_op jit(solution)/shard_map/ppermute | solution.py:65
  11.7 4.1 %collective-permute-start.6 = (f32[18,8,128]{2,1,0:T(8,128)S(1)}, f32[18,8,128]{2,1,0:T(8,128)S(1)}, u32[]{:S(2)}, u32[]{:S(2)}) collective-permute-start(f32[18,8,128]{2,1,0:T(8,128)S(1)} %get-tuple-element.64.refs_16_), channel_id=1, source_target_pairs={{0,30},{1,15},{2,0},{3,17},{4,2},{5,19},{6,4},{7,21},{8,6},{9,23},... | collective-permute-start | bytes 221192 | tf_op jit(solution)/shard_map/ppermute | solution.py:65
  16.2 2.3 %shard_map.170 = (f32[4,8,4096]{2,1,0:T(8,128)S(1)}, f32[4,8,4096]{2,1,0:T(8,128)S(1)}, f32[192,256]{1,0:T(8,128)S(1)}) custom-call(f32[8,8,4096]{2,1,0:T(8,128)S(1)} %shard_map.167.refs_3_.refs_0_, f32[8,8,4096]{2,1,0:T(8,128)S(1)} %collective-permute-done.7.refs_1_, s32[8]{0:T(128)S(1)} %copy-done.13, bf16[4,256,256]{2,1,0:T(8,128)(2,1)S(1)} %copy-done, ...), custom_call_target="tpu_custom_call" | custom-call | flops 1000 | bytes 1000 | tf_op jit(solution)/shard_map/pallas_call | solution.py:1099
  18.5 3.9 %collective-permute-done.3.refs_20_ = f32[9,8,128]{2,1,0:T(8,128)S(1)} collective-permute-done((f32[9,8,128]{2,1,0:T(8,128)S(1)}, f32[9,8,128]{2,1,0:T(8,128)S(1)}, u32[]{:S(2)}, u32[]{:S(2)}) %collective-permute-start.3) | collective-permute-done | bytes 36896 | tf_op jit(solution)/shard_map/ppermute | solution.py:65
  24.7 2.8 %shard_map.171 = (f32[7,2,128,128]{3,2,1,0:T(8,128)S(1)}, f32[35,8,128]{2,1,0:T(8,128)S(1)}, f32[35,8,128]{2,1,0:T(8,128)S(1)}, f32[6,8,128]{2,1,0:T(8,128)S(1)}...) custom-call(f32[4]{0:T(128)S(1)} %copy-done.9, f32[4]{0:T(128)S(1)} %copy-done.8, ...), custom_call_target="tpu_custom_call" | custom-call | flops 1000 | bytes 1000 | tf_op jit(solution)/shard_map/pallas_call | solution.py:1099
  27.5 1.5 %collective-permute-start.16 = (f32[35,8,128]{2,1,0:T(8,128)S(1)}, f32[35,8,128]{2,1,0:T(8,128)S(1)}, u32[]{:S(2)}, u32[]{:S(2)}) collective-permute-start(f32[35,8,128]{2,1,0:T(8,128)S(1)} %get-tuple-element.87.refs_10_.refs_11_), channel_id=1, source_target_pairs={{0,2},{1,3},{2,0},{3,1},{4,6},{5,7},{6,4},{7,5},{8,10},{9,11},{10,... | collective-permute-start | bytes 430088 | tf_op jit(solution)/shard_map/ppermute | solution.py:46
  29.1 2.7 %collective-permute-start.17 = (f32[35,8,128]{2,1,0:T(8,128)S(1)}, f32[35,8,128]{2,1,0:T(8,128)S(1)}, u32[]{:S(2)}, u32[]{:S(2)}) collective-permute-start(f32[35,8,128]{2,1,0:T(8,128)S(1)} %get-tuple-element.88.refs_11_.refs_12_), channel_id=1, source_target_pairs={{0,30},{1,31},{2,4},{3,5},{4,2},{5,3},{6,8},{7,9},{8,6},{9,7},{10,... | collective-permute-start | bytes 430088 | tf_op jit(solution)/shard_map/ppermute | solution.py:46
  32.0 1.3 %collective-permute-start.15 = (f32[9,8,128]{2,1,0:T(8,128)S(1)}, f32[9,8,128]{2,1,0:T(8,128)S(1)}, u32[]{:S(2)}, u32[]{:S(2)}) collective-permute-start(f32[9,8,128]{2,1,0:T(8,128)S(1)} %get-tuple-element.82), channel_id=1, source_target_pairs={{0,8},{1,15},{2,10},{3,17},{4,12},{5,19},{6,14},{7,21},{8,16},{9,2... | collective-permute-start | bytes 110600 | tf_op jit(solution)/shard_map/ppermute | solution.py:65
  33.2 3.2 %shard_map.172 = (f32[5,2,128,128]{3,2,1,0:T(8,128)S(1)}, f32[160,256]{1,0:T(8,128)S(1)}, f32[2,2,128,128]{3,2,1,0:T(8,128)S(1)}) custom-call(f32[4]{0:T(128)S(1)} %copy-done.9, f32[4]{0:T(128)S(1)} %copy-done.8, f32[4]{0:T(128)S(1)} %collective-permute-done.1.refs_6_.refs_2_, f32[4]{0:T(128)S(1)} %collective-permute-done.2.refs_7_.refs_3_, ...), custom_call_target="tpu_custom_call" | custom-call | flops 1000 | bytes 1000 | tf_op jit(solution)/shard_map/pallas_call | solution.py:1099
  36.5 2.4 %collective-permute-done.13.refs_15_.refs_16_ = f32[9,8,128]{2,1,0:T(8,128)S(1)} collective-permute-done((f32[9,8,128]{2,1,0:T(8,128)S(1)}, f32[9,8,128]{2,1,0:T(8,128)S(1)}, u32[]{:S(2)}, u32[]{:S(2)}) %collective-permute-start.13) | collective-permute-done | bytes 36896 | tf_op jit(solution)/shard_map/ppermute | solution.py:65
  39.4 1.3 %shard_map.173 = (f32[224,256]{1,0:T(8,128)S(1)}, f32[21,8,128]{2,1,0:T(8,128)S(1)}, f32[21,8,128]{2,1,0:T(8,128)S(1)}, f32[18,8,128]{2,1,0:T(8,128)S(1)}) custom-call(f32[4]{0:T(128)S(1)} %copy-done.9, f32[4]{0:T(128)S(1)} %copy-done.8, f32[4]{0:T(128)S(1)} %collective-permute-done.1.refs_6_.refs_2_, f32[4]{0:T(128)S(1)} %collective-permute-done.2.refs_7_.refs_3_, ...), custom_call_target="tpu_custom_call" | custom-call | flops 1000 | bytes 1000 | tf_op jit(solution)/shard_map/pallas_call | solution.py:1099
  40.7 1.7 %collective-permute-start.18 = (f32[21,8,128]{2,1,0:T(8,128)S(1)}, f32[21,8,128]{2,1,0:T(8,128)S(1)}, u32[]{:S(2)}, u32[]{:S(2)}) collective-permute-start(f32[21,8,128]{2,1,0:T(8,128)S(1)} %get-tuple-element.95.refs_11_.refs_9_), channel_id=1, source_target_pairs={{0,1},{1,0},{2,4},{3,5},{4,2},{5,3},{6,8},{7,9},{8,6},{9,7},{10,12... | collective-permute-start | bytes 258056 | tf_op jit(solution)/shard_map/ppermute | solution.py:46
  42.4 1.5 %collective-permute-start.19 = (f32[21,8,128]{2,1,0:T(8,128)S(1)}, f32[21,8,128]{2,1,0:T(8,128)S(1)}, u32[]{:S(2)}, u32[]{:S(2)}) collective-permute-start(f32[21,8,128]{2,1,0:T(8,128)S(1)} %get-tuple-element.96.refs_10_.refs_11_), channel_id=1, source_target_pairs={{0,2},{1,3},{2,0},{3,1},{4,6},{5,7},{6,4},{7,5},{8,10},{9,11},{10,... | collective-permute-start | bytes 258056 | tf_op jit(solution)/shard_map/ppermute | solution.py:46
  44.6 3.1 %shard_map.174 = (f32[5,2,128,128]{3,2,1,0:T(8,128)S(1)}, f32[4,2,4096]{2,1,0:T(2,128)}) custom-call(f32[4]{0:T(128)S(1)} %copy-done.9, f32[4]{0:T(128)S(1)} %copy-done.8, f32[4]{0:T(128)S(1)} %collective-permute-done.1.refs_6_.refs_2_, f32[4]{0:T(128)S(1)} %collective-permute-done.2.refs_7_.refs_3_, bf16[256,256]{1,0:T(8,128)(2,1)S(1)} %copy-done.2, ...), custom_call_target="tpu_custom_call" | custom-call | flops 1000 | bytes 1000 | tf_op jit(solution)/shard_map/pallas_call | solution.py:1099
  47.7 1.3 %shard_map.175 = (f32[5,2,128,128]{3,2,1,0:T(8,128)S(1)}, f32[160,256]{1,0:T(8,128)S(1)}) custom-call(f32[4]{0:T(128)S(1)} %copy-done.9, f32[4]{0:T(128)S(1)} %copy-done.8, f32[4]{0:T(128)S(1)} %collective-permute-done.1.refs_6_.refs_2_, f32[4]{0:T(128)S(1)} %collective-permute-done.2.refs_7_.refs_3_, bf16[256,256]{1,0:T(8,128)(2,1)S(1)} %copy-done.2, ...), custom_call_target="tpu_custom_call" | custom-call | flops 1000 | bytes 1000 | tf_op jit(solution)/shard_map/pallas_call | solution.py:1099
  50.2 1.4 %collective-permute-start.22 = (f32[21,8,128]{2,1,0:T(8,128)S(1)}, f32[21,8,128]{2,1,0:T(8,128)S(1)}, u32[]{:S(2)}, u32[]{:S(2)}) collective-permute-start(f32[21,8,128]{2,1,0:T(8,128)S(1)} %get-tuple-element.105.refs_10_.refs_11_), channel_id=1, source_target_pairs={{0,2},{1,3},{2,0},{3,1},{4,6},{5,7},{6,4},{7,5},{8,10},{9,11},{10,... | collective-permute-start | bytes 258056 | tf_op jit(solution)/shard_map/ppermute | solution.py:46
  51.6 3.1 %shard_map.177 = (f32[5,2,128,128]{3,2,1,0:T(8,128)S(1)}, f32[160,256]{1,0:T(8,128)S(1)}) custom-call(f32[4]{0:T(128)S(1)} %copy-done.9, f32[4]{0:T(128)S(1)} %copy-done.8, f32[4]{0:T(128)S(1)} %collective-permute-done.1.refs_6_.refs_2_, f32[4]{0:T(128)S(1)} %collective-permute-done.2.refs_7_.refs_3_, bf16[256,256]{1,0:T(8,128)(2,1)S(1)} %copy-done.2, ...), custom_call_target="tpu_custom_call" | custom-call | flops 1000 | bytes 1000 | tf_op jit(solution)/shard_map/pallas_call | solution.py:1099
  54.7 1.2 %collective-permute-done.22.refs_12_ = f32[21,8,128]{2,1,0:T(8,128)S(1)} collective-permute-done((f32[21,8,128]{2,1,0:T(8,128)S(1)}, f32[21,8,128]{2,1,0:T(8,128)S(1)}, u32[]{:S(2)}, u32[]{:S(2)}) %collective-permute-start.22) | collective-permute-done | bytes 86048 | tf_op jit(solution)/shard_map/ppermute | solution.py:46
  57.1 2.7 %collective-permute-start.24 = (f32[21,8,128]{2,1,0:T(8,128)S(1)}, f32[21,8,128]{2,1,0:T(8,128)S(1)}, u32[]{:S(2)}, u32[]{:S(2)}) collective-permute-start(f32[21,8,128]{2,1,0:T(8,128)S(1)} %get-tuple-element.110.refs_10_.refs_11_), channel_id=1, source_target_pairs={{0,2},{1,3},{2,0},{3,1},{4,6},{5,7},{6,4},{7,5},{8,10},{9,11},{10,... | collective-permute-start | bytes 258056 | tf_op jit(solution)/shard_map/ppermute | solution.py:46
  59.8 2.2 %shard_map.179.refs_13_ = f32[4,2,128,128]{3,2,1,0:T(8,128)S(1)} custom-call(f32[4]{0:T(128)S(1)} %copy-done.9, f32[4]{0:T(128)S(1)} %copy-done.8, f32[4]{0:T(128)S(1)} %collective-permute-done.1.refs_6_.refs_2_, f32[4]{0:T(128)S(1)} %collective-permute-done.2.refs_7_.refs_3_, bf16[256,256]{1,0:T(8,128)(2,1)S(1)} %copy-done.2, ...), custom_call_target="tpu_custom_call" | custom-call | flops 1000 | bytes 1000 | tf_op jit(solution)/shard_map/pallas_call | solution.py:1099
  62.1 1.1 %collective-permute-done.24.refs_12_ = f32[21,8,128]{2,1,0:T(8,128)S(1)} collective-permute-done((f32[21,8,128]{2,1,0:T(8,128)S(1)}, f32[21,8,128]{2,1,0:T(8,128)S(1)}, u32[]{:S(2)}, u32[]{:S(2)}) %collective-permute-start.24) | collective-permute-done | bytes 86048 | tf_op jit(solution)/shard_map/ppermute | solution.py:46
  63.2 2.1 %shard_map.180 = f32[4,8,4096]{2,1,0:T(8,128)} custom-call(f32[4]{0:T(128)S(1)} %copy-done.9, f32[4]{0:T(128)S(1)} %copy-done.8, f32[4]{0:T(128)S(1)} %collective-permute-done.1.refs_6_.refs_2_, f32[4]{0:T(128)S(1)} %collective-permute-done.2.refs_7_.refs_3_, bf16[256,256]{1,0:T(8,128)(2,1)S(1)} %copy-done.2, bf16[128,256]{1,0:T(8,128)(2,1)S(1)} %copy-done.3, ...), custom_call_target="tpu_custom_call" | custom-call | flops 1000 | bytes 1000 | tf_op jit(solution)/shard_map/pallas_call | solution.py:1099
  (70 shorter events, 10.3 us)
Async XLA Ops:
  4.3 1.9 %collective-permute-start = (f32[6,4,4096]{2,1,0:T(4,128)S(1)}, f32[6,4,4096]{2,1,0:T(4,128)S(1)}, u32[]{:S(2)}, u32[]{:S(2)}) collective-permute-start(f32[6,4,4096]{2,1,0:T(4,128)S(1)} %shard_map.168.refs_0_.refs_4_), channel_id=1, source_target_pairs={{0,1},{1,0},{2,3},{3,2},{4,5},{5,4},{6,7},{7,6},{8,9},{9,8},{10,11... | collective-permute-start | bytes 1179656 | tf_op jit(solution)/shard_map/ppermute | solution.py:33
  4.8 1.4 %collective-permute-start.2 = (f32[4]{0:T(128)S(1)}, f32[4]{0:T(128)S(1)}, u32[]{:S(2)}, u32[]{:S(2)}) collective-permute-start(f32[4]{0:T(128)S(1)} %copy-done.8), channel_id=1, source_target_pairs={{0,1},{1,0},{2,3},{3,2},{4,5},{5,4},{6,7},{7,6},{8,9},{9,8},{10,11... | collective-permute-start | bytes 56 | tf_op jit(solution)/shard_map/ppermute | solution.py:33
  4.9 1.3 %collective-permute-start.1 = (f32[4]{0:T(128)S(1)}, f32[4]{0:T(128)S(1)}, u32[]{:S(2)}, u32[]{:S(2)}) collective-permute-start(f32[4]{0:T(128)S(1)} %copy-done.9), channel_id=1, source_target_pairs={{0,1},{1,0},{2,3},{3,2},{4,5},{5,4},{6,7},{7,6},{8,9},{9,8},{10,11... | collective-permute-start | bytes 56 | tf_op jit(solution)/shard_map/ppermute | solution.py:33
  6.2 9.5 %collective-permute-start.7 = (f32[8,8,4096]{2,1,0:T(8,128)S(1)}, f32[8,8,4096]{2,1,0:T(8,128)S(1)}, u32[]{:S(2)}, u32[]{:S(2)}) collective-permute-start(f32[8,8,4096]{2,1,0:T(8,128)S(1)} %shard_map.167.refs_3_.refs_0_), channel_id=1, source_target_pairs={{0,1},{1,0},{2,3},{3,2},{4,5},{5,4},{6,7},{7,6},{8,9},{9,8},{10,11... | collective-permute-start | bytes 3145736 | tf_op jit(solution)/shard_map/ppermute | solution.py:33
  6.6 17.2 %collective-permute-start.8 = (f32[4,8,4096]{2,1,0:T(8,128)S(1)}, f32[4,8,4096]{2,1,0:T(8,128)S(1)}, u32[]{:S(2)}, u32[]{:S(2)}) collective-permute-start(f32[4,8,4096]{2,1,0:T(8,128)S(1)} %copy-done.5), channel_id=1, source_target_pairs={{0,1},{1,0},{2,3},{3,2},{4,5},{5,4},{6,7},{7,6},{8,9},{9,8},{10,11... | collective-permute-start | bytes 1572872 | tf_op jit(solution)/shard_map/ppermute | solution.py:33
  8.7 14.0 %collective-permute-start.5 = (f32[18,8,128]{2,1,0:T(8,128)S(1)}, f32[18,8,128]{2,1,0:T(8,128)S(1)}, u32[]{:S(2)}, u32[]{:S(2)}) collective-permute-start(f32[18,8,128]{2,1,0:T(8,128)S(1)} %get-tuple-element.63.refs_15_), channel_id=1, source_target_pairs={{0,2},{1,13},{2,4},{3,15},{4,6},{5,17},{6,8},{7,19},{8,10},{9,21},... | collective-permute-start | bytes 221192 | tf_op jit(solution)/shard_map/ppermute | solution.py:65
  11.7 11.1 %collective-permute-start.6 = (f32[18,8,128]{2,1,0:T(8,128)S(1)}, f32[18,8,128]{2,1,0:T(8,128)S(1)}, u32[]{:S(2)}, u32[]{:S(2)}) collective-permute-start(f32[18,8,128]{2,1,0:T(8,128)S(1)} %get-tuple-element.64.refs_16_), channel_id=1, source_target_pairs={{0,30},{1,15},{2,0},{3,17},{4,2},{5,19},{6,4},{7,21},{8,6},{9,23},... | collective-permute-start | bytes 221192 | tf_op jit(solution)/shard_map/ppermute | solution.py:65
  15.7 6.7 %collective-permute-start.3 = (f32[9,8,128]{2,1,0:T(8,128)S(1)}, f32[9,8,128]{2,1,0:T(8,128)S(1)}, u32[]{:S(2)}, u32[]{:S(2)}) collective-permute-start(f32[9,8,128]{2,1,0:T(8,128)S(1)} %get-tuple-element.61), channel_id=1, source_target_pairs={{0,4},{1,9},{2,6},{3,11},{4,8},{5,13},{6,10},{7,15},{8,12},{9,17},... | collective-permute-start | bytes 110600 | tf_op jit(solution)/shard_map/ppermute | solution.py:65
  15.7 7.0 %collective-permute-start.4 = (f32[9,8,128]{2,1,0:T(8,128)S(1)}, f32[9,8,128]{2,1,0:T(8,128)S(1)}, u32[]{:S(2)}, u32[]{:S(2)}) collective-permute-start(f32[9,8,128]{2,1,0:T(8,128)S(1)} %get-tuple-element.62), channel_id=1, source_target_pairs={{0,6},{1,11},{2,8},{3,13},{4,10},{5,15},{6,12},{7,17},{8,14},{9,19... | collective-permute-start | bytes 110600 | tf_op jit(solution)/shard_map/ppermute | solution.py:65
  22.8 1.9 %collective-permute-start.11 = (f32[18,8,128]{2,1,0:T(8,128)S(1)}, f32[18,8,128]{2,1,0:T(8,128)S(1)}, u32[]{:S(2)}, u32[]{:S(2)}) collective-permute-start(f32[18,8,128]{2,1,0:T(8,128)S(1)} %collective-permute-done.5.refs_22_), channel_id=1, source_target_pairs={{0,1},{1,0},{2,3},{3,2},{4,5},{5,4},{6,7},{7,6},{8,9},{9,8},{10,11... | collective-permute-start | bytes 221192 | tf_op jit(solution)/shard_map/ppermute | solution.py:33
  22.8 1.9 %collective-permute-start.12 = (f32[18,8,128]{2,1,0:T(8,128)S(1)}, f32[18,8,128]{2,1,0:T(8,128)S(1)}, u32[]{:S(2)}, u32[]{:S(2)}) collective-permute-start(f32[18,8,128]{2,1,0:T(8,128)S(1)} %collective-permute-done.6.refs_23_), channel_id=1, source_target_pairs={{0,1},{1,0},{2,3},{3,2},{4,5},{5,4},{6,7},{7,6},{8,9},{9,8},{10,11... | collective-permute-start | bytes 221192 | tf_op jit(solution)/shard_map/ppermute | solution.py:33
  23.4 1.3 %collective-permute-start.9 = (f32[9,8,128]{2,1,0:T(8,128)S(1)}, f32[9,8,128]{2,1,0:T(8,128)S(1)}, u32[]{:S(2)}, u32[]{:S(2)}) collective-permute-start(f32[9,8,128]{2,1,0:T(8,128)S(1)} %collective-permute-done.3.refs_20_), channel_id=1, source_target_pairs={{0,1},{1,0},{2,3},{3,2},{4,5},{5,4},{6,7},{7,6},{8,9},{9,8},{10,11... | collective-permute-start | bytes 110600 | tf_op jit(solution)/shard_map/ppermute | solution.py:33
  27.5 11.3 %collective-permute-start.16 = (f32[35,8,128]{2,1,0:T(8,128)S(1)}, f32[35,8,128]{2,1,0:T(8,128)S(1)}, u32[]{:S(2)}, u32[]{:S(2)}) collective-permute-start(f32[35,8,128]{2,1,0:T(8,128)S(1)} %get-tuple-element.87.refs_10_.refs_11_), channel_id=1, source_target_pairs={{0,2},{1,3},{2,0},{3,1},{4,6},{5,7},{6,4},{7,5},{8,10},{9,11},{10,... | collective-permute-start | bytes 430088 | tf_op jit(solution)/shard_map/ppermute | solution.py:46
  29.1 10.3 %collective-permute-start.17 = (f32[35,8,128]{2,1,0:T(8,128)S(1)}, f32[35,8,128]{2,1,0:T(8,128)S(1)}, u32[]{:S(2)}, u32[]{:S(2)}) collective-permute-start(f32[35,8,128]{2,1,0:T(8,128)S(1)} %get-tuple-element.88.refs_11_.refs_12_), channel_id=1, source_target_pairs={{0,30},{1,31},{2,4},{3,5},{4,2},{5,3},{6,8},{7,9},{8,6},{9,7},{10,... | collective-permute-start | bytes 430088 | tf_op jit(solution)/shard_map/ppermute | solution.py:46
  31.8 7.0 %collective-permute-start.13 = (f32[9,8,128]{2,1,0:T(8,128)S(1)}, f32[9,8,128]{2,1,0:T(8,128)S(1)}, u32[]{:S(2)}, u32[]{:S(2)}) collective-permute-start(f32[9,8,128]{2,1,0:T(8,128)S(1)} %get-tuple-element.80), channel_id=1, source_target_pairs={{0,4},{1,11},{2,6},{3,13},{4,8},{5,15},{6,10},{7,17},{8,12},{9,19}... | collective-permute-start | bytes 110600 | tf_op jit(solution)/shard_map/ppermute | solution.py:65
  31.8 7.0 %collective-permute-start.14 = (f32[9,8,128]{2,1,0:T(8,128)S(1)}, f32[9,8,128]{2,1,0:T(8,128)S(1)}, u32[]{:S(2)}, u32[]{:S(2)}) collective-permute-start(f32[9,8,128]{2,1,0:T(8,128)S(1)} %get-tuple-element.81), channel_id=1, source_target_pairs={{0,6},{1,13},{2,8},{3,15},{4,10},{5,17},{6,12},{7,19},{8,14},{9,21... | collective-permute-start | bytes 110600 | tf_op jit(solution)/shard_map/ppermute | solution.py:65
  32.0 6.9 %collective-permute-start.15 = (f32[9,8,128]{2,1,0:T(8,128)S(1)}, f32[9,8,128]{2,1,0:T(8,128)S(1)}, u32[]{:S(2)}, u32[]{:S(2)}) collective-permute-start(f32[9,8,128]{2,1,0:T(8,128)S(1)} %get-tuple-element.82), channel_id=1, source_target_pairs={{0,8},{1,15},{2,10},{3,17},{4,12},{5,19},{6,14},{7,21},{8,16},{9,2... | collective-permute-start | bytes 110600 | tf_op jit(solution)/shard_map/ppermute | solution.py:65
  40.7 8.3 %collective-permute-start.18 = (f32[21,8,128]{2,1,0:T(8,128)S(1)}, f32[21,8,128]{2,1,0:T(8,128)S(1)}, u32[]{:S(2)}, u32[]{:S(2)}) collective-permute-start(f32[21,8,128]{2,1,0:T(8,128)S(1)} %get-tuple-element.95.refs_11_.refs_9_), channel_id=1, source_target_pairs={{0,1},{1,0},{2,4},{3,5},{4,2},{5,3},{6,8},{7,9},{8,6},{9,7},{10,12... | collective-permute-start | bytes 258056 | tf_op jit(solution)/shard_map/ppermute | solution.py:46
  42.4 6.6 %collective-permute-start.19 = (f32[21,8,128]{2,1,0:T(8,128)S(1)}, f32[21,8,128]{2,1,0:T(8,128)S(1)}, u32[]{:S(2)}, u32[]{:S(2)}) collective-permute-start(f32[21,8,128]{2,1,0:T(8,128)S(1)} %get-tuple-element.96.refs_10_.refs_11_), channel_id=1, source_target_pairs={{0,2},{1,3},{2,0},{3,1},{4,6},{5,7},{6,4},{7,5},{8,10},{9,11},{10,... | collective-permute-start | bytes 258056 | tf_op jit(solution)/shard_map/ppermute | solution.py:46
  43.9 3.8 %collective-permute-start.20 = (f32[18,8,128]{2,1,0:T(8,128)S(1)}, f32[18,8,128]{2,1,0:T(8,128)S(1)}, u32[]{:S(2)}, u32[]{:S(2)}) collective-permute-start(f32[18,8,128]{2,1,0:T(8,128)S(1)} %get-tuple-element.102), channel_id=1, source_target_pairs={{0,1},{1,0},{2,3},{3,2},{4,5},{5,4},{6,7},{7,6},{8,9},{9,8},{10,11... | collective-permute-start | bytes 221192 | tf_op jit(solution)/shard_map/ppermute | solution.py:33
  50.2 4.6 %collective-permute-start.21 = (f32[21,8,128]{2,1,0:T(8,128)S(1)}, f32[21,8,128]{2,1,0:T(8,128)S(1)}, u32[]{:S(2)}, u32[]{:S(2)}) collective-permute-start(f32[21,8,128]{2,1,0:T(8,128)S(1)} %get-tuple-element.104.refs_11_.refs_9_), channel_id=1, source_target_pairs={{0,1},{1,0},{2,4},{3,5},{4,2},{5,3},{6,8},{7,9},{8,6},{9,7},{10,12... | collective-permute-start | bytes 258056 | tf_op jit(solution)/shard_map/ppermute | solution.py:46
  50.2 5.7 %collective-permute-start.22 = (f32[21,8,128]{2,1,0:T(8,128)S(1)}, f32[21,8,128]{2,1,0:T(8,128)S(1)}, u32[]{:S(2)}, u32[]{:S(2)}) collective-permute-start(f32[21,8,128]{2,1,0:T(8,128)S(1)} %get-tuple-element.105.refs_10_.refs_11_), channel_id=1, source_target_pairs={{0,2},{1,3},{2,0},{3,1},{4,6},{5,7},{6,4},{7,5},{8,10},{9,11},{10,... | collective-permute-start | bytes 258056 | tf_op jit(solution)/shard_map/ppermute | solution.py:46
  57.0 5.0 %collective-permute-start.23 = (f32[21,8,128]{2,1,0:T(8,128)S(1)}, f32[21,8,128]{2,1,0:T(8,128)S(1)}, u32[]{:S(2)}, u32[]{:S(2)}) collective-permute-start(f32[21,8,128]{2,1,0:T(8,128)S(1)} %get-tuple-element.109.refs_11_.refs_9_), channel_id=1, source_target_pairs={{0,1},{1,0},{2,4},{3,5},{4,2},{5,3},{6,8},{7,9},{8,6},{9,7},{10,12... | collective-permute-start | bytes 258056 | tf_op jit(solution)/shard_map/ppermute | solution.py:46
  57.1 6.1 %collective-permute-start.24 = (f32[21,8,128]{2,1,0:T(8,128)S(1)}, f32[21,8,128]{2,1,0:T(8,128)S(1)}, u32[]{:S(2)}, u32[]{:S(2)}) collective-permute-start(f32[21,8,128]{2,1,0:T(8,128)S(1)} %get-tuple-element.110.refs_10_.refs_11_), channel_id=1, source_target_pairs={{0,2},{1,3},{2,0},{3,1},{4,6},{5,7},{6,4},{7,5},{8,10},{9,11},{10,... | collective-permute-start | bytes 258056 | tf_op jit(solution)/shard_map/ppermute | solution.py:46
  (16 other events, 145.2 us)

commit v6 on v5

--- a/solution.py
+++ b/solution.py
@@ -513,7 +513,7 @@
     core = lax.axis_index("fld")
     blocks = coarse_counts.shape[0]
     entries = gain.shape[0]
-    shape = (entries, 4 * LANES)
+    shape = (entries, 8 * LANES)
     counts = jnp.ones(shape, jnp.int32)
     rows = lax.broadcasted_iota(jnp.int32, shape, 0)
     for r in range(entries):
@@ -521,14 +521,14 @@
     lengths = substeps(counts)
 
     def body(t, carry):
-        at = pl.ds(pl.multiple_of(t * 4 * LANES, 4 * LANES), 4 * LANES)
+        at = pl.ds(pl.multiple_of(t * 8 * LANES, 8 * LANES), 8 * LANES)
         start = pick(core, payc[1, :, at], payc_o[1, :, at])
         gain[:, at], weight[:, at] = reaction_tables(
             payc[0, :, at] + payc_o[0, :, at], start, lengths
         )
         return carry
 
-    lax.fori_loop(0, TILES // 4, body, 0)
+    lax.fori_loop(0, TILES // 8, body, 0)
 
 
 def octant_finder(children, count_f):
@@ -896,17 +896,6 @@
                     source[s, jh, rows_of(i), :] = r.state[s, jh, rows_of(i), :] + placed_tile(
                         r.placed, s, i, jh
                     )
-                for p in range(plan.late - slots):
-                    r.coarse_stage[p, :, cols(i, jh)] = r.coarse[p, jh, rows_of(i), :] + placed_tile(
-                        r.placed, slots + p, i, jh
-                    )
-        for p in range(plan.late - slots):
-            for v in range(fields):
-                r.coarse_final[v, pl.ds(p, 1), :] = pick(
-                    core,
-                    r.coarse_stage[p, pl.ds(v, 1), :],
-                    r.coarse_stage[p, pl.ds(fields + v, 1), :],
-                )
 
     def finish(s, i, jh, value):
         if s >= slots:
@@ -934,6 +923,39 @@
         react_bulk(plan, r, out)
 
 
+def coarse_kernel(plan, names, *refs):
+    r = SimpleNamespace(**dict(zip(names, refs)))
+    core = lax.axis_index("fld")
+    fields, count_c = plan.fields, plan.count_c
+    high, low = split(r.late[pl.ds((fields + 1) * HG * 8, count_c * HG * 8), :])
+    r.ends[:, pl.ds(0, 2 * LANES)] = high
+    r.ends[:, pl.ds(2 * LANES, 2 * LANES)] = low
+    place_ends(r.ends, r.placed, count_c * HG * 8, r)
+    for p in range(count_c):
+        for i in range(B):
+            for jh in range(2):
+                r.coarse_stage[p, :, cols(i, jh)] = r.coarse[p, jh, rows_of(i), :] + placed_tile(
+                    r.placed, p, i, jh
+                )
+        for v in range(fields):
+            r.coarse_final[v, pl.ds(p, 1), :] = pick(
+                core,
+                r.coarse_stage[p, pl.ds(v, 1), :],
+                r.coarse_stage[p, pl.ds(fields + v, 1), :],
+            )
+
+
+def share_kernel(plan, names, *refs):
+    r = SimpleNamespace(**dict(zip(names, refs)))
+    slots = plan.fields + 1
+    for n in range(len(plan.later)):
+        ref = getattr(r, numbered("landed", n))
+        tile = all_fields(1 - lax.axis_index("fld"), plan.fields, ref)
+        for s in range(slots):
+            r.shared[n * (slots + 1) + s] = tile(s)
+        r.shared[n * (slots + 1) + slots] = tile(None)
+
+
 def resume_kernel(plan, names, *refs):
     r = SimpleNamespace(**dict(zip(names, refs)))
     core = lax.axis_index("fld")
@@ -976,12 +998,6 @@
             far_a[n] = above[n]
 
     by_parity(sort_strips, r)
-    if plan.share:
-        for n in range(len(plan.later)):
-            tile = all_fields(1 - core, fields, getattr(r, numbered("landed", n)))
-            for s in range(slots):
-                r.shared[n * (slots + 1) + s] = tile(s)
-            r.shared[n * (slots + 1) + slots] = tile(None)
     faces = own_up[arrived * HG]
     rates = rates_of(plan, r)
     near = links_maker(plan, faces, 0, slots)
@@ -1255,7 +1271,6 @@
         add=False,
         near_at=every * HG + 1,
         late=0,
-        share=False,
         pause=False,
         packed=0,
     )
@@ -1306,7 +1321,7 @@
     )
     first_halo = halo(made, True)
     landed = [octant_move(getattr(made, numbered("octant", n)), d) for n, d in enumerate(later)]
-    landed, arrived_halo = lax.optimization_barrier((landed, first_halo))
+    arrived_halo = first_halo
 
     def edge_work(slabs):
         rows = slabs * HG * 8
@@ -1346,14 +1361,9 @@
         if held > slots:
             outputs.update(coarse_out=state_shape(count_c))
         if late is not None:
-            before = every if coarse is not None else slabs
             inputs.update(late=late)
-            scratch.update(whole=state_shape(slabs), **place_work(max(before, slabs)))
-            changes.update(late=before)
-            if coarse is not None:
-                inputs.update(coarse=coarse)
-                outputs.update(coarse_final=seed_coarse.shape)
-                scratch.update(coarse_stage=(count_c, 2 * fields, cells))
+            scratch.update(whole=state_shape(slabs), **place_work(slabs))
+            changes.update(late=slabs)
         paused = step == steps - 3
         if paused:
             for name in ("gain", "weight"):
@@ -1379,9 +1389,8 @@
                 dict(pack_work(slots), **stage_work, near_octant=slots_shape),
             )
             bulk.state_out, bulk.faces_out = whole.state_out, whole.faces_out
-        if coarse is not None:
-            coarse_final = bulk.coarse_final
-        coarse = bulk.coarse_out if held > slots else None
+        if held > slots:
+            coarse = bulk.coarse_out
         inputs = dict(flown)
         scratch = dict(edge_work(slabs), **strip_work(held))
         if final:
@@ -1395,17 +1404,31 @@
             outputs = dict(
                 late=(slabs * HG * 8, 2 * LANES), send_e=strip(slots), send_o=strip(slots)
             )
-        if step == steps - 2:
-            inputs.update(named("landed", landed))
-            outputs.update(shared=(len(later) * (slots + 1), 8, LANES))
-            changes.update(share=True)
         more = dict(hbm=("state_out",), sems=((fields,),)) if final else {}
         made = run(edge_kernel, changes, inputs, outputs, scratch, **more)
         if step == steps - 2:
-            shared = core_swap(made.shared)
+            first_late = made.late
+            part = run(
+                share_kernel,
+                dict(),
+                dict(named("landed", landed), after=first_late),
+                dict(shared=(len(later) * (slots + 1), 8, LANES)),
+                {},
+                hbm=("after",),
+            )
+            shared = core_swap(part.shared)
         if final:
             break
         state, late, held = bulk.state_out, made.late, slots
+        if step == 0:
+            coarse_final = run(
+                coarse_kernel,
+                dict(),
+                dict(coarse=coarse, late=first_late, after=late),
+                dict(coarse_final=seed_coarse.shape),
+                dict(place_work(count_c), coarse_stage=(count_c, 2 * fields, cells)),
+                hbm=("after",),
+            ).coarse_final
         flown = halo(made)
         sent = dict(sent_e=made.send_e, sent_o=made.send_o)
     return made.state_out, coarse_final

time: 65.6 us -> 64.1 us (0.977)
  waiting for transfers between devices: 11.2 us -> 8.72 us
  Pallas kernels: 28.4 us -> 29.8 us
    ppermute x7, waiting for transfers between devices: 6.67 us -> 4.28 us  [octant_move(): return lax.ppermute(value, ('blk', 'fld'), pairs)]
    ppermute x7, starting transfers between devices: 8.83 us -> 10.6 us  [octant_move(): return lax.ppermute(value, ('blk', 'fld'), pairs)]
    ppermute x8, starting transfers between devices: 11.7 us -> 10.1 us  [pair_swap(): return lax.ppermute(value, ('blk', 'fld'), pairs)]
    pallas_call x14 -> x16, Pallas kernels: 28.4 us -> 29.8 us  [call(): pl.pallas_call(functools.partial(kernel, names), out_shape=[jax.ShapeDtyp...]
  transfers between devices with their start and end apart: 25 -> 25, of which waited for: 9 -> 7; matrix products, arithmetic and copies ran while one was open for 0% -> 0% of each run, Pallas kernels for 26% -> 31%
where the time goes in v6:
time: 64.1 us; the launch traced here: 63.8 us
  Pallas kernels  29.8 us (46%)
  starting transfers between devices  23.4 us (37%)
  waiting for transfers between devices  8.72 us (14%)
  between operations  1.14 us (2%)
  local copies, waits for them, and re-layouts  0.8 us (1%)
    pallas_call x16, Pallas kernels, call(): pl.pallas_call(functools.partial(kernel, names), out_shape=[jax.ShapeDtyp...  29.8 us
    ppermute x7, starting transfers between devices, octant_move(): return lax.ppermute(value, ('blk', 'fld'), pairs)  10.6 us
    ppermute x8, starting transfers between devices, pair_swap(): return lax.ppermute(value, ('blk', 'fld'), pairs)  10.1 us
    ppermute x7, waiting for transfers between devices, octant_move(): return lax.ppermute(value, ('blk', 'fld'), pairs)  4.28 us
    ppermute x8, waiting for transfers between devices, pair_swap(): return lax.ppermute(value, ('blk', 'fld'), pairs)  2.72 us
    ppermute x10, starting transfers between devices, core_swap(): return lax.ppermute(value, 'fld', [(0, 1), (1, 0)])  2.63 us
    ppermute x10, waiting for transfers between devices, core_swap(): return lax.ppermute(value, 'fld', [(0, 1), (1, 0)])  1.72 us
  transfers between devices with their start and end apart: 25, of which 7 were waited for; matrix products, arithmetic and copies ran while one was open for 0% of the time, Pallas kernels for 31%

profile of v6, /device:TPU:0, one launch (start us, length us, event | category | flops | bytes accessed | tf_op | source)
XLA Modules:
  0.0 63.8 jit_solution(5492345756264725918)
XLA Ops:
  1.4 2.1 %shard_map.167.refs_3_.refs_0_ = f32[8,8,4096]{2,1,0:T(8,128)S(1)} custom-call(f32[4,4,8,4096]{3,2,1,0:T(8,128)} %refs_0_.14, f32[4]{0:T(128)S(1)} %copy-done.8), custom_call_target="tpu_custom_call" | custom-call | flops 1000 | bytes 1000 | tf_op jit(solution)/shard_map/pallas_call | solution.py:1115
  6.7 1.8 %shard_map.169 = (f32[2,2,128,128]{3,2,1,0:T(8,128)S(1)}, f32[4,4096]{1,0:T(4,128)S(1)}, f32[4,4096]{1,0:T(4,128)S(1)}, f32[6,8,128]{2,1,0:T(8,128)S(1)}, f32[9,...) custom-call(f32[6,4,4096]{2,1,0:T(4,128)S(1)} %shard_map.168.refs_0_.refs_, ...), custom_call_target="tpu_custom_call" | custom-call | flops 1000 | bytes 1000 | tf_op jit(solution)/shard_map/pallas_call | solution.py:1115
  8.5 2.9 %collective-permute-start.5 = (f32[18,8,128]{2,1,0:T(8,128)S(1)}, f32[18,8,128]{2,1,0:T(8,128)S(1)}, u32[]{:S(2)}, u32[]{:S(2)}) collective-permute-start(f32[18,8,128]{2,1,0:T(8,128)S(1)} %get-tuple-element.53.refs_15_), channel_id=1, source_target_pairs={{0,2},{1,13},{2,4},{3,15},{4,6},{5,17},{6,8},{7,19},{8,10},{9,21},... | collective-permute-start | bytes 221192 | tf_op jit(solution)/shard_map/ppermute | solution.py:65
  11.4 4.1 %collective-permute-start.6 = (f32[18,8,128]{2,1,0:T(8,128)S(1)}, f32[18,8,128]{2,1,0:T(8,128)S(1)}, u32[]{:S(2)}, u32[]{:S(2)}) collective-permute-start(f32[18,8,128]{2,1,0:T(8,128)S(1)} %get-tuple-element.54.refs_16_), channel_id=1, source_target_pairs={{0,30},{1,15},{2,0},{3,17},{4,2},{5,19},{6,4},{7,21},{8,6},{9,23},... | collective-permute-start | bytes 221192 | tf_op jit(solution)/shard_map/ppermute | solution.py:65
  15.9 2.3 %shard_map.170 = (f32[4,8,4096]{2,1,0:T(8,128)S(1)}, f32[4,8,4096]{2,1,0:T(8,128)S(1)}, f32[192,256]{1,0:T(8,128)S(1)}) custom-call(f32[8,8,4096]{2,1,0:T(8,128)S(1)} %shard_map.167.refs_3_.refs_0_, f32[8,8,4096]{2,1,0:T(8,128)S(1)} %collective-permute-done.7.refs_1_, s32[8]{0:T(128)S(1)} %copy-done.13, bf16[4,256,256]{2,1,0:T(8,128)(2,1)S(1)} %copy-done, ...), custom_call_target="tpu_custom_call" | custom-call | flops 1000 | bytes 1000 | tf_op jit(solution)/shard_map/pallas_call | solution.py:1115
  18.2 3.9 %collective-permute-done.3.refs_20_ = f32[9,8,128]{2,1,0:T(8,128)S(1)} collective-permute-done((f32[9,8,128]{2,1,0:T(8,128)S(1)}, f32[9,8,128]{2,1,0:T(8,128)S(1)}, u32[]{:S(2)}, u32[]{:S(2)}) %collective-permute-start.3) | collective-permute-done | bytes 36896 | tf_op jit(solution)/shard_map/ppermute | solution.py:65
  24.4 2.8 %shard_map.171 = (f32[7,2,128,128]{3,2,1,0:T(8,128)S(1)}, f32[35,8,128]{2,1,0:T(8,128)S(1)}, f32[35,8,128]{2,1,0:T(8,128)S(1)}, f32[6,8,128]{2,1,0:T(8,128)S(1)}...) custom-call(f32[4]{0:T(128)S(1)} %copy-done.9, f32[4]{0:T(128)S(1)} %copy-done.8, ...), custom_call_target="tpu_custom_call" | custom-call | flops 1000 | bytes 1000 | tf_op jit(solution)/shard_map/pallas_call | solution.py:1115
  27.3 1.7 %collective-permute-start.13 = (f32[35,8,128]{2,1,0:T(8,128)S(1)}, f32[35,8,128]{2,1,0:T(8,128)S(1)}, u32[]{:S(2)}, u32[]{:S(2)}) collective-permute-start(f32[35,8,128]{2,1,0:T(8,128)S(1)} %get-tuple-element.70.refs_11_.refs_9_), channel_id=1, source_target_pairs={{0,30},{1,31},{2,4},{3,5},{4,2},{5,3},{6,8},{7,9},{8,6},{9,7},{10,... | collective-permute-start | bytes 430088 | tf_op jit(solution)/shard_map/ppermute | solution.py:46
  30.3 1.7 %collective-permute-start.18 = (f32[9,8,128]{2,1,0:T(8,128)S(1)}, f32[9,8,128]{2,1,0:T(8,128)S(1)}, u32[]{:S(2)}, u32[]{:S(2)}) collective-permute-start(f32[9,8,128]{2,1,0:T(8,128)S(1)} %get-tuple-element.81), channel_id=1, source_target_pairs={{0,6},{1,13},{2,8},{3,15},{4,10},{5,17},{6,12},{7,19},{8,14},{9,21... | collective-permute-start | bytes 110600 | tf_op jit(solution)/shard_map/ppermute | solution.py:65
  32.0 1.2 %collective-permute-start.19 = (f32[9,8,128]{2,1,0:T(8,128)S(1)}, f32[9,8,128]{2,1,0:T(8,128)S(1)}, u32[]{:S(2)}, u32[]{:S(2)}) collective-permute-start(f32[9,8,128]{2,1,0:T(8,128)S(1)} %get-tuple-element.82), channel_id=1, source_target_pairs={{0,8},{1,15},{2,10},{3,17},{4,12},{5,19},{6,14},{7,21},{8,16},{9,2... | collective-permute-start | bytes 110600 | tf_op jit(solution)/shard_map/ppermute | solution.py:65
  33.2 3.2 %shard_map.172 = (f32[5,2,128,128]{3,2,1,0:T(8,128)S(1)}, f32[160,256]{1,0:T(8,128)S(1)}, f32[2,2,128,128]{3,2,1,0:T(8,128)S(1)}) custom-call(f32[4]{0:T(128)S(1)} %copy-done.9, f32[4]{0:T(128)S(1)} %copy-done.8, f32[4]{0:T(128)S(1)} %collective-permute-done.1.refs_6_.refs_2_, f32[4]{0:T(128)S(1)} %collective-permute-done.2.refs_7_.refs_3_, ...), custom_call_target="tpu_custom_call" | custom-call | flops 1000 | bytes 1000 | tf_op jit(solution)/shard_map/pallas_call | solution.py:1115
  36.4 1.5 %collective-permute-done.13.refs_10_.refs_13_ = f32[35,8,128]{2,1,0:T(8,128)S(1)} collective-permute-done((f32[35,8,128]{2,1,0:T(8,128)S(1)}, f32[35,8,128]{2,1,0:T(8,128)S(1)}, u32[]{:S(2)}, u32[]{:S(2)}) %collective-permute-start.13) | collective-permute-done | bytes 143392 | tf_op jit(solution)/shard_map/ppermute | solution.py:46
  37.9 1.3 %shard_map.173 = (f32[224,256]{1,0:T(8,128)S(1)}, f32[21,8,128]{2,1,0:T(8,128)S(1)}, f32[21,8,128]{2,1,0:T(8,128)S(1)}) custom-call(f32[4]{0:T(128)S(1)} %copy-done.9, f32[4]{0:T(128)S(1)} %copy-done.8, f32[4]{0:T(128)S(1)} %collective-permute-done.1.refs_6_.refs_2_, f32[4]{0:T(128)S(1)} %collective-permute-done.2.refs_7_.refs_3_, ...), custom_call_target="tpu_custom_call" | custom-call | flops 1000 | bytes 1000 | tf_op jit(solution)/shard_map/pallas_call | solution.py:1115
  39.7 2.8 %collective-permute-start.16 = (f32[21,8,128]{2,1,0:T(8,128)S(1)}, f32[21,8,128]{2,1,0:T(8,128)S(1)}, u32[]{:S(2)}, u32[]{:S(2)}) collective-permute-start(f32[21,8,128]{2,1,0:T(8,128)S(1)} %get-tuple-element.76.refs_10_.refs_11_), channel_id=1, source_target_pairs={{0,2},{1,3},{2,0},{3,1},{4,6},{5,7},{6,4},{7,5},{8,10},{9,11},{10,... | collective-permute-start | bytes 258056 | tf_op jit(solution)/shard_map/ppermute | solution.py:46
  43.2 2.5 %shard_map.174.refs_9_ = f32[5,2,128,128]{3,2,1,0:T(8,128)S(1)} custom-call(f32[4]{0:T(128)S(1)} %copy-done.9, f32[4]{0:T(128)S(1)} %copy-done.8, f32[4]{0:T(128)S(1)} %collective-permute-done.1.refs_6_.refs_2_, f32[4]{0:T(128)S(1)} %collective-permute-done.2.refs_7_.refs_3_, bf16[256,256]{1,0:T(8,128)(2,1)S(1)} %copy-done.2, ...), custom_call_target="tpu_custom_call" | custom-call | flops 1000 | bytes 1000 | tf_op jit(solution)/shard_map/pallas_call | solution.py:1115
  45.8 1.3 %shard_map.176 = (f32[5,2,128,128]{3,2,1,0:T(8,128)S(1)}, f32[160,256]{1,0:T(8,128)S(1)}) custom-call(f32[4]{0:T(128)S(1)} %copy-done.9, f32[4]{0:T(128)S(1)} %copy-done.8, f32[4]{0:T(128)S(1)} %collective-permute-done.1.refs_6_.refs_2_, f32[4]{0:T(128)S(1)} %collective-permute-done.2.refs_7_.refs_3_, bf16[256,256]{1,0:T(8,128)(2,1)S(1)} %copy-done.2, ...), custom_call_target="tpu_custom_call" | custom-call | flops 1000 | bytes 1000 | tf_op jit(solution)/shard_map/pallas_call | solution.py:1115
  47.1 1.1 %shard_map.177 = (f32[160,256]{1,0:T(8,128)S(1)}, f32[21,8,128]{2,1,0:T(8,128)S(1)}, f32[21,8,128]{2,1,0:T(8,128)S(1)}) custom-call(f32[4]{0:T(128)S(1)} %copy-done.9, f32[4]{0:T(128)S(1)} %copy-done.8, f32[4]{0:T(128)S(1)} %collective-permute-done.1.refs_6_.refs_2_, f32[4]{0:T(128)S(1)} %collective-permute-done.2.refs_7_.refs_3_, ...), custom_call_target="tpu_custom_call" | custom-call | flops 1000 | bytes 1000 | tf_op jit(solution)/shard_map/pallas_call | solution.py:1115
  49.7 3.1 %shard_map.178 = (f32[5,2,128,128]{3,2,1,0:T(8,128)S(1)}, f32[160,256]{1,0:T(8,128)S(1)}) custom-call(f32[4]{0:T(128)S(1)} %copy-done.9, f32[4]{0:T(128)S(1)} %copy-done.8, f32[4]{0:T(128)S(1)} %collective-permute-done.1.refs_6_.refs_2_, f32[4]{0:T(128)S(1)} %collective-permute-done.2.refs_7_.refs_3_, bf16[256,256]{1,0:T(8,128)(2,1)S(1)} %copy-done.2, ...), custom_call_target="tpu_custom_call" | custom-call | flops 1000 | bytes 1000 | tf_op jit(solution)/shard_map/pallas_call | solution.py:1115
  52.8 1.2 %collective-permute-done.22.refs_12_ = f32[21,8,128]{2,1,0:T(8,128)S(1)} collective-permute-done((f32[21,8,128]{2,1,0:T(8,128)S(1)}, f32[21,8,128]{2,1,0:T(8,128)S(1)}, u32[]{:S(2)}, u32[]{:S(2)}) %collective-permute-start.22) | collective-permute-done | bytes 86048 | tf_op jit(solution)/shard_map/ppermute | solution.py:46
  54.0 1.1 %shard_map.179 = (f32[160,256]{1,0:T(8,128)S(1)}, f32[21,8,128]{2,1,0:T(8,128)S(1)}, f32[21,8,128]{2,1,0:T(8,128)S(1)}) custom-call(f32[4]{0:T(128)S(1)} %copy-done.9, f32[4]{0:T(128)S(1)} %copy-done.8, f32[4]{0:T(128)S(1)} %collective-permute-done.1.refs_6_.refs_2_, f32[4]{0:T(128)S(1)} %collective-permute-done.2.refs_7_.refs_3_, ...), custom_call_target="tpu_custom_call" | custom-call | flops 1000 | bytes 1000 | tf_op jit(solution)/shard_map/pallas_call | solution.py:1115
  55.2 2.6 %collective-permute-start.24 = (f32[21,8,128]{2,1,0:T(8,128)S(1)}, f32[21,8,128]{2,1,0:T(8,128)S(1)}, u32[]{:S(2)}, u32[]{:S(2)}) collective-permute-start(f32[21,8,128]{2,1,0:T(8,128)S(1)} %get-tuple-element.90.refs_10_.refs_11_), channel_id=1, source_target_pairs={{0,2},{1,3},{2,0},{3,1},{4,6},{5,7},{6,4},{7,5},{8,10},{9,11},{10,... | collective-permute-start | bytes 258056 | tf_op jit(solution)/shard_map/ppermute | solution.py:46
  57.8 1.5 %shard_map.182 = f32[4,2,4096]{2,1,0:T(2,128)} custom-call(f32[4]{0:T(128)S(1)} %copy-done.9, f32[4]{0:T(128)S(1)} %copy-done.8, f32[4]{0:T(128)S(1)} %collective-permute-done.1.refs_6_.refs_2_, f32[4]{0:T(128)S(1)} %collective-permute-done.2.refs_7_.refs_3_, bf16[256,256]{1,0:T(8,128)(2,1)S(1)} %copy-done.2, bf16[128,256]{1,0:T(8,128)(2,1)S(1)} %copy-done.3, ...), custom_call_target="tpu_custom_call" | custom-call | flops 1000 | bytes 1000 | tf_op jit(solution)/shard_map/pallas_call | solution.py:1115
  59.3 2.2 %shard_map.180.refs_13_ = f32[4,2,128,128]{3,2,1,0:T(8,128)S(1)} custom-call(f32[4]{0:T(128)S(1)} %copy-done.9, f32[4]{0:T(128)S(1)} %copy-done.8, f32[4]{0:T(128)S(1)} %collective-permute-done.1.refs_6_.refs_2_, f32[4]{0:T(128)S(1)} %collective-permute-done.2.refs_7_.refs_3_, bf16[256,256]{1,0:T(8,128)(2,1)S(1)} %copy-done.2, ...), custom_call_target="tpu_custom_call" | custom-call | flops 1000 | bytes 1000 | tf_op jit(solution)/shard_map/pallas_call | solution.py:1115
  61.6 2.1 %shard_map.181 = f32[4,8,4096]{2,1,0:T(8,128)} custom-call(f32[4]{0:T(128)S(1)} %copy-done.9, f32[4]{0:T(128)S(1)} %copy-done.8, f32[4]{0:T(128)S(1)} %collective-permute-done.1.refs_6_.refs_2_, f32[4]{0:T(128)S(1)} %collective-permute-done.2.refs_7_.refs_3_, bf16[256,256]{1,0:T(8,128)(2,1)S(1)} %copy-done.2, bf16[128,256]{1,0:T(8,128)(2,1)S(1)} %copy-done.3, ...), custom_call_target="tpu_custom_call" | custom-call | flops 1000 | bytes 1000 | tf_op jit(solution)/shard_map/pallas_call | solution.py:1115
  (72 shorter events, 10.6 us)
Async XLA Ops:
  4.3 1.9 %collective-permute-start = (f32[6,4,4096]{2,1,0:T(4,128)S(1)}, f32[6,4,4096]{2,1,0:T(4,128)S(1)}, u32[]{:S(2)}, u32[]{:S(2)}) collective-permute-start(f32[6,4,4096]{2,1,0:T(4,128)S(1)} %shard_map.168.refs_0_.refs_4_), channel_id=1, source_target_pairs={{0,1},{1,0},{2,3},{3,2},{4,5},{5,4},{6,7},{7,6},{8,9},{9,8},{10,11... | collective-permute-start | bytes 1179656 | tf_op jit(solution)/shard_map/ppermute | solution.py:33
  4.8 1.4 %collective-permute-start.2 = (f32[4]{0:T(128)S(1)}, f32[4]{0:T(128)S(1)}, u32[]{:S(2)}, u32[]{:S(2)}) collective-permute-start(f32[4]{0:T(128)S(1)} %copy-done.8), channel_id=1, source_target_pairs={{0,1},{1,0},{2,3},{3,2},{4,5},{5,4},{6,7},{7,6},{8,9},{9,8},{10,11... | collective-permute-start | bytes 56 | tf_op jit(solution)/shard_map/ppermute | solution.py:33
  4.9 1.3 %collective-permute-start.1 = (f32[4]{0:T(128)S(1)}, f32[4]{0:T(128)S(1)}, u32[]{:S(2)}, u32[]{:S(2)}) collective-permute-start(f32[4]{0:T(128)S(1)} %copy-done.9), channel_id=1, source_target_pairs={{0,1},{1,0},{2,3},{3,2},{4,5},{5,4},{6,7},{7,6},{8,9},{9,8},{10,11... | collective-permute-start | bytes 56 | tf_op jit(solution)/shard_map/ppermute | solution.py:33
  6.2 9.3 %collective-permute-start.7 = (f32[8,8,4096]{2,1,0:T(8,128)S(1)}, f32[8,8,4096]{2,1,0:T(8,128)S(1)}, u32[]{:S(2)}, u32[]{:S(2)}) collective-permute-start(f32[8,8,4096]{2,1,0:T(8,128)S(1)} %shard_map.167.refs_3_.refs_0_), channel_id=1, source_target_pairs={{0,1},{1,0},{2,3},{3,2},{4,5},{5,4},{6,7},{7,6},{8,9},{9,8},{10,11... | collective-permute-start | bytes 3145736 | tf_op jit(solution)/shard_map/ppermute | solution.py:33
  6.6 17.0 %collective-permute-start.8 = (f32[4,8,4096]{2,1,0:T(8,128)S(1)}, f32[4,8,4096]{2,1,0:T(8,128)S(1)}, u32[]{:S(2)}, u32[]{:S(2)}) collective-permute-start(f32[4,8,4096]{2,1,0:T(8,128)S(1)} %copy-done.5), channel_id=1, source_target_pairs={{0,1},{1,0},{2,3},{3,2},{4,5},{5,4},{6,7},{7,6},{8,9},{9,8},{10,11... | collective-permute-start | bytes 1572872 | tf_op jit(solution)/shard_map/ppermute | solution.py:33
  8.5 14.0 %collective-permute-start.5 = (f32[18,8,128]{2,1,0:T(8,128)S(1)}, f32[18,8,128]{2,1,0:T(8,128)S(1)}, u32[]{:S(2)}, u32[]{:S(2)}) collective-permute-start(f32[18,8,128]{2,1,0:T(8,128)S(1)} %get-tuple-element.53.refs_15_), channel_id=1, source_target_pairs={{0,2},{1,13},{2,4},{3,15},{4,6},{5,17},{6,8},{7,19},{8,10},{9,21},... | collective-permute-start | bytes 221192 | tf_op jit(solution)/shard_map/ppermute | solution.py:65
  11.4 11.1 %collective-permute-start.6 = (f32[18,8,128]{2,1,0:T(8,128)S(1)}, f32[18,8,128]{2,1,0:T(8,128)S(1)}, u32[]{:S(2)}, u32[]{:S(2)}) collective-permute-start(f32[18,8,128]{2,1,0:T(8,128)S(1)} %get-tuple-element.54.refs_16_), channel_id=1, source_target_pairs={{0,30},{1,15},{2,0},{3,17},{4,2},{5,19},{6,4},{7,21},{8,6},{9,23},... | collective-permute-start | bytes 221192 | tf_op jit(solution)/shard_map/ppermute | solution.py:65
  15.4 6.7 %collective-permute-start.3 = (f32[9,8,128]{2,1,0:T(8,128)S(1)}, f32[9,8,128]{2,1,0:T(8,128)S(1)}, u32[]{:S(2)}, u32[]{:S(2)}) collective-permute-start(f32[9,8,128]{2,1,0:T(8,128)S(1)} %get-tuple-element.51), channel_id=1, source_target_pairs={{0,4},{1,9},{2,6},{3,11},{4,8},{5,13},{6,10},{7,15},{8,12},{9,17},... | collective-permute-start | bytes 110600 | tf_op jit(solution)/shard_map/ppermute | solution.py:65
  15.4 7.0 %collective-permute-start.4 = (f32[9,8,128]{2,1,0:T(8,128)S(1)}, f32[9,8,128]{2,1,0:T(8,128)S(1)}, u32[]{:S(2)}, u32[]{:S(2)}) collective-permute-start(f32[9,8,128]{2,1,0:T(8,128)S(1)} %get-tuple-element.52), channel_id=1, source_target_pairs={{0,6},{1,11},{2,8},{3,13},{4,10},{5,15},{6,12},{7,17},{8,14},{9,19... | collective-permute-start | bytes 110600 | tf_op jit(solution)/shard_map/ppermute | solution.py:65
  22.5 1.9 %collective-permute-start.11 = (f32[18,8,128]{2,1,0:T(8,128)S(1)}, f32[18,8,128]{2,1,0:T(8,128)S(1)}, u32[]{:S(2)}, u32[]{:S(2)}) collective-permute-start(f32[18,8,128]{2,1,0:T(8,128)S(1)} %collective-permute-done.5.refs_22_), channel_id=1, source_target_pairs={{0,1},{1,0},{2,3},{3,2},{4,5},{5,4},{6,7},{7,6},{8,9},{9,8},{10,11... | collective-permute-start | bytes 221192 | tf_op jit(solution)/shard_map/ppermute | solution.py:33
  22.5 1.9 %collective-permute-start.12 = (f32[18,8,128]{2,1,0:T(8,128)S(1)}, f32[18,8,128]{2,1,0:T(8,128)S(1)}, u32[]{:S(2)}, u32[]{:S(2)}) collective-permute-start(f32[18,8,128]{2,1,0:T(8,128)S(1)} %collective-permute-done.6.refs_23_), channel_id=1, source_target_pairs={{0,1},{1,0},{2,3},{3,2},{4,5},{5,4},{6,7},{7,6},{8,9},{9,8},{10,11... | collective-permute-start | bytes 221192 | tf_op jit(solution)/shard_map/ppermute | solution.py:33
  23.1 1.3 %collective-permute-start.9 = (f32[9,8,128]{2,1,0:T(8,128)S(1)}, f32[9,8,128]{2,1,0:T(8,128)S(1)}, u32[]{:S(2)}, u32[]{:S(2)}) collective-permute-start(f32[9,8,128]{2,1,0:T(8,128)S(1)} %collective-permute-done.3.refs_20_), channel_id=1, source_target_pairs={{0,1},{1,0},{2,3},{3,2},{4,5},{5,4},{6,7},{7,6},{8,9},{9,8},{10,11... | collective-permute-start | bytes 110600 | tf_op jit(solution)/shard_map/ppermute | solution.py:33
  27.3 10.7 %collective-permute-start.13 = (f32[35,8,128]{2,1,0:T(8,128)S(1)}, f32[35,8,128]{2,1,0:T(8,128)S(1)}, u32[]{:S(2)}, u32[]{:S(2)}) collective-permute-start(f32[35,8,128]{2,1,0:T(8,128)S(1)} %get-tuple-element.70.refs_11_.refs_9_), channel_id=1, source_target_pairs={{0,30},{1,31},{2,4},{3,5},{4,2},{5,3},{6,8},{7,9},{8,6},{9,7},{10,... | collective-permute-start | bytes 430088 | tf_op jit(solution)/shard_map/ppermute | solution.py:46
  29.0 9.0 %collective-permute-start.14 = (f32[35,8,128]{2,1,0:T(8,128)S(1)}, f32[35,8,128]{2,1,0:T(8,128)S(1)}, u32[]{:S(2)}, u32[]{:S(2)}) collective-permute-start(f32[35,8,128]{2,1,0:T(8,128)S(1)} %get-tuple-element.71.refs_10_.refs_11_), channel_id=1, source_target_pairs={{0,2},{1,3},{2,0},{3,1},{4,6},{5,7},{6,4},{7,5},{8,10},{9,11},{10,... | collective-permute-start | bytes 430088 | tf_op jit(solution)/shard_map/ppermute | solution.py:46
  29.9 12.6 %collective-permute-start.17 = (f32[9,8,128]{2,1,0:T(8,128)S(1)}, f32[9,8,128]{2,1,0:T(8,128)S(1)}, u32[]{:S(2)}, u32[]{:S(2)}) collective-permute-start(f32[9,8,128]{2,1,0:T(8,128)S(1)} %get-tuple-element.80), channel_id=1, source_target_pairs={{0,4},{1,11},{2,6},{3,13},{4,8},{5,15},{6,10},{7,17},{8,12},{9,19}... | collective-permute-start | bytes 110600 | tf_op jit(solution)/shard_map/ppermute | solution.py:65
  30.3 12.3 %collective-permute-start.18 = (f32[9,8,128]{2,1,0:T(8,128)S(1)}, f32[9,8,128]{2,1,0:T(8,128)S(1)}, u32[]{:S(2)}, u32[]{:S(2)}) collective-permute-start(f32[9,8,128]{2,1,0:T(8,128)S(1)} %get-tuple-element.81), channel_id=1, source_target_pairs={{0,6},{1,13},{2,8},{3,15},{4,10},{5,17},{6,12},{7,19},{8,14},{9,21... | collective-permute-start | bytes 110600 | tf_op jit(solution)/shard_map/ppermute | solution.py:65
  32.0 10.6 %collective-permute-start.19 = (f32[9,8,128]{2,1,0:T(8,128)S(1)}, f32[9,8,128]{2,1,0:T(8,128)S(1)}, u32[]{:S(2)}, u32[]{:S(2)}) collective-permute-start(f32[9,8,128]{2,1,0:T(8,128)S(1)} %get-tuple-element.82), channel_id=1, source_target_pairs={{0,8},{1,15},{2,10},{3,17},{4,12},{5,19},{6,14},{7,21},{8,16},{9,2... | collective-permute-start | bytes 110600 | tf_op jit(solution)/shard_map/ppermute | solution.py:65
  39.2 7.9 %collective-permute-start.15 = (f32[21,8,128]{2,1,0:T(8,128)S(1)}, f32[21,8,128]{2,1,0:T(8,128)S(1)}, u32[]{:S(2)}, u32[]{:S(2)}) collective-permute-start(f32[21,8,128]{2,1,0:T(8,128)S(1)} %get-tuple-element.75.refs_11_.refs_9_), channel_id=1, source_target_pairs={{0,1},{1,0},{2,4},{3,5},{4,2},{5,3},{6,8},{7,9},{8,6},{9,7},{10,12... | collective-permute-start | bytes 258056 | tf_op jit(solution)/shard_map/ppermute | solution.py:46
  39.7 7.3 %collective-permute-start.16 = (f32[21,8,128]{2,1,0:T(8,128)S(1)}, f32[21,8,128]{2,1,0:T(8,128)S(1)}, u32[]{:S(2)}, u32[]{:S(2)}) collective-permute-start(f32[21,8,128]{2,1,0:T(8,128)S(1)} %get-tuple-element.76.refs_10_.refs_11_), channel_id=1, source_target_pairs={{0,2},{1,3},{2,0},{3,1},{4,6},{5,7},{6,4},{7,5},{8,10},{9,11},{10,... | collective-permute-start | bytes 258056 | tf_op jit(solution)/shard_map/ppermute | solution.py:46
  43.1 2.6 %collective-permute-start.20 = (f32[18,8,128]{2,1,0:T(8,128)S(1)}, f32[18,8,128]{2,1,0:T(8,128)S(1)}, u32[]{:S(2)}, u32[]{:S(2)}) collective-permute-start(f32[18,8,128]{2,1,0:T(8,128)S(1)} %shard_map.175), channel_id=1, source_target_pairs={{0,1},{1,0},{2,3},{3,2},{4,5},{5,4},{6,7},{7,6},{8,9},{9,8},{10,11... | collective-permute-start | bytes 221192 | tf_op jit(solution)/shard_map/ppermute | solution.py:33
  48.2 4.6 %collective-permute-start.21 = (f32[21,8,128]{2,1,0:T(8,128)S(1)}, f32[21,8,128]{2,1,0:T(8,128)S(1)}, u32[]{:S(2)}, u32[]{:S(2)}) collective-permute-start(f32[21,8,128]{2,1,0:T(8,128)S(1)} %get-tuple-element.84.refs_11_.refs_9_), channel_id=1, source_target_pairs={{0,1},{1,0},{2,4},{3,5},{4,2},{5,3},{6,8},{7,9},{8,6},{9,7},{10,12... | collective-permute-start | bytes 258056 | tf_op jit(solution)/shard_map/ppermute | solution.py:46
  48.8 5.2 %collective-permute-start.22 = (f32[21,8,128]{2,1,0:T(8,128)S(1)}, f32[21,8,128]{2,1,0:T(8,128)S(1)}, u32[]{:S(2)}, u32[]{:S(2)}) collective-permute-start(f32[21,8,128]{2,1,0:T(8,128)S(1)} %get-tuple-element.85.refs_10_.refs_11_), channel_id=1, source_target_pairs={{0,2},{1,3},{2,0},{3,1},{4,6},{5,7},{6,4},{7,5},{8,10},{9,11},{10,... | collective-permute-start | bytes 258056 | tf_op jit(solution)/shard_map/ppermute | solution.py:46
  55.1 6.4 %collective-permute-start.23 = (f32[21,8,128]{2,1,0:T(8,128)S(1)}, f32[21,8,128]{2,1,0:T(8,128)S(1)}, u32[]{:S(2)}, u32[]{:S(2)}) collective-permute-start(f32[21,8,128]{2,1,0:T(8,128)S(1)} %get-tuple-element.89.refs_11_.refs_9_), channel_id=1, source_target_pairs={{0,1},{1,0},{2,4},{3,5},{4,2},{5,3},{6,8},{7,9},{8,6},{9,7},{10,12... | collective-permute-start | bytes 258056 | tf_op jit(solution)/shard_map/ppermute | solution.py:46
  55.2 6.4 %collective-permute-start.24 = (f32[21,8,128]{2,1,0:T(8,128)S(1)}, f32[21,8,128]{2,1,0:T(8,128)S(1)}, u32[]{:S(2)}, u32[]{:S(2)}) collective-permute-start(f32[21,8,128]{2,1,0:T(8,128)S(1)} %get-tuple-element.90.refs_10_.refs_11_), channel_id=1, source_target_pairs={{0,2},{1,3},{2,0},{3,1},{4,6},{5,7},{6,4},{7,5},{8,10},{9,11},{10,... | collective-permute-start | bytes 258056 | tf_op jit(solution)/shard_map/ppermute | solution.py:46
  (16 other events, 143.5 us)

commit v7 on v6

--- a/solution.py
+++ b/solution.py
@@ -778,12 +778,14 @@
     base = 2 * fields + 1
     strip = count_c * HG
 
-    def far(ref, ref_o, n):
-        return pick(core, ref[base + n], ref_o[base + n])
-
     last = len(plan.sends) - 1
-    below = [far(getattr(r, numbered("landed", last - 1)), getattr(r, numbered("shared", last - 1)), n) for n in range(strip + 1)]
-    above = [far(getattr(r, numbered("landed", last)), getattr(r, numbered("shared", last)), n) for n in range(strip + 1)]
+    strips_at = (last + 1) * (slots + 1)
+
+    def far(ref, order, n):
+        return pick(core, ref[base + n], r.shared[strips_at + order * (strip + 1) + n])
+
+    below = [far(getattr(r, numbered("landed", last - 1)), 0, n) for n in range(strip + 1)]
+    above = [far(getattr(r, numbered("landed", last)), 1, n) for n in range(strip + 1)]
     own_up, own_down = r.own_up, r.own_down
     faces = own_up[base + strip]
     rates = 0.5 * spread_vector(core, par, par_o, 0, fields)
@@ -828,8 +830,9 @@
     entries = [own_slots(fields, r.local)]
     for n in range(last):
         entries.append(all_fields(core, fields, getattr(r, numbered("landed", n))))
-        entries.append(all_fields(core, fields, getattr(r, numbered("shared", n))))
-    one, two = (all_fields(core, fields, getattr(r, numbered(word, last))) for word in ("landed", "shared"))
+        entries.append(own_slots(fields, r.shared, n * (slots + 1)))
+    one = all_fields(core, fields, getattr(r, numbered("landed", last)))
+    two = own_slots(fields, r.shared, last * (slots + 1))
     entries.append(lambda s: pick(core, two(s), one(s)))
     add_octants(entries, out, r.stage, fields)
     react_fine(out, fields, par, par_o, r.gain.at[plan.step], r.weight.at[plan.step])
@@ -948,12 +951,18 @@
 def share_kernel(plan, names, *refs):
     r = SimpleNamespace(**dict(zip(names, refs)))
     slots = plan.fields + 1
-    for n in range(len(plan.later)):
+    for n in range(plan.pieces):
         ref = getattr(r, numbered("landed", n))
         tile = all_fields(1 - lax.axis_index("fld"), plan.fields, ref)
         for s in range(slots):
             r.shared[n * (slots + 1) + s] = tile(s)
         r.shared[n * (slots + 1) + slots] = tile(None)
+    at = plan.pieces * (slots + 1)
+    for n in range(plan.pieces - 2, plan.pieces) if plan.strips else ():
+        ref = getattr(r, numbered("landed", n))
+        for m in range(plan.strips):
+            r.shared[at + m] = ref[2 * plan.fields + 1 + m]
+        at += plan.strips
 
 
 def resume_kernel(plan, names, *refs):
@@ -1095,7 +1104,7 @@
 SCALARS = ("dif", "shr", "dif_o", "shr_o", "children", "fine_counts", "coarse_counts")
 MATS = ("plane", "side", "place", "pack", "far")
 MIB = 1024 * 1024
-LIMIT = 51
+LIMIT = 52
 
 
 def call(kernel, inputs, outputs, scratch, hbm=(), sems=(), limit=None, cost=1000):
@@ -1253,7 +1262,6 @@
     landed, (chem.gain, chem.weight, chem.edges) = lax.optimization_barrier(
         (landed, (chem.gain, chem.weight, chem.edges))
     )
-    shared = [core_swap(value) for value in landed]
 
     def named(word, values):
         return {numbered(word, n): value for n, value in enumerate(values)}
@@ -1293,6 +1301,18 @@
         return dict(
             state_out=state_shape(slabs), send_e=strip(slabs, more), send_o=strip(slabs, more)
         )
+
+    def share(landed, before, strips):
+        tiles = len(landed) * (slots + 1) + 2 * strips
+        part = run(
+            share_kernel,
+            dict(pieces=len(landed), strips=strips),
+            dict(named("landed", landed), after=before),
+            dict(shared=(tiles, 8, LANES)),
+            {},
+            hbm=("after",),
+        )
+        return core_swap(part.shared)
 
     made = run(
         open_kernel,
@@ -1310,7 +1330,7 @@
             seed_other=seed_o,
             local=started.local,
             **named("landed", landed),
-            **named("shared", shared),
+            shared=share(landed, chem.edges, count_c * HG + 1),
         ),
         dict(
             sending(every, slots + 1),
@@ -1408,15 +1428,7 @@
         made = run(edge_kernel, changes, inputs, outputs, scratch, **more)
         if step == steps - 2:
             first_late = made.late
-            part = run(
-                share_kernel,
-                dict(),
-                dict(named("landed", landed), after=first_late),
-                dict(shared=(len(later) * (slots + 1), 8, LANES)),
-                {},
-                hbm=("after",),
-            )
-            shared = core_swap(part.shared)
+            shared = share(landed, first_late, 0)
         if final:
             break
         state, late, held = bulk.state_out, made.late, slots

time: 64.1 us -> 64.1 us (level)
  starting transfers between devices: 23.4 us -> 22.1 us
    ppermute x10 -> x7, starting transfers between devices: 2.63 us -> 1.68 us  [core_swap(): return lax.ppermute(value, 'fld', [(0, 1), (1, 0)])]
    ppermute x10 -> x7, waiting for transfers between devices: 1.72 us -> 2.24 us  [core_swap(): return lax.ppermute(value, 'fld', [(0, 1), (1, 0)])]
    pallas_call x16 -> x17, Pallas kernels: 29.8 us -> 30.3 us  [call(): pl.pallas_call(functools.partial(kernel, names), out_shape=[jax.ShapeDtyp...]
  transfers between devices with their start and end apart: 25 -> 22, of which waited for: 7 -> 6; matrix products, arithmetic and copies ran while one was open for 0% -> 0% of each run, Pallas kernels for 31% -> 32%
where the time goes in v7:
time: 64.1 us; the launch traced here: 63.7 us
  Pallas kernels  30.3 us (47%)
  starting transfers between devices  22.1 us (34%)
  waiting for transfers between devices  9.31 us (15%)
  between operations  1.15 us (2%)
  local copies, waits for them, and re-layouts  0.8 us (1%)
    pallas_call x17, Pallas kernels, call(): pl.pallas_call(functools.partial(kernel, names), out_shape=[jax.ShapeDtyp...  30.3 us
    ppermute x7, starting transfers between devices, octant_move(): return lax.ppermute(value, ('blk', 'fld'), pairs)  10.6 us
    ppermute x8, starting transfers between devices, pair_swap(): return lax.ppermute(value, ('blk', 'fld'), pairs)  9.87 us
    ppermute x7, waiting for transfers between devices, octant_move(): return lax.ppermute(value, ('blk', 'fld'), pairs)  4.28 us
    ppermute x8, waiting for transfers between devices, pair_swap(): return lax.ppermute(value, ('blk', 'fld'), pairs)  2.79 us
    ppermute x7, waiting for transfers between devices, core_swap(): return lax.ppermute(value, 'fld', [(0, 1), (1, 0)])  2.24 us
    ppermute x7, starting transfers between devices, core_swap(): return lax.ppermute(value, 'fld', [(0, 1), (1, 0)])  1.68 us
  transfers between devices with their start and end apart: 22, of which 6 were waited for; matrix products, arithmetic and copies ran while one was open for 0% of the time, Pallas kernels for 32%

profile of v7, /device:TPU:0, one launch (start us, length us, event | category | flops | bytes accessed | tf_op | source)
XLA Modules:
  0.0 63.7 jit_solution(17916753916315481297)
XLA Ops:
  1.4 2.1 %shard_map.167.refs_3_.refs_0_ = f32[8,8,4096]{2,1,0:T(8,128)S(1)} custom-call(f32[4,4,8,4096]{3,2,1,0:T(8,128)} %refs_0_.15, f32[4]{0:T(128)S(1)} %copy-done.8), custom_call_target="tpu_custom_call" | custom-call | flops 1000 | bytes 1000 | tf_op jit(solution)/shard_map/pallas_call | solution.py:1124
  6.7 1.8 %shard_map.169 = (f32[2,2,128,128]{3,2,1,0:T(8,128)S(1)}, f32[4,4096]{1,0:T(4,128)S(1)}, f32[4,4096]{1,0:T(4,128)S(1)}, f32[6,8,128]{2,1,0:T(8,128)S(1)}, f32[9,...) custom-call(f32[6,4,4096]{2,1,0:T(4,128)S(1)} %shard_map.168.refs_0_.refs_, ...), custom_call_target="tpu_custom_call" | custom-call | flops 1000 | bytes 1000 | tf_op jit(solution)/shard_map/pallas_call | solution.py:1124
  8.5 2.9 %collective-permute-start.5 = (f32[18,8,128]{2,1,0:T(8,128)S(1)}, f32[18,8,128]{2,1,0:T(8,128)S(1)}, u32[]{:S(2)}, u32[]{:S(2)}) collective-permute-start(f32[18,8,128]{2,1,0:T(8,128)S(1)} %get-tuple-element.53.refs_15_), channel_id=1, source_target_pairs={{0,2},{1,13},{2,4},{3,15},{4,6},{5,17},{6,8},{7,19},{8,10},{9,21},... | collective-permute-start | bytes 221192 | tf_op jit(solution)/shard_map/ppermute | solution.py:65
  11.4 4.1 %collective-permute-start.6 = (f32[18,8,128]{2,1,0:T(8,128)S(1)}, f32[18,8,128]{2,1,0:T(8,128)S(1)}, u32[]{:S(2)}, u32[]{:S(2)}) collective-permute-start(f32[18,8,128]{2,1,0:T(8,128)S(1)} %get-tuple-element.54.refs_16_), channel_id=1, source_target_pairs={{0,30},{1,15},{2,0},{3,17},{4,2},{5,19},{6,4},{7,21},{8,6},{9,23},... | collective-permute-start | bytes 221192 | tf_op jit(solution)/shard_map/ppermute | solution.py:65
  15.9 2.3 %shard_map.170 = (f32[4,8,4096]{2,1,0:T(8,128)S(1)}, f32[4,8,4096]{2,1,0:T(8,128)S(1)}, f32[192,256]{1,0:T(8,128)S(1)}) custom-call(f32[8,8,4096]{2,1,0:T(8,128)S(1)} %shard_map.167.refs_3_.refs_0_, f32[8,8,4096]{2,1,0:T(8,128)S(1)} %collective-permute-done.7.refs_1_, s32[8]{0:T(128)S(1)} %copy-done.13, bf16[4,256,256]{2,1,0:T(8,128)(2,1)S(1)} %copy-done, ...), custom_call_target="tpu_custom_call" | custom-call | flops 1000 | bytes 1000 | tf_op jit(solution)/shard_map/pallas_call | solution.py:1124
  18.2 3.9 %collective-permute-done.3.refs_9_.refs_20_ = f32[9,8,128]{2,1,0:T(8,128)S(1)} collective-permute-done((f32[9,8,128]{2,1,0:T(8,128)S(1)}, f32[9,8,128]{2,1,0:T(8,128)S(1)}, u32[]{:S(2)}, u32[]{:S(2)}) %collective-permute-start.3) | collective-permute-done | bytes 36896 | tf_op jit(solution)/shard_map/ppermute | solution.py:65
  23.2 1.4 %collective-permute-done.9.refs_24_ = f32[42,8,128]{2,1,0:T(8,128)S(1)} collective-permute-done((f32[42,8,128]{2,1,0:T(8,128)S(1)}, f32[42,8,128]{2,1,0:T(8,128)S(1)}, u32[]{:S(2)}, u32[]{:S(2)}) %collective-permute-start.9) | collective-permute-done | bytes 172064 | tf_op jit(solution)/shard_map/ppermute | solution.py:33
  24.6 2.8 %shard_map.172 = (f32[7,2,128,128]{3,2,1,0:T(8,128)S(1)}, f32[35,8,128]{2,1,0:T(8,128)S(1)}, f32[35,8,128]{2,1,0:T(8,128)S(1)}, f32[6,8,128]{2,1,0:T(8,128)S(1)}...) custom-call(f32[4]{0:T(128)S(1)} %copy-done.9, f32[4]{0:T(128)S(1)} %copy-done.8, ...), custom_call_target="tpu_custom_call" | custom-call | flops 1000 | bytes 1000 | tf_op jit(solution)/shard_map/pallas_call | solution.py:1124
  27.4 1.7 %collective-permute-start.10 = (f32[35,8,128]{2,1,0:T(8,128)S(1)}, f32[35,8,128]{2,1,0:T(8,128)S(1)}, u32[]{:S(2)}, u32[]{:S(2)}) collective-permute-start(f32[35,8,128]{2,1,0:T(8,128)S(1)} %get-tuple-element.71.refs_11_.refs_9_), channel_id=1, source_target_pairs={{0,30},{1,31},{2,4},{3,5},{4,2},{5,3},{6,8},{7,9},{8,6},{9,7},{10,... | collective-permute-start | bytes 430088 | tf_op jit(solution)/shard_map/ppermute | solution.py:46
  30.4 1.5 %collective-permute-start.15 = (f32[9,8,128]{2,1,0:T(8,128)S(1)}, f32[9,8,128]{2,1,0:T(8,128)S(1)}, u32[]{:S(2)}, u32[]{:S(2)}) collective-permute-start(f32[9,8,128]{2,1,0:T(8,128)S(1)} %get-tuple-element.81), channel_id=1, source_target_pairs={{0,6},{1,13},{2,8},{3,15},{4,10},{5,17},{6,12},{7,19},{8,14},{9,21... | collective-permute-start | bytes 110600 | tf_op jit(solution)/shard_map/ppermute | solution.py:65
  31.9 1.1 %collective-permute-start.16 = (f32[9,8,128]{2,1,0:T(8,128)S(1)}, f32[9,8,128]{2,1,0:T(8,128)S(1)}, u32[]{:S(2)}, u32[]{:S(2)}) collective-permute-start(f32[9,8,128]{2,1,0:T(8,128)S(1)} %get-tuple-element.82), channel_id=1, source_target_pairs={{0,8},{1,15},{2,10},{3,17},{4,12},{5,19},{6,14},{7,21},{8,16},{9,2... | collective-permute-start | bytes 110600 | tf_op jit(solution)/shard_map/ppermute | solution.py:65
  33.0 3.2 %shard_map.173 = (f32[5,2,128,128]{3,2,1,0:T(8,128)S(1)}, f32[160,256]{1,0:T(8,128)S(1)}, f32[2,2,128,128]{3,2,1,0:T(8,128)S(1)}) custom-call(f32[4]{0:T(128)S(1)} %copy-done.9, f32[4]{0:T(128)S(1)} %copy-done.8, f32[4]{0:T(128)S(1)} %collective-permute-done.1.refs_6_.refs_2_, f32[4]{0:T(128)S(1)} %collective-permute-done.2.refs_7_.refs_3_, ...), custom_call_target="tpu_custom_call" | custom-call | flops 1000 | bytes 1000 | tf_op jit(solution)/shard_map/pallas_call | solution.py:1124
  36.2 1.6 %collective-permute-done.10.refs_10_.refs_13_ = f32[35,8,128]{2,1,0:T(8,128)S(1)} collective-permute-done((f32[35,8,128]{2,1,0:T(8,128)S(1)}, f32[35,8,128]{2,1,0:T(8,128)S(1)}, u32[]{:S(2)}, u32[]{:S(2)}) %collective-permute-start.10) | collective-permute-done | bytes 143392 | tf_op jit(solution)/shard_map/ppermute | solution.py:46
  37.8 1.3 %shard_map.174 = (f32[224,256]{1,0:T(8,128)S(1)}, f32[21,8,128]{2,1,0:T(8,128)S(1)}, f32[21,8,128]{2,1,0:T(8,128)S(1)}) custom-call(f32[4]{0:T(128)S(1)} %copy-done.9, f32[4]{0:T(128)S(1)} %copy-done.8, f32[4]{0:T(128)S(1)} %collective-permute-done.1.refs_6_.refs_2_, f32[4]{0:T(128)S(1)} %collective-permute-done.2.refs_7_.refs_3_, ...), custom_call_target="tpu_custom_call" | custom-call | flops 1000 | bytes 1000 | tf_op jit(solution)/shard_map/pallas_call | solution.py:1124
  39.6 2.8 %collective-permute-start.13 = (f32[21,8,128]{2,1,0:T(8,128)S(1)}, f32[21,8,128]{2,1,0:T(8,128)S(1)}, u32[]{:S(2)}, u32[]{:S(2)}) collective-permute-start(f32[21,8,128]{2,1,0:T(8,128)S(1)} %get-tuple-element.76.refs_10_.refs_11_), channel_id=1, source_target_pairs={{0,2},{1,3},{2,0},{3,1},{4,6},{5,7},{6,4},{7,5},{8,10},{9,11},{10,... | collective-permute-start | bytes 258056 | tf_op jit(solution)/shard_map/ppermute | solution.py:46
  43.1 2.6 %shard_map.175.refs_9_ = f32[5,2,128,128]{3,2,1,0:T(8,128)S(1)} custom-call(f32[4]{0:T(128)S(1)} %copy-done.9, f32[4]{0:T(128)S(1)} %copy-done.8, f32[4]{0:T(128)S(1)} %collective-permute-done.1.refs_6_.refs_2_, f32[4]{0:T(128)S(1)} %collective-permute-done.2.refs_7_.refs_3_, bf16[256,256]{1,0:T(8,128)(2,1)S(1)} %copy-done.2, ...), custom_call_target="tpu_custom_call" | custom-call | flops 1000 | bytes 1000 | tf_op jit(solution)/shard_map/pallas_call | solution.py:1124
  45.7 1.3 %shard_map.177 = (f32[5,2,128,128]{3,2,1,0:T(8,128)S(1)}, f32[160,256]{1,0:T(8,128)S(1)}) custom-call(f32[4]{0:T(128)S(1)} %copy-done.9, f32[4]{0:T(128)S(1)} %copy-done.8, f32[4]{0:T(128)S(1)} %collective-permute-done.1.refs_6_.refs_2_, f32[4]{0:T(128)S(1)} %collective-permute-done.2.refs_7_.refs_3_, bf16[256,256]{1,0:T(8,128)(2,1)S(1)} %copy-done.2, ...), custom_call_target="tpu_custom_call" | custom-call | flops 1000 | bytes 1000 | tf_op jit(solution)/shard_map/pallas_call | solution.py:1124
  47.0 1.1 %shard_map.178 = (f32[160,256]{1,0:T(8,128)S(1)}, f32[21,8,128]{2,1,0:T(8,128)S(1)}, f32[21,8,128]{2,1,0:T(8,128)S(1)}) custom-call(f32[4]{0:T(128)S(1)} %copy-done.9, f32[4]{0:T(128)S(1)} %copy-done.8, f32[4]{0:T(128)S(1)} %collective-permute-done.1.refs_6_.refs_2_, f32[4]{0:T(128)S(1)} %collective-permute-done.2.refs_7_.refs_3_, ...), custom_call_target="tpu_custom_call" | custom-call | flops 1000 | bytes 1000 | tf_op jit(solution)/shard_map/pallas_call | solution.py:1124
  49.8 3.1 %shard_map.179 = (f32[5,2,128,128]{3,2,1,0:T(8,128)S(1)}, f32[160,256]{1,0:T(8,128)S(1)}) custom-call(f32[4]{0:T(128)S(1)} %copy-done.9, f32[4]{0:T(128)S(1)} %copy-done.8, f32[4]{0:T(128)S(1)} %collective-permute-done.1.refs_6_.refs_2_, f32[4]{0:T(128)S(1)} %collective-permute-done.2.refs_7_.refs_3_, bf16[256,256]{1,0:T(8,128)(2,1)S(1)} %copy-done.2, ...), custom_call_target="tpu_custom_call" | custom-call | flops 1000 | bytes 1000 | tf_op jit(solution)/shard_map/pallas_call | solution.py:1124
  52.9 1.2 %collective-permute-done.19.refs_12_ = f32[21,8,128]{2,1,0:T(8,128)S(1)} collective-permute-done((f32[21,8,128]{2,1,0:T(8,128)S(1)}, f32[21,8,128]{2,1,0:T(8,128)S(1)}, u32[]{:S(2)}, u32[]{:S(2)}) %collective-permute-start.19) | collective-permute-done | bytes 86048 | tf_op jit(solution)/shard_map/ppermute | solution.py:46
  55.3 2.4 %collective-permute-start.21 = (f32[21,8,128]{2,1,0:T(8,128)S(1)}, f32[21,8,128]{2,1,0:T(8,128)S(1)}, u32[]{:S(2)}, u32[]{:S(2)}) collective-permute-start(f32[21,8,128]{2,1,0:T(8,128)S(1)} %get-tuple-element.90.refs_10_.refs_11_), channel_id=1, source_target_pairs={{0,2},{1,3},{2,0},{3,1},{4,6},{5,7},{6,4},{7,5},{8,10},{9,11},{10,... | collective-permute-start | bytes 258056 | tf_op jit(solution)/shard_map/ppermute | solution.py:46
  57.6 1.5 %shard_map.183 = f32[4,2,4096]{2,1,0:T(2,128)} custom-call(f32[4]{0:T(128)S(1)} %copy-done.9, f32[4]{0:T(128)S(1)} %copy-done.8, f32[4]{0:T(128)S(1)} %collective-permute-done.1.refs_6_.refs_2_, f32[4]{0:T(128)S(1)} %collective-permute-done.2.refs_7_.refs_3_, bf16[256,256]{1,0:T(8,128)(2,1)S(1)} %copy-done.2, bf16[128,256]{1,0:T(8,128)(2,1)S(1)} %copy-done.3, ...), custom_call_target="tpu_custom_call" | custom-call | flops 1000 | bytes 1000 | tf_op jit(solution)/shard_map/pallas_call | solution.py:1124
  59.2 2.2 %shard_map.181.refs_13_ = f32[4,2,128,128]{3,2,1,0:T(8,128)S(1)} custom-call(f32[4]{0:T(128)S(1)} %copy-done.9, f32[4]{0:T(128)S(1)} %copy-done.8, f32[4]{0:T(128)S(1)} %collective-permute-done.1.refs_6_.refs_2_, f32[4]{0:T(128)S(1)} %collective-permute-done.2.refs_7_.refs_3_, bf16[256,256]{1,0:T(8,128)(2,1)S(1)} %copy-done.2, ...), custom_call_target="tpu_custom_call" | custom-call | flops 1000 | bytes 1000 | tf_op jit(solution)/shard_map/pallas_call | solution.py:1124
  61.4 2.1 %shard_map.182 = f32[4,8,4096]{2,1,0:T(8,128)} custom-call(f32[4]{0:T(128)S(1)} %copy-done.9, f32[4]{0:T(128)S(1)} %copy-done.8, f32[4]{0:T(128)S(1)} %collective-permute-done.1.refs_6_.refs_2_, f32[4]{0:T(128)S(1)} %collective-permute-done.2.refs_7_.refs_3_, bf16[256,256]{1,0:T(8,128)(2,1)S(1)} %copy-done.2, bf16[128,256]{1,0:T(8,128)(2,1)S(1)} %copy-done.3, ...), custom_call_target="tpu_custom_call" | custom-call | flops 1000 | bytes 1000 | tf_op jit(solution)/shard_map/pallas_call | solution.py:1124
  (67 shorter events, 10.7 us)
Async XLA Ops:
  4.3 18.2 %copy-start.1 = (bf16[256,1024]{1,0:T(8,128)(2,1)S(1)}, bf16[256,1024]{1,0:T(8,128)(2,1)}, u32[]{:S(2)}) copy-start(bf16[256,1024]{1,0:T(8,128)(2,1)} %constant.12.clone.refs_6_) | copy-start | bytes 1572868
  4.3 18.2 %copy-start.2 = (bf16[256,256]{1,0:T(8,128)(2,1)S(1)}, bf16[256,256]{1,0:T(8,128)(2,1)}, u32[]{:S(2)}) copy-start(bf16[256,256]{1,0:T(8,128)(2,1)} %constant.10.clone.refs_4_) | copy-start | bytes 393220
  4.3 1.9 %collective-permute-start = (f32[6,4,4096]{2,1,0:T(4,128)S(1)}, f32[6,4,4096]{2,1,0:T(4,128)S(1)}, u32[]{:S(2)}, u32[]{:S(2)}) collective-permute-start(f32[6,4,4096]{2,1,0:T(4,128)S(1)} %shard_map.168.refs_0_.refs_4_), channel_id=1, source_target_pairs={{0,1},{1,0},{2,3},{3,2},{4,5},{5,4},{6,7},{7,6},{8,9},{9,8},{10,11... | collective-permute-start | bytes 1179656 | tf_op jit(solution)/shard_map/ppermute | solution.py:33
  4.8 1.4 %collective-permute-start.2 = (f32[4]{0:T(128)S(1)}, f32[4]{0:T(128)S(1)}, u32[]{:S(2)}, u32[]{:S(2)}) collective-permute-start(f32[4]{0:T(128)S(1)} %copy-done.8), channel_id=1, source_target_pairs={{0,1},{1,0},{2,3},{3,2},{4,5},{5,4},{6,7},{7,6},{8,9},{9,8},{10,11... | collective-permute-start | bytes 56 | tf_op jit(solution)/shard_map/ppermute | solution.py:33
  4.9 1.3 %collective-permute-start.1 = (f32[4]{0:T(128)S(1)}, f32[4]{0:T(128)S(1)}, u32[]{:S(2)}, u32[]{:S(2)}) collective-permute-start(f32[4]{0:T(128)S(1)} %copy-done.9), channel_id=1, source_target_pairs={{0,1},{1,0},{2,3},{3,2},{4,5},{5,4},{6,7},{7,6},{8,9},{9,8},{10,11... | collective-permute-start | bytes 56 | tf_op jit(solution)/shard_map/ppermute | solution.py:33
  6.2 9.3 %collective-permute-start.7 = (f32[8,8,4096]{2,1,0:T(8,128)S(1)}, f32[8,8,4096]{2,1,0:T(8,128)S(1)}, u32[]{:S(2)}, u32[]{:S(2)}) collective-permute-start(f32[8,8,4096]{2,1,0:T(8,128)S(1)} %shard_map.167.refs_3_.refs_0_), channel_id=1, source_target_pairs={{0,1},{1,0},{2,3},{3,2},{4,5},{5,4},{6,7},{7,6},{8,9},{9,8},{10,11... | collective-permute-start | bytes 3145736 | tf_op jit(solution)/shard_map/ppermute | solution.py:33
  6.6 16.6 %collective-permute-start.8 = (f32[4,8,4096]{2,1,0:T(8,128)S(1)}, f32[4,8,4096]{2,1,0:T(8,128)S(1)}, u32[]{:S(2)}, u32[]{:S(2)}) collective-permute-start(f32[4,8,4096]{2,1,0:T(8,128)S(1)} %copy-done.5), channel_id=1, source_target_pairs={{0,1},{1,0},{2,3},{3,2},{4,5},{5,4},{6,7},{7,6},{8,9},{9,8},{10,11... | collective-permute-start | bytes 1572872 | tf_op jit(solution)/shard_map/ppermute | solution.py:33
  8.5 14.0 %collective-permute-start.5 = (f32[18,8,128]{2,1,0:T(8,128)S(1)}, f32[18,8,128]{2,1,0:T(8,128)S(1)}, u32[]{:S(2)}, u32[]{:S(2)}) collective-permute-start(f32[18,8,128]{2,1,0:T(8,128)S(1)} %get-tuple-element.53.refs_15_), channel_id=1, source_target_pairs={{0,2},{1,13},{2,4},{3,15},{4,6},{5,17},{6,8},{7,19},{8,10},{9,21},... | collective-permute-start | bytes 221192 | tf_op jit(solution)/shard_map/ppermute | solution.py:65
  11.4 11.1 %collective-permute-start.6 = (f32[18,8,128]{2,1,0:T(8,128)S(1)}, f32[18,8,128]{2,1,0:T(8,128)S(1)}, u32[]{:S(2)}, u32[]{:S(2)}) collective-permute-start(f32[18,8,128]{2,1,0:T(8,128)S(1)} %get-tuple-element.54.refs_16_), channel_id=1, source_target_pairs={{0,30},{1,15},{2,0},{3,17},{4,2},{5,19},{6,4},{7,21},{8,6},{9,23},... | collective-permute-start | bytes 221192 | tf_op jit(solution)/shard_map/ppermute | solution.py:65
  15.4 6.7 %collective-permute-start.3 = (f32[9,8,128]{2,1,0:T(8,128)S(1)}, f32[9,8,128]{2,1,0:T(8,128)S(1)}, u32[]{:S(2)}, u32[]{:S(2)}) collective-permute-start(f32[9,8,128]{2,1,0:T(8,128)S(1)} %get-tuple-element.51), channel_id=1, source_target_pairs={{0,4},{1,9},{2,6},{3,11},{4,8},{5,13},{6,10},{7,15},{8,12},{9,17},... | collective-permute-start | bytes 110600 | tf_op jit(solution)/shard_map/ppermute | solution.py:65
  15.4 7.0 %collective-permute-start.4 = (f32[9,8,128]{2,1,0:T(8,128)S(1)}, f32[9,8,128]{2,1,0:T(8,128)S(1)}, u32[]{:S(2)}, u32[]{:S(2)}) collective-permute-start(f32[9,8,128]{2,1,0:T(8,128)S(1)} %get-tuple-element.52), channel_id=1, source_target_pairs={{0,6},{1,11},{2,8},{3,13},{4,10},{5,15},{6,12},{7,17},{8,14},{9,19... | collective-permute-start | bytes 110600 | tf_op jit(solution)/shard_map/ppermute | solution.py:65
  23.1 1.5 %collective-permute-start.9 = (f32[42,8,128]{2,1,0:T(8,128)S(1)}, f32[42,8,128]{2,1,0:T(8,128)S(1)}, u32[]{:S(2)}, u32[]{:S(2)}) collective-permute-start(f32[42,8,128]{2,1,0:T(8,128)S(1)} %shard_map.171), channel_id=1, source_target_pairs={{0,1},{1,0},{2,3},{3,2},{4,5},{5,4},{6,7},{7,6},{8,9},{9,8},{10,11... | collective-permute-start | bytes 516104 | tf_op jit(solution)/shard_map/ppermute | solution.py:33
  27.4 10.5 %collective-permute-start.10 = (f32[35,8,128]{2,1,0:T(8,128)S(1)}, f32[35,8,128]{2,1,0:T(8,128)S(1)}, u32[]{:S(2)}, u32[]{:S(2)}) collective-permute-start(f32[35,8,128]{2,1,0:T(8,128)S(1)} %get-tuple-element.71.refs_11_.refs_9_), channel_id=1, source_target_pairs={{0,30},{1,31},{2,4},{3,5},{4,2},{5,3},{6,8},{7,9},{8,6},{9,7},{10,... | collective-permute-start | bytes 430088 | tf_op jit(solution)/shard_map/ppermute | solution.py:46
  29.1 8.8 %collective-permute-start.11 = (f32[35,8,128]{2,1,0:T(8,128)S(1)}, f32[35,8,128]{2,1,0:T(8,128)S(1)}, u32[]{:S(2)}, u32[]{:S(2)}) collective-permute-start(f32[35,8,128]{2,1,0:T(8,128)S(1)} %get-tuple-element.72.refs_10_.refs_11_), channel_id=1, source_target_pairs={{0,2},{1,3},{2,0},{3,1},{4,6},{5,7},{6,4},{7,5},{8,10},{9,11},{10,... | collective-permute-start | bytes 430088 | tf_op jit(solution)/shard_map/ppermute | solution.py:46
  29.8 12.6 %collective-permute-start.14 = (f32[9,8,128]{2,1,0:T(8,128)S(1)}, f32[9,8,128]{2,1,0:T(8,128)S(1)}, u32[]{:S(2)}, u32[]{:S(2)}) collective-permute-start(f32[9,8,128]{2,1,0:T(8,128)S(1)} %get-tuple-element.80), channel_id=1, source_target_pairs={{0,4},{1,11},{2,6},{3,13},{4,8},{5,15},{6,10},{7,17},{8,12},{9,19}... | collective-permute-start | bytes 110600 | tf_op jit(solution)/shard_map/ppermute | solution.py:65
  30.4 12.1 %collective-permute-start.15 = (f32[9,8,128]{2,1,0:T(8,128)S(1)}, f32[9,8,128]{2,1,0:T(8,128)S(1)}, u32[]{:S(2)}, u32[]{:S(2)}) collective-permute-start(f32[9,8,128]{2,1,0:T(8,128)S(1)} %get-tuple-element.81), channel_id=1, source_target_pairs={{0,6},{1,13},{2,8},{3,15},{4,10},{5,17},{6,12},{7,19},{8,14},{9,21... | collective-permute-start | bytes 110600 | tf_op jit(solution)/shard_map/ppermute | solution.py:65
  31.9 10.6 %collective-permute-start.16 = (f32[9,8,128]{2,1,0:T(8,128)S(1)}, f32[9,8,128]{2,1,0:T(8,128)S(1)}, u32[]{:S(2)}, u32[]{:S(2)}) collective-permute-start(f32[9,8,128]{2,1,0:T(8,128)S(1)} %get-tuple-element.82), channel_id=1, source_target_pairs={{0,8},{1,15},{2,10},{3,17},{4,12},{5,19},{6,14},{7,21},{8,16},{9,2... | collective-permute-start | bytes 110600 | tf_op jit(solution)/shard_map/ppermute | solution.py:65
  39.1 7.8 %collective-permute-start.12 = (f32[21,8,128]{2,1,0:T(8,128)S(1)}, f32[21,8,128]{2,1,0:T(8,128)S(1)}, u32[]{:S(2)}, u32[]{:S(2)}) collective-permute-start(f32[21,8,128]{2,1,0:T(8,128)S(1)} %get-tuple-element.75.refs_11_.refs_9_), channel_id=1, source_target_pairs={{0,1},{1,0},{2,4},{3,5},{4,2},{5,3},{6,8},{7,9},{8,6},{9,7},{10,12... | collective-permute-start | bytes 258056 | tf_op jit(solution)/shard_map/ppermute | solution.py:46
  39.6 7.3 %collective-permute-start.13 = (f32[21,8,128]{2,1,0:T(8,128)S(1)}, f32[21,8,128]{2,1,0:T(8,128)S(1)}, u32[]{:S(2)}, u32[]{:S(2)}) collective-permute-start(f32[21,8,128]{2,1,0:T(8,128)S(1)} %get-tuple-element.76.refs_10_.refs_11_), channel_id=1, source_target_pairs={{0,2},{1,3},{2,0},{3,1},{4,6},{5,7},{6,4},{7,5},{8,10},{9,11},{10,... | collective-permute-start | bytes 258056 | tf_op jit(solution)/shard_map/ppermute | solution.py:46
  43.0 2.6 %collective-permute-start.17 = (f32[18,8,128]{2,1,0:T(8,128)S(1)}, f32[18,8,128]{2,1,0:T(8,128)S(1)}, u32[]{:S(2)}, u32[]{:S(2)}) collective-permute-start(f32[18,8,128]{2,1,0:T(8,128)S(1)} %shard_map.176), channel_id=1, source_target_pairs={{0,1},{1,0},{2,3},{3,2},{4,5},{5,4},{6,7},{7,6},{8,9},{9,8},{10,11... | collective-permute-start | bytes 221192 | tf_op jit(solution)/shard_map/ppermute | solution.py:33
  48.1 4.8 %collective-permute-start.18 = (f32[21,8,128]{2,1,0:T(8,128)S(1)}, f32[21,8,128]{2,1,0:T(8,128)S(1)}, u32[]{:S(2)}, u32[]{:S(2)}) collective-permute-start(f32[21,8,128]{2,1,0:T(8,128)S(1)} %get-tuple-element.84.refs_11_.refs_9_), channel_id=1, source_target_pairs={{0,1},{1,0},{2,4},{3,5},{4,2},{5,3},{6,8},{7,9},{8,6},{9,7},{10,12... | collective-permute-start | bytes 258056 | tf_op jit(solution)/shard_map/ppermute | solution.py:46
  48.7 5.4 %collective-permute-start.19 = (f32[21,8,128]{2,1,0:T(8,128)S(1)}, f32[21,8,128]{2,1,0:T(8,128)S(1)}, u32[]{:S(2)}, u32[]{:S(2)}) collective-permute-start(f32[21,8,128]{2,1,0:T(8,128)S(1)} %get-tuple-element.85.refs_10_.refs_11_), channel_id=1, source_target_pairs={{0,2},{1,3},{2,0},{3,1},{4,6},{5,7},{6,4},{7,5},{8,10},{9,11},{10,... | collective-permute-start | bytes 258056 | tf_op jit(solution)/shard_map/ppermute | solution.py:46
  55.2 6.2 %collective-permute-start.20 = (f32[21,8,128]{2,1,0:T(8,128)S(1)}, f32[21,8,128]{2,1,0:T(8,128)S(1)}, u32[]{:S(2)}, u32[]{:S(2)}) collective-permute-start(f32[21,8,128]{2,1,0:T(8,128)S(1)} %get-tuple-element.89.refs_11_.refs_9_), channel_id=1, source_target_pairs={{0,1},{1,0},{2,4},{3,5},{4,2},{5,3},{6,8},{7,9},{8,6},{9,7},{10,12... | collective-permute-start | bytes 258056 | tf_op jit(solution)/shard_map/ppermute | solution.py:46
  55.3 6.1 %collective-permute-start.21 = (f32[21,8,128]{2,1,0:T(8,128)S(1)}, f32[21,8,128]{2,1,0:T(8,128)S(1)}, u32[]{:S(2)}, u32[]{:S(2)}) collective-permute-start(f32[21,8,128]{2,1,0:T(8,128)S(1)} %get-tuple-element.90.refs_10_.refs_11_), channel_id=1, source_target_pairs={{0,2},{1,3},{2,0},{3,1},{4,6},{5,7},{6,4},{7,5},{8,10},{9,11},{10,... | collective-permute-start | bytes 258056 | tf_op jit(solution)/shard_map/ppermute | solution.py:46
  (13 other events, 98.3 us)
